TPU v7x, 32 devices: a whole 2x2x4 slice. The times are simulated.
32 devices in a mesh: group: 2 (over y), dev: 4 (over z), tp: 4 (over x, core).
Axes of the slice: x: 2, y: 2, z: 4, core: 2. Of those that a mesh axis runs over, the one named last changes fastest.
Arguments:
- hidden: bfloat16 [256, 3584], P(('group', 'dev')), parts along dimension 0, may hold values from -6 to 6
- routes: int32 [256, 8], P(('group', 'dev')), parts along dimension 0, may hold values from 0 to 31, all different within a row; in each aligned block of 32 rows (0 to 31, 32 to 63, ...) at most 16 rows name the same one
- router_weight: bfloat16 [3584, 32], replicated, may hold values from -0.1875 to 0.1875
- gate_weight: bfloat16 [32, 3584, 1024], P('dev', None, 'tp'), may hold values from -0.09375 to 0.09375
- up_weight: bfloat16 [32, 3584, 1024], P('dev', None, 'tp'), may hold values from -0.09375 to 0.09375
- down_weight: bfloat16 [32, 1024, 3584], P('dev', 'tp'), may hold values from -0.1875 to 0.1875
- q_latent: bfloat16 [16, 128, 512], P(('group', 'dev')), parts along dimension 0, may hold values from -16 to 16
- q_rope: bfloat16 [16, 64, 128], P(('group', 'dev')), parts along dimension 0, may hold values from -4.2 to 4.2
- cache_latent: bfloat16 [16, 2048, 512], P(('group', 'dev'), 'tp'), parts along dimension 0, may hold values from -6 to 6
- cache_rope: bfloat16 [16, 64, 2048], P(('group', 'dev'), None, 'tp'), parts along dimension 0, may hold values from -8 to 8
- cache_len: int32 [16], P(('group', 'dev')), parts along dimension 0, may hold values from 512 to 2048, as said below
Outputs:
- moe_out: bfloat16 [256, 3584], P(('group', 'dev'), 'tp'), parts along dimension 0
- attended: bfloat16 [16, 128, 512], P(('group', 'dev')), parts along dimension 0
There are 2 independent parts, one for each index of `group`. A program takes and returns all parts, laid end to end along the dimension named above; an argument that names none is the same for every part. Nothing has to cross between parts.
Inputs may be any that keep to these rules, and one draw needn't show every extreme that they name: `routes`: each row names 8 different experts. In each aligned block of 32 rows (the rows of one device) no expert is named by more than 16 rows, and in some block one expert is named by exactly 16 rows. `cache_len`: some row is full in every draw.
All inputs are finite; a program needn't handle non-finite values.
Results may differ from a plain program's by a relative error of at most 0.012.
Values may be sent and summed in bfloat16 or wider, within the bound.
No kernel may reach another device: no remote copies, remote signals or barrier semaphores. Data moves between devices by JAX's collectives and lax.ppermute only.
A program may use at most 192 MiB of HBM per device.

v0:
```python
import jax
import jax.numpy as jnp
from jax import lax
from jax.sharding import PartitionSpec as P

CAP = 16


score_scale = 0.13524
route_scale = 2.5
very_low = -1e30


def merged(value, axis, join):
    gathered = jax.tree.map(
        lambda a, kind: lax.all_gather(a.astype(kind), axis),
        value,
        (jnp.bfloat16, jnp.bfloat16, jnp.bfloat16),
    )

    def take(source):
        return jax.tree.map(
            lambda a, own: lax.dynamic_index_in_dim(a, source, 0, False).astype(own.dtype),
            gathered,
            value,
        )

    return lax.fori_loop(
        1, lax.axis_size(axis), lambda source, state: join(state, take(source)), take(0)
    )


def route_weights(hidden, router_weight, routes):
    logits = jnp.dot(hidden, router_weight, preferred_element_type=jnp.float32)
    scores = jax.nn.sigmoid(logits)
    labels = jnp.arange(router_weight.shape[1], dtype=jnp.int32)
    picked = routes[:, :, None] == labels[None, None, :]
    chosen = jnp.sum(jnp.where(picked, scores[:, None, :], 0.0), axis=2)
    return route_scale * chosen / jnp.sum(chosen, axis=1, keepdims=True)


def slot_table(routes, experts, capacity):
    tokens, picks = routes.shape
    flat = routes.reshape(-1)
    onehot = (flat[:, None] == jnp.arange(experts, dtype=jnp.int32)[None, :]).astype(jnp.int32)
    before = jnp.cumsum(onehot, axis=0) - onehot
    rank = jnp.sum(before * onehot, axis=1)
    return (flat * capacity + rank).reshape(tokens, picks)


def softmax_join(first, second):
    top = jnp.maximum(first[0], second[0])
    scale_one = jnp.exp(first[0] - top)
    scale_two = jnp.exp(second[0] - top)
    total = first[1] * scale_one + second[1] * scale_two
    summed = first[2] * scale_one[..., None] + second[2] * scale_two[..., None]
    return (top, total, summed)


def attention(q_latent, q_rope, cache_latent, cache_rope, cache_len):
    span = cache_latent.shape[1]
    places = lax.axis_index("tp") * span + jnp.arange(span, dtype=jnp.int32)
    valid = places[None, :] < cache_len[:, None]
    logits = jnp.einsum("rhl,rpl->rhp", q_latent, cache_latent, preferred_element_type=jnp.float32)
    logits = logits + jnp.einsum(
        "rkh,rkp->rhp", q_rope, cache_rope, preferred_element_type=jnp.float32
    )
    logits = jnp.where(valid[:, None, :], score_scale * logits, very_low)
    top = jnp.max(logits, axis=2).astype(jnp.bfloat16).astype(jnp.float32)
    probs = jnp.where(valid[:, None, :], jnp.exp(logits - top[..., None]), 0.0)
    total = jnp.sum(probs, axis=2)
    summed = jnp.einsum(
        "rhp,rpl->rhl", probs.astype(jnp.bfloat16), cache_latent, preferred_element_type=jnp.float32
    )
    top, total, summed = merged((top, total, summed), "tp", softmax_join)
    return (summed / total[..., None]).astype(jnp.bfloat16)


def on_device(
    hidden,
    routes,
    router_weight,
    gate_weight,
    up_weight,
    down_weight,
    q_latent,
    q_rope,
    cache_latent,
    cache_rope,
    cache_len,
):
    tokens, width = hidden.shape
    picks = routes.shape[1]
    experts = router_weight.shape[1]
    local_experts = gate_weight.shape[0]
    devices = lax.axis_size("dev")
    weights = route_weights(hidden, router_weight, routes)
    slots = slot_table(routes, experts, CAP)
    targets = jnp.arange(experts * CAP, dtype=jnp.int32)
    placing = jnp.any(slots[None, :, :] == targets[:, None, None], axis=2).astype(jnp.bfloat16)
    outgoing = (
        jnp.dot(placing, hidden, preferred_element_type=jnp.float32)
        .astype(jnp.bfloat16)
        .reshape(experts, CAP, width)
    )
    arrived = lax.all_to_all(outgoing, "dev", split_axis=0, concat_axis=0, tiled=True)
    count = arrived.shape[1]
    grouped = arrived.reshape(devices, local_experts, count, width)
    gate = jnp.einsum("seck,ekf->secf", grouped, gate_weight, preferred_element_type=jnp.float32)
    up = jnp.einsum("seck,ekf->secf", grouped, up_weight, preferred_element_type=jnp.float32)
    act = (jax.nn.silu(gate) * up).astype(jnp.bfloat16)
    part = jnp.einsum("secf,efk->seck", act, down_weight, preferred_element_type=jnp.float32)
    count = part.shape[2]
    back = lax.all_to_all(
        part.astype(jnp.bfloat16).reshape(devices * local_experts, count, width),
        "dev",
        split_axis=0,
        concat_axis=0,
        tiled=True,
    )
    flat_back = back.reshape(experts * CAP, back.shape[2])
    gathered = jnp.take(flat_back, slots.reshape(-1), axis=0).reshape(tokens, picks, back.shape[2])
    combined = jnp.sum(weights[:, :, None] * gathered.astype(jnp.float32), axis=1)
    moe_sum = lax.psum_scatter(combined.astype(jnp.bfloat16), "tp", scatter_dimension=1, tiled=True)
    attended = attention(q_latent, q_rope, cache_latent, cache_rope, cache_len)
    return (moe_sum, attended)


def solution(mesh):
    in_specs = (
        P(("group", "dev"), None),
        P(("group", "dev"), None),
        P(),
        P("dev", None, "tp"),
        P("dev", None, "tp"),
        P("dev", "tp", None),
        P(("group", "dev"), None, None),
        P(("group", "dev"), None, None),
        P(("group", "dev"), "tp", None),
        P(("group", "dev"), None, "tp"),
        P(("group", "dev")),
    )
    out_specs = (P(("group", "dev"), "tp"), P(("group", "dev"), None, None))
    return jax.shard_map(
        on_device, mesh=mesh, in_specs=in_specs, out_specs=out_specs, check_vma=False
    )
```

profile of v0, /device:TPU:0, one launch (start us, length us, event | category | flops | bytes accessed | tf_op | source)
XLA Modules:
  0.0 249.2 jit_solution(17604824231381495947)
XLA Ops:
  7.2 0.8 copy.31
  9.5 2.2 convolution_convert_fusion
  11.8 88.3 %all_to_all.10 = bf16[32,16,3584]{2,1,0:T(8,128)(2,1)S(1)} all-to-all(bf16[32,16,3584]{2,1,0:T(8,128)(2,1)S(1)} %bitcast.121), channel_id=1, replica_groups=mesh['group'=2,'dev'=4,'tp'=4] {'dev'}, dimensions={0} | all-to-all | bytes 7340032 | tf_op jit(solution)/shard_map/all_to_all | solution.py:106
  100.1 8.0 %fusion.21 = f32[4,8,16,256]{3,2,0,1:T(8,128)S(1)} fusion(bf16[8,3584,256]{2,1,0:T(8,128)(2,1)} %param.16, bf16[4,8,16,3584]{3,2,1,0:T(8,128)(2,1)S(1)} %bitcast.116), kind=kOutput, calls=%fused_computation.29 | convolution fusion | flops 939524096 | bytes 18874368 | tf_op jit(solution)/shard_map/seck,ekf->secf/dot_general | solution.py:109
  108.1 2.7 %fusion.36 = bf16[4,8,16,256]{3,2,0,1:T(8,128)(2,1)S(1)} fusion(bf16[8,3584,256]{2,1,0:T(8,128)(2,1)S(1)} %bitcast.120, bf16[4,8,16,3584]{3,2,1,0:T(8,128)(2,1)S(1)} %bitcast.117, f32[4,8,16,256]{3,2,0,1:T(8,128)S(1)} %fusion.21), kind=kOutput, calls=%fused_computation.33 | convolution fusion | flops 940310528 | bytes 19136512 | tf_op jit(solution)/shard_map/seck,ekf->secf/dot_general | solution.py:110
  110.8 7.9 %fusion.14 = bf16[4,8,16,3584]{3,2,0,1:T(8,128)(2,1)S(1)} fusion(bf16[4,8,16,256]{3,2,0,1:T(8,128)(2,1)S(1)} %fusion.36, bf16[8,256,3584]{2,1,0:T(8,128)(2,1)} %param.18), kind=kOutput, calls=%fused_computation.21 | convolution fusion | flops 941359104 | bytes 18612224 | tf_op jit(solution)/shard_map/secf,efk->seck/dot_general | solution.py:112
  118.6 2.1 copy.38
  120.7 4.9 %all-to-all-start.1 = ((bf16[32,16,3584]{2,1,0:T(8,128)(2,1)}), bf16[32,16,3584]{2,1,0:T(8,128)(2,1)}, u32[]{:S(2)}, u32[]{:S(2)}) async-start(bf16[32,16,3584]{2,1,0:T(8,128)(2,1)} %bitcast.118), calls=%async_computation.1 | async-start | bytes 7340032 | tf_op jit(solution)/shard_map/all_to_all | solution.py:114
  126.7 1.1 convolution_convert_fusion.1
  127.9 5.0 %all-gather.3 = bf16[4,2,128]{2,1,0:T(2,128)(2,1)S(1)} all-gather(bf16[1,2,128]{2,1,0:T(2,128)(2,1)S(1)} %bitcast.127), channel_id=2, replica_groups=mesh['group'=2,'dev'=4,'tp'=4] {'tp'}, dimensions={0}, use_global_device_ids=true | all-gather | bytes 2560 | tf_op jit(solution)/shard_map/all_gather | solution.py:16
  133.2 5.2 %all-gather.4 = bf16[4,2,128]{2,1,0:T(2,128)(2,1)S(1)} all-gather(bf16[1,2,128]{2,1,0:T(2,128)(2,1)S(1)} %bitcast.128), channel_id=3, replica_groups=mesh['group'=2,'dev'=4,'tp'=4] {'tp'}, dimensions={0}, use_global_device_ids=true | all-gather | bytes 2560 | tf_op jit(solution)/shard_map/all_gather | solution.py:16
  139.3 7.5 %all-gather.7.cloned.1.call-done = bf16[8,128,512]{2,1,0:T(8,128)(2,1)} async-done(((bf16[2,128,512]{2,1,0:T(8,128)(2,1)}), bf16[8,128,512]{2,1,0:T(8,128)(2,1)}) %all-gather.7.cloned.1.call-update) | async-done | bytes 1048592 | tf_op jit(solution)/shard_map/all_gather | solution.py:16
  146.8 1.0 slice_convert_fusion
  147.8 58.9 %all-to-all-done.1 = bf16[32,16,3584]{2,1,0:T(8,128)(2,1)} async-done(((bf16[32,16,3584]{2,1,0:T(8,128)(2,1)}), bf16[32,16,3584]{2,1,0:T(8,128)(2,1)}, u32[]{:S(2)}, u32[]{:S(2)}) %all-to-all-start.1) | async-done | bytes 3670048 | tf_op jit(solution)/shard_map/all_to_all | solution.py:114
  206.7 6.0 %gather_fusion = bf16[256,3584]{1,0:T(8,128)(2,1)S(1)} fusion(bf16[512,3584]{1,0:T(8,128)(2,1)} %bitcast.17, s32[1024]{0:T(1024)S(1)} %pad_clamp_fusion), kind=kCustom, calls=%fused_computation | custom fusion | bytes 3671040 | tf_op jit(solution)/shard_map/jit(_take)/gather | solution.py:122
  212.8 2.4 multiply_reduce_fusion
  215.2 2.2 copy.42
  217.4 3.5 %while.19 = (s32[]{:T(128)}, f32[2,128]{1,0:T(2,128)S(1)}, f32[2,128]{1,0:T(2,128)S(1)}, f32[2,128,512]{2,1,0:T(8,128)S(1)}, bf16[4,2,128]{2,1,0:T(2,128)(2,1)S(...) while((s32[]{:T(128)}, f32[2,128]{1,0:T(2,128)S(1)}, ...), condition=%wide.region_11.12_spmd, body=%wide.region_10.11_spmd.sunk | while | flops 526341 | bytes 1320087 | solution.py:28
  217.4 1.1 fusion.76
  218.6 1.1 fusion.76
  219.8 1.1 fusion.76
  220.9 0.8 divide_convert_fusion
  221.7 19.0 %reduce-scatter.4.cloned.1.call-done = bf16[896,32]{1,0:T(8,128)(2,1)} async-done(((bf16[3584,32]{1,0:T(8,128)(2,1)}), bf16[896,32]{1,0:T(8,128)(2,1)}) %reduce-scatter.4.cloned.1.call-update) | async-done | bytes 57360
  240.7 1.7 copy.43
  (56 shorter events, 3.7 us)
Async XLA Ops:
  7.2 118.9 %copy-start = (bf16[2,512,512]{2,1,0:T(8,128)(2,1)S(1)}, bf16[2,512,512]{2,1,0:T(8,128)(2,1)}, u32[]{:S(2)}) copy-start(bf16[2,512,512]{2,1,0:T(8,128)(2,1)} %param.21) | copy-start | bytes 3145732
  9.5 98.5 %slice-start = ((s8[14680064]{0:T(1024)(128)(4,1)}), s8[4194304]{0:T(1024)(128)(4,1)S(1)}, s32[]{:S(2)}) async-start(s8[14680064]{0:T(1024)(128)(4,1)} %bitcast.119), calls=%async_computation.5 | async-start | bytes 8388608
  11.8 96.3 %slice-start.1 = ((s8[14680064]{0:T(1024)(128)(4,1)}), s8[4194304]{0:T(1024)(128)(4,1)S(1)}, s32[]{:S(2)}) async-start(s8[14680064]{0:T(1024)(128)(4,1)} %bitcast.119), calls=%async_computation.6 | async-start | bytes 8388608
  100.1 8.0 %slice-start.2 = ((s8[14680064]{0:T(1024)(128)(4,1)}), s8[4194304]{0:T(1024)(128)(4,1)S(1)}, s32[]{:S(2)}) async-start(s8[14680064]{0:T(1024)(128)(4,1)} %bitcast.119), calls=%async_computation.7 | async-start | bytes 8388608
  100.1 8.0 %slice-start.3 = ((s8[14680064]{0:T(1024)(128)(4,1)}), s8[2097152]{0:T(1024)(128)(4,1)S(1)}, s32[]{:S(2)}) async-start(s8[14680064]{0:T(1024)(128)(4,1)} %bitcast.119), calls=%async_computation.8 | async-start | bytes 4194304
  120.7 5.0 %copy-start.6 = (s32[2]{0:T(128)S(1)}, s32[2]{0:T(128)}, u32[]{:S(2)}) copy-start(s32[2]{0:T(128)} %param.23) | copy-start | bytes 28
  120.7 5.1 %copy-start.4 = (bf16[2,64,512]{2,1,0:T(8,128)(2,1)S(1)}, bf16[2,64,512]{2,1,0:T(8,128)(2,1)}, u32[]{:S(2)}) copy-start(bf16[2,64,512]{2,1,0:T(8,128)(2,1)} %param.22) | copy-start | bytes 393220
  120.7 5.1 %copy-start.5 = (bf16[2,64,128]{2,1,0:T(8,128)(2,1)S(1)}, bf16[2,64,128]{2,1,0:T(8,128)(2,1)}, u32[]{:S(2)}) copy-start(bf16[2,64,128]{2,1,0:T(8,128)(2,1)} %param.20) | copy-start | bytes 98308
  120.7 5.4 %copy-start.2 = (bf16[2,128,512]{2,1,0:T(8,128)(2,1)S(1)}, bf16[2,128,512]{2,1,0:T(8,128)(2,1)}, u32[]{:S(2)}) copy-start(bf16[2,128,512]{2,1,0:T(8,128)(2,1)} %param.19) | copy-start | bytes 786436
  120.7 86.0 %all-to-all-start.1 = ((bf16[32,16,3584]{2,1,0:T(8,128)(2,1)}), bf16[32,16,3584]{2,1,0:T(8,128)(2,1)}, u32[]{:S(2)}, u32[]{:S(2)}) async-start(bf16[32,16,3584]{2,1,0:T(8,128)(2,1)} %bitcast.118), calls=%async_computation.1 | async-start | bytes 7340032 | tf_op jit(solution)/shard_map/all_to_all | solution.py:114
  125.6 12.8 %copy-start.1 = (bf16[32,3584]{1,0:T(8,128)(2,1)S(1)}, bf16[32,3584]{1,0:T(8,128)(2,1)}, u32[]{:S(2)}) copy-start(bf16[32,3584]{1,0:T(8,128)(2,1)} %param.13) | copy-start | bytes 688132
  125.7 12.8 %copy-start.3 = (bf16[3584,32]{0,1:T(8,128)(2,1)S(1)}, bf16[3584,32]{0,1:T(8,128)(2,1)}, u32[]{:S(2)}) copy-start(bf16[3584,32]{0,1:T(8,128)(2,1)} %param.15) | copy-start | bytes 688132
  125.7 21.1 %all-gather.7.cloned.1.call-start = ((), (), s32[]{:S(2)}) async-start(), calls=%async_computation.3 | async-start | bytes 1310720 | tf_op jit(solution)/shard_map/all_gather | solution.py:16
  127.8 112.9 %reduce-scatter.4.cloned.1.call-start = ((), (), s32[]{:S(2)}) async-start(), calls=%async_computation.4 | async-start | bytes 1146880
Sparse Core Ops, SparseCore 0:
  128.6 18.0 all-gather.6
  217.5 23.1 reduce-scatter.3
where the time goes:
time: 250 us; the launch traced here: 249 us
  blocking collectives  98.5 us (39%)
  waiting for transfers between devices  85.4 us (34%)
  matrix products  22.8 us (9%)
  between operations  14.3 us (6%)
  local copies, waits for them, and re-layouts  13.4 us (5%)
  other arithmetic  9.56 us (4%)
  starting transfers between devices  4.97 us (2%)
    all_to_all x1, blocking collectives, on_device(): lax.all_to_all(outgoing, 'dev', split_axis=0, concat_axis=0, tiled=True)  88.3 us
    all_to_all x1, waiting for transfers between devices, on_device(): lax.all_to_all(part.astype(jnp.bfloat16).reshape(devices * local_experts,...  58.9 us
    unnamed x3, waiting for transfers between devices  19 us
    all_gather x2, blocking collectives, merged(): lax.all_gather(a.astype(kind), axis)  10.3 us
    dot_general x1, matrix products, on_device(): jnp.einsum('seck,ekf->secf', grouped, gate_weight, preferred_element_type...  7.96 us
    dot_general x1, matrix products, on_device(): jnp.einsum('secf,efk->seck', act, down_weight, preferred_element_type=jnp...  7.85 us
    all_gather x1, waiting for transfers between devices, merged(): lax.all_gather(a.astype(kind), axis)  7.48 us
    gather x1, local copies, waits for them, and re-layouts, on_device(): jnp.take(flat_back, slots.reshape(-1), axis=0)  6.04 us
  transfers between devices with their start and end apart: 3, of which 3 were waited for; matrix products, arithmetic and copies ran while one was open for 3% of the time, Pallas kernels for 0%

commit v1 on v0

v1 whole, which is shorter than its diff:
```python
import functools

import jax
import jax.numpy as jnp
from jax import lax
from jax.experimental import pallas as pl
from jax.experimental.pallas import tpu as pltpu
from jax.sharding import PartitionSpec as P

score_scale = 0.13524
route_scale = 2.5
very_low = -1e30
LANES = 128

f32, bf16 = jnp.float32, jnp.bfloat16
ANY = pl.BlockSpec(memory_space=pl.ANY)
VMEM = pl.BlockSpec(memory_space=pltpu.VMEM)
SMEM = pl.BlockSpec(memory_space=pltpu.SMEM)


def dot(a, b, contract=((1,), (0,))):
    return lax.dot_general(a, b, (contract, ((), ())), preferred_element_type=f32)


def send(value, axis, target):
    size = lax.axis_size(axis)
    return lax.ppermute(value, axis, [(i, target(i)) for i in range(size)])


def attend_kernel(place, q_lat, q_rope, keys, rope, lengths, *rest):
    outs, state = rest[:-1], rest[-1]
    parts = len(outs)
    rows, heads, width = q_lat.shape
    span = keys.shape[1]
    me = place[0]
    start = me * span
    lane = lax.broadcasted_iota(jnp.int32, (heads, LANES), 1)
    for r in range(rows):
        logits = dot(q_lat[r], keys[r], ((1,), (1,)))
        logits += dot(q_rope[r], rope[r], ((0,), (0,)))
        valid = lax.broadcasted_iota(jnp.int32, (heads, span), 1) + start < lengths[r]
        logits = jnp.where(valid, score_scale * logits, very_low)
        top = jnp.max(logits, axis=1, keepdims=True).astype(bf16).astype(f32)
        probs = jnp.where(valid, jnp.exp(logits - top), 0.0)
        total = jnp.sum(probs, axis=1, keepdims=True)
        high = total.astype(bf16).astype(f32)
        stats = jnp.where(lane == 0, top, jnp.where(lane == 1, high, jnp.where(lane == 2, total - high, 0.0)))
        state[r, :, :width] = dot(probs.astype(bf16), keys[r]).astype(bf16)
        state[r, :, width:] = stats.astype(bf16)
    block = heads // parts
    for s in range(parts):
        offset = pl.multiple_of(lax.rem(me + s, parts) * block, block)
        outs[s][...] = state[:, pl.ds(offset, block), :]


def attend(tp, q_latent, q_rope, cache_latent, cache_rope, cache_len, parts):
    rows, heads, width = q_latent.shape
    span = cache_latent.shape[1]
    shape = jax.ShapeDtypeStruct((rows, heads // parts, width + LANES), bf16)
    return pl.pallas_call(
        attend_kernel,
        out_shape=[shape] * parts,
        in_specs=[SMEM, VMEM, VMEM, VMEM, VMEM, SMEM],
        out_specs=[VMEM] * parts,
        scratch_shapes=[pltpu.VMEM((rows, heads, width + LANES), bf16)],
        cost_estimate=pl.CostEstimate(
            flops=4 * rows * heads * span * width, bytes_accessed=2 * rows * span * width, transcendentals=rows * heads * span
        ),
        compiler_params=pltpu.CompilerParams(vmem_limit_bytes=16 << 20),
    )(tp, q_latent, q_rope, cache_latent, cache_rope, cache_len)


def join_kernel(*refs):
    states, out = refs[:-1], refs[-1]
    rows, heads, width = out.shape
    for r in range(rows):
        stats = [s[r, :, width:].astype(f32) for s in states]
        tops = [t[:, 0:1] for t in stats]
        top = functools.reduce(jnp.maximum, tops)
        scales = [jnp.exp(t - top) for t in tops]
        total = sum(c * (t[:, 1:2] + t[:, 2:3]) for c, t in zip(scales, stats))
        summed = sum(c * s[r, :, :width].astype(f32) for c, s in zip(scales, states))
        out[r] = (summed / total).astype(bf16)


def join(states):
    rows, heads, width = states[0].shape
    return pl.pallas_call(
        join_kernel,
        out_shape=jax.ShapeDtypeStruct((rows, heads, width - LANES), bf16),
        in_specs=[VMEM] * len(states),
        out_specs=VMEM,
        cost_estimate=pl.CostEstimate(flops=1 << 20, bytes_accessed=1 << 20, transcendentals=1 << 10),
        compiler_params=pltpu.CompilerParams(vmem_limit_bytes=16 << 20),
    )(*states)


def place_kernel(place, *refs):
    blocks, out = refs[:-1], refs[-1]
    parts, size = len(blocks), blocks[0].shape[1]
    for s in range(parts):
        owner = lax.rem(place[0] + parts - s, parts)
        out[:, pl.ds(pl.multiple_of(owner * size, size), size), :] = blocks[s][...]


def place_heads(tp, blocks):
    rows, size, width = blocks[0].shape
    return pl.pallas_call(
        place_kernel,
        out_shape=jax.ShapeDtypeStruct((rows, size * len(blocks), width), bf16),
        in_specs=[SMEM] + [VMEM] * len(blocks),
        out_specs=VMEM,
        cost_estimate=pl.CostEstimate(flops=0, bytes_accessed=1 << 20, transcendentals=0),
        compiler_params=pltpu.CompilerParams(vmem_limit_bytes=16 << 20),
    )(tp, *blocks)


def pack_kernel(place, hidden, routes, out):
    half = hidden.shape[1] // 2
    picks, rows = routes.shape
    start = pl.multiple_of(lax.rem(place[1], 2) * half, half)
    out[:, :half] = hidden[:, pl.ds(start, half)]
    eye = lax.broadcasted_iota(jnp.int32, (rows, rows), 0) == lax.broadcasted_iota(jnp.int32, (rows, rows), 1)
    turned = dot(eye.astype(f32).astype(bf16), routes[...].astype(f32).astype(bf16), ((1,), (1,)))
    out[:, half:] = jnp.zeros((rows, LANES), bf16)
    out[:, half : half + picks] = turned.astype(bf16)


def pack_rows(place, hidden, routes):
    rows, width = hidden.shape
    return pl.pallas_call(
        pack_kernel,
        out_shape=jax.ShapeDtypeStruct((rows, width // 2 + LANES), bf16),
        in_specs=[SMEM, VMEM, VMEM],
        out_specs=VMEM,
        compiler_params=pltpu.CompilerParams(vmem_limit_bytes=16 << 20),
    )(place, hidden, routes.T)


def experts_kernel(shape, place, own, packs, halves, router, gate, up, down, outs, x, tags, g, u, w, act, sems):
    dev, tp = place[0], place[1]
    core = lax.rem(tp, 2)
    n_dev = len(packs)
    rows, width = own.shape
    half = width // 2
    local, _, hidden = gate.shape
    mine = pl.multiple_of(core * half, half)
    theirs = pl.multiple_of((1 - core) * half, half)

    def copies(e):
        return (
            pltpu.make_async_copy(gate.at[e], g.at[e], sems.at[0, e]),
            pltpu.make_async_copy(up.at[e], u.at[e], sems.at[1, e]),
        )

    def down_copy(e):
        return pltpu.make_async_copy(down.at[e], w.at[pl.ds(e * hidden, hidden), :], sems.at[2, e])

    for e in range(local):
        for copy in copies(e):
            copy.start()
    for e in range(local):
        down_copy(e).start()
    x[pl.ds(0, rows), :] = own[...]
    for s in range(n_dev):
        block = pl.ds(s * rows, rows)
        tags[block, :] = packs[s][:, half:]
        if s:
            x[block, pl.ds(mine, half)] = packs[s][:, :half]
            x[block, pl.ds(theirs, half)] = halves[s - 1][...]

    scores = jax.nn.sigmoid(dot(x[...], router[...], ((1,), (1,))))
    count = x.shape[0]
    experts = scores.shape[1]
    labels = lax.broadcasted_iota(jnp.int32, (count, experts), 1)
    chosen = tags[...].astype(f32).astype(jnp.int32)
    picked = labels < 0
    for k in range(shape):
        picked = picked | (labels == chosen[:, k : k + 1])
    kept = jnp.where(picked, scores, 0.0)
    weights = route_scale * kept / jnp.sum(kept, axis=1, keepdims=True)

    def expert(e, carry):
        for copy in copies(e):
            copy.wait()
        rate = jnp.sum(jnp.where(labels == dev * local + e, weights, 0.0), axis=1, keepdims=True)
        a = dot(x[...], g[e])
        b = dot(x[...], u[e])
        value = a / (1.0 + jnp.exp(-a)) * b * rate
        act[:, pl.ds(pl.multiple_of(e * hidden, hidden), hidden)] = value.astype(bf16)
        return carry

    lax.fori_loop(0, local, expert, 0)
    for e in range(local):
        down_copy(e).wait()
    if len(outs) == 1:
        outs[0][...] = dot(act[...], w[...]).astype(bf16)
        return
    ways = len(outs) // 2
    size = outs[0].shape[1]
    spot = tp // 2
    for i, out in enumerate(outs):
        side = 1 - core if i < ways else core
        owner = lax.rem(spot + i % ways, ways) * 2 + side
        start = pl.multiple_of(owner * size, size)
        out[...] = dot(act[...], w[:, pl.ds(start, size)]).astype(bf16)


def experts_call(place, own, packs, halves, router, gate, up, down, picks, n_tp):
    rows, width = own.shape
    n_dev = len(packs)
    local, _, hidden = gate.shape
    count = rows * n_dev
    n_in = 1 + len(packs) + len(halves)

    def kernel(place, *refs):
        own, rest = refs[0], refs[1:]
        packs, rest = rest[:n_dev], rest[n_dev:]
        halves, rest = rest[: n_dev - 1], rest[n_dev - 1 :]
        router, gate, up, down = rest[:4]
        outs, scratch = rest[4 : 4 + n_out], rest[4 + n_out :]
        experts_kernel(picks, place, own, packs, halves, router, gate, up, down, outs, *scratch)

    size = width // n_tp
    n_out = n_tp if size % LANES == 0 else 1
    shape = jax.ShapeDtypeStruct((count, width // n_out), bf16)
    parts = pl.pallas_call(
        kernel,
        out_shape=[shape] * n_out,
        in_specs=[SMEM] + [VMEM] * n_in + [VMEM] + [ANY] * 3,
        out_specs=[VMEM] * n_out,
        scratch_shapes=[
            pltpu.VMEM((count, width), bf16),
            pltpu.VMEM((count, LANES), bf16),
            pltpu.VMEM(gate.shape, bf16),
            pltpu.VMEM(up.shape, bf16),
            pltpu.VMEM((local * hidden, width), bf16),
            pltpu.VMEM((count, local * hidden), bf16),
            pltpu.SemaphoreType.DMA((3, local)),
        ],
        cost_estimate=pl.CostEstimate(
            flops=6 * count * local * hidden * width, bytes_accessed=6 * local * hidden * width, transcendentals=0
        ),
        compiler_params=pltpu.CompilerParams(vmem_limit_bytes=56 << 20),
    )(place, own, *packs, *halves, router, gate, up, down)
    if n_out == n_tp:
        return parts
    ways = n_tp // 2
    spot, core = place[1] // 2, place[1] % 2
    owners = [((spot + i) % ways) * 2 + side for side in (1 - core, core) for i in range(ways)]
    return [lax.dynamic_slice_in_dim(parts[0], owner * size, size, 1) for owner in owners]


def on_device(
    hidden,
    routes,
    router_weight,
    gate_weight,
    up_weight,
    down_weight,
    q_latent,
    q_rope,
    cache_latent,
    cache_rope,
    cache_len,
):
    rows, width = hidden.shape
    n_dev, n_tp = lax.axis_size("dev"), lax.axis_size("tp")
    ways = n_tp // 2
    dev, tp = lax.axis_index("dev"), lax.axis_index("tp")
    half = width // 2
    place = jnp.stack([dev, tp]).astype(jnp.int32)
    here = tp.reshape(1).astype(jnp.int32)

    def other_core(i):
        return i ^ 1

    def along_x(s):
        return lambda i: ((i // 2 + s) % ways) * 2 + i % 2

    pack = pack_rows(place, hidden, routes)
    packs = [pack] + [send(pack, "dev", lambda i: (i + s) % n_dev) for s in range(1, n_dev)]
    halves = [send(p[:, :half], "tp", other_core) for p in packs[1:]]

    states = attend(here, q_latent, q_rope, cache_latent, cache_rope, cache_len, n_tp)
    halves, states = lax.optimization_barrier((halves, states))
    parts = experts_call(place, hidden, packs, halves, router_weight.T, gate_weight, up_weight, down_weight, routes.shape[1], n_tp)
    states = [states[0]] + [send(states[s], "tp", lambda i: (i + s) % n_tp) for s in range(1, n_tp)]
    joined = join(states)
    blocks = [joined] + [send(joined, "tp", lambda i: (i + s) % n_tp) for s in range(1, n_tp)]
    attended = place_heads(here, blocks)

    got = [send(p, "tp", other_core) for p in parts[:ways]]
    sums = [(a.astype(f32) + b.astype(f32)) for a, b in zip(got, parts[ways:])]
    total = sums[0]
    for s in range(1, ways):
        total = total + send(sums[s].astype(bf16), "tp", along_x(s)).astype(f32)
    total = total.reshape(n_dev, rows, -1)
    moe = total[0]
    for s in range(1, n_dev):
        moe = moe + send(total[s].astype(bf16), "dev", lambda i: (i - s) % n_dev).astype(f32)
    return (moe.astype(bf16), attended)


def solution(mesh):
    in_specs = (
        P(("group", "dev"), None),
        P(("group", "dev"), None),
        P(),
        P("dev", None, "tp"),
        P("dev", None, "tp"),
        P("dev", "tp", None),
        P(("group", "dev"), None, None),
        P(("group", "dev"), None, None),
        P(("group", "dev"), "tp", None),
        P(("group", "dev"), None, "tp"),
        P(("group", "dev")),
    )
    out_specs = (P(("group", "dev"), "tp"), P(("group", "dev"), None, None))
    return jax.shard_map(
        on_device, mesh=mesh, in_specs=in_specs, out_specs=out_specs, check_vma=False
    )
```

time: 250 us -> 70.5 us (0.28)
  blocking collectives: 98.5 us -> 0 us
  waiting for transfers between devices: 85.4 us -> 17.3 us
  matrix products: 22.8 us -> 0 us
  Pallas kernels: 0 us -> 21.8 us
  starting transfers between devices: 4.97 us -> 20.7 us
  between operations: 14.3 us -> 0.83 us
  other arithmetic: 9.56 us -> 2.75 us
  local copies, waits for them, and re-layouts: 13.4 us -> 6.81 us
    all_to_all x1 -> x0, blocking collectives: 88.3 us -> none  [on_device(): lax.all_to_all(outgoing, 'dev', split_axis=0, concat_axis=0, tiled=True)]
    all_to_all x1 -> x0, waiting for transfers between devices: 58.9 us -> none  [on_device(): lax.all_to_all(part.astype(jnp.bfloat16).reshape(devices * local_experts,...]
    dot_general x8 -> x0, matrix products: 22.8 us -> none  [the longest x1 7.96 us: on_device(): jnp.einsum('seck,ekf->secf', grouped, gate_weight, preferred_element_type...]
    pallas_call x0 -> x5, Pallas kernels: none -> 21.8 us  [the longest x1 18.4 us: experts_call(): pl.pallas_call(kernel, out_shape=[shape] * n_out, in_specs=[SMEM] + [VMEM...]
    ppermute x0 -> x18, starting transfers between devices: none -> 20.7 us  [send(): return lax.ppermute(value, axis, [(i, target(i)) for i in range(size)])]
    unnamed x3 -> x0, waiting for transfers between devices: 19 us -> none
    ppermute x0 -> x18, waiting for transfers between devices: none -> 17.3 us  [send(): return lax.ppermute(value, axis, [(i, target(i)) for i in range(size)])]
    all_gather x2 -> x0, blocking collectives: 10.3 us -> none  [merged(): lax.all_gather(a.astype(kind), axis)]
  transfers between devices with their start and end apart: 3 -> 18, of which waited for: 3 -> 7; matrix products, arithmetic and copies ran while one was open for 3% -> 3% of each run, Pallas kernels for 0% -> 4%
where the time goes in v1:
time: 70.5 us; the launch traced here: 70.1 us
  Pallas kernels  21.8 us (31%)
  starting transfers between devices  20.7 us (29%)
  waiting for transfers between devices  17.3 us (25%)
  local copies, waits for them, and re-layouts  6.81 us (10%)
  other arithmetic  2.75 us (4%)
  between operations  0.83 us (1%)
    ppermute x18, starting transfers between devices, send(): return lax.ppermute(value, axis, [(i, target(i)) for i in range(size)])  20.7 us
    pallas_call x1, Pallas kernels, experts_call(): pl.pallas_call(kernel, out_shape=[shape] * n_out, in_specs=[SMEM] + [VMEM...  18.4 us
    ppermute x18, waiting for transfers between devices, send(): return lax.ppermute(value, axis, [(i, target(i)) for i in range(size)])  17.3 us
    unnamed x30, local copies, waits for them, and re-layouts  6.77 us
    pallas_call x1, Pallas kernels, attend(): pl.pallas_call(attend_kernel, out_shape=[shape] * parts, in_specs=[SMEM,...  1.68 us
  transfers between devices with their start and end apart: 18, of which 7 were waited for; matrix products, arithmetic and copies ran while one was open for 3% of the time, Pallas kernels for 4%

profile of v1, /device:TPU:0, one launch (start us, length us, event | category | flops | bytes accessed | tf_op | source)
XLA Modules:
  0.0 70.1 jit_solution(8490059756531519095)
XLA Ops:
  0.7 0.9 %copy-done.1 = bf16[32,3584]{1,0:T(8,128)(2,1)S(1)} copy-done((bf16[32,3584]{1,0:T(8,128)(2,1)S(1)}, bf16[32,3584]{1,0:T(8,128)(2,1)}, u32[]{:S(2)}) %copy-start.1) | copy-done | bytes 229400
  3.0 3.0 %collective-permute-start = (bf16[32,1920]{1,0:T(8,128)(2,1)S(1)}, bf16[32,1920]{1,0:T(8,128)(2,1)S(1)}, u32[]{:S(2)}, u32[]{:S(2)}) collective-permute-start(bf16[32,1920]{1,0:T(8,128)(2,1)S(1)} %shard_map.122.refs_1_), channel_id=1, source_target_pairs={{0,4},{4,8},{8,12},{12,0},{1,5},{5,9},{9,13},{13,1},{2,6},{6,10},{... | collective-permute-start | bytes 368648 | tf_op jit(solution)/shard_map/ppermute | solution.py:27
  6.0 2.6 %collective-permute-start.1 = (bf16[32,1920]{1,0:T(8,128)(2,1)S(1)}, bf16[32,1920]{1,0:T(8,128)(2,1)S(1)}, u32[]{:S(2)}, u32[]{:S(2)}) collective-permute-start(bf16[32,1920]{1,0:T(8,128)(2,1)S(1)} %shard_map.122.refs_1_), channel_id=1, source_target_pairs={{0,8},{4,12},{8,0},{12,4},{1,9},{5,13},{9,1},{13,5},{2,10},{6,14},... | collective-permute-start | bytes 368648 | tf_op jit(solution)/shard_map/ppermute | solution.py:27
  8.6 1.3 %collective-permute-start.2 = (bf16[32,1920]{1,0:T(8,128)(2,1)S(1)}, bf16[32,1920]{1,0:T(8,128)(2,1)S(1)}, u32[]{:S(2)}, u32[]{:S(2)}) collective-permute-start(bf16[32,1920]{1,0:T(8,128)(2,1)S(1)} %shard_map.122.refs_1_), channel_id=1, source_target_pairs={{0,12},{4,0},{8,4},{12,8},{1,13},{5,1},{9,5},{13,9},{2,14},{6,2},{... | collective-permute-start | bytes 368648 | tf_op jit(solution)/shard_map/ppermute | solution.py:27
  10.0 2.3 %collective-permute-done.refs_2_ = bf16[32,1920]{1,0:T(8,128)(2,1)S(1)} collective-permute-done((bf16[32,1920]{1,0:T(8,128)(2,1)S(1)}, bf16[32,1920]{1,0:T(8,128)(2,1)S(1)}, u32[]{:S(2)}, u32[]{:S(2)}) %collective-permute-start) | collective-permute-done | bytes 122912 | tf_op jit(solution)/shard_map/ppermute | solution.py:27
  12.4 4.3 %collective-permute-done.1.refs_3_ = bf16[32,1920]{1,0:T(8,128)(2,1)S(1)} collective-permute-done((bf16[32,1920]{1,0:T(8,128)(2,1)S(1)}, bf16[32,1920]{1,0:T(8,128)(2,1)S(1)}, u32[]{:S(2)}, u32[]{:S(2)}) %collective-permute-start.1) | collective-permute-done | bytes 122912 | tf_op jit(solution)/shard_map/ppermute | solution.py:27
  17.4 1.2 %copy-done = bf16[2,512,512]{2,1,0:T(8,128)(2,1)S(1)} copy-done((bf16[2,512,512]{2,1,0:T(8,128)(2,1)S(1)}, bf16[2,512,512]{2,1,0:T(8,128)(2,1)}, u32[]{:S(2)}) %copy-start) | copy-done | bytes 1048600
  18.6 0.9 %copy-done.3 = bf16[2,128,512]{2,1,0:T(8,128)(2,1)S(1)} copy-done((bf16[2,128,512]{2,1,0:T(8,128)(2,1)S(1)}, bf16[2,128,512]{2,1,0:T(8,128)(2,1)}, u32[]{:S(2)}) %copy-start.3) | copy-done | bytes 262168
  19.6 0.9 %copy-done.4 = bf16[2,64,512]{2,1,0:T(8,128)(2,1)S(1)} copy-done((bf16[2,64,512]{2,1,0:T(8,128)(2,1)S(1)}, bf16[2,64,512]{2,1,0:T(8,128)(2,1)}, u32[]{:S(2)}) %copy-start.4) | copy-done | bytes 131096
  21.9 1.7 %shard_map.123 = (bf16[2,32,640]{2,1,0:T(8,128)(2,1)S(1)}, bf16[2,32,640]{2,1,0:T(8,128)(2,1)S(1)}, bf16[2,32,640]{2,1,0:T(8,128)(2,1)S(1)}, bf16[2,32,640]{2,1,0:T(8,128)(2,1)S(1)}) custom-call(s32[1]{0:T(128)} %bitcast.1.place, bf16[2,128,512]{2,1,0:T(8,128)(2,1)S(1)} %copy-done.3, bf16[2,64,128]{2,1,0:T(8,128)(2,1)S(1)} %copy-done.5, ...), custom_call_target="tpu_custom_call" | custom-call | flops 268435456 | bytes 1048576 | tf_op jit(solution)/shard_map/pallas_call | solution.py:60
  24.3 18.4 %shard_map.124 = (bf16[128,896]{1,0:T(8,128)(2,1)}, bf16[128,896]{1,0:T(8,128)(2,1)}, bf16[128,896]{1,0:T(8,128)(2,1)}, bf16[128,896]{1,0:T(8,128)(2,1)}) custom-call(s32[2]{0:T(128)} %copy-done.7, bf16[32,3584]{1,0:T(8,128)(2,1)} %refs_0_.1, bf16[32,1920]{1,0:T(8,128)(2,1)} %copy-done.2, bf16[32,1920]{1,0:T(8,128)(2,1)} %copy-done.9, ...), custom_call_target="tpu_custom_call" | custom-call | flops 5637144576 | bytes 44040192 | tf_op jit(solution)/shard_map/pallas_call | solution.py:227
  43.4 1.2 %collective-permute-done.7 = bf16[128,896]{1,0:T(8,128)(2,1)S(1)} collective-permute-done((bf16[128,896]{1,0:T(8,128)(2,1)}, bf16[128,896]{1,0:T(8,128)(2,1)S(1)}, u32[]{:S(2)}, u32[]{:S(2)}) %collective-permute-start.7) | collective-permute-done | bytes 229408 | tf_op jit(solution)/shard_map/ppermute | solution.py:27
  44.5 1.0 %add_convert_fusion = bf16[128,896]{1,0:T(8,128)(2,1)S(1)} fusion(bf16[128,896]{1,0:T(8,128)(2,1)} %get-tuple-element.27, bf16[128,896]{1,0:T(8,128)(2,1)S(1)} %collective-permute-done.7), kind=kLoop, calls=%fused_computation.1 | loop fusion | flops 458752 | bytes 688128 | tf_op jit(solution)/shard_map/convert_element_type | solution.py:297
  45.5 1.5 %collective-permute-start.8 = (bf16[128,896]{1,0:T(8,128)(2,1)S(1)}, bf16[128,896]{1,0:T(8,128)(2,1)S(1)}, u32[]{:S(2)}, u32[]{:S(2)}) collective-permute-start(bf16[128,896]{1,0:T(8,128)(2,1)S(1)} %add_convert_fusion), channel_id=1, source_target_pairs={{0,2},{1,3},{2,0},{3,1},{4,6},{5,7},{6,4},{7,5},{8,10},{9,11},{10,... | collective-permute-start | bytes 688136 | tf_op jit(solution)/shard_map/ppermute | solution.py:27
  47.7 1.4 %collective-permute-start.14 = (bf16[2,32,640]{2,1,0:T(8,128)(2,1)S(1)}, bf16[2,32,640]{2,1,0:T(8,128)(2,1)S(1)}, u32[]{:S(2)}, u32[]{:S(2)}) collective-permute-start(bf16[2,32,640]{2,1,0:T(8,128)(2,1)S(1)} %get-tuple-element.31), channel_id=1, source_target_pairs={{0,3},{1,0},{2,1},{3,2},{4,7},{5,4},{6,5},{7,6},{8,11},{9,8},{10,9... | collective-permute-start | bytes 245768 | tf_op jit(solution)/shard_map/ppermute | solution.py:27
  49.1 5.1 %collective-permute-done.12.refs_1_ = bf16[2,32,640]{2,1,0:T(8,128)(2,1)S(1)} collective-permute-done((bf16[2,32,640]{2,1,0:T(8,128)(2,1)S(1)}, bf16[2,32,640]{2,1,0:T(8,128)(2,1)S(1)}, u32[]{:S(2)}, u32[]{:S(2)}) %collective-permute-start.12) | collective-permute-done | bytes 81952 | tf_op jit(solution)/shard_map/ppermute | solution.py:27
  54.2 1.6 %collective-permute-done.13.refs_2_ = bf16[2,32,640]{2,1,0:T(8,128)(2,1)S(1)} collective-permute-done((bf16[2,32,640]{2,1,0:T(8,128)(2,1)S(1)}, bf16[2,32,640]{2,1,0:T(8,128)(2,1)S(1)}, u32[]{:S(2)}, u32[]{:S(2)}) %collective-permute-start.13) | collective-permute-done | bytes 81952 | tf_op jit(solution)/shard_map/ppermute | solution.py:27
  56.1 0.8 %collective-permute-start.15 = (bf16[2,32,512]{2,1,0:T(8,128)(2,1)S(1)}, bf16[2,32,512]{2,1,0:T(8,128)(2,1)S(1)}, u32[]{:S(2)}, u32[]{:S(2)}) collective-permute-start(bf16[2,32,512]{2,1,0:T(8,128)(2,1)S(1)} %shard_map.125.refs_0_), channel_id=1, source_target_pairs={{0,1},{1,2},{2,3},{3,0},{4,5},{5,6},{6,7},{7,4},{8,9},{9,10},{10,1... | collective-permute-start | bytes 196616 | tf_op jit(solution)/shard_map/ppermute | solution.py:27
  56.9 1.5 %collective-permute-start.16 = (bf16[2,32,512]{2,1,0:T(8,128)(2,1)S(1)}, bf16[2,32,512]{2,1,0:T(8,128)(2,1)S(1)}, u32[]{:S(2)}, u32[]{:S(2)}) collective-permute-start(bf16[2,32,512]{2,1,0:T(8,128)(2,1)S(1)} %shard_map.125.refs_0_), channel_id=1, source_target_pairs={{0,2},{1,3},{2,0},{3,1},{4,6},{5,7},{6,4},{7,5},{8,10},{9,11},{10,... | collective-permute-start | bytes 196616 | tf_op jit(solution)/shard_map/ppermute | solution.py:27
  59.1 1.0 %fusion.3 = (bf16[128,896]{1,0:T(8,128)(2,1)S(1)}, f32[128,896]{1,0:T(8,128)S(1)}) fusion(bf16[128,896]{1,0:T(8,128)(2,1)S(1)} %collective-permute-done.8, bf16[128,896]{1,0:T(8,128)(2,1)} %get-tuple-element.25, bf16[128,896]{1,0:T(8,128)(2,1)S(1)} %collective-permute-done.6), kind=kLoop, calls=%fused_computation.7 | loop fusion | flops 688128 | bytes 1376256 | tf_op jit(solution)/shard_map/convert.2
  60.1 2.1 %collective-permute-start.10 = (bf16[32,896]{1,0:T(8,128)(2,1)S(1)}, bf16[32,896]{1,0:T(8,128)(2,1)S(1)}, u32[]{:S(2)}, u32[]{:S(2)}) collective-permute-start(bf16[32,896]{1,0:T(8,128)(2,1)S(1)} %get-tuple-element.36), channel_id=1, source_target_pairs={{0,8},{4,12},{8,0},{12,4},{1,9},{5,13},{9,1},{13,5},{2,10},{6,14},... | collective-permute-start | bytes 172040 | tf_op jit(solution)/shard_map/ppermute | solution.py:27
  62.2 2.7 %collective-permute-start.11 = (bf16[32,896]{1,0:T(8,128)(2,1)S(1)}, bf16[32,896]{1,0:T(8,128)(2,1)S(1)}, u32[]{:S(2)}, u32[]{:S(2)}) collective-permute-start(bf16[32,896]{1,0:T(8,128)(2,1)S(1)} %get-tuple-element.35), channel_id=1, source_target_pairs={{0,4},{4,8},{8,12},{12,0},{1,5},{5,9},{9,13},{13,1},{2,6},{6,10},{... | collective-permute-start | bytes 172040 | tf_op jit(solution)/shard_map/ppermute | solution.py:27
  64.9 1.1 %collective-permute-start.9 = (bf16[32,896]{1,0:T(8,128)(2,1)S(1)}, bf16[32,896]{1,0:T(8,128)(2,1)S(1)}, u32[]{:S(2)}, u32[]{:S(2)}) collective-permute-start(bf16[32,896]{1,0:T(8,128)(2,1)S(1)} %get-tuple-element.34), channel_id=1, source_target_pairs={{0,12},{4,0},{8,4},{12,8},{1,13},{5,1},{9,5},{13,9},{2,14},{6,2},{... | collective-permute-start | bytes 172040 | tf_op jit(solution)/shard_map/ppermute | solution.py:27
  66.8 2.3 %collective-permute-done.11 = bf16[32,896]{1,0:T(8,128)(2,1)S(1)} collective-permute-done((bf16[32,896]{1,0:T(8,128)(2,1)S(1)}, bf16[32,896]{1,0:T(8,128)(2,1)S(1)}, u32[]{:S(2)}, u32[]{:S(2)}) %collective-permute-start.11) | collective-permute-done | bytes 57376 | tf_op jit(solution)/shard_map/ppermute | solution.py:27
  (55 shorter events, 8.2 us)
Async XLA Ops:
  0.7 22.9 %copy-start.7 = (s32[2]{0:T(128)}, s32[2]{0:T(128)S(1)}, u32[]{:S(2)}) copy-start(s32[2]{0:T(128)S(1)} %pad_add_fusion.place) | copy-start | bytes 28
  3.0 20.7 %copy-start.2 = (bf16[32,1920]{1,0:T(8,128)(2,1)}, bf16[32,1920]{1,0:T(8,128)(2,1)S(1)}, u32[]{:S(2)}) copy-start(bf16[32,1920]{1,0:T(8,128)(2,1)S(1)} %shard_map.122.refs_1_) | copy-start | bytes 368644
  3.0 9.3 %collective-permute-start = (bf16[32,1920]{1,0:T(8,128)(2,1)S(1)}, bf16[32,1920]{1,0:T(8,128)(2,1)S(1)}, u32[]{:S(2)}, u32[]{:S(2)}) collective-permute-start(bf16[32,1920]{1,0:T(8,128)(2,1)S(1)} %shard_map.122.refs_1_), channel_id=1, source_target_pairs={{0,4},{4,8},{8,12},{12,0},{1,5},{5,9},{9,13},{13,1},{2,6},{6,10},{... | collective-permute-start | bytes 368648 | tf_op jit(solution)/shard_map/ppermute | solution.py:27
  6.0 10.7 %collective-permute-start.1 = (bf16[32,1920]{1,0:T(8,128)(2,1)S(1)}, bf16[32,1920]{1,0:T(8,128)(2,1)S(1)}, u32[]{:S(2)}, u32[]{:S(2)}) collective-permute-start(bf16[32,1920]{1,0:T(8,128)(2,1)S(1)} %shard_map.122.refs_1_), channel_id=1, source_target_pairs={{0,8},{4,12},{8,0},{12,4},{1,9},{5,13},{9,1},{13,5},{2,10},{6,14},... | collective-permute-start | bytes 368648 | tf_op jit(solution)/shard_map/ppermute | solution.py:27
  8.6 8.2 %collective-permute-start.2 = (bf16[32,1920]{1,0:T(8,128)(2,1)S(1)}, bf16[32,1920]{1,0:T(8,128)(2,1)S(1)}, u32[]{:S(2)}, u32[]{:S(2)}) collective-permute-start(bf16[32,1920]{1,0:T(8,128)(2,1)S(1)} %shard_map.122.refs_1_), channel_id=1, source_target_pairs={{0,12},{4,0},{8,4},{12,8},{1,13},{5,1},{9,5},{13,9},{2,14},{6,2},{... | collective-permute-start | bytes 368648 | tf_op jit(solution)/shard_map/ppermute | solution.py:27
  12.3 11.4 %copy-start.9 = (bf16[32,1920]{1,0:T(8,128)(2,1)}, bf16[32,1920]{1,0:T(8,128)(2,1)S(1)}, u32[]{:S(2)}) copy-start(bf16[32,1920]{1,0:T(8,128)(2,1)S(1)} %collective-permute-done.refs_2_) | copy-start | bytes 368644
  12.3 11.3 %collective-permute-start.3 = (bf16[32,1792]{1,0:T(8,128)(2,1)S(1)}, bf16[32,1792]{1,0:T(8,128)(2,1)S(1)}, u32[]{:S(2)}, u32[]{:S(2)}) collective-permute-start(bf16[32,1792]{1,0:T(8,128)(2,1)S(1)} %slice.35), channel_id=1, source_target_pairs={{0,1},{1,0},{2,3},{3,2},{4,5},{5,4},{6,7},{7,6},{8,9},{9,8},{10,11... | collective-permute-start | bytes 344072 | tf_op jit(solution)/shard_map/ppermute | solution.py:27
  16.7 7.0 %copy-start.10 = (bf16[32,1920]{1,0:T(8,128)(2,1)}, bf16[32,1920]{1,0:T(8,128)(2,1)S(1)}, u32[]{:S(2)}) copy-start(bf16[32,1920]{1,0:T(8,128)(2,1)S(1)} %collective-permute-done.1.refs_3_) | copy-start | bytes 368644
  16.7 6.9 %collective-permute-start.4 = (bf16[32,1792]{1,0:T(8,128)(2,1)S(1)}, bf16[32,1792]{1,0:T(8,128)(2,1)S(1)}, u32[]{:S(2)}, u32[]{:S(2)}) collective-permute-start(bf16[32,1792]{1,0:T(8,128)(2,1)S(1)} %slice.36), channel_id=1, source_target_pairs={{0,1},{1,0},{2,3},{3,2},{4,5},{5,4},{6,7},{7,6},{8,9},{9,8},{10,11... | collective-permute-start | bytes 344072 | tf_op jit(solution)/shard_map/ppermute | solution.py:27
  16.8 6.9 %copy-start.11 = (bf16[32,1920]{1,0:T(8,128)(2,1)}, bf16[32,1920]{1,0:T(8,128)(2,1)S(1)}, u32[]{:S(2)}) copy-start(bf16[32,1920]{1,0:T(8,128)(2,1)S(1)} %collective-permute-done.2.refs_4_) | copy-start | bytes 368644
  16.9 6.8 %collective-permute-start.5 = (bf16[32,1792]{1,0:T(8,128)(2,1)S(1)}, bf16[32,1792]{1,0:T(8,128)(2,1)S(1)}, u32[]{:S(2)}, u32[]{:S(2)}) collective-permute-start(bf16[32,1792]{1,0:T(8,128)(2,1)S(1)} %slice.37), channel_id=1, source_target_pairs={{0,1},{1,0},{2,3},{3,2},{4,5},{5,4},{6,7},{7,6},{8,9},{9,8},{10,11... | collective-permute-start | bytes 344072 | tf_op jit(solution)/shard_map/ppermute | solution.py:27
  17.4 1.2 %copy-start = (bf16[2,512,512]{2,1,0:T(8,128)(2,1)S(1)}, bf16[2,512,512]{2,1,0:T(8,128)(2,1)}, u32[]{:S(2)}) copy-start(bf16[2,512,512]{2,1,0:T(8,128)(2,1)} %keys.1) | copy-start | bytes 3145732
  42.8 1.8 %collective-permute-start.7 = (bf16[128,896]{1,0:T(8,128)(2,1)}, bf16[128,896]{1,0:T(8,128)(2,1)S(1)}, u32[]{:S(2)}, u32[]{:S(2)}) collective-permute-start(bf16[128,896]{1,0:T(8,128)(2,1)} %get-tuple-element.26), channel_id=1, source_target_pairs={{0,1},{1,0},{2,3},{3,2},{4,5},{5,4},{6,7},{7,6},{8,9},{9,8},{10,11... | collective-permute-start | bytes 688136 | tf_op jit(solution)/shard_map/ppermute | solution.py:27
  42.9 16.2 %collective-permute-start.6 = (bf16[128,896]{1,0:T(8,128)(2,1)}, bf16[128,896]{1,0:T(8,128)(2,1)S(1)}, u32[]{:S(2)}, u32[]{:S(2)}) collective-permute-start(bf16[128,896]{1,0:T(8,128)(2,1)} %get-tuple-element.24), channel_id=1, source_target_pairs={{0,1},{1,0},{2,3},{3,2},{4,5},{5,4},{6,7},{7,6},{8,9},{9,8},{10,11... | collective-permute-start | bytes 688136 | tf_op jit(solution)/shard_map/ppermute | solution.py:27
  45.5 13.5 %collective-permute-start.8 = (bf16[128,896]{1,0:T(8,128)(2,1)S(1)}, bf16[128,896]{1,0:T(8,128)(2,1)S(1)}, u32[]{:S(2)}, u32[]{:S(2)}) collective-permute-start(bf16[128,896]{1,0:T(8,128)(2,1)S(1)} %add_convert_fusion), channel_id=1, source_target_pairs={{0,2},{1,3},{2,0},{3,1},{4,6},{5,7},{6,4},{7,5},{8,10},{9,11},{10,... | collective-permute-start | bytes 688136 | tf_op jit(solution)/shard_map/ppermute | solution.py:27
  47.1 7.1 %collective-permute-start.12 = (bf16[2,32,640]{2,1,0:T(8,128)(2,1)S(1)}, bf16[2,32,640]{2,1,0:T(8,128)(2,1)S(1)}, u32[]{:S(2)}, u32[]{:S(2)}) collective-permute-start(bf16[2,32,640]{2,1,0:T(8,128)(2,1)S(1)} %get-tuple-element.29), channel_id=1, source_target_pairs={{0,1},{1,2},{2,3},{3,0},{4,5},{5,6},{6,7},{7,4},{8,9},{9,10},{10,1... | collective-permute-start | bytes 245768 | tf_op jit(solution)/shard_map/ppermute | solution.py:27
  47.1 8.7 %collective-permute-start.13 = (bf16[2,32,640]{2,1,0:T(8,128)(2,1)S(1)}, bf16[2,32,640]{2,1,0:T(8,128)(2,1)S(1)}, u32[]{:S(2)}, u32[]{:S(2)}) collective-permute-start(bf16[2,32,640]{2,1,0:T(8,128)(2,1)S(1)} %get-tuple-element.30), channel_id=1, source_target_pairs={{0,2},{1,3},{2,0},{3,1},{4,6},{5,7},{6,4},{7,5},{8,10},{9,11},{10,... | collective-permute-start | bytes 245768 | tf_op jit(solution)/shard_map/ppermute | solution.py:27
  47.7 8.1 %collective-permute-start.14 = (bf16[2,32,640]{2,1,0:T(8,128)(2,1)S(1)}, bf16[2,32,640]{2,1,0:T(8,128)(2,1)S(1)}, u32[]{:S(2)}, u32[]{:S(2)}) collective-permute-start(bf16[2,32,640]{2,1,0:T(8,128)(2,1)S(1)} %get-tuple-element.31), channel_id=1, source_target_pairs={{0,3},{1,0},{2,1},{3,2},{4,7},{5,4},{6,5},{7,6},{8,11},{9,8},{10,9... | collective-permute-start | bytes 245768 | tf_op jit(solution)/shard_map/ppermute | solution.py:27
  56.1 8.9 %collective-permute-start.15 = (bf16[2,32,512]{2,1,0:T(8,128)(2,1)S(1)}, bf16[2,32,512]{2,1,0:T(8,128)(2,1)S(1)}, u32[]{:S(2)}, u32[]{:S(2)}) collective-permute-start(bf16[2,32,512]{2,1,0:T(8,128)(2,1)S(1)} %shard_map.125.refs_0_), channel_id=1, source_target_pairs={{0,1},{1,2},{2,3},{3,0},{4,5},{5,6},{6,7},{7,4},{8,9},{9,10},{10,1... | collective-permute-start | bytes 196616 | tf_op jit(solution)/shard_map/ppermute | solution.py:27
  56.9 9.1 %collective-permute-start.16 = (bf16[2,32,512]{2,1,0:T(8,128)(2,1)S(1)}, bf16[2,32,512]{2,1,0:T(8,128)(2,1)S(1)}, u32[]{:S(2)}, u32[]{:S(2)}) collective-permute-start(bf16[2,32,512]{2,1,0:T(8,128)(2,1)S(1)} %shard_map.125.refs_0_), channel_id=1, source_target_pairs={{0,2},{1,3},{2,0},{3,1},{4,6},{5,7},{6,4},{7,5},{8,10},{9,11},{10,... | collective-permute-start | bytes 196616 | tf_op jit(solution)/shard_map/ppermute | solution.py:27
  58.4 7.7 %collective-permute-start.17 = (bf16[2,32,512]{2,1,0:T(8,128)(2,1)S(1)}, bf16[2,32,512]{2,1,0:T(8,128)(2,1)S(1)}, u32[]{:S(2)}, u32[]{:S(2)}) collective-permute-start(bf16[2,32,512]{2,1,0:T(8,128)(2,1)S(1)} %shard_map.125.refs_0_), channel_id=1, source_target_pairs={{0,3},{1,0},{2,1},{3,2},{4,7},{5,4},{6,5},{7,6},{8,11},{9,8},{10,9... | collective-permute-start | bytes 196616 | tf_op jit(solution)/shard_map/ppermute | solution.py:27
  60.1 6.6 %collective-permute-start.10 = (bf16[32,896]{1,0:T(8,128)(2,1)S(1)}, bf16[32,896]{1,0:T(8,128)(2,1)S(1)}, u32[]{:S(2)}, u32[]{:S(2)}) collective-permute-start(bf16[32,896]{1,0:T(8,128)(2,1)S(1)} %get-tuple-element.36), channel_id=1, source_target_pairs={{0,8},{4,12},{8,0},{12,4},{1,9},{5,13},{9,1},{13,5},{2,10},{6,14},... | collective-permute-start | bytes 172040 | tf_op jit(solution)/shard_map/ppermute | solution.py:27
  62.2 6.8 %collective-permute-start.11 = (bf16[32,896]{1,0:T(8,128)(2,1)S(1)}, bf16[32,896]{1,0:T(8,128)(2,1)S(1)}, u32[]{:S(2)}, u32[]{:S(2)}) collective-permute-start(bf16[32,896]{1,0:T(8,128)(2,1)S(1)} %get-tuple-element.35), channel_id=1, source_target_pairs={{0,4},{4,8},{8,12},{12,0},{1,5},{5,9},{9,13},{13,1},{2,6},{6,10},{... | collective-permute-start | bytes 172040 | tf_op jit(solution)/shard_map/ppermute | solution.py:27
  64.9 4.5 %collective-permute-start.9 = (bf16[32,896]{1,0:T(8,128)(2,1)S(1)}, bf16[32,896]{1,0:T(8,128)(2,1)S(1)}, u32[]{:S(2)}, u32[]{:S(2)}) collective-permute-start(bf16[32,896]{1,0:T(8,128)(2,1)S(1)} %get-tuple-element.34), channel_id=1, source_target_pairs={{0,12},{4,0},{8,4},{12,8},{1,13},{5,1},{9,5},{13,9},{2,14},{6,2},{... | collective-permute-start | bytes 172040 | tf_op jit(solution)/shard_map/ppermute | solution.py:27
  (9 other events, 6.9 us)

commit v2 on v1

v2 whole, which is shorter than its diff:
```python
import functools

import jax
import jax.numpy as jnp
from jax import lax
from jax.experimental import pallas as pl
from jax.experimental.pallas import tpu as pltpu
from jax.sharding import PartitionSpec as P

score_scale = 0.13524
route_scale = 2.5
very_low = -1e30
LANES = 128
WAIT_FLOPS = 20_000_000_000

f32, bf16 = jnp.float32, jnp.bfloat16
ANY = pl.BlockSpec(memory_space=pl.ANY)
VMEM = pl.BlockSpec(memory_space=pltpu.VMEM)
SMEM = pl.BlockSpec(memory_space=pltpu.SMEM)


def dot(a, b, contract=((1,), (0,))):
    return lax.dot_general(a, b, (contract, ((), ())), preferred_element_type=f32)


def send(value, axis, target):
    size = lax.axis_size(axis)
    return lax.ppermute(value, axis, [(i, target(i)) for i in range(size)])


def attend_kernel(q_lat, q_rope, keys, rope, lengths, *rest):
    outs, state = rest[:-1], rest[-1]
    parts = len(outs)
    rows, heads, width = q_lat.shape
    span = keys.shape[1]
    me = lax.axis_index("tp")
    start = me * span
    lane = lax.broadcasted_iota(jnp.int32, (heads, LANES), 1)
    for r in range(rows):
        logits = dot(q_lat[r], keys[r], ((1,), (1,)))
        logits += dot(q_rope[r], rope[r], ((0,), (0,)))
        valid = lax.broadcasted_iota(jnp.int32, (heads, span), 1) + start < lengths[r]
        logits = jnp.where(valid, score_scale * logits, very_low)
        top = jnp.max(logits, axis=1, keepdims=True).astype(bf16).astype(f32)
        probs = jnp.where(valid, jnp.exp(logits - top), 0.0)
        total = jnp.sum(probs, axis=1, keepdims=True)
        high = total.astype(bf16).astype(f32)
        stats = jnp.where(lane == 0, top, jnp.where(lane == 1, high, jnp.where(lane == 2, total - high, 0.0)))
        state[r, :, :width] = dot(probs.astype(bf16), keys[r]).astype(bf16)
        state[r, :, width:] = stats.astype(bf16)
    block = heads // parts
    for s in range(parts):
        offset = pl.multiple_of(lax.rem(me + s, parts) * block, block)
        outs[s][...] = state[:, pl.ds(offset, block), :]


def attend(q_latent, q_rope, cache_latent, cache_rope, cache_len, parts):
    rows, heads, width = q_latent.shape
    span = cache_latent.shape[1]
    shape = jax.ShapeDtypeStruct((rows, heads // parts, width + LANES), bf16)
    return pl.pallas_call(
        attend_kernel,
        out_shape=[shape] * parts,
        in_specs=[VMEM, VMEM, VMEM, VMEM, SMEM],
        out_specs=[VMEM] * parts,
        scratch_shapes=[pltpu.VMEM((rows, heads, width + LANES), bf16)],
        cost_estimate=pl.CostEstimate(
            flops=4 * rows * heads * span * width, bytes_accessed=2 * rows * span * width, transcendentals=rows * heads * span
        ),
        compiler_params=pltpu.CompilerParams(vmem_limit_bytes=8 << 20),
    )(q_latent, q_rope, cache_latent, cache_rope, cache_len)


def join_kernel(*refs):
    states, out = refs[:-1], refs[-1]
    rows, heads, width = out.shape
    for r in range(rows):
        stats = [s[r, :, width:].astype(f32) for s in states]
        tops = [t[:, 0:1] for t in stats]
        top = functools.reduce(jnp.maximum, tops)
        scales = [jnp.exp(t - top) for t in tops]
        total = sum(c * (t[:, 1:2] + t[:, 2:3]) for c, t in zip(scales, stats))
        summed = sum(c * s[r, :, :width].astype(f32) for c, s in zip(scales, states))
        out[r] = (summed / total).astype(bf16)


def join(states):
    rows, heads, width = states[0].shape
    return pl.pallas_call(
        join_kernel,
        out_shape=jax.ShapeDtypeStruct((rows, heads, width - LANES), bf16),
        in_specs=[VMEM] * len(states),
        out_specs=VMEM,
        cost_estimate=pl.CostEstimate(flops=1 << 20, bytes_accessed=1 << 20, transcendentals=1 << 10),
        compiler_params=pltpu.CompilerParams(vmem_limit_bytes=8 << 20),
    )(*states)


def place_kernel(*refs):
    blocks, out = refs[:-1], refs[-1]
    parts, size = len(blocks), blocks[0].shape[1]
    for s in range(parts):
        owner = lax.rem(lax.axis_index("tp") + parts - s, parts)
        out[:, pl.ds(pl.multiple_of(owner * size, size), size), :] = blocks[s][...]


def place_heads(blocks):
    rows, size, width = blocks[0].shape
    return pl.pallas_call(
        place_kernel,
        out_shape=jax.ShapeDtypeStruct((rows, size * len(blocks), width), bf16),
        in_specs=[VMEM] * len(blocks),
        out_specs=VMEM,
        cost_estimate=pl.CostEstimate(flops=0, bytes_accessed=1 << 20, transcendentals=0),
        compiler_params=pltpu.CompilerParams(vmem_limit_bytes=8 << 20),
    )(*blocks)


def pack_kernel(hidden, routes, out, tags, sems):
    half = hidden.shape[1] // 2
    picks, rows = routes.shape
    start = pl.multiple_of(lax.rem(lax.axis_index("tp"), 2) * half, half)
    columns = pltpu.make_async_copy(hidden.at[:, pl.ds(start, half)], out.at[:, pl.ds(0, half)], sems.at[0])
    named = pltpu.make_async_copy(routes, tags, sems.at[1])
    columns.start()
    named.start()
    out[:, half:] = jnp.zeros((rows, LANES), bf16)
    named.wait()
    eye = lax.broadcasted_iota(jnp.int32, (rows, rows), 0) == lax.broadcasted_iota(jnp.int32, (rows, rows), 1)
    turned = dot(eye.astype(f32).astype(bf16), tags[...].astype(f32).astype(bf16), ((1,), (1,)))
    out[:, half : half + picks] = turned.astype(bf16)
    columns.wait()


def pack_rows(hidden, routes):
    rows, width = hidden.shape
    operands = [pltpu.with_memory_space_constraint(a, pltpu.HBM) for a in (hidden, routes.T)]
    return pl.pallas_call(
        pack_kernel,
        out_shape=jax.ShapeDtypeStruct((rows, width // 2 + LANES), bf16),
        in_specs=[ANY, ANY],
        out_specs=VMEM,
        scratch_shapes=[pltpu.VMEM(routes.shape[::-1], jnp.int32), pltpu.SemaphoreType.DMA((2,))],
        cost_estimate=pl.CostEstimate(flops=WAIT_FLOPS, bytes_accessed=1 << 18, transcendentals=0),
        compiler_params=pltpu.CompilerParams(vmem_limit_bytes=2 << 20),
    )(*operands)


def experts_kernel(shape, own, packs, halves, router, gate, up, down, outs, x, tags, act):
    dev, tp = lax.axis_index("dev"), lax.axis_index("tp")
    core = lax.rem(tp, 2)
    n_dev = len(packs)
    rows, width = own.shape
    half = width // 2
    local, _, hidden = gate.shape
    mine = pl.multiple_of(core * half, half)
    theirs = pl.multiple_of((1 - core) * half, half)

    x[pl.ds(0, rows), :] = own[...]
    for s in range(n_dev):
        block = pl.ds(s * rows, rows)
        tags[block, :] = packs[s][:, half:]
        if s:
            x[block, pl.ds(mine, half)] = packs[s][:, :half]
            x[block, pl.ds(theirs, half)] = halves[s - 1][...]

    scores = jax.nn.sigmoid(dot(x[...], router[...], ((1,), (1,))))
    count = x.shape[0]
    experts = scores.shape[1]
    labels = lax.broadcasted_iota(jnp.int32, (count, experts), 1)
    chosen = tags[...].astype(f32).astype(jnp.int32)
    picked = labels < 0
    for k in range(shape):
        picked = picked | (labels == chosen[:, k : k + 1])
    kept = jnp.where(picked, scores, 0.0)
    weights = route_scale * kept / jnp.sum(kept, axis=1, keepdims=True)

    def expert(e, carry):
        rate = jnp.sum(jnp.where(labels == dev * local + e, weights, 0.0), axis=1, keepdims=True)
        a = dot(x[...], gate[e])
        b = dot(x[...], up[e])
        value = a / (1.0 + jnp.exp(-a)) * b * rate
        act[:, pl.ds(pl.multiple_of(e * hidden, hidden), hidden)] = value.astype(bf16)
        return carry

    lax.fori_loop(0, local, expert, 0)
    if len(outs) == 1:
        outs[0][...] = dot(act[...], down[...]).astype(bf16)
        return
    ways = len(outs) // 2
    size = outs[0].shape[1]
    spot = tp // 2
    for i, out in enumerate(outs):
        side = 1 - core if i < ways else core
        owner = lax.rem(spot + i % ways, ways) * 2 + side
        start = pl.multiple_of(owner * size, size)
        out[...] = dot(act[...], down[:, pl.ds(start, size)]).astype(bf16)


def experts_call(own, packs, halves, router, gate, up, down, picks, n_tp):
    rows, width = own.shape
    n_dev = len(packs)
    local, _, hidden = gate.shape
    count = rows * n_dev
    n_in = 1 + len(packs) + len(halves)

    def kernel(*refs):
        own, rest = refs[0], refs[1:]
        packs, rest = rest[:n_dev], rest[n_dev:]
        halves, rest = rest[: n_dev - 1], rest[n_dev - 1 :]
        router, gate, up, down = rest[:4]
        outs, scratch = rest[4 : 4 + n_out], rest[4 + n_out :]
        experts_kernel(picks, own, packs, halves, router, gate, up, down, outs, *scratch)

    size = width // n_tp
    n_out = n_tp if size % LANES == 0 else 1
    shape = jax.ShapeDtypeStruct((count, width // n_out), bf16)
    parts = pl.pallas_call(
        kernel,
        out_shape=[shape] * n_out,
        in_specs=[VMEM] * n_in + [VMEM] + [VMEM] * 3,
        out_specs=[VMEM] * n_out,
        scratch_shapes=[
            pltpu.VMEM((count, width), bf16),
            pltpu.VMEM((count, LANES), bf16),
            pltpu.VMEM((count, local * hidden), bf16),
        ],
        cost_estimate=pl.CostEstimate(
            flops=6 * count * local * hidden * width, bytes_accessed=6 * local * hidden * width, transcendentals=0
        ),
        compiler_params=pltpu.CompilerParams(vmem_limit_bytes=(10 if count <= 256 else 48) << 20),
    )(own, *packs, *halves, router, *[pltpu.with_memory_space_constraint(w, pltpu.VMEM) for w in (gate, up, down.reshape(local * hidden, width))])
    if n_out == n_tp:
        return parts
    ways = n_tp // 2
    spot, core = lax.axis_index("tp") // 2, lax.axis_index("tp") % 2
    owners = [((spot + i) % ways) * 2 + side for side in (1 - core, core) for i in range(ways)]
    return [lax.dynamic_slice_in_dim(parts[0], owner * size, size, 1) for owner in owners]


def on_device(
    hidden,
    routes,
    router_weight,
    gate_weight,
    up_weight,
    down_weight,
    q_latent,
    q_rope,
    cache_latent,
    cache_rope,
    cache_len,
):
    rows, width = hidden.shape
    n_dev, n_tp = lax.axis_size("dev"), lax.axis_size("tp")
    ways = n_tp // 2
    half = width // 2

    def other_core(i):
        return i ^ 1

    def along_x(s):
        return lambda i: ((i // 2 + s) % ways) * 2 + i % 2

    pack = pack_rows(hidden, routes)
    pack, q_latent = lax.optimization_barrier((pack, q_latent))
    packs = [pack] + [send(pack, "dev", lambda i: (i + s) % n_dev) for s in range(1, n_dev)]
    halves = [send(p[:, :half], "tp", other_core) for p in packs[1:]]

    states = attend(q_latent, q_rope, cache_latent, cache_rope, cache_len, n_tp)
    states = [states[0]] + [send(states[s], "tp", lambda i: (i + s) % n_tp) for s in range(1, n_tp)]
    joined = join(states)
    blocks = [joined] + [send(joined, "tp", lambda i: (i + s) % n_tp) for s in range(1, n_tp)]
    halves, blocks = lax.optimization_barrier((halves, blocks))
    parts = experts_call(hidden, packs, halves, router_weight.T, gate_weight, up_weight, down_weight, routes.shape[1], n_tp)
    got = [send(p, "tp", other_core) for p in parts[:ways]]
    sums = [(a.astype(f32) + b.astype(f32)) for a, b in zip(got, parts[ways:])]
    total = sums[0]
    for s in range(1, ways):
        total = total + send(sums[s].astype(bf16), "tp", along_x(s)).astype(f32)
    total = total.reshape(n_dev, rows, -1)
    moe = total[0]
    for s in range(1, n_dev):
        moe = moe + send(total[s].astype(bf16), "dev", lambda i: (i - s) % n_dev).astype(f32)
    return (moe.astype(bf16), place_heads(blocks))


def solution(mesh):
    in_specs = (
        P(("group", "dev"), None),
        P(("group", "dev"), None),
        P(),
        P("dev", None, "tp"),
        P("dev", None, "tp"),
        P("dev", "tp", None),
        P(("group", "dev"), None, None),
        P(("group", "dev"), None, None),
        P(("group", "dev"), "tp", None),
        P(("group", "dev"), None, "tp"),
        P(("group", "dev")),
    )
    out_specs = (P(("group", "dev"), "tp"), P(("group", "dev"), None, None))
    return jax.shard_map(
        on_device, mesh=mesh, in_specs=in_specs, out_specs=out_specs, check_vma=False
    )
```

time: 70.5 us -> 54.4 us (0.77)
  Pallas kernels: 21.8 us -> 13.1 us
  local copies, waits for them, and re-layouts: 6.81 us -> 0.25 us
  waiting for transfers between devices: 17.3 us -> 21.9 us
  starting transfers between devices: 20.7 us -> 17.4 us
  other arithmetic: 2.75 us -> 0.8 us
    pallas_call x2, Pallas kernels: 20.1 us -> 11 us  [the longest x1 9.35 us: experts_call(): pl.pallas_call(kernel, out_shape=[shape] * n_out, in_specs=[VMEM] * n_in...]
    unnamed x30 -> x18, local copies, waits for them, and re-layouts: 6.77 us -> 0.21 us
    ppermute x18, waiting for transfers between devices: 17.3 us -> 21.9 us  [send(): return lax.ppermute(value, axis, [(i, target(i)) for i in range(size)])]
    ppermute x18, starting transfers between devices: 20.7 us -> 17.4 us  [send(): return lax.ppermute(value, axis, [(i, target(i)) for i in range(size)])]
    another operation x2 -> x1, other arithmetic: 1.1 us -> 0.09 us
    convert_element_type x1, other arithmetic: 0.99 us -> 0.06 us  [on_device(): total = total + send(sums[s].astype(bf16), 'tp', along_x(s)).astype(f32)]
  transfers between devices with their start and end apart: 18 -> 18, of which waited for: 7 -> 8; matrix products, arithmetic and copies ran while one was open for 3% -> 0% of each run, Pallas kernels for 4% -> 2%
where the time goes in v2:
time: 54.4 us; the launch traced here: 54.3 us
  waiting for transfers between devices  21.9 us (40%)
  starting transfers between devices  17.4 us (32%)
  Pallas kernels  13.1 us (24%)
  between operations  0.83 us (2%)
  other arithmetic  0.8 us (1%)
    ppermute x18, waiting for transfers between devices, send(): return lax.ppermute(value, axis, [(i, target(i)) for i in range(size)])  21.9 us
    ppermute x18, starting transfers between devices, send(): return lax.ppermute(value, axis, [(i, target(i)) for i in range(size)])  17.4 us
    pallas_call x1, Pallas kernels, experts_call(): pl.pallas_call(kernel, out_shape=[shape] * n_out, in_specs=[VMEM] * n_in...  9.35 us
    pallas_call x1, Pallas kernels, attend(): pl.pallas_call(attend_kernel, out_shape=[shape] * parts, in_specs=[VMEM,...  1.68 us
  transfers between devices with their start and end apart: 18, of which 8 were waited for; matrix products, arithmetic and copies ran while one was open for 0% of the time, Pallas kernels for 2%

profile of v2, /device:TPU:0, one launch (start us, length us, event | category | flops | bytes accessed | tf_op | source)
XLA Modules:
  0.0 54.3 jit_solution(4205574856235897116)
XLA Ops:
  0.7 1.1 %shard_map.122.refs_1_ = bf16[32,1920]{1,0:T(8,128)(2,1)S(1)} custom-call(bf16[32,3584]{1,0:T(8,128)(2,1)} %refs_0_.1, s32[8,32]{1,0:T(8,128)} %bitcast.5), custom_call_target="tpu_custom_call" | custom-call | flops 20000000000 | bytes 262144 | tf_op jit(solution)/shard_map/pallas_call | solution.py:138
  2.0 1.7 %shard_map.123 = (bf16[2,32,640]{2,1,0:T(8,128)(2,1)S(1)}, bf16[2,32,640]{2,1,0:T(8,128)(2,1)S(1)}, bf16[2,32,640]{2,1,0:T(8,128)(2,1)S(1)}, bf16[2,32,640]{2,1,0:T(8,128)(2,1)S(1)}) custom-call(bf16[2,128,512]{2,1,0:T(8,128)(2,1)S(1)} %copy-done.4, bf16[2,64,128]{2,1,0:T(8,128)(2,1)S(1)} %copy-done.7, bf16[2,512,512]{2,1,0:T(8,128)(2,1)S(1)} %copy-done.3, ...), custom_call_target="tpu_custom_call" | custom-call | flops 268435456 | bytes 1048576 | tf_op jit(solution)/shard_map/pallas_call | solution.py:61
  3.7 0.5 collective-permute-start.6
  4.2 4.7 %collective-permute-start.2 = (bf16[32,1920]{1,0:T(8,128)(2,1)S(1)}, bf16[32,1920]{1,0:T(8,128)(2,1)S(1)}, u32[]{:S(2)}, u32[]{:S(2)}) collective-permute-start(bf16[32,1920]{1,0:T(8,128)(2,1)S(1)} %shard_map.122.refs_1_), channel_id=1, source_target_pairs={{0,12},{4,0},{8,4},{12,8},{1,13},{5,1},{9,5},{13,9},{2,14},{6,2},{... | collective-permute-start | bytes 368648 | tf_op jit(solution)/shard_map/ppermute | solution.py:28
  8.9 1.0 %collective-permute-start = (bf16[32,1920]{1,0:T(8,128)(2,1)S(1)}, bf16[32,1920]{1,0:T(8,128)(2,1)S(1)}, u32[]{:S(2)}, u32[]{:S(2)}) collective-permute-start(bf16[32,1920]{1,0:T(8,128)(2,1)S(1)} %shard_map.122.refs_1_), channel_id=1, source_target_pairs={{0,4},{4,8},{8,12},{12,0},{1,5},{5,9},{9,13},{13,1},{2,6},{6,10},{... | collective-permute-start | bytes 368648 | tf_op jit(solution)/shard_map/ppermute | solution.py:28
  9.9 1.5 %collective-permute-start.7 = (bf16[2,32,640]{2,1,0:T(8,128)(2,1)S(1)}, bf16[2,32,640]{2,1,0:T(8,128)(2,1)S(1)}, u32[]{:S(2)}, u32[]{:S(2)}) collective-permute-start(bf16[2,32,640]{2,1,0:T(8,128)(2,1)S(1)} %get-tuple-element.23), channel_id=1, source_target_pairs={{0,2},{1,3},{2,0},{3,1},{4,6},{5,7},{6,4},{7,5},{8,10},{9,11},{10,... | collective-permute-start | bytes 245768 | tf_op jit(solution)/shard_map/ppermute | solution.py:28
  11.4 0.6 %collective-permute-start.8 = (bf16[2,32,640]{2,1,0:T(8,128)(2,1)S(1)}, bf16[2,32,640]{2,1,0:T(8,128)(2,1)S(1)}, u32[]{:S(2)}, u32[]{:S(2)}) collective-permute-start(bf16[2,32,640]{2,1,0:T(8,128)(2,1)S(1)} %get-tuple-element.24), channel_id=1, source_target_pairs={{0,3},{1,0},{2,1},{3,2},{4,7},{5,4},{6,5},{7,6},{8,11},{9,8},{10,9... | collective-permute-start | bytes 245768 | tf_op jit(solution)/shard_map/ppermute | solution.py:28
  11.9 3.0 %collective-permute-done.7.refs_2_ = bf16[2,32,640]{2,1,0:T(8,128)(2,1)S(1)} collective-permute-done((bf16[2,32,640]{2,1,0:T(8,128)(2,1)S(1)}, bf16[2,32,640]{2,1,0:T(8,128)(2,1)S(1)}, u32[]{:S(2)}, u32[]{:S(2)}) %collective-permute-start.7) | collective-permute-done | bytes 81952 | tf_op jit(solution)/shard_map/ppermute | solution.py:28
  15.2 1.5 %collective-permute-start.11 = (bf16[2,32,512]{2,1,0:T(8,128)(2,1)S(1)}, bf16[2,32,512]{2,1,0:T(8,128)(2,1)S(1)}, u32[]{:S(2)}, u32[]{:S(2)}) collective-permute-start(bf16[2,32,512]{2,1,0:T(8,128)(2,1)S(1)} %shard_map.124.refs_0_), channel_id=1, source_target_pairs={{0,3},{1,0},{2,1},{3,2},{4,7},{5,4},{6,5},{7,6},{8,11},{9,8},{10,9... | collective-permute-start | bytes 196616 | tf_op jit(solution)/shard_map/ppermute | solution.py:28
  16.8 4.1 %collective-permute-done.1.refs_3_ = bf16[32,1920]{1,0:T(8,128)(2,1)S(1)} collective-permute-done((bf16[32,1920]{1,0:T(8,128)(2,1)S(1)}, bf16[32,1920]{1,0:T(8,128)(2,1)S(1)}, u32[]{:S(2)}, u32[]{:S(2)}) %collective-permute-start.1) | collective-permute-done | bytes 122912 | tf_op jit(solution)/shard_map/ppermute | solution.py:28
  21.6 1.1 %collective-permute-start.10 = (bf16[2,32,512]{2,1,0:T(8,128)(2,1)S(1)}, bf16[2,32,512]{2,1,0:T(8,128)(2,1)S(1)}, u32[]{:S(2)}, u32[]{:S(2)}) collective-permute-start(bf16[2,32,512]{2,1,0:T(8,128)(2,1)S(1)} %shard_map.124.refs_0_), channel_id=1, source_target_pairs={{0,2},{1,3},{2,0},{3,1},{4,6},{5,7},{6,4},{7,5},{8,10},{9,11},{10,... | collective-permute-start | bytes 196616 | tf_op jit(solution)/shard_map/ppermute | solution.py:28
  22.7 3.3 %collective-permute-done.10.refs_2_ = bf16[2,32,512]{2,1,0:T(8,128)(2,1)S(1)} collective-permute-done((bf16[2,32,512]{2,1,0:T(8,128)(2,1)S(1)}, bf16[2,32,512]{2,1,0:T(8,128)(2,1)S(1)}, u32[]{:S(2)}, u32[]{:S(2)}) %collective-permute-start.10) | collective-permute-done | bytes 65568 | tf_op jit(solution)/shard_map/ppermute | solution.py:28
  26.0 0.5 collective-permute-done.9.refs_1_
  26.6 9.3 %shard_map.125 = (bf16[128,896]{1,0:T(8,128)(2,1)S(1)}, bf16[128,896]{1,0:T(8,128)(2,1)S(1)}, bf16[128,896]{1,0:T(8,128)(2,1)S(1)}, bf16[128,896]{1,0:T(8,128)(2,1)S(1)}) custom-call(bf16[32,3584]{1,0:T(8,128)(2,1)S(1)} %copy-done.5, bf16[32,1920]{1,0:T(8,128)(2,1)S(1)} %shard_map.122.refs_1_, bf16[32,1920]{1,0:T(8,128)(2,1)S(1)} %collective-permute-done.refs_2_, ...), custom_call_target="tpu_custom_call" | custom-call | flops 5637144576 | bytes 44040192 | tf_op jit(solution)/shard_map/pallas_call | solution.py:218
  36.5 1.0 %collective-permute-done.13 = bf16[128,896]{1,0:T(8,128)(2,1)S(1)} collective-permute-done((bf16[128,896]{1,0:T(8,128)(2,1)S(1)}, bf16[128,896]{1,0:T(8,128)(2,1)S(1)}, u32[]{:S(2)}, u32[]{:S(2)}) %collective-permute-start.13) | collective-permute-done | bytes 229408 | tf_op jit(solution)/shard_map/ppermute | solution.py:28
  37.5 1.2 %collective-permute-start.14 = (bf16[128,896]{1,0:T(8,128)(2,1)S(1)}, bf16[128,896]{1,0:T(8,128)(2,1)S(1)}, u32[]{:S(2)}, u32[]{:S(2)}) collective-permute-start(bf16[128,896]{1,0:T(8,128)(2,1)S(1)} %add_convert_fusion), channel_id=1, source_target_pairs={{0,2},{1,3},{2,0},{3,1},{4,6},{5,7},{6,4},{7,5},{8,10},{9,11},{10,... | collective-permute-start | bytes 688136 | tf_op jit(solution)/shard_map/ppermute | solution.py:28
  38.8 6.5 %collective-permute-done.14 = bf16[128,896]{1,0:T(8,128)(2,1)S(1)} collective-permute-done((bf16[128,896]{1,0:T(8,128)(2,1)S(1)}, bf16[128,896]{1,0:T(8,128)(2,1)S(1)}, u32[]{:S(2)}, u32[]{:S(2)}) %collective-permute-start.14) | collective-permute-done | bytes 229408 | tf_op jit(solution)/shard_map/ppermute | solution.py:28
  45.4 1.0 %collective-permute-start.15 = (bf16[32,896]{1,0:T(8,128)(2,1)S(1)}, bf16[32,896]{1,0:T(8,128)(2,1)S(1)}, u32[]{:S(2)}, u32[]{:S(2)}) collective-permute-start(bf16[32,896]{1,0:T(8,128)(2,1)S(1)} %get-tuple-element.38), channel_id=1, source_target_pairs={{0,12},{4,0},{8,4},{12,8},{1,13},{5,1},{9,5},{13,9},{2,14},{6,2},{... | collective-permute-start | bytes 172040 | tf_op jit(solution)/shard_map/ppermute | solution.py:28
  46.4 1.0 %collective-permute-start.17 = (bf16[32,896]{1,0:T(8,128)(2,1)S(1)}, bf16[32,896]{1,0:T(8,128)(2,1)S(1)}, u32[]{:S(2)}, u32[]{:S(2)}) collective-permute-start(bf16[32,896]{1,0:T(8,128)(2,1)S(1)} %get-tuple-element.39), channel_id=1, source_target_pairs={{0,4},{4,8},{8,12},{12,0},{1,5},{5,9},{9,13},{13,1},{2,6},{6,10},{... | collective-permute-start | bytes 172040 | tf_op jit(solution)/shard_map/ppermute | solution.py:28
  47.5 1.9 %collective-permute-start.16 = (bf16[32,896]{1,0:T(8,128)(2,1)S(1)}, bf16[32,896]{1,0:T(8,128)(2,1)S(1)}, u32[]{:S(2)}, u32[]{:S(2)}) collective-permute-start(bf16[32,896]{1,0:T(8,128)(2,1)S(1)} %get-tuple-element.40), channel_id=1, source_target_pairs={{0,8},{4,12},{8,0},{12,4},{1,9},{5,13},{9,1},{13,5},{2,10},{6,14},... | collective-permute-start | bytes 172040 | tf_op jit(solution)/shard_map/ppermute | solution.py:28
  49.3 0.7 %shard_map.126 = bf16[2,128,512]{2,1,0:T(8,128)(2,1)} custom-call(bf16[2,32,512]{2,1,0:T(8,128)(2,1)S(1)} %shard_map.124.refs_0_, bf16[2,32,512]{2,1,0:T(8,128)(2,1)S(1)} %collective-permute-done.9.refs_1_, bf16[2,32,512]{2,1,0:T(8,128)(2,1)S(1)} %collective-permute-done.10.refs_2_, bf16[2,32,512]{2,1,0:T(8,128)(2,1)S(1)} %collective-permute-done.11.refs_3_), custom_call_target="tpu_custom_call" | custom-call | bytes 1048576 | tf_op jit(solution)/shard_map/pallas_call | solution.py:109
  50.1 2.3 %collective-permute-done.17 = bf16[32,896]{1,0:T(8,128)(2,1)S(1)} collective-permute-done((bf16[32,896]{1,0:T(8,128)(2,1)S(1)}, bf16[32,896]{1,0:T(8,128)(2,1)S(1)}, u32[]{:S(2)}, u32[]{:S(2)}) %collective-permute-start.17) | collective-permute-done | bytes 57376 | tf_op jit(solution)/shard_map/ppermute | solution.py:28
  52.4 1.2 %collective-permute-done.16 = bf16[32,896]{1,0:T(8,128)(2,1)S(1)} collective-permute-done((bf16[32,896]{1,0:T(8,128)(2,1)S(1)}, bf16[32,896]{1,0:T(8,128)(2,1)S(1)}, u32[]{:S(2)}, u32[]{:S(2)}) %collective-permute-start.16) | collective-permute-done | bytes 57376 | tf_op jit(solution)/shard_map/ppermute | solution.py:28
  53.6 0.7 %fusion.2 = bf16[32,896]{1,0:T(8,128)(2,1)} fusion(f32[128,896]{1,0:T(8,128)S(1)} %get-tuple-element.37, bf16[32,896]{1,0:T(8,128)(2,1)S(1)} %collective-permute-done.17, bf16[32,896]{1,0:T(8,128)(2,1)S(1)} %collective-permute-done.16, bf16[32,896]{1,0:T(8,128)(2,1)S(1)} %collective-permute-done.15), kind=kLoop, calls=%fused_computation.5 | loop fusion | flops 200704 | bytes 344064 | tf_op jit(solution)/shard_map/convert_element_type | solution.py:285
  (42 shorter events, 2.0 us)
Async XLA Ops:
  0.7 1.3 %copy-start.6 = (bf16[2,64,512]{2,1,0:T(8,128)(2,1)S(1)}, bf16[2,64,512]{2,1,0:T(8,128)(2,1)}, u32[]{:S(2)}) copy-start(bf16[2,64,512]{2,1,0:T(8,128)(2,1)} %rope.1) | copy-start | bytes 393220
  0.7 1.3 %copy-start.7 = (bf16[2,64,128]{2,1,0:T(8,128)(2,1)S(1)}, bf16[2,64,128]{2,1,0:T(8,128)(2,1)}, u32[]{:S(2)}) copy-start(bf16[2,64,128]{2,1,0:T(8,128)(2,1)} %q_rope.1) | copy-start | bytes 98308
  0.7 25.9 %copy-start = (bf16[8,3584,256]{2,1,0:T(8,128)(2,1)S(1)}, bf16[8,3584,256]{2,1,0:T(8,128)(2,1)}, u32[]{:S(2)}) copy-start(bf16[8,3584,256]{2,1,0:T(8,128)(2,1)} %refs_9_.1) | copy-start | bytes 44040196
  0.7 25.9 %copy-start.1 = (bf16[8,3584,256]{2,1,0:T(8,128)(2,1)S(1)}, bf16[8,3584,256]{2,1,0:T(8,128)(2,1)}, u32[]{:S(2)}) copy-start(bf16[8,3584,256]{2,1,0:T(8,128)(2,1)} %refs_10_.1) | copy-start | bytes 44040196
  0.7 25.9 %copy-start.2 = (bf16[8,256,3584]{2,1,0:T(8,128)(2,1)S(1)}, bf16[8,256,3584]{2,1,0:T(8,128)(2,1)}, u32[]{:S(2)}) copy-start(bf16[8,256,3584]{2,1,0:T(8,128)(2,1)} %param.16) | copy-start | bytes 44040196
  0.7 25.9 %copy-start.5 = (bf16[32,3584]{1,0:T(8,128)(2,1)S(1)}, bf16[32,3584]{1,0:T(8,128)(2,1)}, u32[]{:S(2)}) copy-start(bf16[32,3584]{1,0:T(8,128)(2,1)} %refs_0_.1) | copy-start | bytes 688132
  3.7 7.7 %collective-permute-start.6 = (bf16[2,32,640]{2,1,0:T(8,128)(2,1)S(1)}, bf16[2,32,640]{2,1,0:T(8,128)(2,1)S(1)}, u32[]{:S(2)}, u32[]{:S(2)}) collective-permute-start(bf16[2,32,640]{2,1,0:T(8,128)(2,1)S(1)} %get-tuple-element.22), channel_id=1, source_target_pairs={{0,1},{1,2},{2,3},{3,0},{4,5},{5,6},{6,7},{7,4},{8,9},{9,10},{10,1... | collective-permute-start | bytes 245768 | tf_op jit(solution)/shard_map/ppermute | solution.py:28
  4.2 12.5 %collective-permute-start.2 = (bf16[32,1920]{1,0:T(8,128)(2,1)S(1)}, bf16[32,1920]{1,0:T(8,128)(2,1)S(1)}, u32[]{:S(2)}, u32[]{:S(2)}) collective-permute-start(bf16[32,1920]{1,0:T(8,128)(2,1)S(1)} %shard_map.122.refs_1_), channel_id=1, source_target_pairs={{0,12},{4,0},{8,4},{12,8},{1,13},{5,1},{9,5},{13,9},{2,14},{6,2},{... | collective-permute-start | bytes 368648 | tf_op jit(solution)/shard_map/ppermute | solution.py:28
  8.8 12.0 %collective-permute-start.1 = (bf16[32,1920]{1,0:T(8,128)(2,1)S(1)}, bf16[32,1920]{1,0:T(8,128)(2,1)S(1)}, u32[]{:S(2)}, u32[]{:S(2)}) collective-permute-start(bf16[32,1920]{1,0:T(8,128)(2,1)S(1)} %shard_map.122.refs_1_), channel_id=1, source_target_pairs={{0,8},{4,12},{8,0},{12,4},{1,9},{5,13},{9,1},{13,5},{2,10},{6,14},... | collective-permute-start | bytes 368648 | tf_op jit(solution)/shard_map/ppermute | solution.py:28
  8.9 12.2 %collective-permute-start = (bf16[32,1920]{1,0:T(8,128)(2,1)S(1)}, bf16[32,1920]{1,0:T(8,128)(2,1)S(1)}, u32[]{:S(2)}, u32[]{:S(2)}) collective-permute-start(bf16[32,1920]{1,0:T(8,128)(2,1)S(1)} %shard_map.122.refs_1_), channel_id=1, source_target_pairs={{0,4},{4,8},{8,12},{12,0},{1,5},{5,9},{9,13},{13,1},{2,6},{6,10},{... | collective-permute-start | bytes 368648 | tf_op jit(solution)/shard_map/ppermute | solution.py:28
  9.9 5.0 %collective-permute-start.7 = (bf16[2,32,640]{2,1,0:T(8,128)(2,1)S(1)}, bf16[2,32,640]{2,1,0:T(8,128)(2,1)S(1)}, u32[]{:S(2)}, u32[]{:S(2)}) collective-permute-start(bf16[2,32,640]{2,1,0:T(8,128)(2,1)S(1)} %get-tuple-element.23), channel_id=1, source_target_pairs={{0,2},{1,3},{2,0},{3,1},{4,6},{5,7},{6,4},{7,5},{8,10},{9,11},{10,... | collective-permute-start | bytes 245768 | tf_op jit(solution)/shard_map/ppermute | solution.py:28
  11.4 3.6 %collective-permute-start.8 = (bf16[2,32,640]{2,1,0:T(8,128)(2,1)S(1)}, bf16[2,32,640]{2,1,0:T(8,128)(2,1)S(1)}, u32[]{:S(2)}, u32[]{:S(2)}) collective-permute-start(bf16[2,32,640]{2,1,0:T(8,128)(2,1)S(1)} %get-tuple-element.24), channel_id=1, source_target_pairs={{0,3},{1,0},{2,1},{3,2},{4,7},{5,4},{6,5},{7,6},{8,11},{9,8},{10,9... | collective-permute-start | bytes 245768 | tf_op jit(solution)/shard_map/ppermute | solution.py:28
  15.2 7.5 %collective-permute-start.11 = (bf16[2,32,512]{2,1,0:T(8,128)(2,1)S(1)}, bf16[2,32,512]{2,1,0:T(8,128)(2,1)S(1)}, u32[]{:S(2)}, u32[]{:S(2)}) collective-permute-start(bf16[2,32,512]{2,1,0:T(8,128)(2,1)S(1)} %shard_map.124.refs_0_), channel_id=1, source_target_pairs={{0,3},{1,0},{2,1},{3,2},{4,7},{5,4},{6,5},{7,6},{8,11},{9,8},{10,9... | collective-permute-start | bytes 196616 | tf_op jit(solution)/shard_map/ppermute | solution.py:28
  16.7 9.8 %collective-permute-start.5 = (bf16[32,1792]{1,0:T(8,128)(2,1)S(1)}, bf16[32,1792]{1,0:T(8,128)(2,1)S(1)}, u32[]{:S(2)}, u32[]{:S(2)}) collective-permute-start(bf16[32,1792]{1,0:T(8,128)(2,1)S(1)} %slice.37), channel_id=1, source_target_pairs={{0,1},{1,0},{2,3},{3,2},{4,5},{5,4},{6,7},{7,6},{8,9},{9,8},{10,11... | collective-permute-start | bytes 344072 | tf_op jit(solution)/shard_map/ppermute | solution.py:28
  20.9 5.6 %collective-permute-start.4 = (bf16[32,1792]{1,0:T(8,128)(2,1)S(1)}, bf16[32,1792]{1,0:T(8,128)(2,1)S(1)}, u32[]{:S(2)}, u32[]{:S(2)}) collective-permute-start(bf16[32,1792]{1,0:T(8,128)(2,1)S(1)} %slice.36), channel_id=1, source_target_pairs={{0,1},{1,0},{2,3},{3,2},{4,5},{5,4},{6,7},{7,6},{8,9},{9,8},{10,11... | collective-permute-start | bytes 344072 | tf_op jit(solution)/shard_map/ppermute | solution.py:28
  21.1 5.4 %collective-permute-start.3 = (bf16[32,1792]{1,0:T(8,128)(2,1)S(1)}, bf16[32,1792]{1,0:T(8,128)(2,1)S(1)}, u32[]{:S(2)}, u32[]{:S(2)}) collective-permute-start(bf16[32,1792]{1,0:T(8,128)(2,1)S(1)} %slice.35), channel_id=1, source_target_pairs={{0,1},{1,0},{2,3},{3,2},{4,5},{5,4},{6,7},{7,6},{8,9},{9,8},{10,11... | collective-permute-start | bytes 344072 | tf_op jit(solution)/shard_map/ppermute | solution.py:28
  21.6 4.4 %collective-permute-start.10 = (bf16[2,32,512]{2,1,0:T(8,128)(2,1)S(1)}, bf16[2,32,512]{2,1,0:T(8,128)(2,1)S(1)}, u32[]{:S(2)}, u32[]{:S(2)}) collective-permute-start(bf16[2,32,512]{2,1,0:T(8,128)(2,1)S(1)} %shard_map.124.refs_0_), channel_id=1, source_target_pairs={{0,2},{1,3},{2,0},{3,1},{4,6},{5,7},{6,4},{7,5},{8,10},{9,11},{10,... | collective-permute-start | bytes 196616 | tf_op jit(solution)/shard_map/ppermute | solution.py:28
  22.7 3.8 %collective-permute-start.9 = (bf16[2,32,512]{2,1,0:T(8,128)(2,1)S(1)}, bf16[2,32,512]{2,1,0:T(8,128)(2,1)S(1)}, u32[]{:S(2)}, u32[]{:S(2)}) collective-permute-start(bf16[2,32,512]{2,1,0:T(8,128)(2,1)S(1)} %shard_map.124.refs_0_), channel_id=1, source_target_pairs={{0,1},{1,2},{2,3},{3,0},{4,5},{5,6},{6,7},{7,4},{8,9},{9,10},{10,1... | collective-permute-start | bytes 196616 | tf_op jit(solution)/shard_map/ppermute | solution.py:28
  35.9 1.6 %collective-permute-start.13 = (bf16[128,896]{1,0:T(8,128)(2,1)S(1)}, bf16[128,896]{1,0:T(8,128)(2,1)S(1)}, u32[]{:S(2)}, u32[]{:S(2)}) collective-permute-start(bf16[128,896]{1,0:T(8,128)(2,1)S(1)} %get-tuple-element.30), channel_id=1, source_target_pairs={{0,1},{1,0},{2,3},{3,2},{4,5},{5,4},{6,7},{7,6},{8,9},{9,8},{10,11... | collective-permute-start | bytes 688136 | tf_op jit(solution)/shard_map/ppermute | solution.py:28
  36.0 2.7 %collective-permute-start.12 = (bf16[128,896]{1,0:T(8,128)(2,1)S(1)}, bf16[128,896]{1,0:T(8,128)(2,1)S(1)}, u32[]{:S(2)}, u32[]{:S(2)}) collective-permute-start(bf16[128,896]{1,0:T(8,128)(2,1)S(1)} %get-tuple-element.28), channel_id=1, source_target_pairs={{0,1},{1,0},{2,3},{3,2},{4,5},{5,4},{6,7},{7,6},{8,9},{9,8},{10,11... | collective-permute-start | bytes 688136 | tf_op jit(solution)/shard_map/ppermute | solution.py:28
  37.5 7.7 %collective-permute-start.14 = (bf16[128,896]{1,0:T(8,128)(2,1)S(1)}, bf16[128,896]{1,0:T(8,128)(2,1)S(1)}, u32[]{:S(2)}, u32[]{:S(2)}) collective-permute-start(bf16[128,896]{1,0:T(8,128)(2,1)S(1)} %add_convert_fusion), channel_id=1, source_target_pairs={{0,2},{1,3},{2,0},{3,1},{4,6},{5,7},{6,4},{7,5},{8,10},{9,11},{10,... | collective-permute-start | bytes 688136 | tf_op jit(solution)/shard_map/ppermute | solution.py:28
  45.4 4.7 %collective-permute-start.15 = (bf16[32,896]{1,0:T(8,128)(2,1)S(1)}, bf16[32,896]{1,0:T(8,128)(2,1)S(1)}, u32[]{:S(2)}, u32[]{:S(2)}) collective-permute-start(bf16[32,896]{1,0:T(8,128)(2,1)S(1)} %get-tuple-element.38), channel_id=1, source_target_pairs={{0,12},{4,0},{8,4},{12,8},{1,13},{5,1},{9,5},{13,9},{2,14},{6,2},{... | collective-permute-start | bytes 172040 | tf_op jit(solution)/shard_map/ppermute | solution.py:28
  46.4 6.0 %collective-permute-start.17 = (bf16[32,896]{1,0:T(8,128)(2,1)S(1)}, bf16[32,896]{1,0:T(8,128)(2,1)S(1)}, u32[]{:S(2)}, u32[]{:S(2)}) collective-permute-start(bf16[32,896]{1,0:T(8,128)(2,1)S(1)} %get-tuple-element.39), channel_id=1, source_target_pairs={{0,4},{4,8},{8,12},{12,0},{1,5},{5,9},{9,13},{13,1},{2,6},{6,10},{... | collective-permute-start | bytes 172040 | tf_op jit(solution)/shard_map/ppermute | solution.py:28
  47.5 6.2 %collective-permute-start.16 = (bf16[32,896]{1,0:T(8,128)(2,1)S(1)}, bf16[32,896]{1,0:T(8,128)(2,1)S(1)}, u32[]{:S(2)}, u32[]{:S(2)}) collective-permute-start(bf16[32,896]{1,0:T(8,128)(2,1)S(1)} %get-tuple-element.40), channel_id=1, source_target_pairs={{0,8},{4,12},{8,0},{12,4},{1,9},{5,13},{9,1},{13,5},{2,10},{6,14},... | collective-permute-start | bytes 172040 | tf_op jit(solution)/shard_map/ppermute | solution.py:28
  (3 other events, 3.9 us)

commit v3 on v0

v3 whole, which is shorter than its diff:
```python
import functools

import jax
import jax.numpy as jnp
from jax import lax
from jax.experimental import pallas as pl
from jax.experimental.pallas import tpu as pltpu
from jax.sharding import PartitionSpec as P

score_scale = 0.13524
route_scale = 2.5
very_low = -1e30
LANES = 128
WAIT_FLOPS = 20_000_000_000

f32, bf16 = jnp.float32, jnp.bfloat16
ANY = pl.BlockSpec(memory_space=pl.ANY)
VMEM = pl.BlockSpec(memory_space=pltpu.VMEM)
SMEM = pl.BlockSpec(memory_space=pltpu.SMEM)


def dot(a, b, contract=((1,), (0,))):
    return lax.dot_general(a, b, (contract, ((), ())), preferred_element_type=f32)


def send(value, axis, target):
    size = lax.axis_size(axis)
    return lax.ppermute(value, axis, [(i, target(i)) for i in range(size)])


def other_core(i):
    return i ^ 1


def along_x(shift, ways):
    return lambda i: ((i // 2 + shift) % ways) * 2 + i % 2


def spot_and_core():
    tp = lax.axis_index("tp")
    return tp // 2, lax.rem(tp, 2)


def local_call(kernel, outs, operands, specs, scratch=(), flops=0, nbytes=0, exps=0, limit=8):
    return pl.pallas_call(
        kernel,
        out_shape=outs,
        in_specs=specs,
        out_specs=jax.tree.map(lambda _: VMEM, outs),
        scratch_shapes=list(scratch),
        cost_estimate=pl.CostEstimate(flops=flops, bytes_accessed=nbytes, transcendentals=exps),
        compiler_params=pltpu.CompilerParams(vmem_limit_bytes=limit << 20),
    )(*operands)


def shaped(*shape):
    return jax.ShapeDtypeStruct(shape, bf16)


def stats_of(top, total, heads):
    lane = lax.broadcasted_iota(jnp.int32, (heads, LANES), 1)
    high = total.astype(bf16).astype(f32)
    stats = jnp.where(lane == 0, top, jnp.where(lane == 1, high, jnp.where(lane == 2, total - high, 0.0)))
    return stats.astype(bf16)


def attend_kernel(q_lat, q_rope, keys, rope, lengths, keep, give, state):
    rows, heads, width = q_lat.shape
    span = keys.shape[1]
    start = lax.axis_index("tp") * span
    for r in range(rows):
        logits = dot(q_lat[r], keys[r], ((1,), (1,)))
        logits += dot(q_rope[r], rope[r], ((0,), (0,)))
        valid = lax.broadcasted_iota(jnp.int32, (heads, span), 1) + start < lengths[r]
        logits = jnp.where(valid, score_scale * logits, very_low)
        top = jnp.max(logits, axis=1, keepdims=True).astype(bf16).astype(f32)
        probs = jnp.where(valid, jnp.exp(logits - top), 0.0)
        total = jnp.sum(probs, axis=1, keepdims=True)
        state[r, :, :width] = dot(probs.astype(bf16), keys[r]).astype(bf16)
        state[r, :, width:] = stats_of(top, total, heads)
    half = heads // 2
    core = lax.rem(lax.axis_index("tp"), 2)
    keep[...] = state[:, pl.ds(pl.multiple_of(core * half, half), half), :]
    give[...] = state[:, pl.ds(pl.multiple_of((1 - core) * half, half), half), :]


def attend(q_latent, q_rope, cache_latent, cache_rope, cache_len):
    rows, heads, width = q_latent.shape
    span = cache_latent.shape[1]
    half = shaped(rows, heads // 2, width + LANES)
    return local_call(
        attend_kernel,
        [half, half],
        [q_latent, q_rope, cache_latent, cache_rope, cache_len],
        [VMEM, VMEM, VMEM, VMEM, SMEM],
        [pltpu.VMEM((rows, heads, width + LANES), bf16)],
        flops=2_000_000_000,
    )


def join_kernel(last, *refs):
    states, out = refs[:-1], refs[-1]
    rows, heads, full = states[0].shape
    width = full - LANES
    for r in range(rows):
        stats = [s[r, :, width:].astype(f32) for s in states]
        tops = [t[:, 0:1] for t in stats]
        top = functools.reduce(jnp.maximum, tops)
        scales = [jnp.exp(t - top) for t in tops]
        total = sum(c * (t[:, 1:2] + t[:, 2:3]) for c, t in zip(scales, stats))
        summed = sum(c * s[r, :, :width].astype(f32) for c, s in zip(scales, states))
        if last:
            out[r] = (summed / total).astype(bf16)
        else:
            out[r, :, :width] = summed.astype(bf16)
            out[r, :, width:] = stats_of(top, total, heads)


def join(states, last):
    rows, heads, width = states[0].shape
    out = shaped(rows, heads, width - LANES if last else width)
    return local_call(functools.partial(join_kernel, last), out, states, [VMEM] * len(states))


def place_kernel(mine, theirs, out):
    half = mine.shape[1]
    core = lax.rem(lax.axis_index("tp"), 2)
    out[:, pl.ds(pl.multiple_of(core * half, half), half), :] = mine[...]
    out[:, pl.ds(pl.multiple_of((1 - core) * half, half), half), :] = theirs[...]


def place_heads(mine, theirs):
    rows, half, width = mine.shape
    return local_call(place_kernel, shaped(rows, 2 * half, width), [mine, theirs], [VMEM, VMEM])


def pack_kernel(spots, hidden, routes, out, tags, sems):
    size = out.shape[1] - LANES
    picks, rows = routes.shape
    spot, core = spot_and_core()
    start = pl.multiple_of((spot * 2 + core if spots > 1 else core) * size, size)
    columns = pltpu.make_async_copy(hidden.at[:, pl.ds(start, size)], out.at[:, pl.ds(0, size)], sems.at[0])
    named = pltpu.make_async_copy(routes, tags, sems.at[1])
    columns.start()
    named.start()
    out[:, size:] = jnp.zeros((rows, LANES), bf16)
    named.wait()
    eye = lax.broadcasted_iota(jnp.int32, (rows, rows), 0) == lax.broadcasted_iota(jnp.int32, (rows, rows), 1)
    turned = dot(eye.astype(f32).astype(bf16), tags[...].astype(f32).astype(bf16), ((1,), (1,)))
    out[:, size : size + picks] = turned.astype(bf16)
    columns.wait()


def pack_rows(hidden, routes, spots):
    rows, width = hidden.shape
    return local_call(
        functools.partial(pack_kernel, spots),
        shaped(rows, width // (2 * spots) + LANES),
        [pltpu.with_memory_space_constraint(a, pltpu.HBM) for a in (hidden, routes.T)],
        [ANY, ANY],
        [pltpu.VMEM(routes.shape[::-1], jnp.int32), pltpu.SemaphoreType.DMA((2,))],
        flops=WAIT_FLOPS,
        limit=2,
    )


def act_kernel(picks, ways, packs, own, mine, theirs, router, gate, up, down, act, outs, x, tags):
    rows = own.shape[0]
    spots = len(mine)
    size = mine[0].shape[1]
    local, _, hidden = gate.shape
    spot, core = spot_and_core()
    x[pl.ds(0, rows), :] = own[...]
    later = pl.ds(rows, mine[0].shape[0])
    for s in range(spots):
        first = lax.rem(spot + ways - s, ways) * 2 if spots > 1 else 0
        x[later, pl.ds(pl.multiple_of((first + core) * size, size), size)] = mine[s][...]
        x[later, pl.ds(pl.multiple_of((first + 1 - core) * size, size), size)] = theirs[s][...]
    for s, pack in enumerate(packs):
        tags[pl.ds(s * rows, rows), :] = pack[:, size:]

    scores = jax.nn.sigmoid(dot(x[...], router[...], ((1,), (1,))))
    labels = lax.broadcasted_iota(jnp.int32, scores.shape, 1)
    chosen = tags[...].astype(f32).astype(jnp.int32)
    picked = labels < 0
    for k in range(picks):
        picked = picked | (labels == chosen[:, k : k + 1])
    kept = jnp.where(picked, scores, 0.0)
    weights = route_scale * kept / jnp.sum(kept, axis=1, keepdims=True)
    first = lax.axis_index("dev") * local

    for e in range(local):
        rate = jnp.sum(jnp.where(labels == first + e, weights, 0.0), axis=1, keepdims=True)
        a = dot(x[...], gate[e])
        b = dot(x[...], up[e])
        act[:, e * hidden : (e + 1) * hidden] = (a / (1.0 + jnp.exp(-a)) * b * rate).astype(bf16)
    for out in outs:
        out[...] = dot(act[...], down[0][...]).astype(bf16)


def act_call(packs, own, mine, theirs, router, gate, up, down, picks, ways, whole):
    rows, width = own.shape
    local, _, hidden = gate.shape
    count = rows * len(packs)
    down = [down] if whole else []
    cuts = [len(packs), 1, len(mine), len(theirs), 3, len(down)]

    def kernel(*refs):
        groups = []
        for cut in cuts:
            groups.append(refs[:cut])
            refs = refs[cut:]
        packs, (own,), mine, theirs, (router, gate, up), down = groups
        act_kernel(picks, ways, packs, own, mine, theirs, router, gate, up, down, refs[0], refs[1:-2], *refs[-2:])

    parts = [shaped(count, width)] if whole else []
    operands = [*packs, own, *mine, *theirs, router, gate, up, *down]
    return local_call(
        kernel,
        [pltpu.VMEM((count, local * hidden), bf16)] + parts,
        operands,
        [VMEM] * len(operands),
        [pltpu.VMEM((count, width), bf16), pltpu.VMEM((count, LANES), bf16)],
        flops=4 * count * local * hidden * width,
        limit=10 if count <= 256 else 48,
    )


def down_call(act, down, pairs, ways):
    count, depth = act.shape
    width = down.shape[1]

    def kernel(act, down, *outs):
        spot, core = spot_and_core()
        for out, (shift, side) in zip(outs, pairs):
            size = out.shape[1]
            owner = lax.rem(spot + shift, ways) * 2 + (1 - core if side else core)
            out[...] = dot(act[...], down[:, pl.ds(pl.multiple_of(owner * size, size), size)]).astype(bf16)

    return local_call(
        kernel,
        [shaped(count, width // (2 * ways))] * len(pairs),
        [act, down],
        [VMEM, VMEM],
        flops=2 * count * depth * (width // (2 * ways)) * len(pairs),
    )


def on_device(
    hidden,
    routes,
    router_weight,
    gate_weight,
    up_weight,
    down_weight,
    q_latent,
    q_rope,
    cache_latent,
    cache_rope,
    cache_len,
):
    rows, width = hidden.shape
    local, _, units = gate_weight.shape
    n_dev, n_tp = lax.axis_size("dev"), lax.axis_size("tp")
    ways = n_tp // 2
    aligned = width % (n_tp * LANES) == 0
    spots = ways if aligned else 1
    share = width // (2 * spots)

    pack = pack_rows(hidden, routes, spots)
    packs = [pack] + [send(pack, "dev", lambda i: (i + s) % n_dev) for s in range(1, n_dev)]
    packs[1], q_latent = lax.optimization_barrier((packs[1], q_latent))
    near = jnp.concatenate([p[:, :share] for p in packs[1:]], axis=0)
    mine = [near] + [send(near, "tp", along_x(s, ways)) for s in range(1, spots)]
    theirs = [send(near, "tp", other_core)]

    keep, give = attend(q_latent, q_rope, cache_latent, cache_rope, cache_len)
    mine[1:], keep, give = lax.optimization_barrier((mine[1:], keep, give))
    theirs += [send(m, "tp", other_core) for m in mine[1:]]
    state = join([keep, send(give, "tp", other_core)], False)
    theirs, state = lax.optimization_barrier((theirs, state))
    states = [state] + [send(state, "tp", along_x(s, ways)) for s in range(1, ways)]

    gate, up, down = [
        pltpu.with_memory_space_constraint(w, pltpu.VMEM)
        for w in (gate_weight, up_weight, down_weight.reshape(local * units, width))
    ]
    act, *parts = act_call(
        packs, hidden, mine, theirs, router_weight.T, gate, up, down, routes.shape[1], ways, not aligned
    )
    act, states = lax.optimization_barrier((act, states))
    if aligned:
        shifts = range(1, ways)
        far = [send(p, "tp", other_core) for p in down_call(act, down, [(s, 1) for s in shifts], ways)]
        *own, there = down_call(act, down, [(s, 0) for s in shifts] + [(0, 1)], ways)
        there = send(there, "tp", other_core)
        sums = [(a.astype(f32) + b.astype(f32)).astype(bf16) for a, b in zip(own, far)]
        act, sums = lax.optimization_barrier((act, sums))
        (here,) = down_call(act, down, [(0, 0)], ways)
        total = here.astype(f32) + there.astype(f32)
    else:
        spot, core = spot_and_core()
        size = width // n_tp

        def block(shift, side):
            return lax.dynamic_slice_in_dim(parts[0], ((spot + shift) % ways * 2 + side) * size, size, 1)

        both = [
            block(s, core).astype(f32) + send(block(s, 1 - core), "tp", other_core).astype(f32) for s in range(ways)
        ]
        total, sums = both[0], [b.astype(bf16) for b in both[1:]]
    for s in range(1, ways):
        total = total + send(sums[s - 1], "tp", along_x(s, ways)).astype(f32)
    total = total.reshape(n_dev, rows, -1)
    moe = total[0]
    for s in range(1, n_dev):
        moe = moe + send(total[s].astype(bf16), "dev", lambda i: (i - s) % n_dev).astype(f32)
    joined = join(states, True)
    attended = place_heads(joined, send(joined, "tp", other_core))
    return (moe.astype(bf16), attended)


def solution(mesh):
    in_specs = (
        P(("group", "dev"), None),
        P(("group", "dev"), None),
        P(),
        P("dev", None, "tp"),
        P("dev", None, "tp"),
        P("dev", "tp", None),
        P(("group", "dev"), None, None),
        P(("group", "dev"), None, None),
        P(("group", "dev"), "tp", None),
        P(("group", "dev"), None, "tp"),
        P(("group", "dev")),
    )
    out_specs = (P(("group", "dev"), "tp"), P(("group", "dev"), None, None))
    return jax.shard_map(
        on_device, mesh=mesh, in_specs=in_specs, out_specs=out_specs, check_vma=False
    )
```

time: 250 us -> 48.1 us (0.19)
  blocking collectives: 98.5 us -> 0 us
  waiting for transfers between devices: 85.4 us -> 19.9 us
  matrix products: 22.8 us -> 0 us
  local copies, waits for them, and re-layouts: 13.4 us -> 0.12 us
  between operations: 14.3 us -> 1.02 us
  Pallas kernels: 0 us -> 11.1 us
  starting transfers between devices: 4.97 us -> 14.9 us
  other arithmetic: 9.56 us -> 0.81 us
    all_to_all x1 -> x0, blocking collectives: 88.3 us -> none  [on_device(): lax.all_to_all(outgoing, 'dev', split_axis=0, concat_axis=0, tiled=True)]
    all_to_all x1 -> x0, waiting for transfers between devices: 58.9 us -> none  [on_device(): lax.all_to_all(part.astype(jnp.bfloat16).reshape(devices * local_experts,...]
    dot_general x8 -> x0, matrix products: 22.8 us -> none  [the longest x1 7.96 us: on_device(): jnp.einsum('seck,ekf->secf', grouped, gate_weight, preferred_element_type...]
    ppermute x0 -> x15, waiting for transfers between devices: none -> 19.9 us  [send(): return lax.ppermute(value, axis, [(i, target(i)) for i in range(size)])]
    unnamed x3 -> x0, waiting for transfers between devices: 19 us -> none
    ppermute x0 -> x15, starting transfers between devices: none -> 14.9 us  [send(): return lax.ppermute(value, axis, [(i, target(i)) for i in range(size)])]
    pallas_call x0 -> x9, Pallas kernels: none -> 11.1 us  [local_call(): pl.pallas_call(kernel, out_shape=outs, in_specs=specs, out_specs=jax.tree...]
    all_gather x2 -> x0, blocking collectives: 10.3 us -> none  [merged(): lax.all_gather(a.astype(kind), axis)]
  transfers between devices with their start and end apart: 3 -> 15, of which waited for: 3 -> 9; matrix products, arithmetic and copies ran while one was open for 3% -> 0% of each run, Pallas kernels for 0% -> 19%
where the time goes in v3:
time: 48.1 us; the launch traced here: 47.9 us
  waiting for transfers between devices  19.9 us (41%)
  starting transfers between devices  14.9 us (31%)
  Pallas kernels  11.1 us (23%)
  between operations  1.02 us (2%)
  other arithmetic  0.81 us (2%)
    ppermute x15, waiting for transfers between devices, send(): return lax.ppermute(value, axis, [(i, target(i)) for i in range(size)])  19.9 us
    ppermute x15, starting transfers between devices, send(): return lax.ppermute(value, axis, [(i, target(i)) for i in range(size)])  14.9 us
    pallas_call x9, Pallas kernels, local_call(): pl.pallas_call(kernel, out_shape=outs, in_specs=specs, out_specs=jax.tree...  11.1 us
  transfers between devices with their start and end apart: 15, of which 9 were waited for; matrix products, arithmetic and copies ran while one was open for 0% of the time, Pallas kernels for 19%

profile of v3, /device:TPU:0, one launch (start us, length us, event | category | flops | bytes accessed | tf_op | source)
XLA Modules:
  0.0 47.9 jit_solution(7484243386034449222)
XLA Ops:
  0.8 1.0 %shard_map.122.refs_0_ = bf16[32,1024]{1,0:T(8,128)(2,1)S(1)} custom-call(bf16[32,3584]{1,0:T(8,128)(2,1)} %refs_4_.1, s32[8,32]{1,0:T(8,128)} %bitcast.13), custom_call_target="tpu_custom_call" | custom-call | flops 20000000000 | tf_op jit(solution)/shard_map/pallas_call | solution.py:45
  1.8 3.1 %collective-permute-start = (bf16[32,1024]{1,0:T(8,128)(2,1)S(1)}, bf16[32,1024]{1,0:T(8,128)(2,1)S(1)}, u32[]{:S(2)}, u32[]{:S(2)}) collective-permute-start(bf16[32,1024]{1,0:T(8,128)(2,1)S(1)} %shard_map.122.refs_0_), channel_id=1, source_target_pairs={{0,4},{4,8},{8,12},{12,0},{1,5},{5,9},{9,13},{13,1},{2,6},{6,10},{... | collective-permute-start | bytes 196616 | tf_op jit(solution)/shard_map/ppermute | solution.py:28
  4.9 2.1 %collective-permute-start.2 = (bf16[32,1024]{1,0:T(8,128)(2,1)S(1)}, bf16[32,1024]{1,0:T(8,128)(2,1)S(1)}, u32[]{:S(2)}, u32[]{:S(2)}) collective-permute-start(bf16[32,1024]{1,0:T(8,128)(2,1)S(1)} %shard_map.122.refs_0_), channel_id=1, source_target_pairs={{0,12},{4,0},{8,4},{12,8},{1,13},{5,1},{9,5},{13,9},{2,14},{6,2},{... | collective-permute-start | bytes 196616 | tf_op jit(solution)/shard_map/ppermute | solution.py:28
  7.0 0.9 %collective-permute-start.1 = (bf16[32,1024]{1,0:T(8,128)(2,1)S(1)}, bf16[32,1024]{1,0:T(8,128)(2,1)S(1)}, u32[]{:S(2)}, u32[]{:S(2)}) collective-permute-start(bf16[32,1024]{1,0:T(8,128)(2,1)S(1)} %shard_map.122.refs_0_), channel_id=1, source_target_pairs={{0,8},{4,12},{8,0},{12,4},{1,9},{5,13},{9,1},{13,5},{2,10},{6,14},... | collective-permute-start | bytes 196616 | tf_op jit(solution)/shard_map/ppermute | solution.py:28
  7.9 1.4 %collective-permute-done.refs_1_ = bf16[32,1024]{1,0:T(8,128)(2,1)S(1)} collective-permute-done((bf16[32,1024]{1,0:T(8,128)(2,1)S(1)}, bf16[32,1024]{1,0:T(8,128)(2,1)S(1)}, u32[]{:S(2)}, u32[]{:S(2)}) %collective-permute-start) | collective-permute-done | bytes 65568 | tf_op jit(solution)/shard_map/ppermute | solution.py:28
  9.3 0.5 %collective-permute-done.2.refs_3_ = bf16[32,1024]{1,0:T(8,128)(2,1)S(1)} collective-permute-done((bf16[32,1024]{1,0:T(8,128)(2,1)S(1)}, bf16[32,1024]{1,0:T(8,128)(2,1)S(1)}, u32[]{:S(2)}, u32[]{:S(2)}) %collective-permute-start.2) | collective-permute-done | bytes 65568 | tf_op jit(solution)/shard_map/ppermute | solution.py:28
  9.9 3.4 %collective-permute-done.1.refs_2_ = bf16[32,1024]{1,0:T(8,128)(2,1)S(1)} collective-permute-done((bf16[32,1024]{1,0:T(8,128)(2,1)S(1)}, bf16[32,1024]{1,0:T(8,128)(2,1)S(1)}, u32[]{:S(2)}, u32[]{:S(2)}) %collective-permute-start.1) | collective-permute-done | bytes 65568 | tf_op jit(solution)/shard_map/ppermute | solution.py:28
  13.3 1.6 %collective-permute-start.3 = (bf16[96,896]{1,0:T(8,128)(2,1)S(1)}, bf16[96,896]{1,0:T(8,128)(2,1)S(1)}, u32[]{:S(2)}, u32[]{:S(2)}) collective-permute-start(bf16[96,896]{1,0:T(8,128)(2,1)S(1)} %pad_maximum_fusion.refs_5_), channel_id=1, source_target_pairs={{0,2},{1,3},{2,0},{3,1},{4,6},{5,7},{6,4},{7,5},{8,10},{9,11},{10,... | collective-permute-start | bytes 516104 | tf_op jit(solution)/shard_map/ppermute | solution.py:28
  14.9 1.7 %shard_map.123 = (bf16[2,64,640]{2,1,0:T(8,128)(2,1)S(1)}, bf16[2,64,640]{2,1,0:T(8,128)(2,1)S(1)}) custom-call(bf16[2,128,512]{2,1,0:T(8,128)(2,1)S(1)} %copy-done.3, bf16[2,64,128]{2,1,0:T(8,128)(2,1)S(1)} %copy-done.5, bf16[2,512,512]{2,1,0:T(8,128)(2,1)S(1)} %copy-done.2, bf16[2,64,512]{2,1,0:T(8,128)(2,1)S(1)} %copy-done.4, s32[2]{0:T(128)S(1)} %copy-done.6), custom_call_target="tpu_custom_call" | custom-call | flops 2000000000 | tf_op jit(solution)/shard_map/pallas_call | solution.py:45
  16.6 3.5 %collective-permute-done.3.refs_6_ = bf16[96,896]{1,0:T(8,128)(2,1)S(1)} collective-permute-done((bf16[96,896]{1,0:T(8,128)(2,1)S(1)}, bf16[96,896]{1,0:T(8,128)(2,1)S(1)}, u32[]{:S(2)}, u32[]{:S(2)}) %collective-permute-start.3) | collective-permute-done | bytes 172064 | tf_op jit(solution)/shard_map/ppermute | solution.py:28
  20.6 1.1 %collective-permute-done.6.refs_1_ = bf16[2,64,640]{2,1,0:T(8,128)(2,1)S(1)} collective-permute-done((bf16[2,64,640]{2,1,0:T(8,128)(2,1)S(1)}, bf16[2,64,640]{2,1,0:T(8,128)(2,1)S(1)}, u32[]{:S(2)}, u32[]{:S(2)}) %collective-permute-start.6) | collective-permute-done | bytes 163872 | tf_op jit(solution)/shard_map/ppermute | solution.py:28
  22.1 1.6 %collective-permute-start.7 = (bf16[2,64,640]{2,1,0:T(8,128)(2,1)S(1)}, bf16[2,64,640]{2,1,0:T(8,128)(2,1)S(1)}, u32[]{:S(2)}, u32[]{:S(2)}) collective-permute-start(bf16[2,64,640]{2,1,0:T(8,128)(2,1)S(1)} %shard_map.124.refs_0_), channel_id=1, source_target_pairs={{0,2},{1,3},{2,0},{3,1},{4,6},{5,7},{6,4},{7,5},{8,10},{9,11},{10,... | collective-permute-start | bytes 491528 | tf_op jit(solution)/shard_map/ppermute | solution.py:28
  23.7 4.3 %shard_map.125.act = bf16[128,2048]{1,0:T(8,128)(2,1)S(1)} custom-call(bf16[32,1024]{1,0:T(8,128)(2,1)S(1)} %shard_map.122.refs_0_, bf16[32,1024]{1,0:T(8,128)(2,1)S(1)} %collective-permute-done.refs_1_, bf16[32,1024]{1,0:T(8,128)(2,1)S(1)} %collective-permute-done.1.refs_2_, bf16[32,1024]{1,0:T(8,128)(2,1)S(1)} %collective-permute-done.2.refs_3_, ...), custom_call_target="tpu_custom_call" | custom-call | flops 3758096384 | tf_op jit(solution)/shard_map/pallas_call | solution.py:45
  28.5 0.7 %shard_map.127 = bf16[128,896]{1,0:T(8,128)(2,1)S(1)} custom-call(bf16[128,2048]{1,0:T(8,128)(2,1)S(1)} %shard_map.125.act, bf16[2048,3584]{1,0:T(8,128)(2,1)S(1)} %bitcast.5), custom_call_target="tpu_custom_call" | custom-call | flops 469762048 | tf_op jit(solution)/shard_map/pallas_call | solution.py:45
  29.4 1.3 %shard_map.126 = (bf16[128,896]{1,0:T(8,128)(2,1)S(1)}, bf16[128,896]{1,0:T(8,128)(2,1)S(1)}) custom-call(bf16[128,2048]{1,0:T(8,128)(2,1)S(1)} %shard_map.125.act, bf16[2048,3584]{1,0:T(8,128)(2,1)S(1)} %bitcast.6), custom_call_target="tpu_custom_call" | custom-call | flops 939524096 | tf_op jit(solution)/shard_map/pallas_call | solution.py:45
  31.3 1.6 %collective-permute-start.10 = (bf16[128,896]{1,0:T(8,128)(2,1)S(1)}, bf16[128,896]{1,0:T(8,128)(2,1)S(1)}, u32[]{:S(2)}, u32[]{:S(2)}) collective-permute-start(bf16[128,896]{1,0:T(8,128)(2,1)S(1)} %add_convert_fusion), channel_id=1, source_target_pairs={{0,2},{1,3},{2,0},{3,1},{4,6},{5,7},{6,4},{7,5},{8,10},{9,11},{10,... | collective-permute-start | bytes 688136 | tf_op jit(solution)/shard_map/ppermute | solution.py:28
  33.2 0.7 %shard_map.128 = bf16[128,896]{1,0:T(8,128)(2,1)S(1)} custom-call(bf16[128,2048]{1,0:T(8,128)(2,1)S(1)} %shard_map.125.act, bf16[2048,3584]{1,0:T(8,128)(2,1)S(1)} %bitcast.7), custom_call_target="tpu_custom_call" | custom-call | flops 469762048 | tf_op jit(solution)/shard_map/pallas_call | solution.py:45
  34.0 5.0 %collective-permute-done.10 = bf16[128,896]{1,0:T(8,128)(2,1)S(1)} collective-permute-done((bf16[128,896]{1,0:T(8,128)(2,1)S(1)}, bf16[128,896]{1,0:T(8,128)(2,1)S(1)}, u32[]{:S(2)}, u32[]{:S(2)}) %collective-permute-start.10) | collective-permute-done | bytes 229408 | tf_op jit(solution)/shard_map/ppermute | solution.py:28
  39.0 2.3 %collective-permute-start.11 = (bf16[32,896]{1,0:T(8,128)(2,1)S(1)}, bf16[32,896]{1,0:T(8,128)(2,1)S(1)}, u32[]{:S(2)}, u32[]{:S(2)}) collective-permute-start(bf16[32,896]{1,0:T(8,128)(2,1)S(1)} %get-tuple-element.38), channel_id=1, source_target_pairs={{0,12},{4,0},{8,4},{12,8},{1,13},{5,1},{9,5},{13,9},{2,14},{6,2},{... | collective-permute-start | bytes 172040 | tf_op jit(solution)/shard_map/ppermute | solution.py:28
  41.3 0.6 %collective-permute-start.12 = (bf16[32,896]{1,0:T(8,128)(2,1)S(1)}, bf16[32,896]{1,0:T(8,128)(2,1)S(1)}, u32[]{:S(2)}, u32[]{:S(2)}) collective-permute-start(bf16[32,896]{1,0:T(8,128)(2,1)S(1)} %get-tuple-element.40), channel_id=1, source_target_pairs={{0,8},{4,12},{8,0},{12,4},{1,9},{5,13},{9,1},{13,5},{2,10},{6,14},... | collective-permute-start | bytes 172040 | tf_op jit(solution)/shard_map/ppermute | solution.py:28
  41.9 0.7 %shard_map.130 = bf16[2,128,512]{2,1,0:T(8,128)(2,1)} custom-call(bf16[2,64,512]{2,1,0:T(8,128)(2,1)S(1)} %shard_map.129.mine, bf16[2,64,512]{2,1,0:T(8,128)(2,1)S(1)} %collective-permute-done.14.theirs), custom_call_target="tpu_custom_call" | custom-call | tf_op jit(solution)/shard_map/pallas_call | solution.py:45
  42.6 0.6 %collective-permute-done.11 = bf16[32,896]{1,0:T(8,128)(2,1)S(1)} collective-permute-done((bf16[32,896]{1,0:T(8,128)(2,1)S(1)}, bf16[32,896]{1,0:T(8,128)(2,1)S(1)}, u32[]{:S(2)}, u32[]{:S(2)}) %collective-permute-start.11) | collective-permute-done | bytes 57376 | tf_op jit(solution)/shard_map/ppermute | solution.py:28
  43.3 4.0 %collective-permute-done.13 = bf16[32,896]{1,0:T(8,128)(2,1)S(1)} collective-permute-done((bf16[32,896]{1,0:T(8,128)(2,1)S(1)}, bf16[32,896]{1,0:T(8,128)(2,1)S(1)}, u32[]{:S(2)}, u32[]{:S(2)}) %collective-permute-start.13) | collective-permute-done | bytes 57376 | tf_op jit(solution)/shard_map/ppermute | solution.py:28
  47.3 0.7 %fusion.2 = bf16[32,896]{1,0:T(8,128)(2,1)} fusion(f32[128,896]{1,0:T(8,128)S(1)} %get-tuple-element.37, bf16[32,896]{1,0:T(8,128)(2,1)S(1)} %collective-permute-done.13, bf16[32,896]{1,0:T(8,128)(2,1)S(1)} %collective-permute-done.12, bf16[32,896]{1,0:T(8,128)(2,1)S(1)} %collective-permute-done.11), kind=kLoop, calls=%fused_computation.6 | loop fusion | flops 200704 | bytes 344064 | tf_op jit(solution)/shard_map/convert_element_type | solution.py:320
  (64 shorter events, 2.5 us)
Async XLA Ops:
  0.6 23.0 %slice-start.4 = ((s8[14680064]{0:T(1024)(128)(4,1)}), s8[4194304]{0:T(1024)(128)(4,1)S(1)}, s32[]{:S(2)}) async-start(s8[14680064]{0:T(1024)(128)(4,1)} %bitcast.8), calls=%async_computation.4 | async-start | bytes 8388608
  0.6 23.0 %slice-start.8 = ((s8[14680064]{0:T(1024)(128)(4,1)}), s8[4194304]{0:T(1024)(128)(4,1)S(1)}, s32[]{:S(2)}) async-start(s8[14680064]{0:T(1024)(128)(4,1)} %bitcast.10), calls=%async_computation.8 | async-start | bytes 8388608
  0.7 22.9 %slice-start.5 = ((s8[14680064]{0:T(1024)(128)(4,1)}), s8[4194304]{0:T(1024)(128)(4,1)S(1)}, s32[]{:S(2)}) async-start(s8[14680064]{0:T(1024)(128)(4,1)} %bitcast.8), calls=%async_computation.5 | async-start | bytes 8388608
  0.7 22.9 %slice-start.6 = ((s8[14680064]{0:T(1024)(128)(4,1)}), s8[4194304]{0:T(1024)(128)(4,1)S(1)}, s32[]{:S(2)}) async-start(s8[14680064]{0:T(1024)(128)(4,1)} %bitcast.8), calls=%async_computation.6 | async-start | bytes 8388608
  0.7 22.9 %slice-start.7 = ((s8[14680064]{0:T(1024)(128)(4,1)}), s8[2097152]{0:T(1024)(128)(4,1)S(1)}, s32[]{:S(2)}) async-start(s8[14680064]{0:T(1024)(128)(4,1)} %bitcast.8), calls=%async_computation.7 | async-start | bytes 4194304
  0.7 22.9 %slice-start.9 = ((s8[14680064]{0:T(1024)(128)(4,1)}), s8[4194304]{0:T(1024)(128)(4,1)S(1)}, s32[]{:S(2)}) async-start(s8[14680064]{0:T(1024)(128)(4,1)} %bitcast.10), calls=%async_computation.9 | async-start | bytes 8388608
  0.7 22.9 %slice-start.10 = ((s8[14680064]{0:T(1024)(128)(4,1)}), s8[4194304]{0:T(1024)(128)(4,1)S(1)}, s32[]{:S(2)}) async-start(s8[14680064]{0:T(1024)(128)(4,1)} %bitcast.10), calls=%async_computation.10 | async-start | bytes 8388608
  0.8 22.9 %slice-start.11 = ((s8[14680064]{0:T(1024)(128)(4,1)}), s8[2097152]{0:T(1024)(128)(4,1)S(1)}, s32[]{:S(2)}) async-start(s8[14680064]{0:T(1024)(128)(4,1)} %bitcast.10), calls=%async_computation.11 | async-start | bytes 4194304
  0.8 22.9 %copy-start = (bf16[32,3584]{1,0:T(8,128)(2,1)S(1)}, bf16[32,3584]{1,0:T(8,128)(2,1)}, u32[]{:S(2)}) copy-start(bf16[32,3584]{1,0:T(8,128)(2,1)} %refs_4_.1) | copy-start | bytes 688132
  1.8 7.5 %collective-permute-start = (bf16[32,1024]{1,0:T(8,128)(2,1)S(1)}, bf16[32,1024]{1,0:T(8,128)(2,1)S(1)}, u32[]{:S(2)}, u32[]{:S(2)}) collective-permute-start(bf16[32,1024]{1,0:T(8,128)(2,1)S(1)} %shard_map.122.refs_0_), channel_id=1, source_target_pairs={{0,4},{4,8},{8,12},{12,0},{1,5},{5,9},{9,13},{13,1},{2,6},{6,10},{... | collective-permute-start | bytes 196616 | tf_op jit(solution)/shard_map/ppermute | solution.py:28
  4.9 5.0 %collective-permute-start.2 = (bf16[32,1024]{1,0:T(8,128)(2,1)S(1)}, bf16[32,1024]{1,0:T(8,128)(2,1)S(1)}, u32[]{:S(2)}, u32[]{:S(2)}) collective-permute-start(bf16[32,1024]{1,0:T(8,128)(2,1)S(1)} %shard_map.122.refs_0_), channel_id=1, source_target_pairs={{0,12},{4,0},{8,4},{12,8},{1,13},{5,1},{9,5},{13,9},{2,14},{6,2},{... | collective-permute-start | bytes 196616 | tf_op jit(solution)/shard_map/ppermute | solution.py:28
  7.0 6.2 %collective-permute-start.1 = (bf16[32,1024]{1,0:T(8,128)(2,1)S(1)}, bf16[32,1024]{1,0:T(8,128)(2,1)S(1)}, u32[]{:S(2)}, u32[]{:S(2)}) collective-permute-start(bf16[32,1024]{1,0:T(8,128)(2,1)S(1)} %shard_map.122.refs_0_), channel_id=1, source_target_pairs={{0,8},{4,12},{8,0},{12,4},{1,9},{5,13},{9,1},{13,5},{2,10},{6,14},... | collective-permute-start | bytes 196616 | tf_op jit(solution)/shard_map/ppermute | solution.py:28
  13.2 8.8 %collective-permute-start.4 = (bf16[96,896]{1,0:T(8,128)(2,1)S(1)}, bf16[96,896]{1,0:T(8,128)(2,1)S(1)}, u32[]{:S(2)}, u32[]{:S(2)}) collective-permute-start(bf16[96,896]{1,0:T(8,128)(2,1)S(1)} %pad_maximum_fusion.refs_5_), channel_id=1, source_target_pairs={{0,1},{1,0},{2,3},{3,2},{4,5},{5,4},{6,7},{7,6},{8,9},{9,8},{10,11... | collective-permute-start | bytes 516104 | tf_op jit(solution)/shard_map/ppermute | solution.py:28
  13.3 6.8 %collective-permute-start.3 = (bf16[96,896]{1,0:T(8,128)(2,1)S(1)}, bf16[96,896]{1,0:T(8,128)(2,1)S(1)}, u32[]{:S(2)}, u32[]{:S(2)}) collective-permute-start(bf16[96,896]{1,0:T(8,128)(2,1)S(1)} %pad_maximum_fusion.refs_5_), channel_id=1, source_target_pairs={{0,2},{1,3},{2,0},{3,1},{4,6},{5,7},{6,4},{7,5},{8,10},{9,11},{10,... | collective-permute-start | bytes 516104 | tf_op jit(solution)/shard_map/ppermute | solution.py:28
  20.1 1.9 %collective-permute-start.5 = (bf16[96,896]{1,0:T(8,128)(2,1)S(1)}, bf16[96,896]{1,0:T(8,128)(2,1)S(1)}, u32[]{:S(2)}, u32[]{:S(2)}) collective-permute-start(bf16[96,896]{1,0:T(8,128)(2,1)S(1)} %collective-permute-done.3.refs_6_), channel_id=1, source_target_pairs={{0,1},{1,0},{2,3},{3,2},{4,5},{5,4},{6,7},{7,6},{8,9},{9,8},{10,11... | collective-permute-start | bytes 516104 | tf_op jit(solution)/shard_map/ppermute | solution.py:28
  20.1 1.6 %collective-permute-start.6 = (bf16[2,64,640]{2,1,0:T(8,128)(2,1)S(1)}, bf16[2,64,640]{2,1,0:T(8,128)(2,1)S(1)}, u32[]{:S(2)}, u32[]{:S(2)}) collective-permute-start(bf16[2,64,640]{2,1,0:T(8,128)(2,1)S(1)} %get-tuple-element.25), channel_id=1, source_target_pairs={{0,1},{1,0},{2,3},{3,2},{4,5},{5,4},{6,7},{7,6},{8,9},{9,8},{10,11... | collective-permute-start | bytes 491528 | tf_op jit(solution)/shard_map/ppermute | solution.py:28
  22.1 6.4 %collective-permute-start.7 = (bf16[2,64,640]{2,1,0:T(8,128)(2,1)S(1)}, bf16[2,64,640]{2,1,0:T(8,128)(2,1)S(1)}, u32[]{:S(2)}, u32[]{:S(2)}) collective-permute-start(bf16[2,64,640]{2,1,0:T(8,128)(2,1)S(1)} %shard_map.124.refs_0_), channel_id=1, source_target_pairs={{0,2},{1,3},{2,0},{3,1},{4,6},{5,7},{6,4},{7,5},{8,10},{9,11},{10,... | collective-permute-start | bytes 491528 | tf_op jit(solution)/shard_map/ppermute | solution.py:28
  29.3 1.9 %collective-permute-start.8 = (bf16[128,896]{1,0:T(8,128)(2,1)S(1)}, bf16[128,896]{1,0:T(8,128)(2,1)S(1)}, u32[]{:S(2)}, u32[]{:S(2)}) collective-permute-start(bf16[128,896]{1,0:T(8,128)(2,1)S(1)} %shard_map.127), channel_id=1, source_target_pairs={{0,1},{1,0},{2,3},{3,2},{4,5},{5,4},{6,7},{7,6},{8,9},{9,8},{10,11... | collective-permute-start | bytes 688136 | tf_op jit(solution)/shard_map/ppermute | solution.py:28
  30.7 3.3 %collective-permute-start.9 = (bf16[128,896]{1,0:T(8,128)(2,1)S(1)}, bf16[128,896]{1,0:T(8,128)(2,1)S(1)}, u32[]{:S(2)}, u32[]{:S(2)}) collective-permute-start(bf16[128,896]{1,0:T(8,128)(2,1)S(1)} %get-tuple-element.32), channel_id=1, source_target_pairs={{0,1},{1,0},{2,3},{3,2},{4,5},{5,4},{6,7},{7,6},{8,9},{9,8},{10,11... | collective-permute-start | bytes 688136 | tf_op jit(solution)/shard_map/ppermute | solution.py:28
  31.3 7.7 %collective-permute-start.10 = (bf16[128,896]{1,0:T(8,128)(2,1)S(1)}, bf16[128,896]{1,0:T(8,128)(2,1)S(1)}, u32[]{:S(2)}, u32[]{:S(2)}) collective-permute-start(bf16[128,896]{1,0:T(8,128)(2,1)S(1)} %add_convert_fusion), channel_id=1, source_target_pairs={{0,2},{1,3},{2,0},{3,1},{4,6},{5,7},{6,4},{7,5},{8,10},{9,11},{10,... | collective-permute-start | bytes 688136 | tf_op jit(solution)/shard_map/ppermute | solution.py:28
  33.1 8.8 %collective-permute-start.14 = (bf16[2,64,512]{2,1,0:T(8,128)(2,1)S(1)}, bf16[2,64,512]{2,1,0:T(8,128)(2,1)S(1)}, u32[]{:S(2)}, u32[]{:S(2)}) collective-permute-start(bf16[2,64,512]{2,1,0:T(8,128)(2,1)S(1)} %shard_map.129.mine), channel_id=1, source_target_pairs={{0,1},{1,0},{2,3},{3,2},{4,5},{5,4},{6,7},{7,6},{8,9},{9,8},{10,11... | collective-permute-start | bytes 393224 | tf_op jit(solution)/shard_map/ppermute | solution.py:28
  39.0 4.2 %collective-permute-start.11 = (bf16[32,896]{1,0:T(8,128)(2,1)S(1)}, bf16[32,896]{1,0:T(8,128)(2,1)S(1)}, u32[]{:S(2)}, u32[]{:S(2)}) collective-permute-start(bf16[32,896]{1,0:T(8,128)(2,1)S(1)} %get-tuple-element.38), channel_id=1, source_target_pairs={{0,12},{4,0},{8,4},{12,8},{1,13},{5,1},{9,5},{13,9},{2,14},{6,2},{... | collective-permute-start | bytes 172040 | tf_op jit(solution)/shard_map/ppermute | solution.py:28
  41.3 6.0 %collective-permute-start.13 = (bf16[32,896]{1,0:T(8,128)(2,1)S(1)}, bf16[32,896]{1,0:T(8,128)(2,1)S(1)}, u32[]{:S(2)}, u32[]{:S(2)}) collective-permute-start(bf16[32,896]{1,0:T(8,128)(2,1)S(1)} %get-tuple-element.39), channel_id=1, source_target_pairs={{0,4},{4,8},{8,12},{12,0},{1,5},{5,9},{9,13},{13,1},{2,6},{6,10},{... | collective-permute-start | bytes 172040 | tf_op jit(solution)/shard_map/ppermute | solution.py:28
  41.3 6.0 %collective-permute-start.12 = (bf16[32,896]{1,0:T(8,128)(2,1)S(1)}, bf16[32,896]{1,0:T(8,128)(2,1)S(1)}, u32[]{:S(2)}, u32[]{:S(2)}) collective-permute-start(bf16[32,896]{1,0:T(8,128)(2,1)S(1)} %get-tuple-element.40), channel_id=1, source_target_pairs={{0,8},{4,12},{8,0},{12,4},{1,9},{5,13},{9,1},{13,5},{2,10},{6,14},... | collective-permute-start | bytes 172040 | tf_op jit(solution)/shard_map/ppermute | solution.py:28
  (10 other events, 122.0 us)

commit v4 on v3

--- a/solution.py
+++ b/solution.py
@@ -32,8 +32,16 @@
     return i ^ 1
 
 
-def along_x(shift, ways):
-    return lambda i: ((i // 2 + shift) % ways) * 2 + i % 2
+def partner(place, step, size):
+    return place ^ step if size & (size - 1) == 0 else (step - place) % size
+
+
+def along_x(step, ways):
+    return lambda i: partner(i // 2, step, ways) * 2 + i % 2
+
+
+def over_dev(value, step, size):
+    return send(value, "dev", lambda i: partner(i, step, size))
 
 
 def spot_and_core():
@@ -173,7 +181,7 @@
     x[pl.ds(0, rows), :] = own[...]
     later = pl.ds(rows, mine[0].shape[0])
     for s in range(spots):
-        first = lax.rem(spot + ways - s, ways) * 2 if spots > 1 else 0
+        first = partner(spot, s, ways) * 2 if spots > 1 else 0
         x[later, pl.ds(pl.multiple_of((first + core) * size, size), size)] = mine[s][...]
         x[later, pl.ds(pl.multiple_of((first + 1 - core) * size, size), size)] = theirs[s][...]
     for s, pack in enumerate(packs):
@@ -234,7 +242,7 @@
         spot, core = spot_and_core()
         for out, (shift, side) in zip(outs, pairs):
             size = out.shape[1]
-            owner = lax.rem(spot + shift, ways) * 2 + (1 - core if side else core)
+            owner = partner(spot, shift, ways) * 2 + (1 - core if side else core)
             out[...] = dot(act[...], down[:, pl.ds(pl.multiple_of(owner * size, size), size)]).astype(bf16)
 
     return local_call(
@@ -268,14 +276,20 @@
     share = width // (2 * spots)
 
     pack = pack_rows(hidden, routes, spots)
-    packs = [pack] + [send(pack, "dev", lambda i: (i + s) % n_dev) for s in range(1, n_dev)]
-    packs[1], q_latent = lax.optimization_barrier((packs[1], q_latent))
-    near = jnp.concatenate([p[:, :share] for p in packs[1:]], axis=0)
-    mine = [near] + [send(near, "tp", along_x(s, ways)) for s in range(1, spots)]
-    theirs = [send(near, "tp", other_core)]
+    packs = [pack] + [over_dev(pack, s, n_dev) for s in range(1, n_dev)]
+    near = [p[:, :share] for p in packs[1:]]
+    first = n_dev // 2 - 1
+    rest = jnp.concatenate(near[:first] + near[first + 1 :], axis=0)
+    early = [send(near[first], "tp", along_x(s, ways)) for s in range(1, spots)]
+    late = [send(rest, "tp", along_x(s, ways)) for s in range(1, spots)]
+    early, q_latent = lax.optimization_barrier((early, q_latent))
+    mine = [jnp.concatenate(near, axis=0)]
+    theirs = [send(mine[0], "tp", other_core)]
 
     keep, give = attend(q_latent, q_rope, cache_latent, cache_rope, cache_len)
-    mine[1:], keep, give = lax.optimization_barrier((mine[1:], keep, give))
+    late, keep, give = lax.optimization_barrier((late, keep, give))
+    cut = first * rows
+    mine += [jnp.concatenate([b[:cut], a, b[cut:]], axis=0) for a, b in zip(early, late)]
     theirs += [send(m, "tp", other_core) for m in mine[1:]]
     state = join([keep, send(give, "tp", other_core)], False)
     theirs, state = lax.optimization_barrier((theirs, state))
@@ -288,33 +302,36 @@
     act, *parts = act_call(
         packs, hidden, mine, theirs, router_weight.T, gate, up, down, routes.shape[1], ways, not aligned
     )
+    def added(a, b):
+        return a.astype(f32) + b.astype(f32)
+
     act, states = lax.optimization_barrier((act, states))
     if aligned:
-        shifts = range(1, ways)
-        far = [send(p, "tp", other_core) for p in down_call(act, down, [(s, 1) for s in shifts], ways)]
-        *own, there = down_call(act, down, [(s, 0) for s in shifts] + [(0, 1)], ways)
+        steps = range(1, ways)
+        far = [send(p, "tp", other_core) for p in down_call(act, down, [(s, 1) for s in steps], ways)]
+        *own, there = down_call(act, down, [(s, 0) for s in steps] + [(0, 1)], ways)
         there = send(there, "tp", other_core)
-        sums = [(a.astype(f32) + b.astype(f32)).astype(bf16) for a, b in zip(own, far)]
-        act, sums = lax.optimization_barrier((act, sums))
+        sums = [added(a, b).astype(bf16) for a, b in zip(own, far)]
+        act, sums, states = lax.optimization_barrier((act, sums, states))
         (here,) = down_call(act, down, [(0, 0)], ways)
-        total = here.astype(f32) + there.astype(f32)
     else:
         spot, core = spot_and_core()
         size = width // n_tp
 
-        def block(shift, side):
-            return lax.dynamic_slice_in_dim(parts[0], ((spot + shift) % ways * 2 + side) * size, size, 1)
-
-        both = [
-            block(s, core).astype(f32) + send(block(s, 1 - core), "tp", other_core).astype(f32) for s in range(ways)
-        ]
-        total, sums = both[0], [b.astype(bf16) for b in both[1:]]
-    for s in range(1, ways):
-        total = total + send(sums[s - 1], "tp", along_x(s, ways)).astype(f32)
-    total = total.reshape(n_dev, rows, -1)
-    moe = total[0]
+        def block(step, side):
+            return lax.dynamic_slice_in_dim(parts[0], (partner(spot, step, ways) * 2 + side) * size, size, 1)
+
+        own = [block(s, core) for s in range(ways)]
+        far = [send(block(s, 1 - core), "tp", other_core) for s in range(ways)]
+        sums = [added(a, b).astype(bf16) for a, b in zip(own[1:], far[1:])]
+        here, there = own[0], far[0]
+    total = added(here, there)
+    for s, p in enumerate(sums, 1):
+        total = total + send(p, "tp", along_x(s, ways)).astype(f32)
+    blocks = [total[i : i + rows] for i in range(0, total.shape[0], rows)]
+    moe = blocks[0]
     for s in range(1, n_dev):
-        moe = moe + send(total[s].astype(bf16), "dev", lambda i: (i - s) % n_dev).astype(f32)
+        moe = moe + over_dev(blocks[s].astype(bf16), s, n_dev).astype(f32)
     joined = join(states, True)
     attended = place_heads(joined, send(joined, "tp", other_core))
     return (moe.astype(bf16), attended)

time: 48.1 us -> 47 us (0.977)
  waiting for transfers between devices: 19.9 us -> 14.8 us
  starting transfers between devices: 14.9 us -> 18.9 us
    ppermute x15 -> x16, waiting for transfers between devices: 19.9 us -> 14.8 us  [send(): return lax.ppermute(value, axis, [(i, target(i)) for i in range(size)])]
    ppermute x15 -> x16, starting transfers between devices: 14.9 us -> 18.9 us  [send(): return lax.ppermute(value, axis, [(i, target(i)) for i in range(size)])]
  transfers between devices with their start and end apart: 15 -> 16, of which waited for: 9 -> 8; matrix products, arithmetic and copies ran while one was open for 0% -> 0% of each run, Pallas kernels for 19% -> 20%
where the time goes in v4:
time: 47 us; the launch traced here: 46.8 us
  starting transfers between devices  18.9 us (40%)
  waiting for transfers between devices  14.8 us (31%)
  Pallas kernels  11 us (23%)
  between operations  1.05 us (2%)
  other arithmetic  0.84 us (2%)
    ppermute x16, starting transfers between devices, send(): return lax.ppermute(value, axis, [(i, target(i)) for i in range(size)])  18.9 us
    ppermute x16, waiting for transfers between devices, send(): return lax.ppermute(value, axis, [(i, target(i)) for i in range(size)])  14.8 us
    pallas_call x9, Pallas kernels, local_call(): pl.pallas_call(kernel, out_shape=outs, in_specs=specs, out_specs=jax.tree...  11 us
  transfers between devices with their start and end apart: 16, of which 8 were waited for; matrix products, arithmetic and copies ran while one was open for 0% of the time, Pallas kernels for 20%

profile of v4, /device:TPU:0, one launch (start us, length us, event | category | flops | bytes accessed | tf_op | source)
XLA Modules:
  0.0 46.8 jit_solution(4190972996315609731)
XLA Ops:
  0.8 1.0 %shard_map.122.refs_0_ = bf16[32,1024]{1,0:T(8,128)(2,1)S(1)} custom-call(bf16[32,3584]{1,0:T(8,128)(2,1)} %refs_4_.1, s32[8,32]{1,0:T(8,128)} %bitcast.13), custom_call_target="tpu_custom_call" | custom-call | flops 20000000000 | tf_op jit(solution)/shard_map/pallas_call | solution.py:53
  1.8 4.1 %collective-permute-start.1 = (bf16[32,1024]{1,0:T(8,128)(2,1)S(1)}, bf16[32,1024]{1,0:T(8,128)(2,1)S(1)}, u32[]{:S(2)}, u32[]{:S(2)}) collective-permute-start(bf16[32,1024]{1,0:T(8,128)(2,1)S(1)} %shard_map.122.refs_0_), channel_id=1, source_target_pairs={{0,8},{4,12},{8,0},{12,4},{1,9},{5,13},{9,1},{13,5},{2,10},{6,14},... | collective-permute-start | bytes 196616 | tf_op jit(solution)/shard_map/ppermute | solution.py:28
  5.9 1.3 %collective-permute-start.2 = (bf16[32,1024]{1,0:T(8,128)(2,1)S(1)}, bf16[32,1024]{1,0:T(8,128)(2,1)S(1)}, u32[]{:S(2)}, u32[]{:S(2)}) collective-permute-start(bf16[32,1024]{1,0:T(8,128)(2,1)S(1)} %shard_map.122.refs_0_), channel_id=1, source_target_pairs={{0,12},{4,8},{8,4},{12,0},{1,13},{5,9},{9,5},{13,1},{2,14},{6,10},... | collective-permute-start | bytes 196616 | tf_op jit(solution)/shard_map/ppermute | solution.py:28
  7.5 2.2 %collective-permute-done.1.refs_2_ = bf16[32,1024]{1,0:T(8,128)(2,1)S(1)} collective-permute-done((bf16[32,1024]{1,0:T(8,128)(2,1)S(1)}, bf16[32,1024]{1,0:T(8,128)(2,1)S(1)}, u32[]{:S(2)}, u32[]{:S(2)}) %collective-permute-start.1) | collective-permute-done | bytes 65568 | tf_op jit(solution)/shard_map/ppermute | solution.py:28
  9.7 2.5 %collective-permute-start.4 = (bf16[32,896]{1,0:T(8,128)(2,1)S(1)}, bf16[32,896]{1,0:T(8,128)(2,1)S(1)}, u32[]{:S(2)}, u32[]{:S(2)}) collective-permute-start(bf16[32,896]{1,0:T(8,128)(2,1)S(1)} %slice.40), channel_id=1, source_target_pairs={{0,2},{1,3},{2,0},{3,1},{4,6},{5,7},{6,4},{7,5},{8,10},{9,11},{10,... | collective-permute-start | bytes 172040 | tf_op jit(solution)/shard_map/ppermute | solution.py:28
  12.3 1.5 %collective-permute-start.3 = (bf16[64,896]{1,0:T(8,128)(2,1)S(1)}, bf16[64,896]{1,0:T(8,128)(2,1)S(1)}, u32[]{:S(2)}, u32[]{:S(2)}) collective-permute-start(bf16[64,896]{1,0:T(8,128)(2,1)S(1)} %pad_maximum_fusion.2), channel_id=1, source_target_pairs={{0,2},{1,3},{2,0},{3,1},{4,6},{5,7},{6,4},{7,5},{8,10},{9,11},{10,... | collective-permute-start | bytes 344072 | tf_op jit(solution)/shard_map/ppermute | solution.py:28
  13.8 1.1 %collective-permute-done.4 = bf16[32,896]{1,0:T(8,128)(2,1)S(1)} collective-permute-done((bf16[32,896]{1,0:T(8,128)(2,1)S(1)}, bf16[32,896]{1,0:T(8,128)(2,1)S(1)}, u32[]{:S(2)}, u32[]{:S(2)}) %collective-permute-start.4) | collective-permute-done | bytes 57376 | tf_op jit(solution)/shard_map/ppermute | solution.py:28
  14.9 1.7 %shard_map.123 = (bf16[2,64,640]{2,1,0:T(8,128)(2,1)S(1)}, bf16[2,64,640]{2,1,0:T(8,128)(2,1)S(1)}) custom-call(bf16[2,128,512]{2,1,0:T(8,128)(2,1)S(1)} %copy-done.3, bf16[2,64,128]{2,1,0:T(8,128)(2,1)S(1)} %copy-done.5, bf16[2,512,512]{2,1,0:T(8,128)(2,1)S(1)} %copy-done.2, bf16[2,64,512]{2,1,0:T(8,128)(2,1)S(1)} %copy-done.4, s32[2]{0:T(128)S(1)} %copy-done.6), custom_call_target="tpu_custom_call" | custom-call | flops 2000000000 | tf_op jit(solution)/shard_map/pallas_call | solution.py:53
  16.6 0.5 %collective-permute-done.3 = bf16[64,896]{1,0:T(8,128)(2,1)S(1)} collective-permute-done((bf16[64,896]{1,0:T(8,128)(2,1)S(1)}, bf16[64,896]{1,0:T(8,128)(2,1)S(1)}, u32[]{:S(2)}, u32[]{:S(2)}) %collective-permute-start.3) | collective-permute-done | bytes 114720 | tf_op jit(solution)/shard_map/ppermute | solution.py:28
  17.8 1.1 %collective-permute-done.7.refs_1_ = bf16[2,64,640]{2,1,0:T(8,128)(2,1)S(1)} collective-permute-done((bf16[2,64,640]{2,1,0:T(8,128)(2,1)S(1)}, bf16[2,64,640]{2,1,0:T(8,128)(2,1)S(1)}, u32[]{:S(2)}, u32[]{:S(2)}) %collective-permute-start.7) | collective-permute-done | bytes 163872 | tf_op jit(solution)/shard_map/ppermute | solution.py:28
  19.2 1.5 %collective-permute-start.8 = (bf16[2,64,640]{2,1,0:T(8,128)(2,1)S(1)}, bf16[2,64,640]{2,1,0:T(8,128)(2,1)S(1)}, u32[]{:S(2)}, u32[]{:S(2)}) collective-permute-start(bf16[2,64,640]{2,1,0:T(8,128)(2,1)S(1)} %shard_map.124.refs_0_), channel_id=1, source_target_pairs={{0,2},{1,3},{2,0},{3,1},{4,6},{5,7},{6,4},{7,5},{8,10},{9,11},{10,... | collective-permute-start | bytes 491528 | tf_op jit(solution)/shard_map/ppermute | solution.py:28
  20.9 4.3 %shard_map.125.act = bf16[128,2048]{1,0:T(8,128)(2,1)S(1)} custom-call(bf16[32,1024]{1,0:T(8,128)(2,1)S(1)} %shard_map.122.refs_0_, bf16[32,1024]{1,0:T(8,128)(2,1)S(1)} %collective-permute-done.refs_1_, bf16[32,1024]{1,0:T(8,128)(2,1)S(1)} %collective-permute-done.1.refs_2_, bf16[32,1024]{1,0:T(8,128)(2,1)S(1)} %collective-permute-done.2.refs_3_, ...), custom_call_target="tpu_custom_call" | custom-call | flops 3758096384 | tf_op jit(solution)/shard_map/pallas_call | solution.py:53
  25.7 0.7 %shard_map.127 = bf16[128,896]{1,0:T(8,128)(2,1)S(1)} custom-call(bf16[128,2048]{1,0:T(8,128)(2,1)S(1)} %shard_map.125.act, bf16[2048,3584]{1,0:T(8,128)(2,1)S(1)} %bitcast.5), custom_call_target="tpu_custom_call" | custom-call | flops 469762048 | tf_op jit(solution)/shard_map/pallas_call | solution.py:53
  26.5 1.3 %shard_map.126 = (bf16[128,896]{1,0:T(8,128)(2,1)S(1)}, bf16[128,896]{1,0:T(8,128)(2,1)S(1)}) custom-call(bf16[128,2048]{1,0:T(8,128)(2,1)S(1)} %shard_map.125.act, bf16[2048,3584]{1,0:T(8,128)(2,1)S(1)} %bitcast.6), custom_call_target="tpu_custom_call" | custom-call | flops 939524096 | tf_op jit(solution)/shard_map/pallas_call | solution.py:53
  27.8 0.5 %collective-permute-start.10 = (bf16[128,896]{1,0:T(8,128)(2,1)S(1)}, bf16[128,896]{1,0:T(8,128)(2,1)S(1)}, u32[]{:S(2)}, u32[]{:S(2)}) collective-permute-start(bf16[128,896]{1,0:T(8,128)(2,1)S(1)} %get-tuple-element.36), channel_id=1, source_target_pairs={{0,1},{1,0},{2,3},{3,2},{4,5},{5,4},{6,7},{7,6},{8,9},{9,8},{10,11... | collective-permute-start | bytes 688136 | tf_op jit(solution)/shard_map/ppermute | solution.py:28
  28.4 1.6 %collective-permute-start.11 = (bf16[128,896]{1,0:T(8,128)(2,1)S(1)}, bf16[128,896]{1,0:T(8,128)(2,1)S(1)}, u32[]{:S(2)}, u32[]{:S(2)}) collective-permute-start(bf16[128,896]{1,0:T(8,128)(2,1)S(1)} %add_convert_fusion), channel_id=1, source_target_pairs={{0,2},{1,3},{2,0},{3,1},{4,6},{5,7},{6,4},{7,5},{8,10},{9,11},{10,... | collective-permute-start | bytes 688136 | tf_op jit(solution)/shard_map/ppermute | solution.py:28
  30.3 0.7 %shard_map.128 = bf16[128,896]{1,0:T(8,128)(2,1)S(1)} custom-call(bf16[128,2048]{1,0:T(8,128)(2,1)S(1)} %shard_map.125.act, bf16[2048,3584]{1,0:T(8,128)(2,1)S(1)} %bitcast.7), custom_call_target="tpu_custom_call" | custom-call | flops 469762048 | tf_op jit(solution)/shard_map/pallas_call | solution.py:53
  31.1 5.0 %collective-permute-done.11 = bf16[128,896]{1,0:T(8,128)(2,1)S(1)} collective-permute-done((bf16[128,896]{1,0:T(8,128)(2,1)S(1)}, bf16[128,896]{1,0:T(8,128)(2,1)S(1)}, u32[]{:S(2)}, u32[]{:S(2)}) %collective-permute-start.11) | collective-permute-done | bytes 229408 | tf_op jit(solution)/shard_map/ppermute | solution.py:28
  36.2 1.4 %collective-permute-start.12 = (bf16[32,896]{1,0:T(8,128)(2,1)S(1)}, bf16[32,896]{1,0:T(8,128)(2,1)S(1)}, u32[]{:S(2)}, u32[]{:S(2)}) collective-permute-start(bf16[32,896]{1,0:T(8,128)(2,1)S(1)} %get-tuple-element.42), channel_id=1, source_target_pairs={{0,4},{4,0},{8,12},{12,8},{1,5},{5,1},{9,13},{13,9},{2,6},{6,2},{1... | collective-permute-start | bytes 172040 | tf_op jit(solution)/shard_map/ppermute | solution.py:28
  37.6 2.9 %collective-permute-start.14 = (bf16[32,896]{1,0:T(8,128)(2,1)S(1)}, bf16[32,896]{1,0:T(8,128)(2,1)S(1)}, u32[]{:S(2)}, u32[]{:S(2)}) collective-permute-start(bf16[32,896]{1,0:T(8,128)(2,1)S(1)} %get-tuple-element.43), channel_id=1, source_target_pairs={{0,12},{4,8},{8,4},{12,0},{1,13},{5,9},{9,5},{13,1},{2,14},{6,10},... | collective-permute-start | bytes 172040 | tf_op jit(solution)/shard_map/ppermute | solution.py:28
  40.9 0.7 %shard_map.130 = bf16[2,128,512]{2,1,0:T(8,128)(2,1)} custom-call(bf16[2,64,512]{2,1,0:T(8,128)(2,1)S(1)} %shard_map.129.mine, bf16[2,64,512]{2,1,0:T(8,128)(2,1)S(1)} %collective-permute-done.15.theirs), custom_call_target="tpu_custom_call" | custom-call | tf_op jit(solution)/shard_map/pallas_call | solution.py:53
  41.7 2.4 %collective-permute-done.14 = bf16[32,896]{1,0:T(8,128)(2,1)S(1)} collective-permute-done((bf16[32,896]{1,0:T(8,128)(2,1)S(1)}, bf16[32,896]{1,0:T(8,128)(2,1)S(1)}, u32[]{:S(2)}, u32[]{:S(2)}) %collective-permute-start.14) | collective-permute-done | bytes 57376 | tf_op jit(solution)/shard_map/ppermute | solution.py:28
  44.1 2.0 %collective-permute-done.13 = bf16[32,896]{1,0:T(8,128)(2,1)S(1)} collective-permute-done((bf16[32,896]{1,0:T(8,128)(2,1)S(1)}, bf16[32,896]{1,0:T(8,128)(2,1)S(1)}, u32[]{:S(2)}, u32[]{:S(2)}) %collective-permute-start.13) | collective-permute-done | bytes 57376 | tf_op jit(solution)/shard_map/ppermute | solution.py:28
  46.1 0.7 %fusion.2 = bf16[32,896]{1,0:T(8,128)(2,1)} fusion(f32[128,896]{1,0:T(8,128)S(1)} %get-tuple-element.41, bf16[32,896]{1,0:T(8,128)(2,1)S(1)} %collective-permute-done.14, bf16[32,896]{1,0:T(8,128)(2,1)S(1)} %collective-permute-done.13, bf16[32,896]{1,0:T(8,128)(2,1)S(1)} %collective-permute-done.12), kind=kLoop, calls=%fused_computation.7 | loop fusion | flops 200704 | bytes 344064 | tf_op jit(solution)/shard_map/convert_element_type | solution.py:337
  (69 shorter events, 2.8 us)
Async XLA Ops:
  0.6 20.1 %slice-start.4 = ((s8[14680064]{0:T(1024)(128)(4,1)}), s8[4194304]{0:T(1024)(128)(4,1)S(1)}, s32[]{:S(2)}) async-start(s8[14680064]{0:T(1024)(128)(4,1)} %bitcast.8), calls=%async_computation.4 | async-start | bytes 8388608
  0.6 20.1 %slice-start.8 = ((s8[14680064]{0:T(1024)(128)(4,1)}), s8[4194304]{0:T(1024)(128)(4,1)S(1)}, s32[]{:S(2)}) async-start(s8[14680064]{0:T(1024)(128)(4,1)} %bitcast.10), calls=%async_computation.8 | async-start | bytes 8388608
  0.7 20.1 %slice-start.5 = ((s8[14680064]{0:T(1024)(128)(4,1)}), s8[4194304]{0:T(1024)(128)(4,1)S(1)}, s32[]{:S(2)}) async-start(s8[14680064]{0:T(1024)(128)(4,1)} %bitcast.8), calls=%async_computation.5 | async-start | bytes 8388608
  0.7 20.0 %slice-start.6 = ((s8[14680064]{0:T(1024)(128)(4,1)}), s8[4194304]{0:T(1024)(128)(4,1)S(1)}, s32[]{:S(2)}) async-start(s8[14680064]{0:T(1024)(128)(4,1)} %bitcast.8), calls=%async_computation.6 | async-start | bytes 8388608
  0.7 20.0 %slice-start.7 = ((s8[14680064]{0:T(1024)(128)(4,1)}), s8[2097152]{0:T(1024)(128)(4,1)S(1)}, s32[]{:S(2)}) async-start(s8[14680064]{0:T(1024)(128)(4,1)} %bitcast.8), calls=%async_computation.7 | async-start | bytes 4194304
  0.7 20.0 %slice-start.9 = ((s8[14680064]{0:T(1024)(128)(4,1)}), s8[4194304]{0:T(1024)(128)(4,1)S(1)}, s32[]{:S(2)}) async-start(s8[14680064]{0:T(1024)(128)(4,1)} %bitcast.10), calls=%async_computation.9 | async-start | bytes 8388608
  0.7 20.0 %slice-start.10 = ((s8[14680064]{0:T(1024)(128)(4,1)}), s8[4194304]{0:T(1024)(128)(4,1)S(1)}, s32[]{:S(2)}) async-start(s8[14680064]{0:T(1024)(128)(4,1)} %bitcast.10), calls=%async_computation.10 | async-start | bytes 8388608
  0.8 20.0 %slice-start.11 = ((s8[14680064]{0:T(1024)(128)(4,1)}), s8[2097152]{0:T(1024)(128)(4,1)S(1)}, s32[]{:S(2)}) async-start(s8[14680064]{0:T(1024)(128)(4,1)} %bitcast.10), calls=%async_computation.11 | async-start | bytes 4194304
  1.8 7.9 %collective-permute-start.1 = (bf16[32,1024]{1,0:T(8,128)(2,1)S(1)}, bf16[32,1024]{1,0:T(8,128)(2,1)S(1)}, u32[]{:S(2)}, u32[]{:S(2)}) collective-permute-start(bf16[32,1024]{1,0:T(8,128)(2,1)S(1)} %shard_map.122.refs_0_), channel_id=1, source_target_pairs={{0,8},{4,12},{8,0},{12,4},{1,9},{5,13},{9,1},{13,5},{2,10},{6,14},... | collective-permute-start | bytes 196616 | tf_op jit(solution)/shard_map/ppermute | solution.py:28
  5.9 6.3 %collective-permute-start.2 = (bf16[32,1024]{1,0:T(8,128)(2,1)S(1)}, bf16[32,1024]{1,0:T(8,128)(2,1)S(1)}, u32[]{:S(2)}, u32[]{:S(2)}) collective-permute-start(bf16[32,1024]{1,0:T(8,128)(2,1)S(1)} %shard_map.122.refs_0_), channel_id=1, source_target_pairs={{0,12},{4,8},{8,4},{12,0},{1,13},{5,9},{9,5},{13,1},{2,14},{6,10},... | collective-permute-start | bytes 196616 | tf_op jit(solution)/shard_map/ppermute | solution.py:28
  7.3 5.0 %collective-permute-start = (bf16[32,1024]{1,0:T(8,128)(2,1)S(1)}, bf16[32,1024]{1,0:T(8,128)(2,1)S(1)}, u32[]{:S(2)}, u32[]{:S(2)}) collective-permute-start(bf16[32,1024]{1,0:T(8,128)(2,1)S(1)} %shard_map.122.refs_0_), channel_id=1, source_target_pairs={{0,4},{4,0},{8,12},{12,8},{1,5},{5,1},{9,13},{13,9},{2,6},{6,2},{1... | collective-permute-start | bytes 196616 | tf_op jit(solution)/shard_map/ppermute | solution.py:28
  9.7 5.2 %collective-permute-start.4 = (bf16[32,896]{1,0:T(8,128)(2,1)S(1)}, bf16[32,896]{1,0:T(8,128)(2,1)S(1)}, u32[]{:S(2)}, u32[]{:S(2)}) collective-permute-start(bf16[32,896]{1,0:T(8,128)(2,1)S(1)} %slice.40), channel_id=1, source_target_pairs={{0,2},{1,3},{2,0},{3,1},{4,6},{5,7},{6,4},{7,5},{8,10},{9,11},{10,... | collective-permute-start | bytes 172040 | tf_op jit(solution)/shard_map/ppermute | solution.py:28
  12.3 4.9 %collective-permute-start.3 = (bf16[64,896]{1,0:T(8,128)(2,1)S(1)}, bf16[64,896]{1,0:T(8,128)(2,1)S(1)}, u32[]{:S(2)}, u32[]{:S(2)}) collective-permute-start(bf16[64,896]{1,0:T(8,128)(2,1)S(1)} %pad_maximum_fusion.2), channel_id=1, source_target_pairs={{0,2},{1,3},{2,0},{3,1},{4,6},{5,7},{6,4},{7,5},{8,10},{9,11},{10,... | collective-permute-start | bytes 344072 | tf_op jit(solution)/shard_map/ppermute | solution.py:28
  13.8 5.3 %collective-permute-start.5 = (bf16[96,896]{1,0:T(8,128)(2,1)S(1)}, bf16[96,896]{1,0:T(8,128)(2,1)S(1)}, u32[]{:S(2)}, u32[]{:S(2)}) collective-permute-start(bf16[96,896]{1,0:T(8,128)(2,1)S(1)} %pad_maximum_fusion.refs_5_), channel_id=1, source_target_pairs={{0,1},{1,0},{2,3},{3,2},{4,5},{5,4},{6,7},{7,6},{8,9},{9,8},{10,11... | collective-permute-start | bytes 516104 | tf_op jit(solution)/shard_map/ppermute | solution.py:28
  17.2 2.0 %collective-permute-start.6 = (bf16[96,896]{1,0:T(8,128)(2,1)S(1)}, bf16[96,896]{1,0:T(8,128)(2,1)S(1)}, u32[]{:S(2)}, u32[]{:S(2)}) collective-permute-start(bf16[96,896]{1,0:T(8,128)(2,1)S(1)} %pad_maximum_fusion.1.refs_6_), channel_id=1, source_target_pairs={{0,1},{1,0},{2,3},{3,2},{4,5},{5,4},{6,7},{7,6},{8,9},{9,8},{10,11... | collective-permute-start | bytes 516104 | tf_op jit(solution)/shard_map/ppermute | solution.py:28
  17.3 1.6 %collective-permute-start.7 = (bf16[2,64,640]{2,1,0:T(8,128)(2,1)S(1)}, bf16[2,64,640]{2,1,0:T(8,128)(2,1)S(1)}, u32[]{:S(2)}, u32[]{:S(2)}) collective-permute-start(bf16[2,64,640]{2,1,0:T(8,128)(2,1)S(1)} %get-tuple-element.27), channel_id=1, source_target_pairs={{0,1},{1,0},{2,3},{3,2},{4,5},{5,4},{6,7},{7,6},{8,9},{9,8},{10,11... | collective-permute-start | bytes 491528 | tf_op jit(solution)/shard_map/ppermute | solution.py:28
  19.2 6.4 %collective-permute-start.8 = (bf16[2,64,640]{2,1,0:T(8,128)(2,1)S(1)}, bf16[2,64,640]{2,1,0:T(8,128)(2,1)S(1)}, u32[]{:S(2)}, u32[]{:S(2)}) collective-permute-start(bf16[2,64,640]{2,1,0:T(8,128)(2,1)S(1)} %shard_map.124.refs_0_), channel_id=1, source_target_pairs={{0,2},{1,3},{2,0},{3,1},{4,6},{5,7},{6,4},{7,5},{8,10},{9,11},{10,... | collective-permute-start | bytes 491528 | tf_op jit(solution)/shard_map/ppermute | solution.py:28
  26.4 1.9 %collective-permute-start.9 = (bf16[128,896]{1,0:T(8,128)(2,1)S(1)}, bf16[128,896]{1,0:T(8,128)(2,1)S(1)}, u32[]{:S(2)}, u32[]{:S(2)}) collective-permute-start(bf16[128,896]{1,0:T(8,128)(2,1)S(1)} %shard_map.127), channel_id=1, source_target_pairs={{0,1},{1,0},{2,3},{3,2},{4,5},{5,4},{6,7},{7,6},{8,9},{9,8},{10,11... | collective-permute-start | bytes 688136 | tf_op jit(solution)/shard_map/ppermute | solution.py:28
  27.8 3.2 %collective-permute-start.10 = (bf16[128,896]{1,0:T(8,128)(2,1)S(1)}, bf16[128,896]{1,0:T(8,128)(2,1)S(1)}, u32[]{:S(2)}, u32[]{:S(2)}) collective-permute-start(bf16[128,896]{1,0:T(8,128)(2,1)S(1)} %get-tuple-element.36), channel_id=1, source_target_pairs={{0,1},{1,0},{2,3},{3,2},{4,5},{5,4},{6,7},{7,6},{8,9},{9,8},{10,11... | collective-permute-start | bytes 688136 | tf_op jit(solution)/shard_map/ppermute | solution.py:28
  28.4 7.6 %collective-permute-start.11 = (bf16[128,896]{1,0:T(8,128)(2,1)S(1)}, bf16[128,896]{1,0:T(8,128)(2,1)S(1)}, u32[]{:S(2)}, u32[]{:S(2)}) collective-permute-start(bf16[128,896]{1,0:T(8,128)(2,1)S(1)} %add_convert_fusion), channel_id=1, source_target_pairs={{0,2},{1,3},{2,0},{3,1},{4,6},{5,7},{6,4},{7,5},{8,10},{9,11},{10,... | collective-permute-start | bytes 688136 | tf_op jit(solution)/shard_map/ppermute | solution.py:28
  30.3 10.7 %collective-permute-start.15 = (bf16[2,64,512]{2,1,0:T(8,128)(2,1)S(1)}, bf16[2,64,512]{2,1,0:T(8,128)(2,1)S(1)}, u32[]{:S(2)}, u32[]{:S(2)}) collective-permute-start(bf16[2,64,512]{2,1,0:T(8,128)(2,1)S(1)} %shard_map.129.mine), channel_id=1, source_target_pairs={{0,1},{1,0},{2,3},{3,2},{4,5},{5,4},{6,7},{7,6},{8,9},{9,8},{10,11... | collective-permute-start | bytes 393224 | tf_op jit(solution)/shard_map/ppermute | solution.py:28
  36.2 5.5 %collective-permute-start.12 = (bf16[32,896]{1,0:T(8,128)(2,1)S(1)}, bf16[32,896]{1,0:T(8,128)(2,1)S(1)}, u32[]{:S(2)}, u32[]{:S(2)}) collective-permute-start(bf16[32,896]{1,0:T(8,128)(2,1)S(1)} %get-tuple-element.42), channel_id=1, source_target_pairs={{0,4},{4,0},{8,12},{12,8},{1,5},{5,1},{9,13},{13,9},{2,6},{6,2},{1... | collective-permute-start | bytes 172040 | tf_op jit(solution)/shard_map/ppermute | solution.py:28
  37.6 6.5 %collective-permute-start.14 = (bf16[32,896]{1,0:T(8,128)(2,1)S(1)}, bf16[32,896]{1,0:T(8,128)(2,1)S(1)}, u32[]{:S(2)}, u32[]{:S(2)}) collective-permute-start(bf16[32,896]{1,0:T(8,128)(2,1)S(1)} %get-tuple-element.43), channel_id=1, source_target_pairs={{0,12},{4,8},{8,4},{12,0},{1,13},{5,9},{9,5},{13,1},{2,14},{6,10},... | collective-permute-start | bytes 172040 | tf_op jit(solution)/shard_map/ppermute | solution.py:28
  40.4 5.7 %collective-permute-start.13 = (bf16[32,896]{1,0:T(8,128)(2,1)S(1)}, bf16[32,896]{1,0:T(8,128)(2,1)S(1)}, u32[]{:S(2)}, u32[]{:S(2)}) collective-permute-start(bf16[32,896]{1,0:T(8,128)(2,1)S(1)} %get-tuple-element.44), channel_id=1, source_target_pairs={{0,8},{4,12},{8,0},{12,4},{1,9},{5,13},{9,1},{13,5},{2,10},{6,14},... | collective-permute-start | bytes 172040 | tf_op jit(solution)/shard_map/ppermute | solution.py:28
  (11 other events, 136.3 us)

commit v5 on v4

--- a/solution.py
+++ b/solution.py
@@ -178,14 +178,19 @@
     size = mine[0].shape[1]
     local, _, hidden = gate.shape
     spot, core = spot_and_core()
-    x[pl.ds(0, rows), :] = own[...]
-    later = pl.ds(rows, mine[0].shape[0])
-    for s in range(spots):
-        first = partner(spot, s, ways) * 2 if spots > 1 else 0
-        x[later, pl.ds(pl.multiple_of((first + core) * size, size), size)] = mine[s][...]
-        x[later, pl.ds(pl.multiple_of((first + 1 - core) * size, size), size)] = theirs[s][...]
-    for s, pack in enumerate(packs):
-        tags[pl.ds(s * rows, rows), :] = pack[:, size:]
+    dev = lax.axis_index("dev")
+    n_dev = len(packs)
+    for p in range(n_dev):
+        there = pl.ds(pl.multiple_of(partner(dev, p, n_dev) * rows, rows), rows)
+        tags[there, :] = packs[p][:, size:]
+        if p == 0:
+            x[there, :] = own[...]
+            continue
+        here = pl.ds((p - 1) * rows, rows)
+        for s in range(spots):
+            first = partner(spot, s, ways) * 2 if spots > 1 else 0
+            x[there, pl.ds(pl.multiple_of((first + core) * size, size), size)] = mine[s][here, :]
+            x[there, pl.ds(pl.multiple_of((first + 1 - core) * size, size), size)] = theirs[s][here, :]
 
     scores = jax.nn.sigmoid(dot(x[...], router[...], ((1,), (1,))))
     labels = lax.broadcasted_iota(jnp.int32, scores.shape, 1)
@@ -195,7 +200,7 @@
         picked = picked | (labels == chosen[:, k : k + 1])
     kept = jnp.where(picked, scores, 0.0)
     weights = route_scale * kept / jnp.sum(kept, axis=1, keepdims=True)
-    first = lax.axis_index("dev") * local
+    first = dev * local
 
     for e in range(local):
         rate = jnp.sum(jnp.where(labels == first + e, weights, 0.0), axis=1, keepdims=True)
@@ -229,7 +234,6 @@
         operands,
         [VMEM] * len(operands),
         [pltpu.VMEM((count, width), bf16), pltpu.VMEM((count, LANES), bf16)],
-        flops=4 * count * local * hidden * width,
         limit=10 if count <= 256 else 48,
     )
 
@@ -276,24 +280,26 @@
     share = width // (2 * spots)
 
     pack = pack_rows(hidden, routes, spots)
-    packs = [pack] + [over_dev(pack, s, n_dev) for s in range(1, n_dev)]
+    pack, q_latent = lax.optimization_barrier((pack, q_latent))
+    first = n_dev // 2
+    far = over_dev(pack, first, n_dev)
+    keep, give = attend(q_latent, q_rope, cache_latent, cache_rope, cache_len)
+    again, keep, give = lax.optimization_barrier((pack, keep, give))
+    packs = [pack] + [far if s == first else over_dev(again, s, n_dev) for s in range(1, n_dev)]
     near = [p[:, :share] for p in packs[1:]]
-    first = n_dev // 2 - 1
+    first -= 1
+    early = [send(near[first], "tp", along_x(s, ways)) for s in range(1, spots)]
+    state = join([keep, send(give, "tp", other_core)], False)
     rest = jnp.concatenate(near[:first] + near[first + 1 :], axis=0)
-    early = [send(near[first], "tp", along_x(s, ways)) for s in range(1, spots)]
+    rest, state = lax.optimization_barrier((rest, state))
     late = [send(rest, "tp", along_x(s, ways)) for s in range(1, spots)]
-    early, q_latent = lax.optimization_barrier((early, q_latent))
     mine = [jnp.concatenate(near, axis=0)]
-    theirs = [send(mine[0], "tp", other_core)]
-
-    keep, give = attend(q_latent, q_rope, cache_latent, cache_rope, cache_len)
-    late, keep, give = lax.optimization_barrier((late, keep, give))
     cut = first * rows
     mine += [jnp.concatenate([b[:cut], a, b[cut:]], axis=0) for a, b in zip(early, late)]
-    theirs += [send(m, "tp", other_core) for m in mine[1:]]
-    state = join([keep, send(give, "tp", other_core)], False)
+    theirs = [send(m, "tp", other_core) for m in mine]
+    states = [send(state, "tp", along_x(s, ways)) for s in range(1, ways)]
     theirs, state = lax.optimization_barrier((theirs, state))
-    states = [state] + [send(state, "tp", along_x(s, ways)) for s in range(1, ways)]
+    states = [state] + states
 
     gate, up, down = [
         pltpu.with_memory_space_constraint(w, pltpu.VMEM)
@@ -328,10 +334,8 @@
     total = added(here, there)
     for s, p in enumerate(sums, 1):
         total = total + send(p, "tp", along_x(s, ways)).astype(f32)
-    blocks = [total[i : i + rows] for i in range(0, total.shape[0], rows)]
-    moe = blocks[0]
-    for s in range(1, n_dev):
-        moe = moe + over_dev(blocks[s].astype(bf16), s, n_dev).astype(f32)
+    back = lax.all_to_all(total.astype(bf16), "dev", split_axis=0, concat_axis=0, tiled=True)
+    moe = jnp.sum(back.reshape(n_dev, rows, -1).astype(f32), axis=0)
     joined = join(states, True)
     attended = place_heads(joined, send(joined, "tp", other_core))
     return (moe.astype(bf16), attended)

time: 47 us -> 50.5 us (1.074)
  waiting for transfers between devices: 14.8 us -> 20.3 us
  starting transfers between devices: 18.9 us -> 16.3 us
  other arithmetic: 0.84 us -> 1.55 us
    ppermute x16 -> x13, starting transfers between devices: 18.9 us -> 13 us  [send(): return lax.ppermute(value, axis, [(i, target(i)) for i in range(size)])]
    all_to_all x0 -> x1, waiting for transfers between devices: none -> 5.41 us  [on_device(): lax.all_to_all(total.astype(bf16), 'dev', split_axis=0, concat_axis=0, ti...]
    all_to_all x0 -> x1, starting transfers between devices: none -> 3.38 us  [on_device(): lax.all_to_all(total.astype(bf16), 'dev', split_axis=0, concat_axis=0, ti...]
    reduce_sum x0 -> x1, other arithmetic: none -> 0.66 us  [on_device(): moe = jnp.sum(back.reshape(n_dev, rows, -1).astype(f32), axis=0)]
    ppermute x16 -> x13, waiting for transfers between devices: 14.8 us -> 14.9 us  [send(): return lax.ppermute(value, axis, [(i, target(i)) for i in range(size)])]
  transfers between devices with their start and end apart: 16 -> 14, of which waited for: 8 -> 8; matrix products, arithmetic and copies ran while one was open for 0% -> 0% of each run, Pallas kernels for 20% -> 18%
where the time goes in v5:
time: 50.5 us; the launch traced here: 50.3 us
  waiting for transfers between devices  20.3 us (40%)
  starting transfers between devices  16.3 us (32%)
  Pallas kernels  11 us (22%)
  other arithmetic  1.55 us (3%)
  between operations  0.94 us (2%)
    ppermute x13, waiting for transfers between devices, send(): return lax.ppermute(value, axis, [(i, target(i)) for i in range(size)])  14.9 us
    ppermute x13, starting transfers between devices, send(): return lax.ppermute(value, axis, [(i, target(i)) for i in range(size)])  13 us
    pallas_call x9, Pallas kernels, local_call(): pl.pallas_call(kernel, out_shape=outs, in_specs=specs, out_specs=jax.tree...  11 us
    all_to_all x1, waiting for transfers between devices, on_device(): lax.all_to_all(total.astype(bf16), 'dev', split_axis=0, concat_axis=0, ti...  5.41 us
    all_to_all x1, starting transfers between devices, on_device(): lax.all_to_all(total.astype(bf16), 'dev', split_axis=0, concat_axis=0, ti...  3.38 us
  transfers between devices with their start and end apart: 14, of which 8 were waited for; matrix products, arithmetic and copies ran while one was open for 0% of the time, Pallas kernels for 18%

profile of v5, /device:TPU:0, one launch (start us, length us, event | category | flops | bytes accessed | tf_op | source)
XLA Modules:
  0.0 50.3 jit_solution(11613097681561811618)
XLA Ops:
  0.7 1.0 %shard_map.122.refs_0_ = bf16[32,1024]{1,0:T(8,128)(2,1)S(1)} custom-call(bf16[32,3584]{1,0:T(8,128)(2,1)} %refs_4_.1, s32[8,32]{1,0:T(8,128)} %bitcast.10), custom_call_target="tpu_custom_call" | custom-call | flops 20000000000 | tf_op jit(solution)/shard_map/pallas_call | solution.py:53
  1.8 4.1 %collective-permute-start.1 = (bf16[32,1024]{1,0:T(8,128)(2,1)S(1)}, bf16[32,1024]{1,0:T(8,128)(2,1)S(1)}, u32[]{:S(2)}, u32[]{:S(2)}) collective-permute-start(bf16[32,1024]{1,0:T(8,128)(2,1)S(1)} %shard_map.122.refs_0_), channel_id=1, source_target_pairs={{0,8},{4,12},{8,0},{12,4},{1,9},{5,13},{9,1},{13,5},{2,10},{6,14},... | collective-permute-start | bytes 196616 | tf_op jit(solution)/shard_map/ppermute | solution.py:28
  5.9 1.7 %shard_map.123 = (bf16[2,64,640]{2,1,0:T(8,128)(2,1)S(1)}, bf16[2,64,640]{2,1,0:T(8,128)(2,1)S(1)}) custom-call(bf16[2,128,512]{2,1,0:T(8,128)(2,1)S(1)} %copy-done.5, bf16[2,64,128]{2,1,0:T(8,128)(2,1)S(1)} %copy-done.7, bf16[2,512,512]{2,1,0:T(8,128)(2,1)S(1)} %copy-done.4, bf16[2,64,512]{2,1,0:T(8,128)(2,1)S(1)} %copy-done.6, s32[2]{0:T(128)S(1)} %copy-done.8), custom_call_target="tpu_custom_call" | custom-call | flops 2000000000 | tf_op jit(solution)/shard_map/pallas_call | solution.py:53
  7.6 1.6 %collective-permute-start = (bf16[32,1024]{1,0:T(8,128)(2,1)S(1)}, bf16[32,1024]{1,0:T(8,128)(2,1)S(1)}, u32[]{:S(2)}, u32[]{:S(2)}) collective-permute-start(bf16[32,1024]{1,0:T(8,128)(2,1)S(1)} %shard_map.122.refs_0_), channel_id=1, source_target_pairs={{0,4},{4,0},{8,12},{12,8},{1,5},{5,1},{9,13},{13,9},{2,6},{6,2},{1... | collective-permute-start | bytes 196616 | tf_op jit(solution)/shard_map/ppermute | solution.py:28
  9.5 1.7 %collective-permute-start.5 = (bf16[32,896]{1,0:T(8,128)(2,1)S(1)}, bf16[32,896]{1,0:T(8,128)(2,1)S(1)}, u32[]{:S(2)}, u32[]{:S(2)}) collective-permute-start(bf16[32,896]{1,0:T(8,128)(2,1)S(1)} %slice.21), channel_id=1, source_target_pairs={{0,2},{1,3},{2,0},{3,1},{4,6},{5,7},{6,4},{7,5},{8,10},{9,11},{10,... | collective-permute-start | bytes 172040 | tf_op jit(solution)/shard_map/ppermute | solution.py:28
  11.2 0.7 %collective-permute-done.refs_1_ = bf16[32,1024]{1,0:T(8,128)(2,1)S(1)} collective-permute-done((bf16[32,1024]{1,0:T(8,128)(2,1)S(1)}, bf16[32,1024]{1,0:T(8,128)(2,1)S(1)}, u32[]{:S(2)}, u32[]{:S(2)}) %collective-permute-start) | collective-permute-done | bytes 65568 | tf_op jit(solution)/shard_map/ppermute | solution.py:28
  11.9 3.4 %collective-permute-done.2.refs_3_ = bf16[32,1024]{1,0:T(8,128)(2,1)S(1)} collective-permute-done((bf16[32,1024]{1,0:T(8,128)(2,1)S(1)}, bf16[32,1024]{1,0:T(8,128)(2,1)S(1)}, u32[]{:S(2)}, u32[]{:S(2)}) %collective-permute-start.2) | collective-permute-done | bytes 65568 | tf_op jit(solution)/shard_map/ppermute | solution.py:28
  15.6 1.6 %collective-permute-start.4 = (bf16[64,896]{1,0:T(8,128)(2,1)S(1)}, bf16[64,896]{1,0:T(8,128)(2,1)S(1)}, u32[]{:S(2)}, u32[]{:S(2)}) collective-permute-start(bf16[64,896]{1,0:T(8,128)(2,1)S(1)} %pad_maximum_fusion.2), channel_id=1, source_target_pairs={{0,2},{1,3},{2,0},{3,1},{4,6},{5,7},{6,4},{7,5},{8,10},{9,11},{10,... | collective-permute-start | bytes 344072 | tf_op jit(solution)/shard_map/ppermute | solution.py:28
  17.3 3.2 %collective-permute-done.4 = bf16[64,896]{1,0:T(8,128)(2,1)S(1)} collective-permute-done((bf16[64,896]{1,0:T(8,128)(2,1)S(1)}, bf16[64,896]{1,0:T(8,128)(2,1)S(1)}, u32[]{:S(2)}, u32[]{:S(2)}) %collective-permute-start.4) | collective-permute-done | bytes 114720 | tf_op jit(solution)/shard_map/ppermute | solution.py:28
  20.6 1.6 %collective-permute-start.8 = (bf16[2,64,640]{2,1,0:T(8,128)(2,1)S(1)}, bf16[2,64,640]{2,1,0:T(8,128)(2,1)S(1)}, u32[]{:S(2)}, u32[]{:S(2)}) collective-permute-start(bf16[2,64,640]{2,1,0:T(8,128)(2,1)S(1)} %shard_map.124.refs_0_), channel_id=1, source_target_pairs={{0,2},{1,3},{2,0},{3,1},{4,6},{5,7},{6,4},{7,5},{8,10},{9,11},{10,... | collective-permute-start | bytes 491528 | tf_op jit(solution)/shard_map/ppermute | solution.py:28
  22.2 4.3 %shard_map.125.act = bf16[128,2048]{1,0:T(8,128)(2,1)S(1)} custom-call(bf16[32,1024]{1,0:T(8,128)(2,1)S(1)} %shard_map.122.refs_0_, bf16[32,1024]{1,0:T(8,128)(2,1)S(1)} %collective-permute-done.refs_1_, bf16[32,1024]{1,0:T(8,128)(2,1)S(1)} %collective-permute-done.1.refs_2_, bf16[32,1024]{1,0:T(8,128)(2,1)S(1)} %collective-permute-done.2.refs_3_, ...), custom_call_target="tpu_custom_call" | custom-call | tf_op jit(solution)/shard_map/pallas_call | solution.py:53
  26.5 0.7 %collective-permute-done.8.refs_1_ = bf16[2,64,640]{2,1,0:T(8,128)(2,1)S(1)} collective-permute-done((bf16[2,64,640]{2,1,0:T(8,128)(2,1)S(1)}, bf16[2,64,640]{2,1,0:T(8,128)(2,1)S(1)}, u32[]{:S(2)}, u32[]{:S(2)}) %collective-permute-start.8) | collective-permute-done | bytes 163872 | tf_op jit(solution)/shard_map/ppermute | solution.py:28
  27.2 0.7 %shard_map.127 = bf16[128,896]{1,0:T(8,128)(2,1)S(1)} custom-call(bf16[128,2048]{1,0:T(8,128)(2,1)S(1)} %shard_map.125.act, bf16[2048,3584]{1,0:T(8,128)(2,1)S(1)} %bitcast.6), custom_call_target="tpu_custom_call" | custom-call | flops 469762048 | tf_op jit(solution)/shard_map/pallas_call | solution.py:53
  28.1 1.3 %shard_map.126 = (bf16[128,896]{1,0:T(8,128)(2,1)S(1)}, bf16[128,896]{1,0:T(8,128)(2,1)S(1)}) custom-call(bf16[128,2048]{1,0:T(8,128)(2,1)S(1)} %shard_map.125.act, bf16[2048,3584]{1,0:T(8,128)(2,1)S(1)} %bitcast.7), custom_call_target="tpu_custom_call" | custom-call | flops 939524096 | tf_op jit(solution)/shard_map/pallas_call | solution.py:53
  29.4 0.5 collective-permute-start.10
  30.0 1.6 %collective-permute-start.11 = (bf16[128,896]{1,0:T(8,128)(2,1)S(1)}, bf16[128,896]{1,0:T(8,128)(2,1)S(1)}, u32[]{:S(2)}, u32[]{:S(2)}) collective-permute-start(bf16[128,896]{1,0:T(8,128)(2,1)S(1)} %add_convert_fusion.1), channel_id=1, source_target_pairs={{0,2},{1,3},{2,0},{3,1},{4,6},{5,7},{6,4},{7,5},{8,10},{9,11},{10,... | collective-permute-start | bytes 688136 | tf_op jit(solution)/shard_map/ppermute | solution.py:28
  31.6 0.7 %shard_map.128 = bf16[128,896]{1,0:T(8,128)(2,1)S(1)} custom-call(bf16[128,2048]{1,0:T(8,128)(2,1)S(1)} %shard_map.125.act, bf16[2048,3584]{1,0:T(8,128)(2,1)S(1)} %bitcast.8), custom_call_target="tpu_custom_call" | custom-call | flops 469762048 | tf_op jit(solution)/shard_map/pallas_call | solution.py:53
  32.3 5.3 %collective-permute-done.11 = bf16[128,896]{1,0:T(8,128)(2,1)S(1)} collective-permute-done((bf16[128,896]{1,0:T(8,128)(2,1)S(1)}, bf16[128,896]{1,0:T(8,128)(2,1)S(1)}, u32[]{:S(2)}, u32[]{:S(2)}) %collective-permute-start.11) | collective-permute-done | bytes 229408 | tf_op jit(solution)/shard_map/ppermute | solution.py:28
  37.6 0.8 %add_convert_fusion = bf16[128,896]{1,0:T(8,128)(2,1)} fusion(bf16[128,896]{1,0:T(8,128)(2,1)S(1)} %collective-permute-done.11, bf16[128,896]{1,0:T(8,128)(2,1)S(1)} %collective-permute-done.10, bf16[128,896]{1,0:T(8,128)(2,1)S(1)} %shard_map.128), kind=kLoop, calls=%fused_computation | loop fusion | flops 688128 | bytes 917504 | tf_op jit(solution)/shard_map/convert_element_type | solution.py:337
  38.4 3.4 %all-to-all-start = ((bf16[4,32,896]{2,1,0:T(8,128)(2,1)}), bf16[4,32,896]{2,1,0:T(8,128)(2,1)S(1)}, u32[]{:S(2)}, u32[]{:S(2)}) async-start(bf16[4,32,896]{2,1,0:T(8,128)(2,1)} %bitcast.3), calls=%async_computation | async-start | bytes 458752 | tf_op jit(solution)/shard_map/all_to_all | solution.py:337
  42.1 1.3 %collective-permute-done.12.theirs = bf16[2,64,512]{2,1,0:T(8,128)(2,1)S(1)} collective-permute-done((bf16[2,64,512]{2,1,0:T(8,128)(2,1)S(1)}, bf16[2,64,512]{2,1,0:T(8,128)(2,1)S(1)}, u32[]{:S(2)}, u32[]{:S(2)}) %collective-permute-start.12) | collective-permute-done | bytes 131104 | tf_op jit(solution)/shard_map/ppermute | solution.py:28
  43.5 0.7 %shard_map.130 = bf16[2,128,512]{2,1,0:T(8,128)(2,1)} custom-call(bf16[2,64,512]{2,1,0:T(8,128)(2,1)S(1)} %shard_map.129.mine, bf16[2,64,512]{2,1,0:T(8,128)(2,1)S(1)} %collective-permute-done.12.theirs), custom_call_target="tpu_custom_call" | custom-call | tf_op jit(solution)/shard_map/pallas_call | solution.py:53
  44.2 5.4 %all-to-all-done = bf16[4,32,896]{2,1,0:T(8,128)(2,1)S(1)} async-done(((bf16[4,32,896]{2,1,0:T(8,128)(2,1)}), bf16[4,32,896]{2,1,0:T(8,128)(2,1)S(1)}, u32[]{:S(2)}, u32[]{:S(2)}) %all-to-all-start) | async-done | bytes 229408 | tf_op jit(solution)/shard_map/all_to_all | solution.py:337
  49.6 0.7 %reduce_sum.12 = bf16[32,896]{1,0:T(8,128)(2,1)} reduce(bf16[4,32,896]{2,1,0:T(8,128)(2,1)S(1)} %all-to-all-done, bf16[]{:T(256)} %constant.2.clone.1), dimensions={0}, to_apply=%region_0.0 | reduce | flops 86016 | bytes 286722 | tf_op jit(solution)/shard_map/reduce_sum | solution.py:338
  (50 shorter events, 1.3 us)
Async XLA Ops:
  0.6 5.2 %copy-start.4 = (bf16[2,512,512]{2,1,0:T(8,128)(2,1)S(1)}, bf16[2,512,512]{2,1,0:T(8,128)(2,1)}, u32[]{:S(2)}) copy-start(bf16[2,512,512]{2,1,0:T(8,128)(2,1)} %keys.1) | copy-start | bytes 3145732
  0.6 5.2 %copy-start.5 = (bf16[2,128,512]{2,1,0:T(8,128)(2,1)S(1)}, bf16[2,128,512]{2,1,0:T(8,128)(2,1)}, u32[]{:S(2)}) copy-start(bf16[2,128,512]{2,1,0:T(8,128)(2,1)} %q_lat) | copy-start | bytes 786436
  0.7 5.2 %copy-start.6 = (bf16[2,64,512]{2,1,0:T(8,128)(2,1)S(1)}, bf16[2,64,512]{2,1,0:T(8,128)(2,1)}, u32[]{:S(2)}) copy-start(bf16[2,64,512]{2,1,0:T(8,128)(2,1)} %rope.1) | copy-start | bytes 393220
  0.7 5.2 %copy-start.7 = (bf16[2,64,128]{2,1,0:T(8,128)(2,1)S(1)}, bf16[2,64,128]{2,1,0:T(8,128)(2,1)}, u32[]{:S(2)}) copy-start(bf16[2,64,128]{2,1,0:T(8,128)(2,1)} %q_rope.1) | copy-start | bytes 98308
  0.7 5.2 %copy-start.8 = (s32[2]{0:T(128)S(1)}, s32[2]{0:T(128)}, u32[]{:S(2)}) copy-start(s32[2]{0:T(128)} %lengths.1) | copy-start | bytes 28
  0.7 21.5 %copy-start = (bf16[8,3584,256]{2,1,0:T(8,128)(2,1)S(1)}, bf16[8,3584,256]{2,1,0:T(8,128)(2,1)}, u32[]{:S(2)}) copy-start(bf16[8,3584,256]{2,1,0:T(8,128)(2,1)} %refs_10_.1) | copy-start | bytes 44040196
  0.7 21.5 %copy-start.1 = (bf16[8,3584,256]{2,1,0:T(8,128)(2,1)S(1)}, bf16[8,3584,256]{2,1,0:T(8,128)(2,1)}, u32[]{:S(2)}) copy-start(bf16[8,3584,256]{2,1,0:T(8,128)(2,1)} %refs_11_.1) | copy-start | bytes 44040196
  0.7 21.5 %copy-start.2 = (bf16[32,3584]{1,0:T(8,128)(2,1)S(1)}, bf16[32,3584]{1,0:T(8,128)(2,1)}, u32[]{:S(2)}) copy-start(bf16[32,3584]{1,0:T(8,128)(2,1)} %refs_4_.1) | copy-start | bytes 688132
  0.7 21.5 %copy-start.3 = (bf16[3584,32]{0,1:T(8,128)(2,1)S(1)}, bf16[3584,32]{0,1:T(8,128)(2,1)}, u32[]{:S(2)}) copy-start(bf16[3584,32]{0,1:T(8,128)(2,1)} %param.13) | copy-start | bytes 688132
  1.8 7.8 %collective-permute-start.1 = (bf16[32,1024]{1,0:T(8,128)(2,1)S(1)}, bf16[32,1024]{1,0:T(8,128)(2,1)S(1)}, u32[]{:S(2)}, u32[]{:S(2)}) collective-permute-start(bf16[32,1024]{1,0:T(8,128)(2,1)S(1)} %shard_map.122.refs_0_), channel_id=1, source_target_pairs={{0,8},{4,12},{8,0},{12,4},{1,9},{5,13},{9,1},{13,5},{2,10},{6,14},... | collective-permute-start | bytes 196616 | tf_op jit(solution)/shard_map/ppermute | solution.py:28
  7.6 4.3 %collective-permute-start = (bf16[32,1024]{1,0:T(8,128)(2,1)S(1)}, bf16[32,1024]{1,0:T(8,128)(2,1)S(1)}, u32[]{:S(2)}, u32[]{:S(2)}) collective-permute-start(bf16[32,1024]{1,0:T(8,128)(2,1)S(1)} %shard_map.122.refs_0_), channel_id=1, source_target_pairs={{0,4},{4,0},{8,12},{12,8},{1,5},{5,1},{9,13},{13,9},{2,6},{6,2},{1... | collective-permute-start | bytes 196616 | tf_op jit(solution)/shard_map/ppermute | solution.py:28
  9.2 6.1 %collective-permute-start.2 = (bf16[32,1024]{1,0:T(8,128)(2,1)S(1)}, bf16[32,1024]{1,0:T(8,128)(2,1)S(1)}, u32[]{:S(2)}, u32[]{:S(2)}) collective-permute-start(bf16[32,1024]{1,0:T(8,128)(2,1)S(1)} %shard_map.122.refs_0_), channel_id=1, source_target_pairs={{0,12},{4,8},{8,4},{12,0},{1,13},{5,9},{9,5},{13,1},{2,14},{6,10},... | collective-permute-start | bytes 196616 | tf_op jit(solution)/shard_map/ppermute | solution.py:28
  9.2 6.1 %collective-permute-start.3 = (bf16[2,64,640]{2,1,0:T(8,128)(2,1)S(1)}, bf16[2,64,640]{2,1,0:T(8,128)(2,1)S(1)}, u32[]{:S(2)}, u32[]{:S(2)}) collective-permute-start(bf16[2,64,640]{2,1,0:T(8,128)(2,1)S(1)} %get-tuple-element.29), channel_id=1, source_target_pairs={{0,1},{1,0},{2,3},{3,2},{4,5},{5,4},{6,7},{7,6},{8,9},{9,8},{10,11... | collective-permute-start | bytes 491528 | tf_op jit(solution)/shard_map/ppermute | solution.py:28
  9.5 11.0 %collective-permute-start.5 = (bf16[32,896]{1,0:T(8,128)(2,1)S(1)}, bf16[32,896]{1,0:T(8,128)(2,1)S(1)}, u32[]{:S(2)}, u32[]{:S(2)}) collective-permute-start(bf16[32,896]{1,0:T(8,128)(2,1)S(1)} %slice.21), channel_id=1, source_target_pairs={{0,2},{1,3},{2,0},{3,1},{4,6},{5,7},{6,4},{7,5},{8,10},{9,11},{10,... | collective-permute-start | bytes 172040 | tf_op jit(solution)/shard_map/ppermute | solution.py:28
  15.3 11.9 %slice-start = ((s8[14680064]{0:T(1024)(128)(4,1)}), s8[4194304]{0:T(1024)(128)(4,1)S(1)}, s32[]{:S(2)}) async-start(s8[14680064]{0:T(1024)(128)(4,1)} %bitcast.4), calls=%async_computation.1 | async-start | bytes 8388608
  15.6 4.9 %collective-permute-start.4 = (bf16[64,896]{1,0:T(8,128)(2,1)S(1)}, bf16[64,896]{1,0:T(8,128)(2,1)S(1)}, u32[]{:S(2)}, u32[]{:S(2)}) collective-permute-start(bf16[64,896]{1,0:T(8,128)(2,1)S(1)} %pad_maximum_fusion.2), channel_id=1, source_target_pairs={{0,2},{1,3},{2,0},{3,1},{4,6},{5,7},{6,4},{7,5},{8,10},{9,11},{10,... | collective-permute-start | bytes 344072 | tf_op jit(solution)/shard_map/ppermute | solution.py:28
  17.2 5.0 %collective-permute-start.6 = (bf16[96,896]{1,0:T(8,128)(2,1)S(1)}, bf16[96,896]{1,0:T(8,128)(2,1)S(1)}, u32[]{:S(2)}, u32[]{:S(2)}) collective-permute-start(bf16[96,896]{1,0:T(8,128)(2,1)S(1)} %pad_maximum_fusion.refs_5_), channel_id=1, source_target_pairs={{0,1},{1,0},{2,3},{3,2},{4,5},{5,4},{6,7},{7,6},{8,9},{9,8},{10,11... | collective-permute-start | bytes 516104 | tf_op jit(solution)/shard_map/ppermute | solution.py:28
  20.5 1.6 %collective-permute-start.7 = (bf16[96,896]{1,0:T(8,128)(2,1)S(1)}, bf16[96,896]{1,0:T(8,128)(2,1)S(1)}, u32[]{:S(2)}, u32[]{:S(2)}) collective-permute-start(bf16[96,896]{1,0:T(8,128)(2,1)S(1)} %pad_maximum_fusion.1.refs_6_), channel_id=1, source_target_pairs={{0,1},{1,0},{2,3},{3,2},{4,5},{5,4},{6,7},{7,6},{8,9},{9,8},{10,11... | collective-permute-start | bytes 516104 | tf_op jit(solution)/shard_map/ppermute | solution.py:28
  20.6 6.6 %collective-permute-start.8 = (bf16[2,64,640]{2,1,0:T(8,128)(2,1)S(1)}, bf16[2,64,640]{2,1,0:T(8,128)(2,1)S(1)}, u32[]{:S(2)}, u32[]{:S(2)}) collective-permute-start(bf16[2,64,640]{2,1,0:T(8,128)(2,1)S(1)} %shard_map.124.refs_0_), channel_id=1, source_target_pairs={{0,2},{1,3},{2,0},{3,1},{4,6},{5,7},{6,4},{7,5},{8,10},{9,11},{10,... | collective-permute-start | bytes 491528 | tf_op jit(solution)/shard_map/ppermute | solution.py:28
  28.0 1.9 %collective-permute-start.9 = (bf16[128,896]{1,0:T(8,128)(2,1)S(1)}, bf16[128,896]{1,0:T(8,128)(2,1)S(1)}, u32[]{:S(2)}, u32[]{:S(2)}) collective-permute-start(bf16[128,896]{1,0:T(8,128)(2,1)S(1)} %shard_map.127), channel_id=1, source_target_pairs={{0,1},{1,0},{2,3},{3,2},{4,5},{5,4},{6,7},{7,6},{8,9},{9,8},{10,11... | collective-permute-start | bytes 688136 | tf_op jit(solution)/shard_map/ppermute | solution.py:28
  29.4 2.9 %collective-permute-start.10 = (bf16[128,896]{1,0:T(8,128)(2,1)S(1)}, bf16[128,896]{1,0:T(8,128)(2,1)S(1)}, u32[]{:S(2)}, u32[]{:S(2)}) collective-permute-start(bf16[128,896]{1,0:T(8,128)(2,1)S(1)} %get-tuple-element.40), channel_id=1, source_target_pairs={{0,1},{1,0},{2,3},{3,2},{4,5},{5,4},{6,7},{7,6},{8,9},{9,8},{10,11... | collective-permute-start | bytes 688136 | tf_op jit(solution)/shard_map/ppermute | solution.py:28
  30.0 7.7 %collective-permute-start.11 = (bf16[128,896]{1,0:T(8,128)(2,1)S(1)}, bf16[128,896]{1,0:T(8,128)(2,1)S(1)}, u32[]{:S(2)}, u32[]{:S(2)}) collective-permute-start(bf16[128,896]{1,0:T(8,128)(2,1)S(1)} %add_convert_fusion.1), channel_id=1, source_target_pairs={{0,2},{1,3},{2,0},{3,1},{4,6},{5,7},{6,4},{7,5},{8,10},{9,11},{10,... | collective-permute-start | bytes 688136 | tf_op jit(solution)/shard_map/ppermute | solution.py:28
  38.4 11.2 %all-to-all-start = ((bf16[4,32,896]{2,1,0:T(8,128)(2,1)}), bf16[4,32,896]{2,1,0:T(8,128)(2,1)S(1)}, u32[]{:S(2)}, u32[]{:S(2)}) async-start(bf16[4,32,896]{2,1,0:T(8,128)(2,1)} %bitcast.3), calls=%async_computation | async-start | bytes 458752 | tf_op jit(solution)/shard_map/all_to_all | solution.py:337
  42.1 1.4 %collective-permute-start.12 = (bf16[2,64,512]{2,1,0:T(8,128)(2,1)S(1)}, bf16[2,64,512]{2,1,0:T(8,128)(2,1)S(1)}, u32[]{:S(2)}, u32[]{:S(2)}) collective-permute-start(bf16[2,64,512]{2,1,0:T(8,128)(2,1)S(1)} %shard_map.129.mine), channel_id=1, source_target_pairs={{0,1},{1,0},{2,3},{3,2},{4,5},{5,4},{6,7},{7,6},{8,9},{9,8},{10,11... | collective-permute-start | bytes 393224 | tf_op jit(solution)/shard_map/ppermute | solution.py:28
  (3 other events, 15.0 us)

commit v6 on v4

--- a/solution.py
+++ b/solution.py
@@ -102,7 +102,6 @@
         [q_latent, q_rope, cache_latent, cache_rope, cache_len],
         [VMEM, VMEM, VMEM, VMEM, SMEM],
         [pltpu.VMEM((rows, heads, width + LANES), bf16)],
-        flops=2_000_000_000,
     )
 
 
@@ -142,11 +141,11 @@
     return local_call(place_kernel, shaped(rows, 2 * half, width), [mine, theirs], [VMEM, VMEM])
 
 
-def pack_kernel(spots, hidden, routes, out, tags, sems):
+def pack_kernel(hidden, routes, out, tags, sems):
     size = out.shape[1] - LANES
     picks, rows = routes.shape
-    spot, core = spot_and_core()
-    start = pl.multiple_of((spot * 2 + core if spots > 1 else core) * size, size)
+    _, core = spot_and_core()
+    start = pl.multiple_of(core * size, size)
     columns = pltpu.make_async_copy(hidden.at[:, pl.ds(start, size)], out.at[:, pl.ds(0, size)], sems.at[0])
     named = pltpu.make_async_copy(routes, tags, sems.at[1])
     columns.start()
@@ -159,11 +158,11 @@
     columns.wait()
 
 
-def pack_rows(hidden, routes, spots):
+def pack_rows(hidden, routes):
     rows, width = hidden.shape
     return local_call(
-        functools.partial(pack_kernel, spots),
-        shaped(rows, width // (2 * spots) + LANES),
+        pack_kernel,
+        shaped(rows, width // 2 + LANES),
         [pltpu.with_memory_space_constraint(a, pltpu.HBM) for a in (hidden, routes.T)],
         [ANY, ANY],
         [pltpu.VMEM(routes.shape[::-1], jnp.int32), pltpu.SemaphoreType.DMA((2,))],
@@ -172,18 +171,19 @@
     )
 
 
-def act_kernel(picks, ways, packs, own, mine, theirs, router, gate, up, down, act, outs, x, tags):
+def act_kernel(picks, packs, own, theirs, router, gate, up, down, act, outs, x, tags):
     rows = own.shape[0]
-    spots = len(mine)
-    size = mine[0].shape[1]
+    size = packs[0].shape[1] - LANES
     local, _, hidden = gate.shape
-    spot, core = spot_and_core()
+    _, core = spot_and_core()
+    mine = pl.ds(pl.multiple_of(core * size, size), size)
+    other = pl.ds(pl.multiple_of((1 - core) * size, size), size)
     x[pl.ds(0, rows), :] = own[...]
-    later = pl.ds(rows, mine[0].shape[0])
-    for s in range(spots):
-        first = partner(spot, s, ways) * 2 if spots > 1 else 0
-        x[later, pl.ds(pl.multiple_of((first + core) * size, size), size)] = mine[s][...]
-        x[later, pl.ds(pl.multiple_of((first + 1 - core) * size, size), size)] = theirs[s][...]
+    for s, pack in enumerate(packs):
+        if s:
+            x[pl.ds(s * rows, rows), mine] = pack[:, :size]
+    for ref, start, first in theirs:
+        x[pl.ds(first, rows), other] = ref[pl.ds(start, rows), :]
     for s, pack in enumerate(packs):
         tags[pl.ds(s * rows, rows), :] = pack[:, size:]
 
@@ -206,36 +206,36 @@
         out[...] = dot(act[...], down[0][...]).astype(bf16)
 
 
-def act_call(packs, own, mine, theirs, router, gate, up, down, picks, ways, whole):
+def act_call(packs, own, theirs, places, router, gate, up, down, picks, whole):
     rows, width = own.shape
     local, _, hidden = gate.shape
     count = rows * len(packs)
     down = [down] if whole else []
-    cuts = [len(packs), 1, len(mine), len(theirs), 3, len(down)]
+    cuts = [len(packs), 1, len(theirs), 3, len(down)]
 
     def kernel(*refs):
         groups = []
         for cut in cuts:
             groups.append(refs[:cut])
             refs = refs[cut:]
-        packs, (own,), mine, theirs, (router, gate, up), down = groups
-        act_kernel(picks, ways, packs, own, mine, theirs, router, gate, up, down, refs[0], refs[1:-2], *refs[-2:])
+        packs, (own,), theirs, (router, gate, up), down = groups
+        theirs = [(ref, i * rows, s * rows) for ref, steps in zip(theirs, places) for i, s in enumerate(steps)]
+        act_kernel(picks, packs, own, theirs, router, gate, up, down, refs[0], refs[1:-2], *refs[-2:])
 
     parts = [shaped(count, width)] if whole else []
-    operands = [*packs, own, *mine, *theirs, router, gate, up, *down]
+    operands = [*packs, own, *theirs, router, gate, up, *down]
     return local_call(
         kernel,
         [pltpu.VMEM((count, local * hidden), bf16)] + parts,
         operands,
         [VMEM] * len(operands),
         [pltpu.VMEM((count, width), bf16), pltpu.VMEM((count, LANES), bf16)],
-        flops=4 * count * local * hidden * width,
         limit=10 if count <= 256 else 48,
     )
 
 
 def down_call(act, down, pairs, ways):
-    count, depth = act.shape
+    count = act.shape[0]
     width = down.shape[1]
 
     def kernel(act, down, *outs):
@@ -250,7 +250,6 @@
         [shaped(count, width // (2 * ways))] * len(pairs),
         [act, down],
         [VMEM, VMEM],
-        flops=2 * count * depth * (width // (2 * ways)) * len(pairs),
     )
 
 
@@ -272,25 +271,17 @@
     n_dev, n_tp = lax.axis_size("dev"), lax.axis_size("tp")
     ways = n_tp // 2
     aligned = width % (n_tp * LANES) == 0
-    spots = ways if aligned else 1
-    share = width // (2 * spots)
-
-    pack = pack_rows(hidden, routes, spots)
+    half = width // 2
+
+    pack = pack_rows(hidden, routes)
     packs = [pack] + [over_dev(pack, s, n_dev) for s in range(1, n_dev)]
-    near = [p[:, :share] for p in packs[1:]]
-    first = n_dev // 2 - 1
-    rest = jnp.concatenate(near[:first] + near[first + 1 :], axis=0)
-    early = [send(near[first], "tp", along_x(s, ways)) for s in range(1, spots)]
-    late = [send(rest, "tp", along_x(s, ways)) for s in range(1, spots)]
-    early, q_latent = lax.optimization_barrier((early, q_latent))
-    mine = [jnp.concatenate(near, axis=0)]
-    theirs = [send(mine[0], "tp", other_core)]
-
+    first = n_dev // 2
+    places = [[first], [s for s in range(1, n_dev) if s != first]]
+    early, q_latent = lax.optimization_barrier((packs[first], q_latent))
     keep, give = attend(q_latent, q_rope, cache_latent, cache_rope, cache_len)
-    late, keep, give = lax.optimization_barrier((late, keep, give))
-    cut = first * rows
-    mine += [jnp.concatenate([b[:cut], a, b[cut:]], axis=0) for a, b in zip(early, late)]
-    theirs += [send(m, "tp", other_core) for m in mine[1:]]
+    packs, keep, give = lax.optimization_barrier((packs, keep, give))
+    packs[first] = early
+    theirs = [send(jnp.concatenate([packs[s][:, :half] for s in p], axis=0), "tp", other_core) for p in places]
     state = join([keep, send(give, "tp", other_core)], False)
     theirs, state = lax.optimization_barrier((theirs, state))
     states = [state] + [send(state, "tp", along_x(s, ways)) for s in range(1, ways)]
@@ -300,7 +291,7 @@
         for w in (gate_weight, up_weight, down_weight.reshape(local * units, width))
     ]
     act, *parts = act_call(
-        packs, hidden, mine, theirs, router_weight.T, gate, up, down, routes.shape[1], ways, not aligned
+        packs, hidden, theirs, places, router_weight.T, gate, up, down, routes.shape[1], not aligned
     )
     def added(a, b):
         return a.astype(f32) + b.astype(f32)

time: 47 us -> 51 us (1.085)
  starting transfers between devices: 18.9 us -> 13.1 us
  local copies, waits for them, and re-layouts: 0.13 us -> 5.26 us
  waiting for transfers between devices: 14.8 us -> 19.6 us
    ppermute x16 -> x14, starting transfers between devices: 18.9 us -> 13.1 us  [send(): return lax.ppermute(value, axis, [(i, target(i)) for i in range(size)])]
    unnamed x38 -> x26, local copies, waits for them, and re-layouts: 0.09 us -> 5.22 us
    ppermute x16 -> x14, waiting for transfers between devices: 14.8 us -> 19.6 us  [send(): return lax.ppermute(value, axis, [(i, target(i)) for i in range(size)])]
  transfers between devices with their start and end apart: 16 -> 14, of which waited for: 8 -> 5; matrix products, arithmetic and copies ran while one was open for 0% -> 0% of each run, Pallas kernels for 20% -> 18%
where the time goes in v6:
time: 51 us; the launch traced here: 50.8 us
  waiting for transfers between devices  19.6 us (38%)
  starting transfers between devices  13.1 us (26%)
  Pallas kernels  11.1 us (22%)
  local copies, waits for them, and re-layouts  5.26 us (10%)
  between operations  0.95 us (2%)
  other arithmetic  0.82 us (2%)
    ppermute x14, waiting for transfers between devices, send(): return lax.ppermute(value, axis, [(i, target(i)) for i in range(size)])  19.6 us
    ppermute x14, starting transfers between devices, send(): return lax.ppermute(value, axis, [(i, target(i)) for i in range(size)])  13.1 us
    pallas_call x9, Pallas kernels, local_call(): pl.pallas_call(kernel, out_shape=outs, in_specs=specs, out_specs=jax.tree...  11.1 us
    unnamed x26, local copies, waits for them, and re-layouts  5.22 us
  transfers between devices with their start and end apart: 14, of which 5 were waited for; matrix products, arithmetic and copies ran while one was open for 0% of the time, Pallas kernels for 18%

profile of v6, /device:TPU:0, one launch (start us, length us, event | category | flops | bytes accessed | tf_op | source)
XLA Modules:
  0.0 50.8 jit_solution(3683265362923563611)
XLA Ops:
  0.7 1.1 %shard_map.122.refs_0_ = bf16[32,1920]{1,0:T(8,128)(2,1)S(1)} custom-call(bf16[32,3584]{1,0:T(8,128)(2,1)} %refs_4_.1, s32[8,32]{1,0:T(8,128)} %bitcast.9), custom_call_target="tpu_custom_call" | custom-call | flops 20000000000 | tf_op jit(solution)/shard_map/pallas_call | solution.py:53
  1.8 4.1 %collective-permute-start.1 = (bf16[32,1920]{1,0:T(8,128)(2,1)S(1)}, bf16[32,1920]{1,0:T(8,128)(2,1)S(1)}, u32[]{:S(2)}, u32[]{:S(2)}) collective-permute-start(bf16[32,1920]{1,0:T(8,128)(2,1)S(1)} %shard_map.122.refs_0_), channel_id=1, source_target_pairs={{0,8},{4,12},{8,0},{12,4},{1,9},{5,13},{9,1},{13,5},{2,10},{6,14},... | collective-permute-start | bytes 368648 | tf_op jit(solution)/shard_map/ppermute | solution.py:28
  5.9 1.3 %collective-permute-start.2 = (bf16[32,1920]{1,0:T(8,128)(2,1)S(1)}, bf16[32,1920]{1,0:T(8,128)(2,1)S(1)}, u32[]{:S(2)}, u32[]{:S(2)}) collective-permute-start(bf16[32,1920]{1,0:T(8,128)(2,1)S(1)} %shard_map.122.refs_0_), channel_id=1, source_target_pairs={{0,12},{4,8},{8,4},{12,0},{1,13},{5,9},{9,5},{13,1},{2,14},{6,10},... | collective-permute-start | bytes 368648 | tf_op jit(solution)/shard_map/ppermute | solution.py:28
  7.5 7.9 %collective-permute-done.1.refs_2_ = bf16[32,1920]{1,0:T(8,128)(2,1)S(1)} collective-permute-done((bf16[32,1920]{1,0:T(8,128)(2,1)S(1)}, bf16[32,1920]{1,0:T(8,128)(2,1)S(1)}, u32[]{:S(2)}, u32[]{:S(2)}) %collective-permute-start.1) | collective-permute-done | bytes 122912 | tf_op jit(solution)/shard_map/ppermute | solution.py:28
  15.4 1.7 %shard_map.123 = (bf16[2,64,640]{2,1,0:T(8,128)(2,1)S(1)}, bf16[2,64,640]{2,1,0:T(8,128)(2,1)S(1)}) custom-call(bf16[2,128,512]{2,1,0:T(8,128)(2,1)S(1)} %copy-done.3, bf16[2,64,128]{2,1,0:T(8,128)(2,1)S(1)} %copy-done.7, bf16[2,512,512]{2,1,0:T(8,128)(2,1)S(1)} %copy-done.2, bf16[2,64,512]{2,1,0:T(8,128)(2,1)S(1)} %copy-done.6, s32[2]{0:T(128)S(1)} %copy-done.8), custom_call_target="tpu_custom_call" | custom-call | tf_op jit(solution)/shard_map/pallas_call | solution.py:53
  17.3 0.5 collective-permute-start.5
  17.9 1.1 %collective-permute-done.5.refs_1_ = bf16[2,64,640]{2,1,0:T(8,128)(2,1)S(1)} collective-permute-done((bf16[2,64,640]{2,1,0:T(8,128)(2,1)S(1)}, bf16[2,64,640]{2,1,0:T(8,128)(2,1)S(1)}, u32[]{:S(2)}, u32[]{:S(2)}) %collective-permute-start.5) | collective-permute-done | bytes 163872 | tf_op jit(solution)/shard_map/ppermute | solution.py:28
  19.0 0.3 shard_map.124.refs_0_
  19.3 1.9 %collective-permute-start.6 = (bf16[2,64,640]{2,1,0:T(8,128)(2,1)S(1)}, bf16[2,64,640]{2,1,0:T(8,128)(2,1)S(1)}, u32[]{:S(2)}, u32[]{:S(2)}) collective-permute-start(bf16[2,64,640]{2,1,0:T(8,128)(2,1)S(1)} %shard_map.124.refs_0_), channel_id=1, source_target_pairs={{0,2},{1,3},{2,0},{3,1},{4,6},{5,7},{6,4},{7,5},{8,10},{9,11},{10,... | collective-permute-start | bytes 491528 | tf_op jit(solution)/shard_map/ppermute | solution.py:28
  21.2 5.2 %copy-done = bf16[8,3584,256]{2,1,0:T(8,128)(2,1)S(1)} copy-done((bf16[8,3584,256]{2,1,0:T(8,128)(2,1)S(1)}, bf16[8,3584,256]{2,1,0:T(8,128)(2,1)}, u32[]{:S(2)}) %copy-start) | copy-done | bytes 14680088
  26.4 4.3 %shard_map.125.act = bf16[128,2048]{1,0:T(8,128)(2,1)S(1)} custom-call(bf16[32,1920]{1,0:T(8,128)(2,1)S(1)} %shard_map.122.refs_0_, bf16[32,1920]{1,0:T(8,128)(2,1)S(1)} %collective-permute-done.refs_1_, bf16[32,1920]{1,0:T(8,128)(2,1)S(1)} %collective-permute-done.1.refs_2_, bf16[32,1920]{1,0:T(8,128)(2,1)S(1)} %collective-permute-done.2.refs_3_, ...), custom_call_target="tpu_custom_call" | custom-call | tf_op jit(solution)/shard_map/pallas_call | solution.py:53
  30.7 0.7 %shard_map.127 = bf16[128,896]{1,0:T(8,128)(2,1)S(1)} custom-call(bf16[128,2048]{1,0:T(8,128)(2,1)S(1)} %shard_map.125.act, bf16[2048,3584]{1,0:T(8,128)(2,1)S(1)} %bitcast.5), custom_call_target="tpu_custom_call" | custom-call | tf_op jit(solution)/shard_map/pallas_call | solution.py:53
  31.5 1.3 %shard_map.126 = (bf16[128,896]{1,0:T(8,128)(2,1)S(1)}, bf16[128,896]{1,0:T(8,128)(2,1)S(1)}) custom-call(bf16[128,2048]{1,0:T(8,128)(2,1)S(1)} %shard_map.125.act, bf16[2048,3584]{1,0:T(8,128)(2,1)S(1)} %bitcast.6), custom_call_target="tpu_custom_call" | custom-call | tf_op jit(solution)/shard_map/pallas_call | solution.py:53
  32.9 0.5 collective-permute-start.8
  33.4 0.3 collective-permute-start.9
  33.8 0.7 %shard_map.128 = bf16[128,896]{1,0:T(8,128)(2,1)S(1)} custom-call(bf16[128,2048]{1,0:T(8,128)(2,1)S(1)} %shard_map.125.act, bf16[2048,3584]{1,0:T(8,128)(2,1)S(1)} %bitcast.7), custom_call_target="tpu_custom_call" | custom-call | tf_op jit(solution)/shard_map/pallas_call | solution.py:53
  34.5 0.3 shard_map.129.mine
  34.8 6.3 %collective-permute-done.9 = bf16[128,896]{1,0:T(8,128)(2,1)S(1)} collective-permute-done((bf16[128,896]{1,0:T(8,128)(2,1)S(1)}, bf16[128,896]{1,0:T(8,128)(2,1)S(1)}, u32[]{:S(2)}, u32[]{:S(2)}) %collective-permute-start.9) | collective-permute-done | bytes 229408 | tf_op jit(solution)/shard_map/ppermute | solution.py:28
  41.2 0.5 collective-permute-start.10
  41.7 3.4 %collective-permute-start.12 = (bf16[32,896]{1,0:T(8,128)(2,1)S(1)}, bf16[32,896]{1,0:T(8,128)(2,1)S(1)}, u32[]{:S(2)}, u32[]{:S(2)}) collective-permute-start(bf16[32,896]{1,0:T(8,128)(2,1)S(1)} %get-tuple-element.47), channel_id=1, source_target_pairs={{0,12},{4,8},{8,4},{12,0},{1,13},{5,9},{9,5},{13,1},{2,14},{6,10},... | collective-permute-start | bytes 172040 | tf_op jit(solution)/shard_map/ppermute | solution.py:28
  45.1 0.7 %shard_map.130 = bf16[2,128,512]{2,1,0:T(8,128)(2,1)} custom-call(bf16[2,64,512]{2,1,0:T(8,128)(2,1)S(1)} %shard_map.129.mine, bf16[2,64,512]{2,1,0:T(8,128)(2,1)S(1)} %collective-permute-done.13.theirs), custom_call_target="tpu_custom_call" | custom-call | tf_op jit(solution)/shard_map/pallas_call | solution.py:53
  45.8 2.5 %collective-permute-done.12 = bf16[32,896]{1,0:T(8,128)(2,1)S(1)} collective-permute-done((bf16[32,896]{1,0:T(8,128)(2,1)S(1)}, bf16[32,896]{1,0:T(8,128)(2,1)S(1)}, u32[]{:S(2)}, u32[]{:S(2)}) %collective-permute-start.12) | collective-permute-done | bytes 57376 | tf_op jit(solution)/shard_map/ppermute | solution.py:28
  48.3 1.8 %collective-permute-done.11 = bf16[32,896]{1,0:T(8,128)(2,1)S(1)} collective-permute-done((bf16[32,896]{1,0:T(8,128)(2,1)S(1)}, bf16[32,896]{1,0:T(8,128)(2,1)S(1)}, u32[]{:S(2)}, u32[]{:S(2)}) %collective-permute-start.11) | collective-permute-done | bytes 57376 | tf_op jit(solution)/shard_map/ppermute | solution.py:28
  50.2 0.7 %fusion.2 = bf16[32,896]{1,0:T(8,128)(2,1)} fusion(f32[128,896]{1,0:T(8,128)S(1)} %get-tuple-element.45, bf16[32,896]{1,0:T(8,128)(2,1)S(1)} %collective-permute-done.12, bf16[32,896]{1,0:T(8,128)(2,1)S(1)} %collective-permute-done.11, bf16[32,896]{1,0:T(8,128)(2,1)S(1)} %collective-permute-done.10), kind=kLoop, calls=%fused_computation.6 | loop fusion | flops 200704 | bytes 344064 | tf_op jit(solution)/shard_map/convert_element_type | solution.py:328
  (48 shorter events, 0.9 us)
Async XLA Ops:
  0.6 14.7 %copy-start.2 = (bf16[2,512,512]{2,1,0:T(8,128)(2,1)S(1)}, bf16[2,512,512]{2,1,0:T(8,128)(2,1)}, u32[]{:S(2)}) copy-start(bf16[2,512,512]{2,1,0:T(8,128)(2,1)} %keys.1) | copy-start | bytes 3145732
  0.6 14.7 %copy-start.3 = (bf16[2,128,512]{2,1,0:T(8,128)(2,1)S(1)}, bf16[2,128,512]{2,1,0:T(8,128)(2,1)}, u32[]{:S(2)}) copy-start(bf16[2,128,512]{2,1,0:T(8,128)(2,1)} %q_lat) | copy-start | bytes 786436
  0.7 14.7 %copy-start.6 = (bf16[2,64,512]{2,1,0:T(8,128)(2,1)S(1)}, bf16[2,64,512]{2,1,0:T(8,128)(2,1)}, u32[]{:S(2)}) copy-start(bf16[2,64,512]{2,1,0:T(8,128)(2,1)} %rope.1) | copy-start | bytes 393220
  0.7 14.7 %copy-start.7 = (bf16[2,64,128]{2,1,0:T(8,128)(2,1)S(1)}, bf16[2,64,128]{2,1,0:T(8,128)(2,1)}, u32[]{:S(2)}) copy-start(bf16[2,64,128]{2,1,0:T(8,128)(2,1)} %q_rope.1) | copy-start | bytes 98308
  0.7 14.7 %copy-start.8 = (s32[2]{0:T(128)S(1)}, s32[2]{0:T(128)}, u32[]{:S(2)}) copy-start(s32[2]{0:T(128)} %lengths.1) | copy-start | bytes 28
  0.7 20.5 %copy-start.1 = (bf16[8,3584,256]{2,1,0:T(8,128)(2,1)S(1)}, bf16[8,3584,256]{2,1,0:T(8,128)(2,1)}, u32[]{:S(2)}) copy-start(bf16[8,3584,256]{2,1,0:T(8,128)(2,1)} %refs_9_.1) | copy-start | bytes 44040196
  0.7 20.5 %copy-start.4 = (bf16[32,3584]{1,0:T(8,128)(2,1)S(1)}, bf16[32,3584]{1,0:T(8,128)(2,1)}, u32[]{:S(2)}) copy-start(bf16[32,3584]{1,0:T(8,128)(2,1)} %refs_4_.1) | copy-start | bytes 688132
  0.7 20.5 %copy-start.5 = (bf16[3584,32]{0,1:T(8,128)(2,1)S(1)}, bf16[3584,32]{0,1:T(8,128)(2,1)}, u32[]{:S(2)}) copy-start(bf16[3584,32]{0,1:T(8,128)(2,1)} %param.13) | copy-start | bytes 688132
  1.8 13.6 %collective-permute-start.1 = (bf16[32,1920]{1,0:T(8,128)(2,1)S(1)}, bf16[32,1920]{1,0:T(8,128)(2,1)S(1)}, u32[]{:S(2)}, u32[]{:S(2)}) collective-permute-start(bf16[32,1920]{1,0:T(8,128)(2,1)S(1)} %shard_map.122.refs_0_), channel_id=1, source_target_pairs={{0,8},{4,12},{8,0},{12,4},{1,9},{5,13},{9,1},{13,5},{2,10},{6,14},... | collective-permute-start | bytes 368648 | tf_op jit(solution)/shard_map/ppermute | solution.py:28
  5.9 11.2 %collective-permute-start.2 = (bf16[32,1920]{1,0:T(8,128)(2,1)S(1)}, bf16[32,1920]{1,0:T(8,128)(2,1)S(1)}, u32[]{:S(2)}, u32[]{:S(2)}) collective-permute-start(bf16[32,1920]{1,0:T(8,128)(2,1)S(1)} %shard_map.122.refs_0_), channel_id=1, source_target_pairs={{0,12},{4,8},{8,4},{12,0},{1,13},{5,9},{9,5},{13,1},{2,14},{6,10},... | collective-permute-start | bytes 368648 | tf_op jit(solution)/shard_map/ppermute | solution.py:28
  7.2 9.9 %collective-permute-start = (bf16[32,1920]{1,0:T(8,128)(2,1)S(1)}, bf16[32,1920]{1,0:T(8,128)(2,1)S(1)}, u32[]{:S(2)}, u32[]{:S(2)}) collective-permute-start(bf16[32,1920]{1,0:T(8,128)(2,1)S(1)} %shard_map.122.refs_0_), channel_id=1, source_target_pairs={{0,4},{4,0},{8,12},{12,8},{1,5},{5,1},{9,13},{13,9},{2,6},{6,2},{1... | collective-permute-start | bytes 368648 | tf_op jit(solution)/shard_map/ppermute | solution.py:28
  17.1 13.5 %slice-start = ((s8[14680064]{0:T(1024)(128)(4,1)}), s8[4194304]{0:T(1024)(128)(4,1)S(1)}, s32[]{:S(2)}) async-start(s8[14680064]{0:T(1024)(128)(4,1)} %bitcast.3), calls=%async_computation | async-start | bytes 8388608
  17.2 2.1 %collective-permute-start.4 = (bf16[64,1792]{1,0:T(8,128)(2,1)S(1)}, bf16[64,1792]{1,0:T(8,128)(2,1)S(1)}, u32[]{:S(2)}, u32[]{:S(2)}) collective-permute-start(bf16[64,1792]{1,0:T(8,128)(2,1)S(1)} %pad_maximum_fusion), channel_id=1, source_target_pairs={{0,1},{1,0},{2,3},{3,2},{4,5},{5,4},{6,7},{7,6},{8,9},{9,8},{10,11... | collective-permute-start | bytes 688136 | tf_op jit(solution)/shard_map/ppermute | solution.py:28
  17.3 1.7 %collective-permute-start.5 = (bf16[2,64,640]{2,1,0:T(8,128)(2,1)S(1)}, bf16[2,64,640]{2,1,0:T(8,128)(2,1)S(1)}, u32[]{:S(2)}, u32[]{:S(2)}) collective-permute-start(bf16[2,64,640]{2,1,0:T(8,128)(2,1)S(1)} %get-tuple-element.31), channel_id=1, source_target_pairs={{0,1},{1,0},{2,3},{3,2},{4,5},{5,4},{6,7},{7,6},{8,9},{9,8},{10,11... | collective-permute-start | bytes 491528 | tf_op jit(solution)/shard_map/ppermute | solution.py:28
  17.8 1.5 %collective-permute-start.3 = (bf16[32,1792]{1,0:T(8,128)(2,1)S(1)}, bf16[32,1792]{1,0:T(8,128)(2,1)S(1)}, u32[]{:S(2)}, u32[]{:S(2)}) collective-permute-start(bf16[32,1792]{1,0:T(8,128)(2,1)S(1)} %slice.24), channel_id=1, source_target_pairs={{0,1},{1,0},{2,3},{3,2},{4,5},{5,4},{6,7},{7,6},{8,9},{9,8},{10,11... | collective-permute-start | bytes 344072 | tf_op jit(solution)/shard_map/ppermute | solution.py:28
  19.3 11.4 %collective-permute-start.6 = (bf16[2,64,640]{2,1,0:T(8,128)(2,1)S(1)}, bf16[2,64,640]{2,1,0:T(8,128)(2,1)S(1)}, u32[]{:S(2)}, u32[]{:S(2)}) collective-permute-start(bf16[2,64,640]{2,1,0:T(8,128)(2,1)S(1)} %shard_map.124.refs_0_), channel_id=1, source_target_pairs={{0,2},{1,3},{2,0},{3,1},{4,6},{5,7},{6,4},{7,5},{8,10},{9,11},{10,... | collective-permute-start | bytes 491528 | tf_op jit(solution)/shard_map/ppermute | solution.py:28
  21.2 5.2 %copy-start = (bf16[8,3584,256]{2,1,0:T(8,128)(2,1)S(1)}, bf16[8,3584,256]{2,1,0:T(8,128)(2,1)}, u32[]{:S(2)}) copy-start(bf16[8,3584,256]{2,1,0:T(8,128)(2,1)} %refs_8_.1) | copy-start | bytes 44040196
  31.5 1.9 %collective-permute-start.7 = (bf16[128,896]{1,0:T(8,128)(2,1)S(1)}, bf16[128,896]{1,0:T(8,128)(2,1)S(1)}, u32[]{:S(2)}, u32[]{:S(2)}) collective-permute-start(bf16[128,896]{1,0:T(8,128)(2,1)S(1)} %shard_map.127), channel_id=1, source_target_pairs={{0,1},{1,0},{2,3},{3,2},{4,5},{5,4},{6,7},{7,6},{8,9},{9,8},{10,11... | collective-permute-start | bytes 688136 | tf_op jit(solution)/shard_map/ppermute | solution.py:28
  32.9 2.0 %collective-permute-start.8 = (bf16[128,896]{1,0:T(8,128)(2,1)S(1)}, bf16[128,896]{1,0:T(8,128)(2,1)S(1)}, u32[]{:S(2)}, u32[]{:S(2)}) collective-permute-start(bf16[128,896]{1,0:T(8,128)(2,1)S(1)} %get-tuple-element.40), channel_id=1, source_target_pairs={{0,1},{1,0},{2,3},{3,2},{4,5},{5,4},{6,7},{7,6},{8,9},{9,8},{10,11... | collective-permute-start | bytes 688136 | tf_op jit(solution)/shard_map/ppermute | solution.py:28
  33.4 7.6 %collective-permute-start.9 = (bf16[128,896]{1,0:T(8,128)(2,1)S(1)}, bf16[128,896]{1,0:T(8,128)(2,1)S(1)}, u32[]{:S(2)}, u32[]{:S(2)}) collective-permute-start(bf16[128,896]{1,0:T(8,128)(2,1)S(1)} %add_convert_fusion), channel_id=1, source_target_pairs={{0,2},{1,3},{2,0},{3,1},{4,6},{5,7},{6,4},{7,5},{8,10},{9,11},{10,... | collective-permute-start | bytes 688136 | tf_op jit(solution)/shard_map/ppermute | solution.py:28
  34.8 10.4 %collective-permute-start.13 = (bf16[2,64,512]{2,1,0:T(8,128)(2,1)S(1)}, bf16[2,64,512]{2,1,0:T(8,128)(2,1)S(1)}, u32[]{:S(2)}, u32[]{:S(2)}) collective-permute-start(bf16[2,64,512]{2,1,0:T(8,128)(2,1)S(1)} %shard_map.129.mine), channel_id=1, source_target_pairs={{0,1},{1,0},{2,3},{3,2},{4,5},{5,4},{6,7},{7,6},{8,9},{9,8},{10,11... | collective-permute-start | bytes 393224 | tf_op jit(solution)/shard_map/ppermute | solution.py:28
  41.2 4.6 %collective-permute-start.10 = (bf16[32,896]{1,0:T(8,128)(2,1)S(1)}, bf16[32,896]{1,0:T(8,128)(2,1)S(1)}, u32[]{:S(2)}, u32[]{:S(2)}) collective-permute-start(bf16[32,896]{1,0:T(8,128)(2,1)S(1)} %get-tuple-element.46), channel_id=1, source_target_pairs={{0,4},{4,0},{8,12},{12,8},{1,5},{5,1},{9,13},{13,9},{2,6},{6,2},{1... | collective-permute-start | bytes 172040 | tf_op jit(solution)/shard_map/ppermute | solution.py:28
  41.7 6.6 %collective-permute-start.12 = (bf16[32,896]{1,0:T(8,128)(2,1)S(1)}, bf16[32,896]{1,0:T(8,128)(2,1)S(1)}, u32[]{:S(2)}, u32[]{:S(2)}) collective-permute-start(bf16[32,896]{1,0:T(8,128)(2,1)S(1)} %get-tuple-element.47), channel_id=1, source_target_pairs={{0,12},{4,8},{8,4},{12,0},{1,13},{5,9},{9,5},{13,1},{2,14},{6,10},... | collective-permute-start | bytes 172040 | tf_op jit(solution)/shard_map/ppermute | solution.py:28
  45.1 5.1 %collective-permute-start.11 = (bf16[32,896]{1,0:T(8,128)(2,1)S(1)}, bf16[32,896]{1,0:T(8,128)(2,1)S(1)}, u32[]{:S(2)}, u32[]{:S(2)}) collective-permute-start(bf16[32,896]{1,0:T(8,128)(2,1)S(1)} %get-tuple-element.48), channel_id=1, source_target_pairs={{0,8},{4,12},{8,0},{12,4},{1,9},{5,13},{9,1},{13,5},{2,10},{6,14},... | collective-permute-start | bytes 172040 | tf_op jit(solution)/shard_map/ppermute | solution.py:28
  (3 other events, 13.0 us)

commit v7 on v4

--- a/solution.py
+++ b/solution.py
@@ -11,7 +11,7 @@
 route_scale = 2.5
 very_low = -1e30
 LANES = 128
-WAIT_FLOPS = 20_000_000_000
+WAIT_FLOPS = 100_000_000_000
 
 f32, bf16 = jnp.float32, jnp.bfloat16
 ANY = pl.BlockSpec(memory_space=pl.ANY)
@@ -229,13 +229,12 @@
         operands,
         [VMEM] * len(operands),
         [pltpu.VMEM((count, width), bf16), pltpu.VMEM((count, LANES), bf16)],
-        flops=4 * count * local * hidden * width,
         limit=10 if count <= 256 else 48,
     )
 
 
 def down_call(act, down, pairs, ways):
-    count, depth = act.shape
+    count = act.shape[0]
     width = down.shape[1]
 
     def kernel(act, down, *outs):
@@ -250,7 +249,6 @@
         [shaped(count, width // (2 * ways))] * len(pairs),
         [act, down],
         [VMEM, VMEM],
-        flops=2 * count * depth * (width // (2 * ways)) * len(pairs),
     )
 
 
@@ -277,22 +275,22 @@
 
     pack = pack_rows(hidden, routes, spots)
     packs = [pack] + [over_dev(pack, s, n_dev) for s in range(1, n_dev)]
-    near = [p[:, :share] for p in packs[1:]]
-    first = n_dev // 2 - 1
-    rest = jnp.concatenate(near[:first] + near[first + 1 :], axis=0)
-    early = [send(near[first], "tp", along_x(s, ways)) for s in range(1, spots)]
-    late = [send(rest, "tp", along_x(s, ways)) for s in range(1, spots)]
-    early, q_latent = lax.optimization_barrier((early, q_latent))
+    first = n_dev // 2
+    early, q_latent = lax.optimization_barrier((packs[first], q_latent))
+    keep, give = attend(q_latent, q_rope, cache_latent, cache_rope, cache_len)
+    early = early[:, :share]
+    early_x = [send(early, "tp", along_x(s, ways)) for s in range(1, spots)]
+    packs, early_x, keep, give = lax.optimization_barrier((packs, early_x, keep, give))
+    near = [early if s == first else packs[s][:, :share] for s in range(1, n_dev)]
+    rest = jnp.concatenate(near[: first - 1] + near[first:], axis=0)
+    late_x = [send(rest, "tp", along_x(s, ways)) for s in range(1, spots)]
     mine = [jnp.concatenate(near, axis=0)]
     theirs = [send(mine[0], "tp", other_core)]
-
-    keep, give = attend(q_latent, q_rope, cache_latent, cache_rope, cache_len)
-    late, keep, give = lax.optimization_barrier((late, keep, give))
-    cut = first * rows
-    mine += [jnp.concatenate([b[:cut], a, b[cut:]], axis=0) for a, b in zip(early, late)]
+    state = join([keep, send(give, "tp", other_core)], False)
+    late_x, state = lax.optimization_barrier((late_x, state))
+    cut = (first - 1) * rows
+    mine += [jnp.concatenate([b[:cut], a, b[cut:]], axis=0) for a, b in zip(early_x, late_x)]
     theirs += [send(m, "tp", other_core) for m in mine[1:]]
-    state = join([keep, send(give, "tp", other_core)], False)
-    theirs, state = lax.optimization_barrier((theirs, state))
     states = [state] + [send(state, "tp", along_x(s, ways)) for s in range(1, ways)]
 
     gate, up, down = [

time: 47 us -> 49.4 us (1.051)
  waiting for transfers between devices: 14.8 us -> 16.8 us
  starting transfers between devices: 18.9 us -> 19.4 us
    ppermute x16, waiting for transfers between devices: 14.8 us -> 16.8 us  [send(): return lax.ppermute(value, axis, [(i, target(i)) for i in range(size)])]
  transfers between devices with their start and end apart: 16 -> 16, of which waited for: 8 -> 7; matrix products, arithmetic and copies ran while one was open for 0% -> 0% of each run, Pallas kernels for 20% -> 19%
where the time goes in v7:
time: 49.4 us; the launch traced here: 49.2 us
  starting transfers between devices  19.4 us (39%)
  waiting for transfers between devices  16.8 us (34%)
  Pallas kernels  11 us (22%)
  between operations  1.06 us (2%)
  other arithmetic  0.84 us (2%)
    ppermute x16, starting transfers between devices, send(): return lax.ppermute(value, axis, [(i, target(i)) for i in range(size)])  19.4 us
    ppermute x16, waiting for transfers between devices, send(): return lax.ppermute(value, axis, [(i, target(i)) for i in range(size)])  16.8 us
    pallas_call x9, Pallas kernels, local_call(): pl.pallas_call(kernel, out_shape=outs, in_specs=specs, out_specs=jax.tree...  11 us
  transfers between devices with their start and end apart: 16, of which 7 were waited for; matrix products, arithmetic and copies ran while one was open for 0% of the time, Pallas kernels for 19%

profile of v7, /device:TPU:0, one launch (start us, length us, event | category | flops | bytes accessed | tf_op | source)
XLA Modules:
  0.0 49.2 jit_solution(3984983302876810895)
XLA Ops:
  0.8 1.0 %shard_map.122.refs_0_ = bf16[32,1024]{1,0:T(8,128)(2,1)S(1)} custom-call(bf16[32,3584]{1,0:T(8,128)(2,1)} %refs_4_.1, s32[8,32]{1,0:T(8,128)} %bitcast.13), custom_call_target="tpu_custom_call" | custom-call | flops 99999997952 | tf_op jit(solution)/shard_map/pallas_call | solution.py:53
  1.8 4.1 %collective-permute-start.1 = (bf16[32,1024]{1,0:T(8,128)(2,1)S(1)}, bf16[32,1024]{1,0:T(8,128)(2,1)S(1)}, u32[]{:S(2)}, u32[]{:S(2)}) collective-permute-start(bf16[32,1024]{1,0:T(8,128)(2,1)S(1)} %shard_map.122.refs_0_), channel_id=1, source_target_pairs={{0,8},{4,12},{8,0},{12,4},{1,9},{5,13},{9,1},{13,5},{2,10},{6,14},... | collective-permute-start | bytes 196616 | tf_op jit(solution)/shard_map/ppermute | solution.py:28
  5.9 1.6 %collective-permute-start = (bf16[32,1024]{1,0:T(8,128)(2,1)S(1)}, bf16[32,1024]{1,0:T(8,128)(2,1)S(1)}, u32[]{:S(2)}, u32[]{:S(2)}) collective-permute-start(bf16[32,1024]{1,0:T(8,128)(2,1)S(1)} %shard_map.122.refs_0_), channel_id=1, source_target_pairs={{0,4},{4,0},{8,12},{12,8},{1,5},{5,1},{9,13},{13,9},{2,6},{6,2},{1... | collective-permute-start | bytes 196616 | tf_op jit(solution)/shard_map/ppermute | solution.py:28
  7.5 1.5 %collective-permute-done.1.refs_2_ = bf16[32,1024]{1,0:T(8,128)(2,1)S(1)} collective-permute-done((bf16[32,1024]{1,0:T(8,128)(2,1)S(1)}, bf16[32,1024]{1,0:T(8,128)(2,1)S(1)}, u32[]{:S(2)}, u32[]{:S(2)}) %collective-permute-start.1) | collective-permute-done | bytes 65568 | tf_op jit(solution)/shard_map/ppermute | solution.py:28
  9.0 1.8 %collective-permute-start.3 = (bf16[32,896]{1,0:T(8,128)(2,1)S(1)}, bf16[32,896]{1,0:T(8,128)(2,1)S(1)}, u32[]{:S(2)}, u32[]{:S(2)}) collective-permute-start(bf16[32,896]{1,0:T(8,128)(2,1)S(1)} %slice.30), channel_id=1, source_target_pairs={{0,2},{1,3},{2,0},{3,1},{4,6},{5,7},{6,4},{7,5},{8,10},{9,11},{10,... | collective-permute-start | bytes 172040 | tf_op jit(solution)/shard_map/ppermute | solution.py:28
  10.9 1.7 %shard_map.123 = (bf16[2,64,640]{2,1,0:T(8,128)(2,1)S(1)}, bf16[2,64,640]{2,1,0:T(8,128)(2,1)S(1)}) custom-call(bf16[2,128,512]{2,1,0:T(8,128)(2,1)S(1)} %copy-done.3, bf16[2,64,128]{2,1,0:T(8,128)(2,1)S(1)} %copy-done.5, bf16[2,512,512]{2,1,0:T(8,128)(2,1)S(1)} %copy-done.2, bf16[2,64,512]{2,1,0:T(8,128)(2,1)S(1)} %copy-done.4, s32[2]{0:T(128)S(1)} %copy-done.6), custom_call_target="tpu_custom_call" | custom-call | flops 2000000000 | tf_op jit(solution)/shard_map/pallas_call | solution.py:53
  12.6 1.0 %collective-permute-done.2.refs_3_ = bf16[32,1024]{1,0:T(8,128)(2,1)S(1)} collective-permute-done((bf16[32,1024]{1,0:T(8,128)(2,1)S(1)}, bf16[32,1024]{1,0:T(8,128)(2,1)S(1)}, u32[]{:S(2)}, u32[]{:S(2)}) %collective-permute-start.2) | collective-permute-done | bytes 65568 | tf_op jit(solution)/shard_map/ppermute | solution.py:28
  13.7 1.6 %collective-permute-start.4 = (bf16[64,896]{1,0:T(8,128)(2,1)S(1)}, bf16[64,896]{1,0:T(8,128)(2,1)S(1)}, u32[]{:S(2)}, u32[]{:S(2)}) collective-permute-start(bf16[64,896]{1,0:T(8,128)(2,1)S(1)} %pad_maximum_fusion.2), channel_id=1, source_target_pairs={{0,2},{1,3},{2,0},{3,1},{4,6},{5,7},{6,4},{7,5},{8,10},{9,11},{10,... | collective-permute-start | bytes 344072 | tf_op jit(solution)/shard_map/ppermute | solution.py:28
  15.8 3.5 %collective-permute-done.4 = bf16[64,896]{1,0:T(8,128)(2,1)S(1)} collective-permute-done((bf16[64,896]{1,0:T(8,128)(2,1)S(1)}, bf16[64,896]{1,0:T(8,128)(2,1)S(1)}, u32[]{:S(2)}, u32[]{:S(2)}) %collective-permute-start.4) | collective-permute-done | bytes 114720 | tf_op jit(solution)/shard_map/ppermute | solution.py:28
  19.4 1.6 %collective-permute-start.8 = (bf16[2,64,640]{2,1,0:T(8,128)(2,1)S(1)}, bf16[2,64,640]{2,1,0:T(8,128)(2,1)S(1)}, u32[]{:S(2)}, u32[]{:S(2)}) collective-permute-start(bf16[2,64,640]{2,1,0:T(8,128)(2,1)S(1)} %shard_map.124.refs_0_), channel_id=1, source_target_pairs={{0,2},{1,3},{2,0},{3,1},{4,6},{5,7},{6,4},{7,5},{8,10},{9,11},{10,... | collective-permute-start | bytes 491528 | tf_op jit(solution)/shard_map/ppermute | solution.py:28
  21.1 4.3 %shard_map.125.act = bf16[128,2048]{1,0:T(8,128)(2,1)S(1)} custom-call(bf16[32,1024]{1,0:T(8,128)(2,1)S(1)} %shard_map.122.refs_0_, bf16[32,1024]{1,0:T(8,128)(2,1)S(1)} %collective-permute-done.refs_1_, bf16[32,1024]{1,0:T(8,128)(2,1)S(1)} %collective-permute-done.1.refs_2_, bf16[32,1024]{1,0:T(8,128)(2,1)S(1)} %collective-permute-done.2.refs_3_, ...), custom_call_target="tpu_custom_call" | custom-call | tf_op jit(solution)/shard_map/pallas_call | solution.py:53
  25.4 0.6 %collective-permute-done.8.refs_1_ = bf16[2,64,640]{2,1,0:T(8,128)(2,1)S(1)} collective-permute-done((bf16[2,64,640]{2,1,0:T(8,128)(2,1)S(1)}, bf16[2,64,640]{2,1,0:T(8,128)(2,1)S(1)}, u32[]{:S(2)}, u32[]{:S(2)}) %collective-permute-start.8) | collective-permute-done | bytes 163872 | tf_op jit(solution)/shard_map/ppermute | solution.py:28
  26.1 0.7 %shard_map.127 = bf16[128,896]{1,0:T(8,128)(2,1)S(1)} custom-call(bf16[128,2048]{1,0:T(8,128)(2,1)S(1)} %shard_map.125.act, bf16[2048,3584]{1,0:T(8,128)(2,1)S(1)} %bitcast.5), custom_call_target="tpu_custom_call" | custom-call | tf_op jit(solution)/shard_map/pallas_call | solution.py:53
  26.9 1.3 %shard_map.126 = (bf16[128,896]{1,0:T(8,128)(2,1)S(1)}, bf16[128,896]{1,0:T(8,128)(2,1)S(1)}) custom-call(bf16[128,2048]{1,0:T(8,128)(2,1)S(1)} %shard_map.125.act, bf16[2048,3584]{1,0:T(8,128)(2,1)S(1)} %bitcast.6), custom_call_target="tpu_custom_call" | custom-call | tf_op jit(solution)/shard_map/pallas_call | solution.py:53
  28.2 0.5 %collective-permute-start.10 = (bf16[128,896]{1,0:T(8,128)(2,1)S(1)}, bf16[128,896]{1,0:T(8,128)(2,1)S(1)}, u32[]{:S(2)}, u32[]{:S(2)}) collective-permute-start(bf16[128,896]{1,0:T(8,128)(2,1)S(1)} %get-tuple-element.42), channel_id=1, source_target_pairs={{0,1},{1,0},{2,3},{3,2},{4,5},{5,4},{6,7},{7,6},{8,9},{9,8},{10,11... | collective-permute-start | bytes 688136 | tf_op jit(solution)/shard_map/ppermute | solution.py:28
  28.8 1.6 %collective-permute-start.11 = (bf16[128,896]{1,0:T(8,128)(2,1)S(1)}, bf16[128,896]{1,0:T(8,128)(2,1)S(1)}, u32[]{:S(2)}, u32[]{:S(2)}) collective-permute-start(bf16[128,896]{1,0:T(8,128)(2,1)S(1)} %add_convert_fusion), channel_id=1, source_target_pairs={{0,2},{1,3},{2,0},{3,1},{4,6},{5,7},{6,4},{7,5},{8,10},{9,11},{10,... | collective-permute-start | bytes 688136 | tf_op jit(solution)/shard_map/ppermute | solution.py:28
  30.7 0.7 %shard_map.128 = bf16[128,896]{1,0:T(8,128)(2,1)S(1)} custom-call(bf16[128,2048]{1,0:T(8,128)(2,1)S(1)} %shard_map.125.act, bf16[2048,3584]{1,0:T(8,128)(2,1)S(1)} %bitcast.7), custom_call_target="tpu_custom_call" | custom-call | tf_op jit(solution)/shard_map/pallas_call | solution.py:53
  31.5 5.0 %collective-permute-done.11 = bf16[128,896]{1,0:T(8,128)(2,1)S(1)} collective-permute-done((bf16[128,896]{1,0:T(8,128)(2,1)S(1)}, bf16[128,896]{1,0:T(8,128)(2,1)S(1)}, u32[]{:S(2)}, u32[]{:S(2)}) %collective-permute-start.11) | collective-permute-done | bytes 229408 | tf_op jit(solution)/shard_map/ppermute | solution.py:28
  36.5 1.7 %collective-permute-start.12 = (bf16[32,896]{1,0:T(8,128)(2,1)S(1)}, bf16[32,896]{1,0:T(8,128)(2,1)S(1)}, u32[]{:S(2)}, u32[]{:S(2)}) collective-permute-start(bf16[32,896]{1,0:T(8,128)(2,1)S(1)} %get-tuple-element.48), channel_id=1, source_target_pairs={{0,4},{4,0},{8,12},{12,8},{1,5},{5,1},{9,13},{13,9},{2,6},{6,2},{1... | collective-permute-start | bytes 172040 | tf_op jit(solution)/shard_map/ppermute | solution.py:28
  38.3 4.3 %collective-permute-start.13 = (bf16[32,896]{1,0:T(8,128)(2,1)S(1)}, bf16[32,896]{1,0:T(8,128)(2,1)S(1)}, u32[]{:S(2)}, u32[]{:S(2)}) collective-permute-start(bf16[32,896]{1,0:T(8,128)(2,1)S(1)} %get-tuple-element.50), channel_id=1, source_target_pairs={{0,8},{4,12},{8,0},{12,4},{1,9},{5,13},{9,1},{13,5},{2,10},{6,14},... | collective-permute-start | bytes 172040 | tf_op jit(solution)/shard_map/ppermute | solution.py:28
  42.6 0.7 %shard_map.130 = bf16[2,128,512]{2,1,0:T(8,128)(2,1)} custom-call(bf16[2,64,512]{2,1,0:T(8,128)(2,1)S(1)} %shard_map.129.mine, bf16[2,64,512]{2,1,0:T(8,128)(2,1)S(1)} %collective-permute-done.15.theirs), custom_call_target="tpu_custom_call" | custom-call | tf_op jit(solution)/shard_map/pallas_call | solution.py:53
  43.3 2.2 %collective-permute-done.13 = bf16[32,896]{1,0:T(8,128)(2,1)S(1)} collective-permute-done((bf16[32,896]{1,0:T(8,128)(2,1)S(1)}, bf16[32,896]{1,0:T(8,128)(2,1)S(1)}, u32[]{:S(2)}, u32[]{:S(2)}) %collective-permute-start.13) | collective-permute-done | bytes 57376 | tf_op jit(solution)/shard_map/ppermute | solution.py:28
  45.5 3.1 %collective-permute-done.14 = bf16[32,896]{1,0:T(8,128)(2,1)S(1)} collective-permute-done((bf16[32,896]{1,0:T(8,128)(2,1)S(1)}, bf16[32,896]{1,0:T(8,128)(2,1)S(1)}, u32[]{:S(2)}, u32[]{:S(2)}) %collective-permute-start.14) | collective-permute-done | bytes 57376 | tf_op jit(solution)/shard_map/ppermute | solution.py:28
  48.6 0.7 %fusion.2 = bf16[32,896]{1,0:T(8,128)(2,1)} fusion(f32[128,896]{1,0:T(8,128)S(1)} %get-tuple-element.47, bf16[32,896]{1,0:T(8,128)(2,1)S(1)} %collective-permute-done.14, bf16[32,896]{1,0:T(8,128)(2,1)S(1)} %collective-permute-done.13, bf16[32,896]{1,0:T(8,128)(2,1)S(1)} %collective-permute-done.12), kind=kLoop, calls=%fused_computation.7 | loop fusion | flops 200704 | bytes 344064 | tf_op jit(solution)/shard_map/convert_element_type | solution.py:335
  (69 shorter events, 1.5 us)
Async XLA Ops:
  0.6 20.3 %slice-start.4 = ((s8[14680064]{0:T(1024)(128)(4,1)}), s8[4194304]{0:T(1024)(128)(4,1)S(1)}, s32[]{:S(2)}) async-start(s8[14680064]{0:T(1024)(128)(4,1)} %bitcast.8), calls=%async_computation.4 | async-start | bytes 8388608
  0.6 20.3 %slice-start.8 = ((s8[14680064]{0:T(1024)(128)(4,1)}), s8[4194304]{0:T(1024)(128)(4,1)S(1)}, s32[]{:S(2)}) async-start(s8[14680064]{0:T(1024)(128)(4,1)} %bitcast.10), calls=%async_computation.8 | async-start | bytes 8388608
  0.7 20.3 %slice-start.5 = ((s8[14680064]{0:T(1024)(128)(4,1)}), s8[4194304]{0:T(1024)(128)(4,1)S(1)}, s32[]{:S(2)}) async-start(s8[14680064]{0:T(1024)(128)(4,1)} %bitcast.8), calls=%async_computation.5 | async-start | bytes 8388608
  0.7 20.3 %slice-start.6 = ((s8[14680064]{0:T(1024)(128)(4,1)}), s8[4194304]{0:T(1024)(128)(4,1)S(1)}, s32[]{:S(2)}) async-start(s8[14680064]{0:T(1024)(128)(4,1)} %bitcast.8), calls=%async_computation.6 | async-start | bytes 8388608
  0.7 20.3 %slice-start.7 = ((s8[14680064]{0:T(1024)(128)(4,1)}), s8[2097152]{0:T(1024)(128)(4,1)S(1)}, s32[]{:S(2)}) async-start(s8[14680064]{0:T(1024)(128)(4,1)} %bitcast.8), calls=%async_computation.7 | async-start | bytes 4194304
  0.7 20.3 %slice-start.9 = ((s8[14680064]{0:T(1024)(128)(4,1)}), s8[4194304]{0:T(1024)(128)(4,1)S(1)}, s32[]{:S(2)}) async-start(s8[14680064]{0:T(1024)(128)(4,1)} %bitcast.10), calls=%async_computation.9 | async-start | bytes 8388608
  0.7 20.3 %slice-start.10 = ((s8[14680064]{0:T(1024)(128)(4,1)}), s8[4194304]{0:T(1024)(128)(4,1)S(1)}, s32[]{:S(2)}) async-start(s8[14680064]{0:T(1024)(128)(4,1)} %bitcast.10), calls=%async_computation.10 | async-start | bytes 8388608
  0.8 20.3 %slice-start.11 = ((s8[14680064]{0:T(1024)(128)(4,1)}), s8[2097152]{0:T(1024)(128)(4,1)S(1)}, s32[]{:S(2)}) async-start(s8[14680064]{0:T(1024)(128)(4,1)} %bitcast.10), calls=%async_computation.11 | async-start | bytes 4194304
  1.8 7.2 %collective-permute-start.1 = (bf16[32,1024]{1,0:T(8,128)(2,1)S(1)}, bf16[32,1024]{1,0:T(8,128)(2,1)S(1)}, u32[]{:S(2)}, u32[]{:S(2)}) collective-permute-start(bf16[32,1024]{1,0:T(8,128)(2,1)S(1)} %shard_map.122.refs_0_), channel_id=1, source_target_pairs={{0,8},{4,12},{8,0},{12,4},{1,9},{5,13},{9,1},{13,5},{2,10},{6,14},... | collective-permute-start | bytes 196616 | tf_op jit(solution)/shard_map/ppermute | solution.py:28
  5.9 6.6 %collective-permute-start = (bf16[32,1024]{1,0:T(8,128)(2,1)S(1)}, bf16[32,1024]{1,0:T(8,128)(2,1)S(1)}, u32[]{:S(2)}, u32[]{:S(2)}) collective-permute-start(bf16[32,1024]{1,0:T(8,128)(2,1)S(1)} %shard_map.122.refs_0_), channel_id=1, source_target_pairs={{0,4},{4,0},{8,12},{12,8},{1,5},{5,1},{9,13},{13,9},{2,6},{6,2},{1... | collective-permute-start | bytes 196616 | tf_op jit(solution)/shard_map/ppermute | solution.py:28
  7.5 6.1 %collective-permute-start.2 = (bf16[32,1024]{1,0:T(8,128)(2,1)S(1)}, bf16[32,1024]{1,0:T(8,128)(2,1)S(1)}, u32[]{:S(2)}, u32[]{:S(2)}) collective-permute-start(bf16[32,1024]{1,0:T(8,128)(2,1)S(1)} %shard_map.122.refs_0_), channel_id=1, source_target_pairs={{0,12},{4,8},{8,4},{12,0},{1,13},{5,9},{9,5},{13,1},{2,14},{6,10},... | collective-permute-start | bytes 196616 | tf_op jit(solution)/shard_map/ppermute | solution.py:28
  9.0 4.6 %collective-permute-start.3 = (bf16[32,896]{1,0:T(8,128)(2,1)S(1)}, bf16[32,896]{1,0:T(8,128)(2,1)S(1)}, u32[]{:S(2)}, u32[]{:S(2)}) collective-permute-start(bf16[32,896]{1,0:T(8,128)(2,1)S(1)} %slice.30), channel_id=1, source_target_pairs={{0,2},{1,3},{2,0},{3,1},{4,6},{5,7},{6,4},{7,5},{8,10},{9,11},{10,... | collective-permute-start | bytes 172040 | tf_op jit(solution)/shard_map/ppermute | solution.py:28
  13.6 2.0 %collective-permute-start.5 = (bf16[2,64,640]{2,1,0:T(8,128)(2,1)S(1)}, bf16[2,64,640]{2,1,0:T(8,128)(2,1)S(1)}, u32[]{:S(2)}, u32[]{:S(2)}) collective-permute-start(bf16[2,64,640]{2,1,0:T(8,128)(2,1)S(1)} %get-tuple-element.33), channel_id=1, source_target_pairs={{0,1},{1,0},{2,3},{3,2},{4,5},{5,4},{6,7},{7,6},{8,9},{9,8},{10,11... | collective-permute-start | bytes 491528 | tf_op jit(solution)/shard_map/ppermute | solution.py:28
  13.7 5.6 %collective-permute-start.4 = (bf16[64,896]{1,0:T(8,128)(2,1)S(1)}, bf16[64,896]{1,0:T(8,128)(2,1)S(1)}, u32[]{:S(2)}, u32[]{:S(2)}) collective-permute-start(bf16[64,896]{1,0:T(8,128)(2,1)S(1)} %pad_maximum_fusion.2), channel_id=1, source_target_pairs={{0,2},{1,3},{2,0},{3,1},{4,6},{5,7},{6,4},{7,5},{8,10},{9,11},{10,... | collective-permute-start | bytes 344072 | tf_op jit(solution)/shard_map/ppermute | solution.py:28
  15.3 5.7 %collective-permute-start.6 = (bf16[96,896]{1,0:T(8,128)(2,1)S(1)}, bf16[96,896]{1,0:T(8,128)(2,1)S(1)}, u32[]{:S(2)}, u32[]{:S(2)}) collective-permute-start(bf16[96,896]{1,0:T(8,128)(2,1)S(1)} %pad_maximum_fusion.refs_5_), channel_id=1, source_target_pairs={{0,1},{1,0},{2,3},{3,2},{4,5},{5,4},{6,7},{7,6},{8,9},{9,8},{10,11... | collective-permute-start | bytes 516104 | tf_op jit(solution)/shard_map/ppermute | solution.py:28
  19.3 1.6 %collective-permute-start.7 = (bf16[96,896]{1,0:T(8,128)(2,1)S(1)}, bf16[96,896]{1,0:T(8,128)(2,1)S(1)}, u32[]{:S(2)}, u32[]{:S(2)}) collective-permute-start(bf16[96,896]{1,0:T(8,128)(2,1)S(1)} %pad_maximum_fusion.1.refs_6_), channel_id=1, source_target_pairs={{0,1},{1,0},{2,3},{3,2},{4,5},{5,4},{6,7},{7,6},{8,9},{9,8},{10,11... | collective-permute-start | bytes 516104 | tf_op jit(solution)/shard_map/ppermute | solution.py:28
  19.4 6.6 %collective-permute-start.8 = (bf16[2,64,640]{2,1,0:T(8,128)(2,1)S(1)}, bf16[2,64,640]{2,1,0:T(8,128)(2,1)S(1)}, u32[]{:S(2)}, u32[]{:S(2)}) collective-permute-start(bf16[2,64,640]{2,1,0:T(8,128)(2,1)S(1)} %shard_map.124.refs_0_), channel_id=1, source_target_pairs={{0,2},{1,3},{2,0},{3,1},{4,6},{5,7},{6,4},{7,5},{8,10},{9,11},{10,... | collective-permute-start | bytes 491528 | tf_op jit(solution)/shard_map/ppermute | solution.py:28
  26.8 1.9 %collective-permute-start.9 = (bf16[128,896]{1,0:T(8,128)(2,1)S(1)}, bf16[128,896]{1,0:T(8,128)(2,1)S(1)}, u32[]{:S(2)}, u32[]{:S(2)}) collective-permute-start(bf16[128,896]{1,0:T(8,128)(2,1)S(1)} %shard_map.127), channel_id=1, source_target_pairs={{0,1},{1,0},{2,3},{3,2},{4,5},{5,4},{6,7},{7,6},{8,9},{9,8},{10,11... | collective-permute-start | bytes 688136 | tf_op jit(solution)/shard_map/ppermute | solution.py:28
  28.2 3.3 %collective-permute-start.10 = (bf16[128,896]{1,0:T(8,128)(2,1)S(1)}, bf16[128,896]{1,0:T(8,128)(2,1)S(1)}, u32[]{:S(2)}, u32[]{:S(2)}) collective-permute-start(bf16[128,896]{1,0:T(8,128)(2,1)S(1)} %get-tuple-element.42), channel_id=1, source_target_pairs={{0,1},{1,0},{2,3},{3,2},{4,5},{5,4},{6,7},{7,6},{8,9},{9,8},{10,11... | collective-permute-start | bytes 688136 | tf_op jit(solution)/shard_map/ppermute | solution.py:28
  28.8 7.6 %collective-permute-start.11 = (bf16[128,896]{1,0:T(8,128)(2,1)S(1)}, bf16[128,896]{1,0:T(8,128)(2,1)S(1)}, u32[]{:S(2)}, u32[]{:S(2)}) collective-permute-start(bf16[128,896]{1,0:T(8,128)(2,1)S(1)} %add_convert_fusion), channel_id=1, source_target_pairs={{0,2},{1,3},{2,0},{3,1},{4,6},{5,7},{6,4},{7,5},{8,10},{9,11},{10,... | collective-permute-start | bytes 688136 | tf_op jit(solution)/shard_map/ppermute | solution.py:28
  30.7 11.9 %collective-permute-start.15 = (bf16[2,64,512]{2,1,0:T(8,128)(2,1)S(1)}, bf16[2,64,512]{2,1,0:T(8,128)(2,1)S(1)}, u32[]{:S(2)}, u32[]{:S(2)}) collective-permute-start(bf16[2,64,512]{2,1,0:T(8,128)(2,1)S(1)} %shard_map.129.mine), channel_id=1, source_target_pairs={{0,1},{1,0},{2,3},{3,2},{4,5},{5,4},{6,7},{7,6},{8,9},{9,8},{10,11... | collective-permute-start | bytes 393224 | tf_op jit(solution)/shard_map/ppermute | solution.py:28
  36.5 6.8 %collective-permute-start.12 = (bf16[32,896]{1,0:T(8,128)(2,1)S(1)}, bf16[32,896]{1,0:T(8,128)(2,1)S(1)}, u32[]{:S(2)}, u32[]{:S(2)}) collective-permute-start(bf16[32,896]{1,0:T(8,128)(2,1)S(1)} %get-tuple-element.48), channel_id=1, source_target_pairs={{0,4},{4,0},{8,12},{12,8},{1,5},{5,1},{9,13},{13,9},{2,6},{6,2},{1... | collective-permute-start | bytes 172040 | tf_op jit(solution)/shard_map/ppermute | solution.py:28
  38.3 7.2 %collective-permute-start.13 = (bf16[32,896]{1,0:T(8,128)(2,1)S(1)}, bf16[32,896]{1,0:T(8,128)(2,1)S(1)}, u32[]{:S(2)}, u32[]{:S(2)}) collective-permute-start(bf16[32,896]{1,0:T(8,128)(2,1)S(1)} %get-tuple-element.50), channel_id=1, source_target_pairs={{0,8},{4,12},{8,0},{12,4},{1,9},{5,13},{9,1},{13,5},{2,10},{6,14},... | collective-permute-start | bytes 172040 | tf_op jit(solution)/shard_map/ppermute | solution.py:28
  42.6 6.0 %collective-permute-start.14 = (bf16[32,896]{1,0:T(8,128)(2,1)S(1)}, bf16[32,896]{1,0:T(8,128)(2,1)S(1)}, u32[]{:S(2)}, u32[]{:S(2)}) collective-permute-start(bf16[32,896]{1,0:T(8,128)(2,1)S(1)} %get-tuple-element.49), channel_id=1, source_target_pairs={{0,12},{4,8},{8,4},{12,0},{1,13},{5,9},{9,5},{13,1},{2,14},{6,10},... | collective-permute-start | bytes 172040 | tf_op jit(solution)/shard_map/ppermute | solution.py:28
  (11 other events, 121.4 us)

commit v8 on v7

--- a/solution.py
+++ b/solution.py
@@ -18,36 +18,28 @@
 VMEM = pl.BlockSpec(memory_space=pltpu.VMEM)
 SMEM = pl.BlockSpec(memory_space=pltpu.SMEM)
 
-
 def dot(a, b, contract=((1,), (0,))):
     return lax.dot_general(a, b, (contract, ((), ())), preferred_element_type=f32)
-
 
 def send(value, axis, target):
     size = lax.axis_size(axis)
     return lax.ppermute(value, axis, [(i, target(i)) for i in range(size)])
 
-
 def other_core(i):
     return i ^ 1
 
-
 def partner(place, step, size):
     return place ^ step if size & (size - 1) == 0 else (step - place) % size
 
-
 def along_x(step, ways):
     return lambda i: partner(i // 2, step, ways) * 2 + i % 2
 
-
 def over_dev(value, step, size):
     return send(value, "dev", lambda i: partner(i, step, size))
-
 
 def spot_and_core():
     tp = lax.axis_index("tp")
     return tp // 2, lax.rem(tp, 2)
-
 
 def local_call(kernel, outs, operands, specs, scratch=(), flops=0, nbytes=0, exps=0, limit=8):
     return pl.pallas_call(
@@ -60,7 +52,6 @@
         compiler_params=pltpu.CompilerParams(vmem_limit_bytes=limit << 20),
     )(*operands)
 
-
 def shaped(*shape):
     return jax.ShapeDtypeStruct(shape, bf16)
 
@@ -70,7 +61,6 @@
     high = total.astype(bf16).astype(f32)
     stats = jnp.where(lane == 0, top, jnp.where(lane == 1, high, jnp.where(lane == 2, total - high, 0.0)))
     return stats.astype(bf16)
-
 
 def attend_kernel(q_lat, q_rope, keys, rope, lengths, keep, give, state):
     rows, heads, width = q_lat.shape
@@ -91,7 +81,6 @@
     keep[...] = state[:, pl.ds(pl.multiple_of(core * half, half), half), :]
     give[...] = state[:, pl.ds(pl.multiple_of((1 - core) * half, half), half), :]
 
-
 def attend(q_latent, q_rope, cache_latent, cache_rope, cache_len):
     rows, heads, width = q_latent.shape
     span = cache_latent.shape[1]
@@ -104,7 +93,6 @@
         [pltpu.VMEM((rows, heads, width + LANES), bf16)],
         flops=2_000_000_000,
     )
-
 
 def join_kernel(last, *refs):
     states, out = refs[:-1], refs[-1]
@@ -123,19 +111,16 @@
             out[r, :, :width] = summed.astype(bf16)
             out[r, :, width:] = stats_of(top, total, heads)
 
-
 def join(states, last):
     rows, heads, width = states[0].shape
     out = shaped(rows, heads, width - LANES if last else width)
     return local_call(functools.partial(join_kernel, last), out, states, [VMEM] * len(states))
-
 
 def place_kernel(mine, theirs, out):
     half = mine.shape[1]
     core = lax.rem(lax.axis_index("tp"), 2)
     out[:, pl.ds(pl.multiple_of(core * half, half), half), :] = mine[...]
     out[:, pl.ds(pl.multiple_of((1 - core) * half, half), half), :] = theirs[...]
-
 
 def place_heads(mine, theirs):
     rows, half, width = mine.shape
@@ -158,7 +143,6 @@
     out[:, size : size + picks] = turned.astype(bf16)
     columns.wait()
 
-
 def pack_rows(hidden, routes, spots):
     rows, width = hidden.shape
     return local_call(
@@ -170,7 +154,6 @@
         flops=WAIT_FLOPS,
         limit=2,
     )
-
 
 def act_kernel(picks, ways, packs, own, mine, theirs, router, gate, up, down, act, outs, x, tags):
     rows = own.shape[0]
@@ -205,7 +188,6 @@
     for out in outs:
         out[...] = dot(act[...], down[0][...]).astype(bf16)
 
-
 def act_call(packs, own, mine, theirs, router, gate, up, down, picks, ways, whole):
     rows, width = own.shape
     local, _, hidden = gate.shape
@@ -232,7 +214,6 @@
         limit=10 if count <= 256 else 48,
     )
 
-
 def down_call(act, down, pairs, ways):
     count = act.shape[0]
     width = down.shape[1]
@@ -249,6 +230,7 @@
         [shaped(count, width // (2 * ways))] * len(pairs),
         [act, down],
         [VMEM, VMEM],
+
     )
 
 
@@ -274,24 +256,28 @@
     share = width // (2 * spots)
 
     pack = pack_rows(hidden, routes, spots)
-    packs = [pack] + [over_dev(pack, s, n_dev) for s in range(1, n_dev)]
+    pack, q_latent = lax.optimization_barrier((pack, q_latent))
     first = n_dev // 2
-    early, q_latent = lax.optimization_barrier((packs[first], q_latent))
+    far = over_dev(pack, first, n_dev)
     keep, give = attend(q_latent, q_rope, cache_latent, cache_rope, cache_len)
-    early = early[:, :share]
-    early_x = [send(early, "tp", along_x(s, ways)) for s in range(1, spots)]
-    packs, early_x, keep, give = lax.optimization_barrier((packs, early_x, keep, give))
-    near = [early if s == first else packs[s][:, :share] for s in range(1, n_dev)]
-    rest = jnp.concatenate(near[: first - 1] + near[first:], axis=0)
-    late_x = [send(rest, "tp", along_x(s, ways)) for s in range(1, spots)]
+    again, keep, give = lax.optimization_barrier((pack, keep, give))
+    packs = [pack] + [far if s == first else over_dev(again, s, n_dev) for s in range(1, n_dev)]
+    near = [p[:, :share] for p in packs[1:]]
+    first -= 1
+    early = [send(near[first], "tp", along_x(s, ways)) for s in range(1, spots)]
+    state = join([keep, send(give, "tp", other_core)], False)
+    others = [s for s in reversed(range(1, n_dev)) if s != first + 1]
+    rest = jnp.concatenate([near[s - 1] for s in others], axis=0)
+    rest, state = lax.optimization_barrier((rest, state))
+    late = [send(rest, "tp", along_x(s, ways)) for s in range(1, spots)]
     mine = [jnp.concatenate(near, axis=0)]
-    theirs = [send(mine[0], "tp", other_core)]
-    state = join([keep, send(give, "tp", other_core)], False)
-    late_x, state = lax.optimization_barrier((late_x, state))
-    cut = (first - 1) * rows
-    mine += [jnp.concatenate([b[:cut], a, b[cut:]], axis=0) for a, b in zip(early_x, late_x)]
-    theirs += [send(m, "tp", other_core) for m in mine[1:]]
-    states = [state] + [send(state, "tp", along_x(s, ways)) for s in range(1, ways)]
+    for a, b in zip(early, late):
+        come = {s: b[i * rows : (i + 1) * rows] for i, s in enumerate(others)}
+        mine.append(jnp.concatenate([come.get(s, a) for s in range(1, n_dev)], axis=0))
+    theirs = [send(m, "tp", other_core) for m in mine]
+    states = [send(state, "tp", along_x(s, ways)) for s in range(1, ways)]
+    theirs, state = lax.optimization_barrier((theirs, state))
+    states = [state] + states
 
     gate, up, down = [
         pltpu.with_memory_space_constraint(w, pltpu.VMEM)
@@ -310,7 +296,7 @@
         *own, there = down_call(act, down, [(s, 0) for s in steps] + [(0, 1)], ways)
         there = send(there, "tp", other_core)
         sums = [added(a, b).astype(bf16) for a, b in zip(own, far)]
-        act, sums, states = lax.optimization_barrier((act, sums, states))
+        act, sums = lax.optimization_barrier((act, sums))
         (here,) = down_call(act, down, [(0, 0)], ways)
     else:
         spot, core = spot_and_core()
@@ -323,17 +309,26 @@
         far = [send(block(s, 1 - core), "tp", other_core) for s in range(ways)]
         sums = [added(a, b).astype(bf16) for a, b in zip(own[1:], far[1:])]
         here, there = own[0], far[0]
-    total = added(here, there)
-    for s, p in enumerate(sums, 1):
-        total = total + send(p, "tp", along_x(s, ways)).astype(f32)
-    blocks = [total[i : i + rows] for i in range(0, total.shape[0], rows)]
-    moe = blocks[0]
-    for s in range(1, n_dev):
-        moe = moe + over_dev(blocks[s].astype(bf16), s, n_dev).astype(f32)
+    far_rows = [send(p[2 * rows :], "tp", along_x(s, ways)) for s, p in enumerate(sums, 1)]
+    kept = added(here, there)
+    near_rows = [kept[rows : 2 * rows].astype(bf16)] + [p[rows : 2 * rows] for p in sums]
+    near_rows, far_rows = lax.optimization_barrier((jnp.concatenate(near_rows, axis=1), far_rows))
+    near_rows = over_dev(near_rows, 1, n_dev).astype(f32)
+    near_rows, states = lax.optimization_barrier((jnp.split(near_rows, ways, axis=1), states))
+    mine = lax.optimization_barrier([added(p[:rows], q).astype(bf16) for p, q in zip(sums, near_rows[1:])])
+    mine = [send(p, "tp", along_x(s, ways)) for s, p in enumerate(mine, 1)]
+    kept_far = lax.optimization_barrier(kept[2 * rows :])
+    for p in far_rows:
+        kept_far = kept_far + p.astype(f32)
     joined = join(states, True)
     attended = place_heads(joined, send(joined, "tp", other_core))
+    moe = kept[:rows] + near_rows[0]
+    for s in reversed(range(2, n_dev)):
+        block = kept_far[(s - 2) * rows : (s - 1) * rows].astype(bf16)
+        moe, attended = lax.optimization_barrier((moe + over_dev(block, s, n_dev).astype(f32), attended))
+    for p in mine:
+        moe = moe + p.astype(f32)
     return (moe.astype(bf16), attended)
-
 
 def solution(mesh):
     in_specs = (

time: 49.4 us -> 47.9 us (0.970)
  starting transfers between devices: 19.4 us -> 18.1 us
    ppermute x16 -> x17, starting transfers between devices: 19.4 us -> 18.1 us  [send(): return lax.ppermute(value, axis, [(i, target(i)) for i in range(size)])]
    ppermute x16 -> x17, waiting for transfers between devices: 16.8 us -> 16.5 us  [send(): return lax.ppermute(value, axis, [(i, target(i)) for i in range(size)])]
  transfers between devices with their start and end apart: 16 -> 17, of which waited for: 7 -> 10; matrix products, arithmetic and copies ran while one was open for 0% -> 1% of each run, Pallas kernels for 19% -> 19%
where the time goes in v8:
time: 47.9 us; the launch traced here: 47.7 us
  starting transfers between devices  18.1 us (38%)
  waiting for transfers between devices  16.5 us (34%)
  Pallas kernels  11 us (23%)
  between operations  1 us (2%)
  other arithmetic  0.89 us (2%)
    ppermute x17, starting transfers between devices, send(): return lax.ppermute(value, axis, [(i, target(i)) for i in range(size)])  18.1 us
    ppermute x17, waiting for transfers between devices, send(): return lax.ppermute(value, axis, [(i, target(i)) for i in range(size)])  16.5 us
    pallas_call x9, Pallas kernels, local_call(): pl.pallas_call(kernel, out_shape=outs, in_specs=specs, out_specs=jax.tree...  11 us
  transfers between devices with their start and end apart: 17, of which 10 were waited for; matrix products, arithmetic and copies ran while one was open for 1% of the time, Pallas kernels for 19%

profile of v8, /device:TPU:0, one launch (start us, length us, event | category | flops | bytes accessed | tf_op | source)
XLA Modules:
  0.0 47.7 jit_solution(7091482439246414405)
XLA Ops:
  0.7 1.0 %shard_map.122.refs_0_ = bf16[32,1024]{1,0:T(8,128)(2,1)S(1)} custom-call(bf16[32,3584]{1,0:T(8,128)(2,1)} %refs_4_.1, s32[8,32]{1,0:T(8,128)} %bitcast.9), custom_call_target="tpu_custom_call" | custom-call | flops 99999997952 | tf_op jit(solution)/shard_map/pallas_call | solution.py:45
  1.8 4.1 %collective-permute-start.1 = (bf16[32,1024]{1,0:T(8,128)(2,1)S(1)}, bf16[32,1024]{1,0:T(8,128)(2,1)S(1)}, u32[]{:S(2)}, u32[]{:S(2)}) collective-permute-start(bf16[32,1024]{1,0:T(8,128)(2,1)S(1)} %shard_map.122.refs_0_), channel_id=1, source_target_pairs={{0,8},{4,12},{8,0},{12,4},{1,9},{5,13},{9,1},{13,5},{2,10},{6,14},... | collective-permute-start | bytes 196616 | tf_op jit(solution)/shard_map/ppermute | solution.py:26
  5.9 1.7 %shard_map.123 = (bf16[2,64,640]{2,1,0:T(8,128)(2,1)S(1)}, bf16[2,64,640]{2,1,0:T(8,128)(2,1)S(1)}) custom-call(bf16[2,128,512]{2,1,0:T(8,128)(2,1)S(1)} %copy-done.5, bf16[2,64,128]{2,1,0:T(8,128)(2,1)S(1)} %copy-done.7, bf16[2,512,512]{2,1,0:T(8,128)(2,1)S(1)} %copy-done.4, bf16[2,64,512]{2,1,0:T(8,128)(2,1)S(1)} %copy-done.6, s32[2]{0:T(128)S(1)} %copy-done.8), custom_call_target="tpu_custom_call" | custom-call | flops 2000000000 | tf_op jit(solution)/shard_map/pallas_call | solution.py:45
  7.6 1.6 %collective-permute-start = (bf16[32,1024]{1,0:T(8,128)(2,1)S(1)}, bf16[32,1024]{1,0:T(8,128)(2,1)S(1)}, u32[]{:S(2)}, u32[]{:S(2)}) collective-permute-start(bf16[32,1024]{1,0:T(8,128)(2,1)S(1)} %shard_map.122.refs_0_), channel_id=1, source_target_pairs={{0,4},{4,0},{8,12},{12,8},{1,5},{5,1},{9,13},{13,9},{2,6},{6,2},{1... | collective-permute-start | bytes 196616 | tf_op jit(solution)/shard_map/ppermute | solution.py:26
  9.5 1.7 %collective-permute-start.5 = (bf16[32,896]{1,0:T(8,128)(2,1)S(1)}, bf16[32,896]{1,0:T(8,128)(2,1)S(1)}, u32[]{:S(2)}, u32[]{:S(2)}) collective-permute-start(bf16[32,896]{1,0:T(8,128)(2,1)S(1)} %slice.56), channel_id=1, source_target_pairs={{0,2},{1,3},{2,0},{3,1},{4,6},{5,7},{6,4},{7,5},{8,10},{9,11},{10,... | collective-permute-start | bytes 172040 | tf_op jit(solution)/shard_map/ppermute | solution.py:26
  11.2 0.7 %collective-permute-done.refs_1_ = bf16[32,1024]{1,0:T(8,128)(2,1)S(1)} collective-permute-done((bf16[32,1024]{1,0:T(8,128)(2,1)S(1)}, bf16[32,1024]{1,0:T(8,128)(2,1)S(1)}, u32[]{:S(2)}, u32[]{:S(2)}) %collective-permute-start) | collective-permute-done | bytes 65568 | tf_op jit(solution)/shard_map/ppermute | solution.py:26
  11.9 3.4 %collective-permute-done.2.refs_3_ = bf16[32,1024]{1,0:T(8,128)(2,1)S(1)} collective-permute-done((bf16[32,1024]{1,0:T(8,128)(2,1)S(1)}, bf16[32,1024]{1,0:T(8,128)(2,1)S(1)}, u32[]{:S(2)}, u32[]{:S(2)}) %collective-permute-start.2) | collective-permute-done | bytes 65568 | tf_op jit(solution)/shard_map/ppermute | solution.py:26
  15.6 1.6 %collective-permute-start.4 = (bf16[64,896]{1,0:T(8,128)(2,1)S(1)}, bf16[64,896]{1,0:T(8,128)(2,1)S(1)}, u32[]{:S(2)}, u32[]{:S(2)}) collective-permute-start(bf16[64,896]{1,0:T(8,128)(2,1)S(1)} %pad_maximum_fusion.2), channel_id=1, source_target_pairs={{0,2},{1,3},{2,0},{3,1},{4,6},{5,7},{6,4},{7,5},{8,10},{9,11},{10,... | collective-permute-start | bytes 344072 | tf_op jit(solution)/shard_map/ppermute | solution.py:26
  17.3 3.2 %collective-permute-done.4 = bf16[64,896]{1,0:T(8,128)(2,1)S(1)} collective-permute-done((bf16[64,896]{1,0:T(8,128)(2,1)S(1)}, bf16[64,896]{1,0:T(8,128)(2,1)S(1)}, u32[]{:S(2)}, u32[]{:S(2)}) %collective-permute-start.4) | collective-permute-done | bytes 114720 | tf_op jit(solution)/shard_map/ppermute | solution.py:26
  20.6 1.6 %collective-permute-start.8 = (bf16[2,64,640]{2,1,0:T(8,128)(2,1)S(1)}, bf16[2,64,640]{2,1,0:T(8,128)(2,1)S(1)}, u32[]{:S(2)}, u32[]{:S(2)}) collective-permute-start(bf16[2,64,640]{2,1,0:T(8,128)(2,1)S(1)} %shard_map.124.refs_0_), channel_id=1, source_target_pairs={{0,2},{1,3},{2,0},{3,1},{4,6},{5,7},{6,4},{7,5},{8,10},{9,11},{10,... | collective-permute-start | bytes 491528 | tf_op jit(solution)/shard_map/ppermute | solution.py:26
  22.2 4.3 %shard_map.125.act = bf16[128,2048]{1,0:T(8,128)(2,1)S(1)} custom-call(bf16[32,1024]{1,0:T(8,128)(2,1)S(1)} %shard_map.122.refs_0_, bf16[32,1024]{1,0:T(8,128)(2,1)S(1)} %collective-permute-done.refs_1_, bf16[32,1024]{1,0:T(8,128)(2,1)S(1)} %collective-permute-done.1.refs_2_, bf16[32,1024]{1,0:T(8,128)(2,1)S(1)} %collective-permute-done.2.refs_3_, ...), custom_call_target="tpu_custom_call" | custom-call | tf_op jit(solution)/shard_map/pallas_call | solution.py:45
  26.5 0.7 %collective-permute-done.8.refs_1_ = bf16[2,64,640]{2,1,0:T(8,128)(2,1)S(1)} collective-permute-done((bf16[2,64,640]{2,1,0:T(8,128)(2,1)S(1)}, bf16[2,64,640]{2,1,0:T(8,128)(2,1)S(1)}, u32[]{:S(2)}, u32[]{:S(2)}) %collective-permute-start.8) | collective-permute-done | bytes 163872 | tf_op jit(solution)/shard_map/ppermute | solution.py:26
  27.2 0.7 %shard_map.127 = bf16[128,896]{1,0:T(8,128)(2,1)S(1)} custom-call(bf16[128,2048]{1,0:T(8,128)(2,1)S(1)} %shard_map.125.act, bf16[2048,3584]{1,0:T(8,128)(2,1)S(1)} %bitcast.5), custom_call_target="tpu_custom_call" | custom-call | tf_op jit(solution)/shard_map/pallas_call | solution.py:45
  28.1 1.3 %shard_map.126 = (bf16[128,896]{1,0:T(8,128)(2,1)S(1)}, bf16[128,896]{1,0:T(8,128)(2,1)S(1)}) custom-call(bf16[128,2048]{1,0:T(8,128)(2,1)S(1)} %shard_map.125.act, bf16[2048,3584]{1,0:T(8,128)(2,1)S(1)} %bitcast.6), custom_call_target="tpu_custom_call" | custom-call | tf_op jit(solution)/shard_map/pallas_call | solution.py:45
  30.0 0.7 %shard_map.128 = bf16[128,896]{1,0:T(8,128)(2,1)S(1)} custom-call(bf16[128,2048]{1,0:T(8,128)(2,1)S(1)} %shard_map.125.act, bf16[2048,3584]{1,0:T(8,128)(2,1)S(1)} %bitcast.7), custom_call_target="tpu_custom_call" | custom-call | tf_op jit(solution)/shard_map/pallas_call | solution.py:45
  31.1 1.6 %collective-permute-start.11 = (bf16[64,896]{1,0:T(8,128)(2,1)S(1)}, bf16[64,896]{1,0:T(8,128)(2,1)S(1)}, u32[]{:S(2)}, u32[]{:S(2)}) collective-permute-start(bf16[64,896]{1,0:T(8,128)(2,1)S(1)} %slice.50), channel_id=1, source_target_pairs={{0,2},{1,3},{2,0},{3,1},{4,6},{5,7},{6,4},{7,5},{8,10},{9,11},{10,... | collective-permute-start | bytes 344072 | tf_op jit(solution)/shard_map/ppermute | solution.py:26
  32.8 3.9 %collective-permute-done.11 = bf16[64,896]{1,0:T(8,128)(2,1)S(1)} collective-permute-done((bf16[64,896]{1,0:T(8,128)(2,1)S(1)}, bf16[64,896]{1,0:T(8,128)(2,1)S(1)}, u32[]{:S(2)}, u32[]{:S(2)}) %collective-permute-start.11) | collective-permute-done | bytes 114720 | tf_op jit(solution)/shard_map/ppermute | solution.py:26
  36.7 0.8 %collective-permute-start.13 = (bf16[32,896]{1,0:T(8,128)(2,1)S(1)}, bf16[32,896]{1,0:T(8,128)(2,1)S(1)}, u32[]{:S(2)}, u32[]{:S(2)}) collective-permute-start(bf16[32,896]{1,0:T(8,128)(2,1)S(1)} %get-tuple-element.61), channel_id=1, source_target_pairs={{0,12},{4,8},{8,4},{12,0},{1,13},{5,9},{9,5},{13,1},{2,14},{6,10},... | collective-permute-start | bytes 172040 | tf_op jit(solution)/shard_map/ppermute | solution.py:26
  37.4 2.8 %collective-permute-start.15 = (bf16[32,896]{1,0:T(8,128)(2,1)S(1)}, bf16[32,896]{1,0:T(8,128)(2,1)S(1)}, u32[]{:S(2)}, u32[]{:S(2)}) collective-permute-start(bf16[32,896]{1,0:T(8,128)(2,1)S(1)} %get-tuple-element.60), channel_id=1, source_target_pairs={{0,8},{4,12},{8,0},{12,4},{1,9},{5,13},{9,1},{13,5},{2,10},{6,14},... | collective-permute-start | bytes 172040 | tf_op jit(solution)/shard_map/ppermute | solution.py:26
  40.2 2.6 %collective-permute-done.12 = bf16[32,1792]{1,0:T(8,128)(2,1)S(1)} collective-permute-done((bf16[32,1792]{1,0:T(8,128)(2,1)S(1)}, bf16[32,1792]{1,0:T(8,128)(2,1)S(1)}, u32[]{:S(2)}, u32[]{:S(2)}) %collective-permute-start.12) | collective-permute-done | bytes 114720 | tf_op jit(solution)/shard_map/ppermute | solution.py:26
  42.9 1.6 %collective-permute-start.16 = (bf16[32,896]{1,0:T(8,128)(2,1)S(1)}, bf16[32,896]{1,0:T(8,128)(2,1)S(1)}, u32[]{:S(2)}, u32[]{:S(2)}) collective-permute-start(bf16[32,896]{1,0:T(8,128)(2,1)S(1)} %add_convert_fusion.3), channel_id=1, source_target_pairs={{0,2},{1,3},{2,0},{3,1},{4,6},{5,7},{6,4},{7,5},{8,10},{9,11},{10,... | collective-permute-start | bytes 172040 | tf_op jit(solution)/shard_map/ppermute | solution.py:26
  44.9 1.3 %collective-permute-done.14.theirs = bf16[2,64,512]{2,1,0:T(8,128)(2,1)S(1)} collective-permute-done((bf16[2,64,512]{2,1,0:T(8,128)(2,1)S(1)}, bf16[2,64,512]{2,1,0:T(8,128)(2,1)S(1)}, u32[]{:S(2)}, u32[]{:S(2)}) %collective-permute-start.14) | collective-permute-done | bytes 131104 | tf_op jit(solution)/shard_map/ppermute | solution.py:26
  46.2 0.7 %shard_map.130 = bf16[2,128,512]{2,1,0:T(8,128)(2,1)} custom-call(bf16[2,64,512]{2,1,0:T(8,128)(2,1)S(1)} %shard_map.129.mine, bf16[2,64,512]{2,1,0:T(8,128)(2,1)S(1)} %collective-permute-done.14.theirs), custom_call_target="tpu_custom_call" | custom-call | tf_op jit(solution)/shard_map/pallas_call | solution.py:45
  47.1 0.6 %add_convert_fusion.2 = bf16[32,896]{1,0:T(8,128)(2,1)} fusion(f32[32,896]{1,0:T(8,128)S(1)} %convert_add_fusion.1, bf16[32,896]{1,0:T(8,128)(2,1)S(1)} %collective-permute-done.16), kind=kLoop, calls=%fused_computation.10 | loop fusion | flops 86016 | bytes 229376 | tf_op jit(solution)/shard_map/convert_element_type | solution.py:331
  (67 shorter events, 2.5 us)
Async XLA Ops:
  0.6 5.2 %copy-start.4 = (bf16[2,512,512]{2,1,0:T(8,128)(2,1)S(1)}, bf16[2,512,512]{2,1,0:T(8,128)(2,1)}, u32[]{:S(2)}) copy-start(bf16[2,512,512]{2,1,0:T(8,128)(2,1)} %keys.1) | copy-start | bytes 3145732
  0.6 5.2 %copy-start.5 = (bf16[2,128,512]{2,1,0:T(8,128)(2,1)S(1)}, bf16[2,128,512]{2,1,0:T(8,128)(2,1)}, u32[]{:S(2)}) copy-start(bf16[2,128,512]{2,1,0:T(8,128)(2,1)} %q_lat) | copy-start | bytes 786436
  0.7 21.5 %copy-start = (bf16[8,3584,256]{2,1,0:T(8,128)(2,1)S(1)}, bf16[8,3584,256]{2,1,0:T(8,128)(2,1)}, u32[]{:S(2)}) copy-start(bf16[8,3584,256]{2,1,0:T(8,128)(2,1)} %refs_10_.1) | copy-start | bytes 44040196
  0.7 21.5 %copy-start.1 = (bf16[8,3584,256]{2,1,0:T(8,128)(2,1)S(1)}, bf16[8,3584,256]{2,1,0:T(8,128)(2,1)}, u32[]{:S(2)}) copy-start(bf16[8,3584,256]{2,1,0:T(8,128)(2,1)} %refs_11_.1) | copy-start | bytes 44040196
  0.7 21.5 %copy-start.2 = (bf16[32,3584]{1,0:T(8,128)(2,1)S(1)}, bf16[32,3584]{1,0:T(8,128)(2,1)}, u32[]{:S(2)}) copy-start(bf16[32,3584]{1,0:T(8,128)(2,1)} %refs_4_.1) | copy-start | bytes 688132
  0.7 21.5 %copy-start.3 = (bf16[3584,32]{0,1:T(8,128)(2,1)S(1)}, bf16[3584,32]{0,1:T(8,128)(2,1)}, u32[]{:S(2)}) copy-start(bf16[3584,32]{0,1:T(8,128)(2,1)} %param.13) | copy-start | bytes 688132
  1.8 7.8 %collective-permute-start.1 = (bf16[32,1024]{1,0:T(8,128)(2,1)S(1)}, bf16[32,1024]{1,0:T(8,128)(2,1)S(1)}, u32[]{:S(2)}, u32[]{:S(2)}) collective-permute-start(bf16[32,1024]{1,0:T(8,128)(2,1)S(1)} %shard_map.122.refs_0_), channel_id=1, source_target_pairs={{0,8},{4,12},{8,0},{12,4},{1,9},{5,13},{9,1},{13,5},{2,10},{6,14},... | collective-permute-start | bytes 196616 | tf_op jit(solution)/shard_map/ppermute | solution.py:26
  5.9 21.3 %slice-start = ((s8[14680064]{0:T(1024)(128)(4,1)}), s8[4194304]{0:T(1024)(128)(4,1)S(1)}, s32[]{:S(2)}) async-start(s8[14680064]{0:T(1024)(128)(4,1)} %bitcast.3), calls=%async_computation | async-start | bytes 8388608
  7.6 4.3 %collective-permute-start = (bf16[32,1024]{1,0:T(8,128)(2,1)S(1)}, bf16[32,1024]{1,0:T(8,128)(2,1)S(1)}, u32[]{:S(2)}, u32[]{:S(2)}) collective-permute-start(bf16[32,1024]{1,0:T(8,128)(2,1)S(1)} %shard_map.122.refs_0_), channel_id=1, source_target_pairs={{0,4},{4,0},{8,12},{12,8},{1,5},{5,1},{9,13},{13,9},{2,6},{6,2},{1... | collective-permute-start | bytes 196616 | tf_op jit(solution)/shard_map/ppermute | solution.py:26
  9.2 6.1 %collective-permute-start.2 = (bf16[32,1024]{1,0:T(8,128)(2,1)S(1)}, bf16[32,1024]{1,0:T(8,128)(2,1)S(1)}, u32[]{:S(2)}, u32[]{:S(2)}) collective-permute-start(bf16[32,1024]{1,0:T(8,128)(2,1)S(1)} %shard_map.122.refs_0_), channel_id=1, source_target_pairs={{0,12},{4,8},{8,4},{12,0},{1,13},{5,9},{9,5},{13,1},{2,14},{6,10},... | collective-permute-start | bytes 196616 | tf_op jit(solution)/shard_map/ppermute | solution.py:26
  9.2 6.1 %collective-permute-start.3 = (bf16[2,64,640]{2,1,0:T(8,128)(2,1)S(1)}, bf16[2,64,640]{2,1,0:T(8,128)(2,1)S(1)}, u32[]{:S(2)}, u32[]{:S(2)}) collective-permute-start(bf16[2,64,640]{2,1,0:T(8,128)(2,1)S(1)} %get-tuple-element.37), channel_id=1, source_target_pairs={{0,1},{1,0},{2,3},{3,2},{4,5},{5,4},{6,7},{7,6},{8,9},{9,8},{10,11... | collective-permute-start | bytes 491528 | tf_op jit(solution)/shard_map/ppermute | solution.py:26
  9.5 11.0 %collective-permute-start.5 = (bf16[32,896]{1,0:T(8,128)(2,1)S(1)}, bf16[32,896]{1,0:T(8,128)(2,1)S(1)}, u32[]{:S(2)}, u32[]{:S(2)}) collective-permute-start(bf16[32,896]{1,0:T(8,128)(2,1)S(1)} %slice.56), channel_id=1, source_target_pairs={{0,2},{1,3},{2,0},{3,1},{4,6},{5,7},{6,4},{7,5},{8,10},{9,11},{10,... | collective-permute-start | bytes 172040 | tf_op jit(solution)/shard_map/ppermute | solution.py:26
  15.6 4.9 %collective-permute-start.4 = (bf16[64,896]{1,0:T(8,128)(2,1)S(1)}, bf16[64,896]{1,0:T(8,128)(2,1)S(1)}, u32[]{:S(2)}, u32[]{:S(2)}) collective-permute-start(bf16[64,896]{1,0:T(8,128)(2,1)S(1)} %pad_maximum_fusion.2), channel_id=1, source_target_pairs={{0,2},{1,3},{2,0},{3,1},{4,6},{5,7},{6,4},{7,5},{8,10},{9,11},{10,... | collective-permute-start | bytes 344072 | tf_op jit(solution)/shard_map/ppermute | solution.py:26
  17.2 5.0 %collective-permute-start.6 = (bf16[96,896]{1,0:T(8,128)(2,1)S(1)}, bf16[96,896]{1,0:T(8,128)(2,1)S(1)}, u32[]{:S(2)}, u32[]{:S(2)}) collective-permute-start(bf16[96,896]{1,0:T(8,128)(2,1)S(1)} %pad_maximum_fusion.refs_5_), channel_id=1, source_target_pairs={{0,1},{1,0},{2,3},{3,2},{4,5},{5,4},{6,7},{7,6},{8,9},{9,8},{10,11... | collective-permute-start | bytes 516104 | tf_op jit(solution)/shard_map/ppermute | solution.py:26
  20.5 1.6 %collective-permute-start.7 = (bf16[96,896]{1,0:T(8,128)(2,1)S(1)}, bf16[96,896]{1,0:T(8,128)(2,1)S(1)}, u32[]{:S(2)}, u32[]{:S(2)}) collective-permute-start(bf16[96,896]{1,0:T(8,128)(2,1)S(1)} %pad_maximum_fusion.1.refs_6_), channel_id=1, source_target_pairs={{0,1},{1,0},{2,3},{3,2},{4,5},{5,4},{6,7},{7,6},{8,9},{9,8},{10,11... | collective-permute-start | bytes 516104 | tf_op jit(solution)/shard_map/ppermute | solution.py:26
  20.6 6.6 %collective-permute-start.8 = (bf16[2,64,640]{2,1,0:T(8,128)(2,1)S(1)}, bf16[2,64,640]{2,1,0:T(8,128)(2,1)S(1)}, u32[]{:S(2)}, u32[]{:S(2)}) collective-permute-start(bf16[2,64,640]{2,1,0:T(8,128)(2,1)S(1)} %shard_map.124.refs_0_), channel_id=1, source_target_pairs={{0,2},{1,3},{2,0},{3,1},{4,6},{5,7},{6,4},{7,5},{8,10},{9,11},{10,... | collective-permute-start | bytes 491528 | tf_op jit(solution)/shard_map/ppermute | solution.py:26
  28.0 1.9 %collective-permute-start.9 = (bf16[128,896]{1,0:T(8,128)(2,1)S(1)}, bf16[128,896]{1,0:T(8,128)(2,1)S(1)}, u32[]{:S(2)}, u32[]{:S(2)}) collective-permute-start(bf16[128,896]{1,0:T(8,128)(2,1)S(1)} %shard_map.127), channel_id=1, source_target_pairs={{0,1},{1,0},{2,3},{3,2},{4,5},{5,4},{6,7},{7,6},{8,9},{9,8},{10,11... | collective-permute-start | bytes 688136 | tf_op jit(solution)/shard_map/ppermute | solution.py:26
  29.4 1.6 %collective-permute-start.10 = (bf16[128,896]{1,0:T(8,128)(2,1)S(1)}, bf16[128,896]{1,0:T(8,128)(2,1)S(1)}, u32[]{:S(2)}, u32[]{:S(2)}) collective-permute-start(bf16[128,896]{1,0:T(8,128)(2,1)S(1)} %get-tuple-element.46), channel_id=1, source_target_pairs={{0,1},{1,0},{2,3},{3,2},{4,5},{5,4},{6,7},{7,6},{8,9},{9,8},{10,11... | collective-permute-start | bytes 688136 | tf_op jit(solution)/shard_map/ppermute | solution.py:26
  31.1 5.5 %collective-permute-start.11 = (bf16[64,896]{1,0:T(8,128)(2,1)S(1)}, bf16[64,896]{1,0:T(8,128)(2,1)S(1)}, u32[]{:S(2)}, u32[]{:S(2)}) collective-permute-start(bf16[64,896]{1,0:T(8,128)(2,1)S(1)} %slice.50), channel_id=1, source_target_pairs={{0,2},{1,3},{2,0},{3,1},{4,6},{5,7},{6,4},{7,5},{8,10},{9,11},{10,... | collective-permute-start | bytes 344072 | tf_op jit(solution)/shard_map/ppermute | solution.py:26
  36.6 6.2 %collective-permute-start.12 = (bf16[32,1792]{1,0:T(8,128)(2,1)S(1)}, bf16[32,1792]{1,0:T(8,128)(2,1)S(1)}, u32[]{:S(2)}, u32[]{:S(2)}) collective-permute-start(bf16[32,1792]{1,0:T(8,128)(2,1)S(1)} %pad_maximum_fusion.3), channel_id=1, source_target_pairs={{0,4},{4,0},{8,12},{12,8},{1,5},{5,1},{9,13},{13,9},{2,6},{6,2},{1... | collective-permute-start | bytes 344072 | tf_op jit(solution)/shard_map/ppermute | solution.py:26
  36.7 8.2 %collective-permute-start.13 = (bf16[32,896]{1,0:T(8,128)(2,1)S(1)}, bf16[32,896]{1,0:T(8,128)(2,1)S(1)}, u32[]{:S(2)}, u32[]{:S(2)}) collective-permute-start(bf16[32,896]{1,0:T(8,128)(2,1)S(1)} %get-tuple-element.61), channel_id=1, source_target_pairs={{0,12},{4,8},{8,4},{12,0},{1,13},{5,9},{9,5},{13,1},{2,14},{6,10},... | collective-permute-start | bytes 172040 | tf_op jit(solution)/shard_map/ppermute | solution.py:26
  37.4 9.5 %collective-permute-start.15 = (bf16[32,896]{1,0:T(8,128)(2,1)S(1)}, bf16[32,896]{1,0:T(8,128)(2,1)S(1)}, u32[]{:S(2)}, u32[]{:S(2)}) collective-permute-start(bf16[32,896]{1,0:T(8,128)(2,1)S(1)} %get-tuple-element.60), channel_id=1, source_target_pairs={{0,8},{4,12},{8,0},{12,4},{1,9},{5,13},{9,1},{13,5},{2,10},{6,14},... | collective-permute-start | bytes 172040 | tf_op jit(solution)/shard_map/ppermute | solution.py:26
  42.9 4.2 %collective-permute-start.16 = (bf16[32,896]{1,0:T(8,128)(2,1)S(1)}, bf16[32,896]{1,0:T(8,128)(2,1)S(1)}, u32[]{:S(2)}, u32[]{:S(2)}) collective-permute-start(bf16[32,896]{1,0:T(8,128)(2,1)S(1)} %add_convert_fusion.3), channel_id=1, source_target_pairs={{0,2},{1,3},{2,0},{3,1},{4,6},{5,7},{6,4},{7,5},{8,10},{9,11},{10,... | collective-permute-start | bytes 172040 | tf_op jit(solution)/shard_map/ppermute | solution.py:26
  44.7 1.4 %collective-permute-start.14 = (bf16[2,64,512]{2,1,0:T(8,128)(2,1)S(1)}, bf16[2,64,512]{2,1,0:T(8,128)(2,1)S(1)}, u32[]{:S(2)}, u32[]{:S(2)}) collective-permute-start(bf16[2,64,512]{2,1,0:T(8,128)(2,1)S(1)} %shard_map.129.mine), channel_id=1, source_target_pairs={{0,1},{1,0},{2,3},{3,2},{4,5},{5,4},{6,7},{7,6},{8,9},{9,8},{10,11... | collective-permute-start | bytes 393224 | tf_op jit(solution)/shard_map/ppermute | solution.py:26
  (6 other events, 30.6 us)

commit v9 on v8

--- a/solution.py
+++ b/solution.py
@@ -230,7 +230,6 @@
         [shaped(count, width // (2 * ways))] * len(pairs),
         [act, down],
         [VMEM, VMEM],
-
     )
 
 
@@ -257,7 +256,7 @@
 
     pack = pack_rows(hidden, routes, spots)
     pack, q_latent = lax.optimization_barrier((pack, q_latent))
-    first = n_dev // 2
+    first = n_dev - 1
     far = over_dev(pack, first, n_dev)
     keep, give = attend(q_latent, q_rope, cache_latent, cache_rope, cache_len)
     again, keep, give = lax.optimization_barrier((pack, keep, give))
@@ -296,7 +295,7 @@
         *own, there = down_call(act, down, [(s, 0) for s in steps] + [(0, 1)], ways)
         there = send(there, "tp", other_core)
         sums = [added(a, b).astype(bf16) for a, b in zip(own, far)]
-        act, sums = lax.optimization_barrier((act, sums))
+        act, sums, states = lax.optimization_barrier((act, sums, states))
         (here,) = down_call(act, down, [(0, 0)], ways)
     else:
         spot, core = spot_and_core()
@@ -309,25 +308,16 @@
         far = [send(block(s, 1 - core), "tp", other_core) for s in range(ways)]
         sums = [added(a, b).astype(bf16) for a, b in zip(own[1:], far[1:])]
         here, there = own[0], far[0]
-    far_rows = [send(p[2 * rows :], "tp", along_x(s, ways)) for s, p in enumerate(sums, 1)]
-    kept = added(here, there)
-    near_rows = [kept[rows : 2 * rows].astype(bf16)] + [p[rows : 2 * rows] for p in sums]
-    near_rows, far_rows = lax.optimization_barrier((jnp.concatenate(near_rows, axis=1), far_rows))
-    near_rows = over_dev(near_rows, 1, n_dev).astype(f32)
-    near_rows, states = lax.optimization_barrier((jnp.split(near_rows, ways, axis=1), states))
-    mine = lax.optimization_barrier([added(p[:rows], q).astype(bf16) for p, q in zip(sums, near_rows[1:])])
-    mine = [send(p, "tp", along_x(s, ways)) for s, p in enumerate(mine, 1)]
-    kept_far = lax.optimization_barrier(kept[2 * rows :])
-    for p in far_rows:
-        kept_far = kept_far + p.astype(f32)
+    total = added(here, there)
+    for s, p in enumerate(sums, 1):
+        total = total + send(p, "tp", along_x(s, ways)).astype(f32)
     joined = join(states, True)
     attended = place_heads(joined, send(joined, "tp", other_core))
-    moe = kept[:rows] + near_rows[0]
-    for s in reversed(range(2, n_dev)):
-        block = kept_far[(s - 2) * rows : (s - 1) * rows].astype(bf16)
-        moe, attended = lax.optimization_barrier((moe + over_dev(block, s, n_dev).astype(f32), attended))
-    for p in mine:
-        moe = moe + p.astype(f32)
+    blocks = [total[i : i + rows] for i in range(0, total.shape[0], rows)]
+    moe = blocks[0]
+    for s in reversed(range(1, n_dev)):
+        moe, attended = lax.optimization_barrier((moe, attended))
+        moe = moe + over_dev(blocks[s].astype(bf16), s, n_dev).astype(f32)
     return (moe.astype(bf16), attended)
 
 def solution(mesh):

time: 47.9 us -> 46.4 us (0.969)
  waiting for transfers between devices: 16.5 us -> 15.7 us
  starting transfers between devices: 18.1 us -> 17.5 us
    ppermute x17 -> x16, waiting for transfers between devices: 16.5 us -> 15.7 us  [send(): return lax.ppermute(value, axis, [(i, target(i)) for i in range(size)])]
    ppermute x17 -> x16, starting transfers between devices: 18.1 us -> 17.5 us  [send(): return lax.ppermute(value, axis, [(i, target(i)) for i in range(size)])]
  transfers between devices with their start and end apart: 17 -> 16, of which waited for: 10 -> 8; matrix products, arithmetic and copies ran while one was open for 1% -> 1% of each run, Pallas kernels for 19% -> 20%
where the time goes in v9:
time: 46.4 us; the launch traced here: 46.2 us
  starting transfers between devices  17.5 us (38%)
  waiting for transfers between devices  15.7 us (34%)
  Pallas kernels  11 us (24%)
  between operations  0.96 us (2%)
  other arithmetic  0.85 us (2%)
    ppermute x16, starting transfers between devices, send(): return lax.ppermute(value, axis, [(i, target(i)) for i in range(size)])  17.5 us
    ppermute x16, waiting for transfers between devices, send(): return lax.ppermute(value, axis, [(i, target(i)) for i in range(size)])  15.7 us
    pallas_call x9, Pallas kernels, local_call(): pl.pallas_call(kernel, out_shape=outs, in_specs=specs, out_specs=jax.tree...  11 us
  transfers between devices with their start and end apart: 16, of which 8 were waited for; matrix products, arithmetic and copies ran while one was open for 1% of the time, Pallas kernels for 20%

profile of v9, /device:TPU:0, one launch (start us, length us, event | category | flops | bytes accessed | tf_op | source)
XLA Modules:
  0.0 46.2 jit_solution(12320484465064512660)
XLA Ops:
  0.7 1.0 %shard_map.122.refs_0_ = bf16[32,1024]{1,0:T(8,128)(2,1)S(1)} custom-call(bf16[32,3584]{1,0:T(8,128)(2,1)} %refs_4_.1, s32[8,32]{1,0:T(8,128)} %bitcast.9), custom_call_target="tpu_custom_call" | custom-call | flops 99999997952 | tf_op jit(solution)/shard_map/pallas_call | solution.py:45
  1.8 5.1 %collective-permute-start.2 = (bf16[32,1024]{1,0:T(8,128)(2,1)S(1)}, bf16[32,1024]{1,0:T(8,128)(2,1)S(1)}, u32[]{:S(2)}, u32[]{:S(2)}) collective-permute-start(bf16[32,1024]{1,0:T(8,128)(2,1)S(1)} %shard_map.122.refs_0_), channel_id=1, source_target_pairs={{0,12},{4,8},{8,4},{12,0},{1,13},{5,9},{9,5},{13,1},{2,14},{6,10},... | collective-permute-start | bytes 196616 | tf_op jit(solution)/shard_map/ppermute | solution.py:26
  6.9 1.7 %shard_map.123 = (bf16[2,64,640]{2,1,0:T(8,128)(2,1)S(1)}, bf16[2,64,640]{2,1,0:T(8,128)(2,1)S(1)}) custom-call(bf16[2,128,512]{2,1,0:T(8,128)(2,1)S(1)} %copy-done.5, bf16[2,64,128]{2,1,0:T(8,128)(2,1)S(1)} %copy-done.7, bf16[2,512,512]{2,1,0:T(8,128)(2,1)S(1)} %copy-done.4, bf16[2,64,512]{2,1,0:T(8,128)(2,1)S(1)} %copy-done.6, s32[2]{0:T(128)S(1)} %copy-done.8), custom_call_target="tpu_custom_call" | custom-call | flops 2000000000 | tf_op jit(solution)/shard_map/pallas_call | solution.py:45
  8.7 0.7 %collective-permute-start.1 = (bf16[32,1024]{1,0:T(8,128)(2,1)S(1)}, bf16[32,1024]{1,0:T(8,128)(2,1)S(1)}, u32[]{:S(2)}, u32[]{:S(2)}) collective-permute-start(bf16[32,1024]{1,0:T(8,128)(2,1)S(1)} %shard_map.122.refs_0_), channel_id=1, source_target_pairs={{0,8},{4,12},{8,0},{12,4},{1,9},{5,13},{9,1},{13,5},{2,10},{6,14},... | collective-permute-start | bytes 196616 | tf_op jit(solution)/shard_map/ppermute | solution.py:26
  9.4 1.7 %collective-permute-start.5 = (bf16[32,896]{1,0:T(8,128)(2,1)S(1)}, bf16[32,896]{1,0:T(8,128)(2,1)S(1)}, u32[]{:S(2)}, u32[]{:S(2)}) collective-permute-start(bf16[32,896]{1,0:T(8,128)(2,1)S(1)} %slice.41), channel_id=1, source_target_pairs={{0,2},{1,3},{2,0},{3,1},{4,6},{5,7},{6,4},{7,5},{8,10},{9,11},{10,... | collective-permute-start | bytes 172040 | tf_op jit(solution)/shard_map/ppermute | solution.py:26
  11.0 2.2 %collective-permute-done.refs_1_ = bf16[32,1024]{1,0:T(8,128)(2,1)S(1)} collective-permute-done((bf16[32,1024]{1,0:T(8,128)(2,1)S(1)}, bf16[32,1024]{1,0:T(8,128)(2,1)S(1)}, u32[]{:S(2)}, u32[]{:S(2)}) %collective-permute-start) | collective-permute-done | bytes 65568 | tf_op jit(solution)/shard_map/ppermute | solution.py:26
  13.2 1.1 %collective-permute-done.1.refs_2_ = bf16[32,1024]{1,0:T(8,128)(2,1)S(1)} collective-permute-done((bf16[32,1024]{1,0:T(8,128)(2,1)S(1)}, bf16[32,1024]{1,0:T(8,128)(2,1)S(1)}, u32[]{:S(2)}, u32[]{:S(2)}) %collective-permute-start.1) | collective-permute-done | bytes 65568 | tf_op jit(solution)/shard_map/ppermute | solution.py:26
  14.6 1.6 %collective-permute-start.4 = (bf16[64,896]{1,0:T(8,128)(2,1)S(1)}, bf16[64,896]{1,0:T(8,128)(2,1)S(1)}, u32[]{:S(2)}, u32[]{:S(2)}) collective-permute-start(bf16[64,896]{1,0:T(8,128)(2,1)S(1)} %pad_maximum_fusion.2), channel_id=1, source_target_pairs={{0,2},{1,3},{2,0},{3,1},{4,6},{5,7},{6,4},{7,5},{8,10},{9,11},{10,... | collective-permute-start | bytes 344072 | tf_op jit(solution)/shard_map/ppermute | solution.py:26
  16.3 3.2 %collective-permute-done.4 = bf16[64,896]{1,0:T(8,128)(2,1)S(1)} collective-permute-done((bf16[64,896]{1,0:T(8,128)(2,1)S(1)}, bf16[64,896]{1,0:T(8,128)(2,1)S(1)}, u32[]{:S(2)}, u32[]{:S(2)}) %collective-permute-start.4) | collective-permute-done | bytes 114720 | tf_op jit(solution)/shard_map/ppermute | solution.py:26
  19.6 1.6 %collective-permute-start.8 = (bf16[2,64,640]{2,1,0:T(8,128)(2,1)S(1)}, bf16[2,64,640]{2,1,0:T(8,128)(2,1)S(1)}, u32[]{:S(2)}, u32[]{:S(2)}) collective-permute-start(bf16[2,64,640]{2,1,0:T(8,128)(2,1)S(1)} %shard_map.124.refs_0_), channel_id=1, source_target_pairs={{0,2},{1,3},{2,0},{3,1},{4,6},{5,7},{6,4},{7,5},{8,10},{9,11},{10,... | collective-permute-start | bytes 491528 | tf_op jit(solution)/shard_map/ppermute | solution.py:26
  21.2 4.3 %shard_map.125.act = bf16[128,2048]{1,0:T(8,128)(2,1)S(1)} custom-call(bf16[32,1024]{1,0:T(8,128)(2,1)S(1)} %shard_map.122.refs_0_, bf16[32,1024]{1,0:T(8,128)(2,1)S(1)} %collective-permute-done.refs_1_, bf16[32,1024]{1,0:T(8,128)(2,1)S(1)} %collective-permute-done.1.refs_2_, bf16[32,1024]{1,0:T(8,128)(2,1)S(1)} %collective-permute-done.2.refs_3_, ...), custom_call_target="tpu_custom_call" | custom-call | tf_op jit(solution)/shard_map/pallas_call | solution.py:45
  25.5 0.7 %collective-permute-done.8.refs_1_ = bf16[2,64,640]{2,1,0:T(8,128)(2,1)S(1)} collective-permute-done((bf16[2,64,640]{2,1,0:T(8,128)(2,1)S(1)}, bf16[2,64,640]{2,1,0:T(8,128)(2,1)S(1)}, u32[]{:S(2)}, u32[]{:S(2)}) %collective-permute-start.8) | collective-permute-done | bytes 163872 | tf_op jit(solution)/shard_map/ppermute | solution.py:26
  26.3 0.7 %shard_map.127 = bf16[128,896]{1,0:T(8,128)(2,1)S(1)} custom-call(bf16[128,2048]{1,0:T(8,128)(2,1)S(1)} %shard_map.125.act, bf16[2048,3584]{1,0:T(8,128)(2,1)S(1)} %bitcast.5), custom_call_target="tpu_custom_call" | custom-call | tf_op jit(solution)/shard_map/pallas_call | solution.py:45
  27.1 1.3 %shard_map.126 = (bf16[128,896]{1,0:T(8,128)(2,1)S(1)}, bf16[128,896]{1,0:T(8,128)(2,1)S(1)}) custom-call(bf16[128,2048]{1,0:T(8,128)(2,1)S(1)} %shard_map.125.act, bf16[2048,3584]{1,0:T(8,128)(2,1)S(1)} %bitcast.6), custom_call_target="tpu_custom_call" | custom-call | tf_op jit(solution)/shard_map/pallas_call | solution.py:45
  29.0 1.6 %collective-permute-start.11 = (bf16[128,896]{1,0:T(8,128)(2,1)S(1)}, bf16[128,896]{1,0:T(8,128)(2,1)S(1)}, u32[]{:S(2)}, u32[]{:S(2)}) collective-permute-start(bf16[128,896]{1,0:T(8,128)(2,1)S(1)} %add_convert_fusion), channel_id=1, source_target_pairs={{0,2},{1,3},{2,0},{3,1},{4,6},{5,7},{6,4},{7,5},{8,10},{9,11},{10,... | collective-permute-start | bytes 688136 | tf_op jit(solution)/shard_map/ppermute | solution.py:26
  30.9 0.7 %shard_map.128 = bf16[128,896]{1,0:T(8,128)(2,1)S(1)} custom-call(bf16[128,2048]{1,0:T(8,128)(2,1)S(1)} %shard_map.125.act, bf16[2048,3584]{1,0:T(8,128)(2,1)S(1)} %bitcast.7), custom_call_target="tpu_custom_call" | custom-call | tf_op jit(solution)/shard_map/pallas_call | solution.py:45
  31.7 5.0 %collective-permute-done.11 = bf16[128,896]{1,0:T(8,128)(2,1)S(1)} collective-permute-done((bf16[128,896]{1,0:T(8,128)(2,1)S(1)}, bf16[128,896]{1,0:T(8,128)(2,1)S(1)}, u32[]{:S(2)}, u32[]{:S(2)}) %collective-permute-start.11) | collective-permute-done | bytes 229408 | tf_op jit(solution)/shard_map/ppermute | solution.py:26
  36.7 1.8 %collective-permute-start.13 = (bf16[32,896]{1,0:T(8,128)(2,1)S(1)}, bf16[32,896]{1,0:T(8,128)(2,1)S(1)}, u32[]{:S(2)}, u32[]{:S(2)}) collective-permute-start(bf16[32,896]{1,0:T(8,128)(2,1)S(1)} %get-tuple-element.60), channel_id=1, source_target_pairs={{0,12},{4,8},{8,4},{12,0},{1,13},{5,9},{9,5},{13,1},{2,14},{6,10},... | collective-permute-start | bytes 172040 | tf_op jit(solution)/shard_map/ppermute | solution.py:26
  38.5 0.7 %shard_map.130 = bf16[2,128,512]{2,1,0:T(8,128)(2,1)} custom-call(bf16[2,64,512]{2,1,0:T(8,128)(2,1)S(1)} %shard_map.129.mine, bf16[2,64,512]{2,1,0:T(8,128)(2,1)S(1)} %collective-permute-done.12.theirs), custom_call_target="tpu_custom_call" | custom-call | tf_op jit(solution)/shard_map/pallas_call | solution.py:45
  39.3 1.4 %collective-permute-start.14 = (bf16[32,896]{1,0:T(8,128)(2,1)S(1)}, bf16[32,896]{1,0:T(8,128)(2,1)S(1)}, u32[]{:S(2)}, u32[]{:S(2)}) collective-permute-start(bf16[32,896]{1,0:T(8,128)(2,1)S(1)} %get-tuple-element.59), channel_id=1, source_target_pairs={{0,8},{4,12},{8,0},{12,4},{1,9},{5,13},{9,1},{13,5},{2,10},{6,14},... | collective-permute-start | bytes 172040 | tf_op jit(solution)/shard_map/ppermute | solution.py:26
  40.6 1.4 %collective-permute-start.15 = (bf16[32,896]{1,0:T(8,128)(2,1)S(1)}, bf16[32,896]{1,0:T(8,128)(2,1)S(1)}, u32[]{:S(2)}, u32[]{:S(2)}) collective-permute-start(bf16[32,896]{1,0:T(8,128)(2,1)S(1)} %get-tuple-element.58), channel_id=1, source_target_pairs={{0,4},{4,0},{8,12},{12,8},{1,5},{5,1},{9,13},{13,9},{2,6},{6,2},{1... | collective-permute-start | bytes 172040 | tf_op jit(solution)/shard_map/ppermute | solution.py:26
  42.0 0.9 %collective-permute-done.13 = bf16[32,896]{1,0:T(8,128)(2,1)S(1)} collective-permute-done((bf16[32,896]{1,0:T(8,128)(2,1)S(1)}, bf16[32,896]{1,0:T(8,128)(2,1)S(1)}, u32[]{:S(2)}, u32[]{:S(2)}) %collective-permute-start.13) | collective-permute-done | bytes 57376 | tf_op jit(solution)/shard_map/ppermute | solution.py:26
  42.9 2.2 %collective-permute-done.14 = bf16[32,896]{1,0:T(8,128)(2,1)S(1)} collective-permute-done((bf16[32,896]{1,0:T(8,128)(2,1)S(1)}, bf16[32,896]{1,0:T(8,128)(2,1)S(1)}, u32[]{:S(2)}, u32[]{:S(2)}) %collective-permute-start.14) | collective-permute-done | bytes 57376 | tf_op jit(solution)/shard_map/ppermute | solution.py:26
  45.6 0.6 %add_convert_fusion.1 = bf16[32,896]{1,0:T(8,128)(2,1)} fusion(f32[32,896]{1,0:T(8,128)S(1)} %convert_add_fusion.1, bf16[32,896]{1,0:T(8,128)(2,1)S(1)} %collective-permute-done.15), kind=kLoop, calls=%fused_computation.5 | loop fusion | flops 86016 | bytes 229376 | tf_op jit(solution)/shard_map/convert_element_type | solution.py:321
  (58 shorter events, 2.2 us)
Async XLA Ops:
  0.6 6.2 %copy-start.4 = (bf16[2,512,512]{2,1,0:T(8,128)(2,1)S(1)}, bf16[2,512,512]{2,1,0:T(8,128)(2,1)}, u32[]{:S(2)}) copy-start(bf16[2,512,512]{2,1,0:T(8,128)(2,1)} %keys.1) | copy-start | bytes 3145732
  0.6 6.2 %copy-start.5 = (bf16[2,128,512]{2,1,0:T(8,128)(2,1)S(1)}, bf16[2,128,512]{2,1,0:T(8,128)(2,1)}, u32[]{:S(2)}) copy-start(bf16[2,128,512]{2,1,0:T(8,128)(2,1)} %q_lat) | copy-start | bytes 786436
  0.7 6.2 %copy-start.6 = (bf16[2,64,512]{2,1,0:T(8,128)(2,1)S(1)}, bf16[2,64,512]{2,1,0:T(8,128)(2,1)}, u32[]{:S(2)}) copy-start(bf16[2,64,512]{2,1,0:T(8,128)(2,1)} %rope.1) | copy-start | bytes 393220
  0.7 20.5 %copy-start = (bf16[8,3584,256]{2,1,0:T(8,128)(2,1)S(1)}, bf16[8,3584,256]{2,1,0:T(8,128)(2,1)}, u32[]{:S(2)}) copy-start(bf16[8,3584,256]{2,1,0:T(8,128)(2,1)} %refs_10_.1) | copy-start | bytes 44040196
  0.7 20.5 %copy-start.1 = (bf16[8,3584,256]{2,1,0:T(8,128)(2,1)S(1)}, bf16[8,3584,256]{2,1,0:T(8,128)(2,1)}, u32[]{:S(2)}) copy-start(bf16[8,3584,256]{2,1,0:T(8,128)(2,1)} %refs_11_.1) | copy-start | bytes 44040196
  0.7 20.5 %copy-start.2 = (bf16[32,3584]{1,0:T(8,128)(2,1)S(1)}, bf16[32,3584]{1,0:T(8,128)(2,1)}, u32[]{:S(2)}) copy-start(bf16[32,3584]{1,0:T(8,128)(2,1)} %refs_4_.1) | copy-start | bytes 688132
  0.7 20.5 %copy-start.3 = (bf16[3584,32]{0,1:T(8,128)(2,1)S(1)}, bf16[3584,32]{0,1:T(8,128)(2,1)}, u32[]{:S(2)}) copy-start(bf16[3584,32]{0,1:T(8,128)(2,1)} %param.13) | copy-start | bytes 688132
  1.8 7.6 %collective-permute-start.2 = (bf16[32,1024]{1,0:T(8,128)(2,1)S(1)}, bf16[32,1024]{1,0:T(8,128)(2,1)S(1)}, u32[]{:S(2)}, u32[]{:S(2)}) collective-permute-start(bf16[32,1024]{1,0:T(8,128)(2,1)S(1)} %shard_map.122.refs_0_), channel_id=1, source_target_pairs={{0,12},{4,8},{8,4},{12,0},{1,13},{5,9},{9,5},{13,1},{2,14},{6,10},... | collective-permute-start | bytes 196616 | tf_op jit(solution)/shard_map/ppermute | solution.py:26
  6.9 19.3 %slice-start = ((s8[14680064]{0:T(1024)(128)(4,1)}), s8[4194304]{0:T(1024)(128)(4,1)S(1)}, s32[]{:S(2)}) async-start(s8[14680064]{0:T(1024)(128)(4,1)} %bitcast.3), calls=%async_computation | async-start | bytes 8388608
  8.6 4.6 %collective-permute-start = (bf16[32,1024]{1,0:T(8,128)(2,1)S(1)}, bf16[32,1024]{1,0:T(8,128)(2,1)S(1)}, u32[]{:S(2)}, u32[]{:S(2)}) collective-permute-start(bf16[32,1024]{1,0:T(8,128)(2,1)S(1)} %shard_map.122.refs_0_), channel_id=1, source_target_pairs={{0,4},{4,0},{8,12},{12,8},{1,5},{5,1},{9,13},{13,9},{2,6},{6,2},{1... | collective-permute-start | bytes 196616 | tf_op jit(solution)/shard_map/ppermute | solution.py:26
  8.7 5.6 %collective-permute-start.1 = (bf16[32,1024]{1,0:T(8,128)(2,1)S(1)}, bf16[32,1024]{1,0:T(8,128)(2,1)S(1)}, u32[]{:S(2)}, u32[]{:S(2)}) collective-permute-start(bf16[32,1024]{1,0:T(8,128)(2,1)S(1)} %shard_map.122.refs_0_), channel_id=1, source_target_pairs={{0,8},{4,12},{8,0},{12,4},{1,9},{5,13},{9,1},{13,5},{2,10},{6,14},... | collective-permute-start | bytes 196616 | tf_op jit(solution)/shard_map/ppermute | solution.py:26
  9.3 5.0 %collective-permute-start.3 = (bf16[2,64,640]{2,1,0:T(8,128)(2,1)S(1)}, bf16[2,64,640]{2,1,0:T(8,128)(2,1)S(1)}, u32[]{:S(2)}, u32[]{:S(2)}) collective-permute-start(bf16[2,64,640]{2,1,0:T(8,128)(2,1)S(1)} %get-tuple-element.35), channel_id=1, source_target_pairs={{0,1},{1,0},{2,3},{3,2},{4,5},{5,4},{6,7},{7,6},{8,9},{9,8},{10,11... | collective-permute-start | bytes 491528 | tf_op jit(solution)/shard_map/ppermute | solution.py:26
  9.4 10.1 %collective-permute-start.5 = (bf16[32,896]{1,0:T(8,128)(2,1)S(1)}, bf16[32,896]{1,0:T(8,128)(2,1)S(1)}, u32[]{:S(2)}, u32[]{:S(2)}) collective-permute-start(bf16[32,896]{1,0:T(8,128)(2,1)S(1)} %slice.41), channel_id=1, source_target_pairs={{0,2},{1,3},{2,0},{3,1},{4,6},{5,7},{6,4},{7,5},{8,10},{9,11},{10,... | collective-permute-start | bytes 172040 | tf_op jit(solution)/shard_map/ppermute | solution.py:26
  14.6 4.9 %collective-permute-start.4 = (bf16[64,896]{1,0:T(8,128)(2,1)S(1)}, bf16[64,896]{1,0:T(8,128)(2,1)S(1)}, u32[]{:S(2)}, u32[]{:S(2)}) collective-permute-start(bf16[64,896]{1,0:T(8,128)(2,1)S(1)} %pad_maximum_fusion.2), channel_id=1, source_target_pairs={{0,2},{1,3},{2,0},{3,1},{4,6},{5,7},{6,4},{7,5},{8,10},{9,11},{10,... | collective-permute-start | bytes 344072 | tf_op jit(solution)/shard_map/ppermute | solution.py:26
  16.2 5.0 %collective-permute-start.6 = (bf16[96,896]{1,0:T(8,128)(2,1)S(1)}, bf16[96,896]{1,0:T(8,128)(2,1)S(1)}, u32[]{:S(2)}, u32[]{:S(2)}) collective-permute-start(bf16[96,896]{1,0:T(8,128)(2,1)S(1)} %pad_maximum_fusion.refs_5_), channel_id=1, source_target_pairs={{0,1},{1,0},{2,3},{3,2},{4,5},{5,4},{6,7},{7,6},{8,9},{9,8},{10,11... | collective-permute-start | bytes 516104 | tf_op jit(solution)/shard_map/ppermute | solution.py:26
  19.5 1.6 %collective-permute-start.7 = (bf16[96,896]{1,0:T(8,128)(2,1)S(1)}, bf16[96,896]{1,0:T(8,128)(2,1)S(1)}, u32[]{:S(2)}, u32[]{:S(2)}) collective-permute-start(bf16[96,896]{1,0:T(8,128)(2,1)S(1)} %pad_maximum_fusion.1.refs_6_), channel_id=1, source_target_pairs={{0,1},{1,0},{2,3},{3,2},{4,5},{5,4},{6,7},{7,6},{8,9},{9,8},{10,11... | collective-permute-start | bytes 516104 | tf_op jit(solution)/shard_map/ppermute | solution.py:26
  19.6 6.6 %collective-permute-start.8 = (bf16[2,64,640]{2,1,0:T(8,128)(2,1)S(1)}, bf16[2,64,640]{2,1,0:T(8,128)(2,1)S(1)}, u32[]{:S(2)}, u32[]{:S(2)}) collective-permute-start(bf16[2,64,640]{2,1,0:T(8,128)(2,1)S(1)} %shard_map.124.refs_0_), channel_id=1, source_target_pairs={{0,2},{1,3},{2,0},{3,1},{4,6},{5,7},{6,4},{7,5},{8,10},{9,11},{10,... | collective-permute-start | bytes 491528 | tf_op jit(solution)/shard_map/ppermute | solution.py:26
  27.0 1.9 %collective-permute-start.9 = (bf16[128,896]{1,0:T(8,128)(2,1)S(1)}, bf16[128,896]{1,0:T(8,128)(2,1)S(1)}, u32[]{:S(2)}, u32[]{:S(2)}) collective-permute-start(bf16[128,896]{1,0:T(8,128)(2,1)S(1)} %shard_map.127), channel_id=1, source_target_pairs={{0,1},{1,0},{2,3},{3,2},{4,5},{5,4},{6,7},{7,6},{8,9},{9,8},{10,11... | collective-permute-start | bytes 688136 | tf_op jit(solution)/shard_map/ppermute | solution.py:26
  28.4 3.3 %collective-permute-start.10 = (bf16[128,896]{1,0:T(8,128)(2,1)S(1)}, bf16[128,896]{1,0:T(8,128)(2,1)S(1)}, u32[]{:S(2)}, u32[]{:S(2)}) collective-permute-start(bf16[128,896]{1,0:T(8,128)(2,1)S(1)} %get-tuple-element.46), channel_id=1, source_target_pairs={{0,1},{1,0},{2,3},{3,2},{4,5},{5,4},{6,7},{7,6},{8,9},{9,8},{10,11... | collective-permute-start | bytes 688136 | tf_op jit(solution)/shard_map/ppermute | solution.py:26
  29.0 7.6 %collective-permute-start.11 = (bf16[128,896]{1,0:T(8,128)(2,1)S(1)}, bf16[128,896]{1,0:T(8,128)(2,1)S(1)}, u32[]{:S(2)}, u32[]{:S(2)}) collective-permute-start(bf16[128,896]{1,0:T(8,128)(2,1)S(1)} %add_convert_fusion), channel_id=1, source_target_pairs={{0,2},{1,3},{2,0},{3,1},{4,6},{5,7},{6,4},{7,5},{8,10},{9,11},{10,... | collective-permute-start | bytes 688136 | tf_op jit(solution)/shard_map/ppermute | solution.py:26
  30.9 7.7 %collective-permute-start.12 = (bf16[2,64,512]{2,1,0:T(8,128)(2,1)S(1)}, bf16[2,64,512]{2,1,0:T(8,128)(2,1)S(1)}, u32[]{:S(2)}, u32[]{:S(2)}) collective-permute-start(bf16[2,64,512]{2,1,0:T(8,128)(2,1)S(1)} %shard_map.129.mine), channel_id=1, source_target_pairs={{0,1},{1,0},{2,3},{3,2},{4,5},{5,4},{6,7},{7,6},{8,9},{9,8},{10,11... | collective-permute-start | bytes 393224 | tf_op jit(solution)/shard_map/ppermute | solution.py:26
  36.7 6.1 %collective-permute-start.13 = (bf16[32,896]{1,0:T(8,128)(2,1)S(1)}, bf16[32,896]{1,0:T(8,128)(2,1)S(1)}, u32[]{:S(2)}, u32[]{:S(2)}) collective-permute-start(bf16[32,896]{1,0:T(8,128)(2,1)S(1)} %get-tuple-element.60), channel_id=1, source_target_pairs={{0,12},{4,8},{8,4},{12,0},{1,13},{5,9},{9,5},{13,1},{2,14},{6,10},... | collective-permute-start | bytes 172040 | tf_op jit(solution)/shard_map/ppermute | solution.py:26
  39.3 5.8 %collective-permute-start.14 = (bf16[32,896]{1,0:T(8,128)(2,1)S(1)}, bf16[32,896]{1,0:T(8,128)(2,1)S(1)}, u32[]{:S(2)}, u32[]{:S(2)}) collective-permute-start(bf16[32,896]{1,0:T(8,128)(2,1)S(1)} %get-tuple-element.59), channel_id=1, source_target_pairs={{0,8},{4,12},{8,0},{12,4},{1,9},{5,13},{9,1},{13,5},{2,10},{6,14},... | collective-permute-start | bytes 172040 | tf_op jit(solution)/shard_map/ppermute | solution.py:26
  40.6 4.9 %collective-permute-start.15 = (bf16[32,896]{1,0:T(8,128)(2,1)S(1)}, bf16[32,896]{1,0:T(8,128)(2,1)S(1)}, u32[]{:S(2)}, u32[]{:S(2)}) collective-permute-start(bf16[32,896]{1,0:T(8,128)(2,1)S(1)} %get-tuple-element.58), channel_id=1, source_target_pairs={{0,4},{4,0},{8,12},{12,8},{1,5},{5,1},{9,13},{13,9},{2,6},{6,2},{1... | collective-permute-start | bytes 172040 | tf_op jit(solution)/shard_map/ppermute | solution.py:26
  (5 other events, 27.5 us)

commit v10 on v9

--- a/solution.py
+++ b/solution.py
@@ -127,30 +127,38 @@
     return local_call(place_kernel, shaped(rows, 2 * half, width), [mine, theirs], [VMEM, VMEM])
 
 
-def pack_kernel(spots, hidden, routes, out, tags, sems):
-    size = out.shape[1] - LANES
+def pack_kernel(spots, ways, hidden, routes, wide, narrow, tags, sems):
+    size = narrow.shape[1] - LANES
     picks, rows = routes.shape
     spot, core = spot_and_core()
-    start = pl.multiple_of((spot * 2 + core if spots > 1 else core) * size, size)
-    columns = pltpu.make_async_copy(hidden.at[:, pl.ds(start, size)], out.at[:, pl.ds(0, size)], sems.at[0])
-    named = pltpu.make_async_copy(routes, tags, sems.at[1])
-    columns.start()
-    named.start()
-    out[:, size:] = jnp.zeros((rows, LANES), bf16)
-    named.wait()
+    copies = [pltpu.make_async_copy(routes, tags, sems.at[0])]
+    for s in range(spots):
+        first = partner(spot, s, ways) * 2 if spots > 1 else 0
+        columns = hidden.at[:, pl.ds(pl.multiple_of((first + core) * size, size), size)]
+        copies.append(pltpu.make_async_copy(columns, wide.at[:, pl.ds(s * size, size)], sems.at[1 + s]))
+        if s == 0:
+            copies.append(pltpu.make_async_copy(columns, narrow.at[:, pl.ds(0, size)], sems.at[1 + spots]))
+    for copy in copies:
+        copy.start()
+    blank = jnp.zeros((rows, LANES), bf16)
+    wide[:, spots * size :] = blank
+    narrow[:, size:] = blank
+    copies[0].wait()
     eye = lax.broadcasted_iota(jnp.int32, (rows, rows), 0) == lax.broadcasted_iota(jnp.int32, (rows, rows), 1)
-    turned = dot(eye.astype(f32).astype(bf16), tags[...].astype(f32).astype(bf16), ((1,), (1,)))
-    out[:, size : size + picks] = turned.astype(bf16)
-    columns.wait()
-
-def pack_rows(hidden, routes, spots):
+    turned = dot(eye.astype(f32).astype(bf16), tags[...].astype(f32).astype(bf16), ((1,), (1,))).astype(bf16)
+    wide[:, spots * size : spots * size + picks] = turned
+    narrow[:, size : size + picks] = turned
+    for copy in copies[1:]:
+        copy.wait()
+
+def pack_rows(hidden, routes, spots, ways):
     rows, width = hidden.shape
     return local_call(
-        functools.partial(pack_kernel, spots),
-        shaped(rows, width // (2 * spots) + LANES),
+        functools.partial(pack_kernel, spots, ways),
+        [shaped(rows, width // 2 + LANES), shaped(rows, width // (2 * spots) + LANES)],
         [pltpu.with_memory_space_constraint(a, pltpu.HBM) for a in (hidden, routes.T)],
         [ANY, ANY],
-        [pltpu.VMEM(routes.shape[::-1], jnp.int32), pltpu.SemaphoreType.DMA((2,))],
+        [pltpu.VMEM(routes.shape[::-1], jnp.int32), pltpu.SemaphoreType.DMA((2 + spots,))],
         flops=WAIT_FLOPS,
         limit=2,
     )
@@ -168,7 +176,7 @@
         x[later, pl.ds(pl.multiple_of((first + core) * size, size), size)] = mine[s][...]
         x[later, pl.ds(pl.multiple_of((first + 1 - core) * size, size), size)] = theirs[s][...]
     for s, pack in enumerate(packs):
-        tags[pl.ds(s * rows, rows), :] = pack[:, size:]
+        tags[pl.ds(s * rows, rows), :] = pack[:, pack.shape[1] - LANES :]
 
     scores = jax.nn.sigmoid(dot(x[...], router[...], ((1,), (1,))))
     labels = lax.broadcasted_iota(jnp.int32, scores.shape, 1)
@@ -254,26 +262,27 @@
     spots = ways if aligned else 1
     share = width // (2 * spots)
 
-    pack = pack_rows(hidden, routes, spots)
-    pack, q_latent = lax.optimization_barrier((pack, q_latent))
+    wide, narrow = pack_rows(hidden, routes, spots, ways)
+    wide, narrow, q_latent = lax.optimization_barrier((wide, narrow, q_latent))
     first = n_dev - 1
-    far = over_dev(pack, first, n_dev)
+    far = over_dev(narrow, first, n_dev)
     keep, give = attend(q_latent, q_rope, cache_latent, cache_rope, cache_len)
-    again, keep, give = lax.optimization_barrier((pack, keep, give))
-    packs = [pack] + [far if s == first else over_dev(again, s, n_dev) for s in range(1, n_dev)]
+    wide, again, keep, give = lax.optimization_barrier((wide, narrow, keep, give))
+    packs = [narrow, over_dev(wide, 1, n_dev)]
+    packs += [far if s == first else over_dev(again, s, n_dev) for s in range(2, n_dev)]
     near = [p[:, :share] for p in packs[1:]]
-    first -= 1
-    early = [send(near[first], "tp", along_x(s, ways)) for s in range(1, spots)]
+    early = [send(near[first - 1], "tp", along_x(s, ways)) for s in range(1, spots)]
     state = join([keep, send(give, "tp", other_core)], False)
-    others = [s for s in reversed(range(1, n_dev)) if s != first + 1]
-    rest = jnp.concatenate([near[s - 1] for s in others], axis=0)
-    rest, state = lax.optimization_barrier((rest, state))
+    rest = jnp.concatenate(near[1 : first - 1], axis=0)
+    rest, early = lax.optimization_barrier((rest, early))
     late = [send(rest, "tp", along_x(s, ways)) for s in range(1, spots)]
+    neighbour, late, state = lax.optimization_barrier((packs[1], late, state))
+    packs[1] = neighbour
+    near[0] = neighbour[:, :share]
     mine = [jnp.concatenate(near, axis=0)]
-    for a, b in zip(early, late):
-        come = {s: b[i * rows : (i + 1) * rows] for i, s in enumerate(others)}
-        mine.append(jnp.concatenate([come.get(s, a) for s in range(1, n_dev)], axis=0))
-    theirs = [send(m, "tp", other_core) for m in mine]
+    for s, (a, b) in enumerate(zip(early, late), 1):
+        mine.append(jnp.concatenate([neighbour[:, s * share : (s + 1) * share], b, a], axis=0))
+    theirs = jnp.split(send(jnp.concatenate(mine, axis=0), "tp", other_core), spots)
     states = [send(state, "tp", along_x(s, ways)) for s in range(1, ways)]
     theirs, state = lax.optimization_barrier((theirs, state))
     states = [state] + states
@@ -288,10 +297,11 @@
     def added(a, b):
         return a.astype(f32) + b.astype(f32)
 
-    act, states = lax.optimization_barrier((act, states))
     if aligned:
         steps = range(1, ways)
-        far = [send(p, "tp", other_core) for p in down_call(act, down, [(s, 1) for s in steps], ways)]
+        far = down_call(act, down, [(s, 1) for s in steps], ways)
+        far, act, states = lax.optimization_barrier((far, act, states))
+        far = [send(p, "tp", other_core) for p in far]
         *own, there = down_call(act, down, [(s, 0) for s in steps] + [(0, 1)], ways)
         there = send(there, "tp", other_core)
         sums = [added(a, b).astype(bf16) for a, b in zip(own, far)]
@@ -308,15 +318,17 @@
         far = [send(block(s, 1 - core), "tp", other_core) for s in range(ways)]
         sums = [added(a, b).astype(bf16) for a, b in zip(own[1:], far[1:])]
         here, there = own[0], far[0]
-    total = added(here, there)
-    for s, p in enumerate(sums, 1):
-        total = total + send(p, "tp", along_x(s, ways)).astype(f32)
+    sums = [send(p, "tp", along_x(s, ways)) for s, p in enumerate(sums, 1)]
     joined = join(states, True)
     attended = place_heads(joined, send(joined, "tp", other_core))
+    sums, attended = lax.optimization_barrier((sums, attended))
+    total = added(here, there)
+    for p in sums:
+        total = total + p.astype(f32)
     blocks = [total[i : i + rows] for i in range(0, total.shape[0], rows)]
     moe = blocks[0]
     for s in reversed(range(1, n_dev)):
-        moe, attended = lax.optimization_barrier((moe, attended))
+        moe = lax.optimization_barrier(moe)
         moe = moe + over_dev(blocks[s].astype(bf16), s, n_dev).astype(f32)
     return (moe.astype(bf16), attended)
 

time: 46.4 us -> 49.9 us (1.075)
  local copies, waits for them, and re-layouts: 0.11 us -> 5.37 us
  waiting for transfers between devices: 15.7 us -> 13.7 us
    unnamed x26 -> x37, local copies, waits for them, and re-layouts: 0.06 us -> 5.3 us
    ppermute x16 -> x15, waiting for transfers between devices: 15.7 us -> 13.7 us  [send(): return lax.ppermute(value, axis, [(i, target(i)) for i in range(size)])]
    ppermute x16 -> x15, starting transfers between devices: 17.5 us -> 17.7 us  [send(): return lax.ppermute(value, axis, [(i, target(i)) for i in range(size)])]
  transfers between devices with their start and end apart: 16 -> 15, of which waited for: 8 -> 7; matrix products, arithmetic and copies ran while one was open for 1% -> 0% of each run, Pallas kernels for 20% -> 20%
where the time goes in v10:
time: 49.9 us; the launch traced here: 49.7 us
  starting transfers between devices  17.7 us (35%)
  waiting for transfers between devices  13.7 us (27%)
  Pallas kernels  11.1 us (22%)
  local copies, waits for them, and re-layouts  5.37 us (11%)
  between operations  1.02 us (2%)
  other arithmetic  0.85 us (2%)
    ppermute x15, starting transfers between devices, send(): return lax.ppermute(value, axis, [(i, target(i)) for i in range(size)])  17.7 us
    ppermute x15, waiting for transfers between devices, send(): return lax.ppermute(value, axis, [(i, target(i)) for i in range(size)])  13.7 us
    pallas_call x9, Pallas kernels, local_call(): pl.pallas_call(kernel, out_shape=outs, in_specs=specs, out_specs=jax.tree...  11.1 us
    unnamed x37, local copies, waits for them, and re-layouts  5.3 us
  transfers between devices with their start and end apart: 15, of which 7 were waited for; matrix products, arithmetic and copies ran while one was open for 0% of the time, Pallas kernels for 20%

profile of v10, /device:TPU:0, one launch (start us, length us, event | category | flops | bytes accessed | tf_op | source)
XLA Modules:
  0.0 49.7 jit_solution(844923699747696868)
XLA Ops:
  0.7 1.1 %shard_map.122 = (bf16[32,1920]{1,0:T(8,128)(2,1)S(1)}, bf16[32,1024]{1,0:T(8,128)(2,1)S(1)}) custom-call(bf16[32,3584]{1,0:T(8,128)(2,1)} %refs_4_.1, s32[8,32]{1,0:T(8,128)} %bitcast.11), custom_call_target="tpu_custom_call" | custom-call | flops 99999997952 | tf_op jit(solution)/shard_map/pallas_call | solution.py:45
  1.8 5.1 %collective-permute-start.2 = (bf16[32,1024]{1,0:T(8,128)(2,1)S(1)}, bf16[32,1024]{1,0:T(8,128)(2,1)S(1)}, u32[]{:S(2)}, u32[]{:S(2)}) collective-permute-start(bf16[32,1024]{1,0:T(8,128)(2,1)S(1)} %get-tuple-element.41.refs_0_), channel_id=1, source_target_pairs={{0,12},{4,8},{8,4},{12,0},{1,13},{5,9},{9,5},{13,1},{2,14},{6,10},... | collective-permute-start | bytes 196616 | tf_op jit(solution)/shard_map/ppermute | solution.py:26
  7.0 1.7 %shard_map.123 = (bf16[2,64,640]{2,1,0:T(8,128)(2,1)S(1)}, bf16[2,64,640]{2,1,0:T(8,128)(2,1)S(1)}) custom-call(bf16[2,128,512]{2,1,0:T(8,128)(2,1)S(1)} %copy-done.4, bf16[2,64,128]{2,1,0:T(8,128)(2,1)S(1)} %copy-done.6, bf16[2,512,512]{2,1,0:T(8,128)(2,1)S(1)} %copy-done.3, bf16[2,64,512]{2,1,0:T(8,128)(2,1)S(1)} %copy-done.5, s32[2]{0:T(128)S(1)} %copy-done.7), custom_call_target="tpu_custom_call" | custom-call | flops 2000000000 | tf_op jit(solution)/shard_map/pallas_call | solution.py:45
  8.8 0.8 %collective-permute-start = (bf16[32,1920]{1,0:T(8,128)(2,1)S(1)}, bf16[32,1920]{1,0:T(8,128)(2,1)S(1)}, u32[]{:S(2)}, u32[]{:S(2)}) collective-permute-start(bf16[32,1920]{1,0:T(8,128)(2,1)S(1)} %get-tuple-element.40), channel_id=1, source_target_pairs={{0,4},{4,0},{8,12},{12,8},{1,5},{5,1},{9,13},{13,9},{2,6},{6,2},{1... | collective-permute-start | bytes 368648 | tf_op jit(solution)/shard_map/ppermute | solution.py:26
  9.6 1.6 %collective-permute-start.3 = (bf16[32,896]{1,0:T(8,128)(2,1)S(1)}, bf16[32,896]{1,0:T(8,128)(2,1)S(1)}, u32[]{:S(2)}, u32[]{:S(2)}) collective-permute-start(bf16[32,896]{1,0:T(8,128)(2,1)S(1)} %slice.36), channel_id=1, source_target_pairs={{0,2},{1,3},{2,0},{3,1},{4,6},{5,7},{6,4},{7,5},{8,10},{9,11},{10,... | collective-permute-start | bytes 172040 | tf_op jit(solution)/shard_map/ppermute | solution.py:26
  11.2 3.4 %collective-permute-done.1.refs_2_ = bf16[32,1024]{1,0:T(8,128)(2,1)S(1)} collective-permute-done((bf16[32,1024]{1,0:T(8,128)(2,1)S(1)}, bf16[32,1024]{1,0:T(8,128)(2,1)S(1)}, u32[]{:S(2)}, u32[]{:S(2)}) %collective-permute-start.1) | collective-permute-done | bytes 65568 | tf_op jit(solution)/shard_map/ppermute | solution.py:26
  14.7 1.6 %collective-permute-start.4 = (bf16[32,896]{1,0:T(8,128)(2,1)S(1)}, bf16[32,896]{1,0:T(8,128)(2,1)S(1)}, u32[]{:S(2)}, u32[]{:S(2)}) collective-permute-start(bf16[32,896]{1,0:T(8,128)(2,1)S(1)} %slice.35), channel_id=1, source_target_pairs={{0,2},{1,3},{2,0},{3,1},{4,6},{5,7},{6,4},{7,5},{8,10},{9,11},{10,... | collective-permute-start | bytes 172040 | tf_op jit(solution)/shard_map/ppermute | solution.py:26
  16.5 2.4 %collective-permute-done.4 = bf16[32,896]{1,0:T(8,128)(2,1)S(1)} collective-permute-done((bf16[32,896]{1,0:T(8,128)(2,1)S(1)}, bf16[32,896]{1,0:T(8,128)(2,1)S(1)}, u32[]{:S(2)}, u32[]{:S(2)}) %collective-permute-start.4) | collective-permute-done | bytes 57376 | tf_op jit(solution)/shard_map/ppermute | solution.py:26
  19.1 1.6 %collective-permute-start.7 = (bf16[2,64,640]{2,1,0:T(8,128)(2,1)S(1)}, bf16[2,64,640]{2,1,0:T(8,128)(2,1)S(1)}, u32[]{:S(2)}, u32[]{:S(2)}) collective-permute-start(bf16[2,64,640]{2,1,0:T(8,128)(2,1)S(1)} %shard_map.124.refs_0_), channel_id=1, source_target_pairs={{0,2},{1,3},{2,0},{3,1},{4,6},{5,7},{6,4},{7,5},{8,10},{9,11},{10,... | collective-permute-start | bytes 491528 | tf_op jit(solution)/shard_map/ppermute | solution.py:26
  20.8 5.2 %copy-done = bf16[8,3584,256]{2,1,0:T(8,128)(2,1)S(1)} copy-done((bf16[8,3584,256]{2,1,0:T(8,128)(2,1)S(1)}, bf16[8,3584,256]{2,1,0:T(8,128)(2,1)}, u32[]{:S(2)}) %copy-start) | copy-done | bytes 14680088
  26.0 4.3 %shard_map.125.act = bf16[128,2048]{1,0:T(8,128)(2,1)S(1)} custom-call(bf16[32,1024]{1,0:T(8,128)(2,1)S(1)} %get-tuple-element.41.refs_0_, bf16[32,1920]{1,0:T(8,128)(2,1)S(1)} %collective-permute-done.refs_1_, bf16[32,1024]{1,0:T(8,128)(2,1)S(1)} %collective-permute-done.1.refs_2_, bf16[32,1024]{1,0:T(8,128)(2,1)S(1)} %collective-permute-done.2.refs_3_, ...), custom_call_target="tpu_custom_call" | custom-call | tf_op jit(solution)/shard_map/pallas_call | solution.py:45
  30.3 0.7 %shard_map.126 = bf16[128,896]{1,0:T(8,128)(2,1)S(1)} custom-call(bf16[128,2048]{1,0:T(8,128)(2,1)S(1)} %shard_map.125.act, bf16[2048,3584]{1,0:T(8,128)(2,1)S(1)} %bitcast.5), custom_call_target="tpu_custom_call" | custom-call | tf_op jit(solution)/shard_map/pallas_call | solution.py:45
  31.3 1.3 %shard_map.127 = (bf16[128,896]{1,0:T(8,128)(2,1)S(1)}, bf16[128,896]{1,0:T(8,128)(2,1)S(1)}) custom-call(bf16[128,2048]{1,0:T(8,128)(2,1)S(1)} %shard_map.125.act, bf16[2048,3584]{1,0:T(8,128)(2,1)S(1)} %bitcast.6), custom_call_target="tpu_custom_call" | custom-call | tf_op jit(solution)/shard_map/pallas_call | solution.py:45
  32.7 1.6 %collective-permute-start.10 = (bf16[128,896]{1,0:T(8,128)(2,1)S(1)}, bf16[128,896]{1,0:T(8,128)(2,1)S(1)}, u32[]{:S(2)}, u32[]{:S(2)}) collective-permute-start(bf16[128,896]{1,0:T(8,128)(2,1)S(1)} %add_convert_fusion), channel_id=1, source_target_pairs={{0,2},{1,3},{2,0},{3,1},{4,6},{5,7},{6,4},{7,5},{8,10},{9,11},{10,... | collective-permute-start | bytes 688136 | tf_op jit(solution)/shard_map/ppermute | solution.py:26
  34.6 0.5 %collective-permute-start.11 = (bf16[2,64,512]{2,1,0:T(8,128)(2,1)S(1)}, bf16[2,64,512]{2,1,0:T(8,128)(2,1)S(1)}, u32[]{:S(2)}, u32[]{:S(2)}) collective-permute-start(bf16[2,64,512]{2,1,0:T(8,128)(2,1)S(1)} %shard_map.129.mine), channel_id=1, source_target_pairs={{0,1},{1,0},{2,3},{3,2},{4,5},{5,4},{6,7},{7,6},{8,9},{9,8},{10,11... | collective-permute-start | bytes 393224 | tf_op jit(solution)/shard_map/ppermute | solution.py:26
  35.1 0.7 %shard_map.128 = bf16[128,896]{1,0:T(8,128)(2,1)S(1)} custom-call(bf16[128,2048]{1,0:T(8,128)(2,1)S(1)} %shard_map.125.act, bf16[2048,3584]{1,0:T(8,128)(2,1)S(1)} %bitcast.7), custom_call_target="tpu_custom_call" | custom-call | tf_op jit(solution)/shard_map/pallas_call | solution.py:45
  36.1 0.7 %shard_map.130 = bf16[2,128,512]{2,1,0:T(8,128)(2,1)} custom-call(bf16[2,64,512]{2,1,0:T(8,128)(2,1)S(1)} %shard_map.129.mine, bf16[2,64,512]{2,1,0:T(8,128)(2,1)S(1)} %collective-permute-done.11.theirs), custom_call_target="tpu_custom_call" | custom-call | tf_op jit(solution)/shard_map/pallas_call | solution.py:45
  36.8 3.8 %collective-permute-done.10 = bf16[128,896]{1,0:T(8,128)(2,1)S(1)} collective-permute-done((bf16[128,896]{1,0:T(8,128)(2,1)S(1)}, bf16[128,896]{1,0:T(8,128)(2,1)S(1)}, u32[]{:S(2)}, u32[]{:S(2)}) %collective-permute-start.10) | collective-permute-done | bytes 229408 | tf_op jit(solution)/shard_map/ppermute | solution.py:26
  40.7 2.8 %collective-permute-start.12 = (bf16[32,896]{1,0:T(8,128)(2,1)S(1)}, bf16[32,896]{1,0:T(8,128)(2,1)S(1)}, u32[]{:S(2)}, u32[]{:S(2)}) collective-permute-start(bf16[32,896]{1,0:T(8,128)(2,1)S(1)} %get-tuple-element.70), channel_id=1, source_target_pairs={{0,12},{4,8},{8,4},{12,0},{1,13},{5,9},{9,5},{13,1},{2,14},{6,10},... | collective-permute-start | bytes 172040 | tf_op jit(solution)/shard_map/ppermute | solution.py:26
  43.6 1.6 %collective-permute-start.14 = (bf16[32,896]{1,0:T(8,128)(2,1)S(1)}, bf16[32,896]{1,0:T(8,128)(2,1)S(1)}, u32[]{:S(2)}, u32[]{:S(2)}) collective-permute-start(bf16[32,896]{1,0:T(8,128)(2,1)S(1)} %get-tuple-element.68), channel_id=1, source_target_pairs={{0,4},{4,0},{8,12},{12,8},{1,5},{5,1},{9,13},{13,9},{2,6},{6,2},{1... | collective-permute-start | bytes 172040 | tf_op jit(solution)/shard_map/ppermute | solution.py:26
  45.2 1.5 %collective-permute-done.12 = bf16[32,896]{1,0:T(8,128)(2,1)S(1)} collective-permute-done((bf16[32,896]{1,0:T(8,128)(2,1)S(1)}, bf16[32,896]{1,0:T(8,128)(2,1)S(1)}, u32[]{:S(2)}, u32[]{:S(2)}) %collective-permute-start.12) | collective-permute-done | bytes 57376 | tf_op jit(solution)/shard_map/ppermute | solution.py:26
  46.8 1.9 %collective-permute-done.13 = bf16[32,896]{1,0:T(8,128)(2,1)S(1)} collective-permute-done((bf16[32,896]{1,0:T(8,128)(2,1)S(1)}, bf16[32,896]{1,0:T(8,128)(2,1)S(1)}, u32[]{:S(2)}, u32[]{:S(2)}) %collective-permute-start.13) | collective-permute-done | bytes 57376 | tf_op jit(solution)/shard_map/ppermute | solution.py:26
  48.7 0.3 collective-permute-done.14
  49.1 0.6 %add_convert_fusion.1 = bf16[32,896]{1,0:T(8,128)(2,1)} fusion(f32[32,896]{1,0:T(8,128)S(1)} %convert_add_fusion.1, bf16[32,896]{1,0:T(8,128)(2,1)S(1)} %collective-permute-done.14), kind=kLoop, calls=%fused_computation.4 | loop fusion | flops 86016 | bytes 229376 | tf_op jit(solution)/shard_map/convert_element_type | solution.py:333
  (67 shorter events, 1.8 us)
Async XLA Ops:
  0.6 20.1 %slice-start.4 = ((s8[14680064]{0:T(1024)(128)(4,1)}), s8[4194304]{0:T(1024)(128)(4,1)S(1)}, s32[]{:S(2)}) async-start(s8[14680064]{0:T(1024)(128)(4,1)} %bitcast.8), calls=%async_computation.4 | async-start | bytes 8388608
  0.6 6.3 %copy-start.3 = (bf16[2,512,512]{2,1,0:T(8,128)(2,1)S(1)}, bf16[2,512,512]{2,1,0:T(8,128)(2,1)}, u32[]{:S(2)}) copy-start(bf16[2,512,512]{2,1,0:T(8,128)(2,1)} %keys.1) | copy-start | bytes 3145732
  0.7 6.3 %copy-start.4 = (bf16[2,128,512]{2,1,0:T(8,128)(2,1)S(1)}, bf16[2,128,512]{2,1,0:T(8,128)(2,1)}, u32[]{:S(2)}) copy-start(bf16[2,128,512]{2,1,0:T(8,128)(2,1)} %q_lat) | copy-start | bytes 786436
  0.7 20.1 %slice-start.5 = ((s8[14680064]{0:T(1024)(128)(4,1)}), s8[4194304]{0:T(1024)(128)(4,1)S(1)}, s32[]{:S(2)}) async-start(s8[14680064]{0:T(1024)(128)(4,1)} %bitcast.8), calls=%async_computation.5 | async-start | bytes 8388608
  0.7 20.1 %slice-start.6 = ((s8[14680064]{0:T(1024)(128)(4,1)}), s8[4194304]{0:T(1024)(128)(4,1)S(1)}, s32[]{:S(2)}) async-start(s8[14680064]{0:T(1024)(128)(4,1)} %bitcast.8), calls=%async_computation.6 | async-start | bytes 8388608
  0.7 20.1 %slice-start.7 = ((s8[14680064]{0:T(1024)(128)(4,1)}), s8[2097152]{0:T(1024)(128)(4,1)S(1)}, s32[]{:S(2)}) async-start(s8[14680064]{0:T(1024)(128)(4,1)} %bitcast.8), calls=%async_computation.7 | async-start | bytes 4194304
  0.7 20.1 %copy-start.1 = (bf16[32,3584]{1,0:T(8,128)(2,1)S(1)}, bf16[32,3584]{1,0:T(8,128)(2,1)}, u32[]{:S(2)}) copy-start(bf16[32,3584]{1,0:T(8,128)(2,1)} %refs_4_.1) | copy-start | bytes 688132
  0.7 20.1 %copy-start.2 = (bf16[3584,32]{0,1:T(8,128)(2,1)S(1)}, bf16[3584,32]{0,1:T(8,128)(2,1)}, u32[]{:S(2)}) copy-start(bf16[3584,32]{0,1:T(8,128)(2,1)} %param.13) | copy-start | bytes 688132
  1.8 7.8 %collective-permute-start.2 = (bf16[32,1024]{1,0:T(8,128)(2,1)S(1)}, bf16[32,1024]{1,0:T(8,128)(2,1)S(1)}, u32[]{:S(2)}, u32[]{:S(2)}) collective-permute-start(bf16[32,1024]{1,0:T(8,128)(2,1)S(1)} %get-tuple-element.41.refs_0_), channel_id=1, source_target_pairs={{0,12},{4,8},{8,4},{12,0},{1,13},{5,9},{9,5},{13,1},{2,14},{6,10},... | collective-permute-start | bytes 196616 | tf_op jit(solution)/shard_map/ppermute | solution.py:26
  7.0 23.3 %slice-start = ((s8[14680064]{0:T(1024)(128)(4,1)}), s8[4194304]{0:T(1024)(128)(4,1)S(1)}, s32[]{:S(2)}) async-start(s8[14680064]{0:T(1024)(128)(4,1)} %bitcast.3), calls=%async_computation | async-start | bytes 8388608
  8.7 7.6 %collective-permute-start.5 = (bf16[2,64,640]{2,1,0:T(8,128)(2,1)S(1)}, bf16[2,64,640]{2,1,0:T(8,128)(2,1)S(1)}, u32[]{:S(2)}, u32[]{:S(2)}) collective-permute-start(bf16[2,64,640]{2,1,0:T(8,128)(2,1)S(1)} %get-tuple-element.44), channel_id=1, source_target_pairs={{0,1},{1,0},{2,3},{3,2},{4,5},{5,4},{6,7},{7,6},{8,9},{9,8},{10,11... | collective-permute-start | bytes 491528 | tf_op jit(solution)/shard_map/ppermute | solution.py:26
  8.7 5.9 %collective-permute-start.1 = (bf16[32,1024]{1,0:T(8,128)(2,1)S(1)}, bf16[32,1024]{1,0:T(8,128)(2,1)S(1)}, u32[]{:S(2)}, u32[]{:S(2)}) collective-permute-start(bf16[32,1024]{1,0:T(8,128)(2,1)S(1)} %get-tuple-element.41.refs_0_), channel_id=1, source_target_pairs={{0,8},{4,12},{8,0},{12,4},{1,9},{5,13},{9,1},{13,5},{2,10},{6,14},... | collective-permute-start | bytes 196616 | tf_op jit(solution)/shard_map/ppermute | solution.py:26
  8.8 7.7 %collective-permute-start = (bf16[32,1920]{1,0:T(8,128)(2,1)S(1)}, bf16[32,1920]{1,0:T(8,128)(2,1)S(1)}, u32[]{:S(2)}, u32[]{:S(2)}) collective-permute-start(bf16[32,1920]{1,0:T(8,128)(2,1)S(1)} %get-tuple-element.40), channel_id=1, source_target_pairs={{0,4},{4,0},{8,12},{12,8},{1,5},{5,1},{9,13},{13,9},{2,6},{6,2},{1... | collective-permute-start | bytes 368648 | tf_op jit(solution)/shard_map/ppermute | solution.py:26
  9.6 5.0 %collective-permute-start.3 = (bf16[32,896]{1,0:T(8,128)(2,1)S(1)}, bf16[32,896]{1,0:T(8,128)(2,1)S(1)}, u32[]{:S(2)}, u32[]{:S(2)}) collective-permute-start(bf16[32,896]{1,0:T(8,128)(2,1)S(1)} %slice.36), channel_id=1, source_target_pairs={{0,2},{1,3},{2,0},{3,1},{4,6},{5,7},{6,4},{7,5},{8,10},{9,11},{10,... | collective-permute-start | bytes 172040 | tf_op jit(solution)/shard_map/ppermute | solution.py:26
  14.7 4.2 %collective-permute-start.4 = (bf16[32,896]{1,0:T(8,128)(2,1)S(1)}, bf16[32,896]{1,0:T(8,128)(2,1)S(1)}, u32[]{:S(2)}, u32[]{:S(2)}) collective-permute-start(bf16[32,896]{1,0:T(8,128)(2,1)S(1)} %slice.35), channel_id=1, source_target_pairs={{0,2},{1,3},{2,0},{3,1},{4,6},{5,7},{6,4},{7,5},{8,10},{9,11},{10,... | collective-permute-start | bytes 172040 | tf_op jit(solution)/shard_map/ppermute | solution.py:26
  19.0 1.7 %collective-permute-start.6 = (bf16[192,896]{1,0:T(8,128)(2,1)S(1)}, bf16[192,896]{1,0:T(8,128)(2,1)S(1)}, u32[]{:S(2)}, u32[]{:S(2)}) collective-permute-start(bf16[192,896]{1,0:T(8,128)(2,1)S(1)} %constant_dynamic-update-slice_fusion), channel_id=1, source_target_pairs={{0,1},{1,0},{2,3},{3,2},{4,5},{5,4},{6,7},{7,6},{8,9},{9,8},{10,11... | collective-permute-start | bytes 1032200 | tf_op jit(solution)/shard_map/ppermute | solution.py:26
  19.1 12.0 %collective-permute-start.7 = (bf16[2,64,640]{2,1,0:T(8,128)(2,1)S(1)}, bf16[2,64,640]{2,1,0:T(8,128)(2,1)S(1)}, u32[]{:S(2)}, u32[]{:S(2)}) collective-permute-start(bf16[2,64,640]{2,1,0:T(8,128)(2,1)S(1)} %shard_map.124.refs_0_), channel_id=1, source_target_pairs={{0,2},{1,3},{2,0},{3,1},{4,6},{5,7},{6,4},{7,5},{8,10},{9,11},{10,... | collective-permute-start | bytes 491528 | tf_op jit(solution)/shard_map/ppermute | solution.py:26
  31.1 1.6 %collective-permute-start.8 = (bf16[128,896]{1,0:T(8,128)(2,1)S(1)}, bf16[128,896]{1,0:T(8,128)(2,1)S(1)}, u32[]{:S(2)}, u32[]{:S(2)}) collective-permute-start(bf16[128,896]{1,0:T(8,128)(2,1)S(1)} %shard_map.126), channel_id=1, source_target_pairs={{0,1},{1,0},{2,3},{3,2},{4,5},{5,4},{6,7},{7,6},{8,9},{9,8},{10,11... | collective-permute-start | bytes 688136 | tf_op jit(solution)/shard_map/ppermute | solution.py:26
  32.7 7.9 %collective-permute-start.10 = (bf16[128,896]{1,0:T(8,128)(2,1)S(1)}, bf16[128,896]{1,0:T(8,128)(2,1)S(1)}, u32[]{:S(2)}, u32[]{:S(2)}) collective-permute-start(bf16[128,896]{1,0:T(8,128)(2,1)S(1)} %add_convert_fusion), channel_id=1, source_target_pairs={{0,2},{1,3},{2,0},{3,1},{4,6},{5,7},{6,4},{7,5},{8,10},{9,11},{10,... | collective-permute-start | bytes 688136 | tf_op jit(solution)/shard_map/ppermute | solution.py:26
  34.3 6.3 %collective-permute-start.9 = (bf16[128,896]{1,0:T(8,128)(2,1)S(1)}, bf16[128,896]{1,0:T(8,128)(2,1)S(1)}, u32[]{:S(2)}, u32[]{:S(2)}) collective-permute-start(bf16[128,896]{1,0:T(8,128)(2,1)S(1)} %get-tuple-element.58), channel_id=1, source_target_pairs={{0,1},{1,0},{2,3},{3,2},{4,5},{5,4},{6,7},{7,6},{8,9},{9,8},{10,11... | collective-permute-start | bytes 688136 | tf_op jit(solution)/shard_map/ppermute | solution.py:26
  34.6 1.5 %collective-permute-start.11 = (bf16[2,64,512]{2,1,0:T(8,128)(2,1)S(1)}, bf16[2,64,512]{2,1,0:T(8,128)(2,1)S(1)}, u32[]{:S(2)}, u32[]{:S(2)}) collective-permute-start(bf16[2,64,512]{2,1,0:T(8,128)(2,1)S(1)} %shard_map.129.mine), channel_id=1, source_target_pairs={{0,1},{1,0},{2,3},{3,2},{4,5},{5,4},{6,7},{7,6},{8,9},{9,8},{10,11... | collective-permute-start | bytes 393224 | tf_op jit(solution)/shard_map/ppermute | solution.py:26
  40.7 6.0 %collective-permute-start.12 = (bf16[32,896]{1,0:T(8,128)(2,1)S(1)}, bf16[32,896]{1,0:T(8,128)(2,1)S(1)}, u32[]{:S(2)}, u32[]{:S(2)}) collective-permute-start(bf16[32,896]{1,0:T(8,128)(2,1)S(1)} %get-tuple-element.70), channel_id=1, source_target_pairs={{0,12},{4,8},{8,4},{12,0},{1,13},{5,9},{9,5},{13,1},{2,14},{6,10},... | collective-permute-start | bytes 172040 | tf_op jit(solution)/shard_map/ppermute | solution.py:26
  43.5 5.2 %collective-permute-start.13 = (bf16[32,896]{1,0:T(8,128)(2,1)S(1)}, bf16[32,896]{1,0:T(8,128)(2,1)S(1)}, u32[]{:S(2)}, u32[]{:S(2)}) collective-permute-start(bf16[32,896]{1,0:T(8,128)(2,1)S(1)} %get-tuple-element.69), channel_id=1, source_target_pairs={{0,8},{4,12},{8,0},{12,4},{1,9},{5,13},{9,1},{13,5},{2,10},{6,14},... | collective-permute-start | bytes 172040 | tf_op jit(solution)/shard_map/ppermute | solution.py:26
  43.6 5.5 %collective-permute-start.14 = (bf16[32,896]{1,0:T(8,128)(2,1)S(1)}, bf16[32,896]{1,0:T(8,128)(2,1)S(1)}, u32[]{:S(2)}, u32[]{:S(2)}) collective-permute-start(bf16[32,896]{1,0:T(8,128)(2,1)S(1)} %get-tuple-element.68), channel_id=1, source_target_pairs={{0,4},{4,0},{8,12},{12,8},{1,5},{5,1},{9,13},{13,9},{2,6},{6,2},{1... | collective-permute-start | bytes 172040 | tf_op jit(solution)/shard_map/ppermute | solution.py:26
  (7 other events, 36.9 us)

commit v11 on v9

--- a/solution.py
+++ b/solution.py
@@ -288,10 +288,11 @@
     def added(a, b):
         return a.astype(f32) + b.astype(f32)
 
-    act, states = lax.optimization_barrier((act, states))
     if aligned:
         steps = range(1, ways)
-        far = [send(p, "tp", other_core) for p in down_call(act, down, [(s, 1) for s in steps], ways)]
+        far = down_call(act, down, [(s, 1) for s in steps], ways)
+        far, act, states = lax.optimization_barrier((far, act, states))
+        far = [send(p, "tp", other_core) for p in far]
         *own, there = down_call(act, down, [(s, 0) for s in steps] + [(0, 1)], ways)
         there = send(there, "tp", other_core)
         sums = [added(a, b).astype(bf16) for a, b in zip(own, far)]
@@ -308,15 +309,17 @@
         far = [send(block(s, 1 - core), "tp", other_core) for s in range(ways)]
         sums = [added(a, b).astype(bf16) for a, b in zip(own[1:], far[1:])]
         here, there = own[0], far[0]
-    total = added(here, there)
-    for s, p in enumerate(sums, 1):
-        total = total + send(p, "tp", along_x(s, ways)).astype(f32)
+    sums = [send(p, "tp", along_x(s, ways)) for s, p in enumerate(sums, 1)]
     joined = join(states, True)
     attended = place_heads(joined, send(joined, "tp", other_core))
+    sums, attended = lax.optimization_barrier((sums, attended))
+    total = added(here, there)
+    for p in sums:
+        total = total + p.astype(f32)
     blocks = [total[i : i + rows] for i in range(0, total.shape[0], rows)]
     moe = blocks[0]
     for s in reversed(range(1, n_dev)):
-        moe, attended = lax.optimization_barrier((moe, attended))
+        moe = lax.optimization_barrier(moe)
         moe = moe + over_dev(blocks[s].astype(bf16), s, n_dev).astype(f32)
     return (moe.astype(bf16), attended)
 

time: 46.4 us -> 44.2 us (0.953)
  waiting for transfers between devices: 15.7 us -> 13.6 us
    ppermute x16, waiting for transfers between devices: 15.7 us -> 13.6 us  [send(): return lax.ppermute(value, axis, [(i, target(i)) for i in range(size)])]
  transfers between devices with their start and end apart: 16 -> 16, of which waited for: 8 -> 6; matrix products, arithmetic and copies ran while one was open for 1% -> 0% of each run, Pallas kernels for 20% -> 23%
where the time goes in v11:
time: 44.2 us; the launch traced here: 44.1 us
  starting transfers between devices  17.5 us (40%)
  waiting for transfers between devices  13.6 us (31%)
  Pallas kernels  11 us (25%)
  between operations  1.01 us (2%)
  other arithmetic  0.86 us (2%)
    ppermute x16, starting transfers between devices, send(): return lax.ppermute(value, axis, [(i, target(i)) for i in range(size)])  17.5 us
    ppermute x16, waiting for transfers between devices, send(): return lax.ppermute(value, axis, [(i, target(i)) for i in range(size)])  13.6 us
    pallas_call x9, Pallas kernels, local_call(): pl.pallas_call(kernel, out_shape=outs, in_specs=specs, out_specs=jax.tree...  11 us
  transfers between devices with their start and end apart: 16, of which 6 were waited for; matrix products, arithmetic and copies ran while one was open for 0% of the time, Pallas kernels for 23%

profile of v11, /device:TPU:0, one launch (start us, length us, event | category | flops | bytes accessed | tf_op | source)
XLA Modules:
  0.0 44.1 jit_solution(18236258444554340945)
XLA Ops:
  0.7 1.0 %shard_map.122.refs_0_ = bf16[32,1024]{1,0:T(8,128)(2,1)S(1)} custom-call(bf16[32,3584]{1,0:T(8,128)(2,1)} %refs_4_.1, s32[8,32]{1,0:T(8,128)} %bitcast.9), custom_call_target="tpu_custom_call" | custom-call | flops 99999997952 | tf_op jit(solution)/shard_map/pallas_call | solution.py:45
  1.8 5.1 %collective-permute-start.2 = (bf16[32,1024]{1,0:T(8,128)(2,1)S(1)}, bf16[32,1024]{1,0:T(8,128)(2,1)S(1)}, u32[]{:S(2)}, u32[]{:S(2)}) collective-permute-start(bf16[32,1024]{1,0:T(8,128)(2,1)S(1)} %shard_map.122.refs_0_), channel_id=1, source_target_pairs={{0,12},{4,8},{8,4},{12,0},{1,13},{5,9},{9,5},{13,1},{2,14},{6,10},... | collective-permute-start | bytes 196616 | tf_op jit(solution)/shard_map/ppermute | solution.py:26
  6.9 1.7 %shard_map.123 = (bf16[2,64,640]{2,1,0:T(8,128)(2,1)S(1)}, bf16[2,64,640]{2,1,0:T(8,128)(2,1)S(1)}) custom-call(bf16[2,128,512]{2,1,0:T(8,128)(2,1)S(1)} %copy-done.5, bf16[2,64,128]{2,1,0:T(8,128)(2,1)S(1)} %copy-done.7, bf16[2,512,512]{2,1,0:T(8,128)(2,1)S(1)} %copy-done.4, bf16[2,64,512]{2,1,0:T(8,128)(2,1)S(1)} %copy-done.6, s32[2]{0:T(128)S(1)} %copy-done.8), custom_call_target="tpu_custom_call" | custom-call | flops 2000000000 | tf_op jit(solution)/shard_map/pallas_call | solution.py:45
  8.7 0.7 %collective-permute-start = (bf16[32,1024]{1,0:T(8,128)(2,1)S(1)}, bf16[32,1024]{1,0:T(8,128)(2,1)S(1)}, u32[]{:S(2)}, u32[]{:S(2)}) collective-permute-start(bf16[32,1024]{1,0:T(8,128)(2,1)S(1)} %shard_map.122.refs_0_), channel_id=1, source_target_pairs={{0,4},{4,0},{8,12},{12,8},{1,5},{5,1},{9,13},{13,9},{2,6},{6,2},{1... | collective-permute-start | bytes 196616 | tf_op jit(solution)/shard_map/ppermute | solution.py:26
  9.4 1.7 %collective-permute-start.5 = (bf16[32,896]{1,0:T(8,128)(2,1)S(1)}, bf16[32,896]{1,0:T(8,128)(2,1)S(1)}, u32[]{:S(2)}, u32[]{:S(2)}) collective-permute-start(bf16[32,896]{1,0:T(8,128)(2,1)S(1)} %slice.41), channel_id=1, source_target_pairs={{0,2},{1,3},{2,0},{3,1},{4,6},{5,7},{6,4},{7,5},{8,10},{9,11},{10,... | collective-permute-start | bytes 172040 | tf_op jit(solution)/shard_map/ppermute | solution.py:26
  11.0 2.9 %collective-permute-done.1.refs_2_ = bf16[32,1024]{1,0:T(8,128)(2,1)S(1)} collective-permute-done((bf16[32,1024]{1,0:T(8,128)(2,1)S(1)}, bf16[32,1024]{1,0:T(8,128)(2,1)S(1)}, u32[]{:S(2)}, u32[]{:S(2)}) %collective-permute-start.1) | collective-permute-done | bytes 65568 | tf_op jit(solution)/shard_map/ppermute | solution.py:26
  14.0 0.3 shard_map.124.refs_0_
  14.3 1.6 %collective-permute-start.4 = (bf16[64,896]{1,0:T(8,128)(2,1)S(1)}, bf16[64,896]{1,0:T(8,128)(2,1)S(1)}, u32[]{:S(2)}, u32[]{:S(2)}) collective-permute-start(bf16[64,896]{1,0:T(8,128)(2,1)S(1)} %pad_maximum_fusion.2), channel_id=1, source_target_pairs={{0,2},{1,3},{2,0},{3,1},{4,6},{5,7},{6,4},{7,5},{8,10},{9,11},{10,... | collective-permute-start | bytes 344072 | tf_op jit(solution)/shard_map/ppermute | solution.py:26
  15.9 3.2 %collective-permute-done.4 = bf16[64,896]{1,0:T(8,128)(2,1)S(1)} collective-permute-done((bf16[64,896]{1,0:T(8,128)(2,1)S(1)}, bf16[64,896]{1,0:T(8,128)(2,1)S(1)}, u32[]{:S(2)}, u32[]{:S(2)}) %collective-permute-start.4) | collective-permute-done | bytes 114720 | tf_op jit(solution)/shard_map/ppermute | solution.py:26
  19.2 1.6 %collective-permute-start.8 = (bf16[2,64,640]{2,1,0:T(8,128)(2,1)S(1)}, bf16[2,64,640]{2,1,0:T(8,128)(2,1)S(1)}, u32[]{:S(2)}, u32[]{:S(2)}) collective-permute-start(bf16[2,64,640]{2,1,0:T(8,128)(2,1)S(1)} %shard_map.124.refs_0_), channel_id=1, source_target_pairs={{0,2},{1,3},{2,0},{3,1},{4,6},{5,7},{6,4},{7,5},{8,10},{9,11},{10,... | collective-permute-start | bytes 491528 | tf_op jit(solution)/shard_map/ppermute | solution.py:26
  20.9 4.3 %shard_map.125.act = bf16[128,2048]{1,0:T(8,128)(2,1)S(1)} custom-call(bf16[32,1024]{1,0:T(8,128)(2,1)S(1)} %shard_map.122.refs_0_, bf16[32,1024]{1,0:T(8,128)(2,1)S(1)} %collective-permute-done.refs_1_, bf16[32,1024]{1,0:T(8,128)(2,1)S(1)} %collective-permute-done.1.refs_2_, bf16[32,1024]{1,0:T(8,128)(2,1)S(1)} %collective-permute-done.2.refs_3_, ...), custom_call_target="tpu_custom_call" | custom-call | tf_op jit(solution)/shard_map/pallas_call | solution.py:45
  25.2 0.7 %shard_map.126 = bf16[128,896]{1,0:T(8,128)(2,1)S(1)} custom-call(bf16[128,2048]{1,0:T(8,128)(2,1)S(1)} %shard_map.125.act, bf16[2048,3584]{1,0:T(8,128)(2,1)S(1)} %bitcast.5), custom_call_target="tpu_custom_call" | custom-call | tf_op jit(solution)/shard_map/pallas_call | solution.py:45
  26.2 1.3 %shard_map.127 = (bf16[128,896]{1,0:T(8,128)(2,1)S(1)}, bf16[128,896]{1,0:T(8,128)(2,1)S(1)}) custom-call(bf16[128,2048]{1,0:T(8,128)(2,1)S(1)} %shard_map.125.act, bf16[2048,3584]{1,0:T(8,128)(2,1)S(1)} %bitcast.6), custom_call_target="tpu_custom_call" | custom-call | tf_op jit(solution)/shard_map/pallas_call | solution.py:45
  27.6 1.4 %collective-permute-start.11 = (bf16[128,896]{1,0:T(8,128)(2,1)S(1)}, bf16[128,896]{1,0:T(8,128)(2,1)S(1)}, u32[]{:S(2)}, u32[]{:S(2)}) collective-permute-start(bf16[128,896]{1,0:T(8,128)(2,1)S(1)} %add_convert_fusion), channel_id=1, source_target_pairs={{0,2},{1,3},{2,0},{3,1},{4,6},{5,7},{6,4},{7,5},{8,10},{9,11},{10,... | collective-permute-start | bytes 688136 | tf_op jit(solution)/shard_map/ppermute | solution.py:26
  29.3 0.5 %collective-permute-start.12 = (bf16[2,64,512]{2,1,0:T(8,128)(2,1)S(1)}, bf16[2,64,512]{2,1,0:T(8,128)(2,1)S(1)}, u32[]{:S(2)}, u32[]{:S(2)}) collective-permute-start(bf16[2,64,512]{2,1,0:T(8,128)(2,1)S(1)} %shard_map.129.mine), channel_id=1, source_target_pairs={{0,1},{1,0},{2,3},{3,2},{4,5},{5,4},{6,7},{7,6},{8,9},{9,8},{10,11... | collective-permute-start | bytes 393224 | tf_op jit(solution)/shard_map/ppermute | solution.py:26
  29.8 0.7 %shard_map.128 = bf16[128,896]{1,0:T(8,128)(2,1)S(1)} custom-call(bf16[128,2048]{1,0:T(8,128)(2,1)S(1)} %shard_map.125.act, bf16[2048,3584]{1,0:T(8,128)(2,1)S(1)} %bitcast.7), custom_call_target="tpu_custom_call" | custom-call | tf_op jit(solution)/shard_map/pallas_call | solution.py:45
  30.5 0.3 collective-permute-done.12.theirs
  30.8 0.7 %shard_map.130 = bf16[2,128,512]{2,1,0:T(8,128)(2,1)} custom-call(bf16[2,64,512]{2,1,0:T(8,128)(2,1)S(1)} %shard_map.129.mine, bf16[2,64,512]{2,1,0:T(8,128)(2,1)S(1)} %collective-permute-done.12.theirs), custom_call_target="tpu_custom_call" | custom-call | tf_op jit(solution)/shard_map/pallas_call | solution.py:45
  31.5 3.9 %collective-permute-done.11 = bf16[128,896]{1,0:T(8,128)(2,1)S(1)} collective-permute-done((bf16[128,896]{1,0:T(8,128)(2,1)S(1)}, bf16[128,896]{1,0:T(8,128)(2,1)S(1)}, u32[]{:S(2)}, u32[]{:S(2)}) %collective-permute-start.11) | collective-permute-done | bytes 229408 | tf_op jit(solution)/shard_map/ppermute | solution.py:26
  35.6 2.0 %collective-permute-start.13 = (bf16[32,896]{1,0:T(8,128)(2,1)S(1)}, bf16[32,896]{1,0:T(8,128)(2,1)S(1)}, u32[]{:S(2)}, u32[]{:S(2)}) collective-permute-start(bf16[32,896]{1,0:T(8,128)(2,1)S(1)} %get-tuple-element.54), channel_id=1, source_target_pairs={{0,12},{4,8},{8,4},{12,0},{1,13},{5,9},{9,5},{13,1},{2,14},{6,10},... | collective-permute-start | bytes 172040 | tf_op jit(solution)/shard_map/ppermute | solution.py:26
  37.7 2.4 %collective-permute-start.15 = (bf16[32,896]{1,0:T(8,128)(2,1)S(1)}, bf16[32,896]{1,0:T(8,128)(2,1)S(1)}, u32[]{:S(2)}, u32[]{:S(2)}) collective-permute-start(bf16[32,896]{1,0:T(8,128)(2,1)S(1)} %get-tuple-element.52), channel_id=1, source_target_pairs={{0,4},{4,0},{8,12},{12,8},{1,5},{5,1},{9,13},{13,9},{2,6},{6,2},{1... | collective-permute-start | bytes 172040 | tf_op jit(solution)/shard_map/ppermute | solution.py:26
  40.1 1.7 %collective-permute-done.13 = bf16[32,896]{1,0:T(8,128)(2,1)S(1)} collective-permute-done((bf16[32,896]{1,0:T(8,128)(2,1)S(1)}, bf16[32,896]{1,0:T(8,128)(2,1)S(1)}, u32[]{:S(2)}, u32[]{:S(2)}) %collective-permute-start.13) | collective-permute-done | bytes 57376 | tf_op jit(solution)/shard_map/ppermute | solution.py:26
  41.8 1.6 %collective-permute-done.14 = bf16[32,896]{1,0:T(8,128)(2,1)S(1)} collective-permute-done((bf16[32,896]{1,0:T(8,128)(2,1)S(1)}, bf16[32,896]{1,0:T(8,128)(2,1)S(1)}, u32[]{:S(2)}, u32[]{:S(2)}) %collective-permute-start.14) | collective-permute-done | bytes 57376 | tf_op jit(solution)/shard_map/ppermute | solution.py:26
  43.4 0.6 %add_convert_fusion.1 = bf16[32,896]{1,0:T(8,128)(2,1)} fusion(f32[32,896]{1,0:T(8,128)S(1)} %convert_add_fusion.1, bf16[32,896]{1,0:T(8,128)(2,1)S(1)} %collective-permute-done.15), kind=kLoop, calls=%fused_computation.5 | loop fusion | flops 86016 | bytes 229376 | tf_op jit(solution)/shard_map/convert_element_type | solution.py:324
  (58 shorter events, 1.2 us)
Async XLA Ops:
  0.6 6.2 %copy-start.4 = (bf16[2,512,512]{2,1,0:T(8,128)(2,1)S(1)}, bf16[2,512,512]{2,1,0:T(8,128)(2,1)}, u32[]{:S(2)}) copy-start(bf16[2,512,512]{2,1,0:T(8,128)(2,1)} %keys.1) | copy-start | bytes 3145732
  0.6 6.2 %copy-start.5 = (bf16[2,128,512]{2,1,0:T(8,128)(2,1)S(1)}, bf16[2,128,512]{2,1,0:T(8,128)(2,1)}, u32[]{:S(2)}) copy-start(bf16[2,128,512]{2,1,0:T(8,128)(2,1)} %q_lat) | copy-start | bytes 786436
  0.7 6.2 %copy-start.6 = (bf16[2,64,512]{2,1,0:T(8,128)(2,1)S(1)}, bf16[2,64,512]{2,1,0:T(8,128)(2,1)}, u32[]{:S(2)}) copy-start(bf16[2,64,512]{2,1,0:T(8,128)(2,1)} %rope.1) | copy-start | bytes 393220
  0.7 20.1 %copy-start = (bf16[8,3584,256]{2,1,0:T(8,128)(2,1)S(1)}, bf16[8,3584,256]{2,1,0:T(8,128)(2,1)}, u32[]{:S(2)}) copy-start(bf16[8,3584,256]{2,1,0:T(8,128)(2,1)} %refs_10_.1) | copy-start | bytes 44040196
  0.7 20.1 %copy-start.1 = (bf16[8,3584,256]{2,1,0:T(8,128)(2,1)S(1)}, bf16[8,3584,256]{2,1,0:T(8,128)(2,1)}, u32[]{:S(2)}) copy-start(bf16[8,3584,256]{2,1,0:T(8,128)(2,1)} %refs_11_.1) | copy-start | bytes 44040196
  0.7 20.1 %copy-start.2 = (bf16[32,3584]{1,0:T(8,128)(2,1)S(1)}, bf16[32,3584]{1,0:T(8,128)(2,1)}, u32[]{:S(2)}) copy-start(bf16[32,3584]{1,0:T(8,128)(2,1)} %refs_4_.1) | copy-start | bytes 688132
  0.7 20.1 %copy-start.3 = (bf16[3584,32]{0,1:T(8,128)(2,1)S(1)}, bf16[3584,32]{0,1:T(8,128)(2,1)}, u32[]{:S(2)}) copy-start(bf16[3584,32]{0,1:T(8,128)(2,1)} %param.13) | copy-start | bytes 688132
  1.8 7.6 %collective-permute-start.2 = (bf16[32,1024]{1,0:T(8,128)(2,1)S(1)}, bf16[32,1024]{1,0:T(8,128)(2,1)S(1)}, u32[]{:S(2)}, u32[]{:S(2)}) collective-permute-start(bf16[32,1024]{1,0:T(8,128)(2,1)S(1)} %shard_map.122.refs_0_), channel_id=1, source_target_pairs={{0,12},{4,8},{8,4},{12,0},{1,13},{5,9},{9,5},{13,1},{2,14},{6,10},... | collective-permute-start | bytes 196616 | tf_op jit(solution)/shard_map/ppermute | solution.py:26
  6.9 18.2 %slice-start = ((s8[14680064]{0:T(1024)(128)(4,1)}), s8[4194304]{0:T(1024)(128)(4,1)S(1)}, s32[]{:S(2)}) async-start(s8[14680064]{0:T(1024)(128)(4,1)} %bitcast.3), calls=%async_computation | async-start | bytes 8388608
  8.6 5.3 %collective-permute-start.1 = (bf16[32,1024]{1,0:T(8,128)(2,1)S(1)}, bf16[32,1024]{1,0:T(8,128)(2,1)S(1)}, u32[]{:S(2)}, u32[]{:S(2)}) collective-permute-start(bf16[32,1024]{1,0:T(8,128)(2,1)S(1)} %shard_map.122.refs_0_), channel_id=1, source_target_pairs={{0,8},{4,12},{8,0},{12,4},{1,9},{5,13},{9,1},{13,5},{2,10},{6,14},... | collective-permute-start | bytes 196616 | tf_op jit(solution)/shard_map/ppermute | solution.py:26
  8.7 5.2 %collective-permute-start = (bf16[32,1024]{1,0:T(8,128)(2,1)S(1)}, bf16[32,1024]{1,0:T(8,128)(2,1)S(1)}, u32[]{:S(2)}, u32[]{:S(2)}) collective-permute-start(bf16[32,1024]{1,0:T(8,128)(2,1)S(1)} %shard_map.122.refs_0_), channel_id=1, source_target_pairs={{0,4},{4,0},{8,12},{12,8},{1,5},{5,1},{9,13},{13,9},{2,6},{6,2},{1... | collective-permute-start | bytes 196616 | tf_op jit(solution)/shard_map/ppermute | solution.py:26
  9.3 4.6 %collective-permute-start.3 = (bf16[2,64,640]{2,1,0:T(8,128)(2,1)S(1)}, bf16[2,64,640]{2,1,0:T(8,128)(2,1)S(1)}, u32[]{:S(2)}, u32[]{:S(2)}) collective-permute-start(bf16[2,64,640]{2,1,0:T(8,128)(2,1)S(1)} %get-tuple-element.32), channel_id=1, source_target_pairs={{0,1},{1,0},{2,3},{3,2},{4,5},{5,4},{6,7},{7,6},{8,9},{9,8},{10,11... | collective-permute-start | bytes 491528 | tf_op jit(solution)/shard_map/ppermute | solution.py:26
  9.4 9.8 %collective-permute-start.5 = (bf16[32,896]{1,0:T(8,128)(2,1)S(1)}, bf16[32,896]{1,0:T(8,128)(2,1)S(1)}, u32[]{:S(2)}, u32[]{:S(2)}) collective-permute-start(bf16[32,896]{1,0:T(8,128)(2,1)S(1)} %slice.41), channel_id=1, source_target_pairs={{0,2},{1,3},{2,0},{3,1},{4,6},{5,7},{6,4},{7,5},{8,10},{9,11},{10,... | collective-permute-start | bytes 172040 | tf_op jit(solution)/shard_map/ppermute | solution.py:26
  14.3 4.9 %collective-permute-start.4 = (bf16[64,896]{1,0:T(8,128)(2,1)S(1)}, bf16[64,896]{1,0:T(8,128)(2,1)S(1)}, u32[]{:S(2)}, u32[]{:S(2)}) collective-permute-start(bf16[64,896]{1,0:T(8,128)(2,1)S(1)} %pad_maximum_fusion.2), channel_id=1, source_target_pairs={{0,2},{1,3},{2,0},{3,1},{4,6},{5,7},{6,4},{7,5},{8,10},{9,11},{10,... | collective-permute-start | bytes 344072 | tf_op jit(solution)/shard_map/ppermute | solution.py:26
  15.8 5.0 %collective-permute-start.6 = (bf16[96,896]{1,0:T(8,128)(2,1)S(1)}, bf16[96,896]{1,0:T(8,128)(2,1)S(1)}, u32[]{:S(2)}, u32[]{:S(2)}) collective-permute-start(bf16[96,896]{1,0:T(8,128)(2,1)S(1)} %pad_maximum_fusion.refs_5_), channel_id=1, source_target_pairs={{0,1},{1,0},{2,3},{3,2},{4,5},{5,4},{6,7},{7,6},{8,9},{9,8},{10,11... | collective-permute-start | bytes 516104 | tf_op jit(solution)/shard_map/ppermute | solution.py:26
  19.2 1.6 %collective-permute-start.7 = (bf16[96,896]{1,0:T(8,128)(2,1)S(1)}, bf16[96,896]{1,0:T(8,128)(2,1)S(1)}, u32[]{:S(2)}, u32[]{:S(2)}) collective-permute-start(bf16[96,896]{1,0:T(8,128)(2,1)S(1)} %pad_maximum_fusion.1.refs_6_), channel_id=1, source_target_pairs={{0,1},{1,0},{2,3},{3,2},{4,5},{5,4},{6,7},{7,6},{8,9},{9,8},{10,11... | collective-permute-start | bytes 516104 | tf_op jit(solution)/shard_map/ppermute | solution.py:26
  19.2 6.7 %collective-permute-start.8 = (bf16[2,64,640]{2,1,0:T(8,128)(2,1)S(1)}, bf16[2,64,640]{2,1,0:T(8,128)(2,1)S(1)}, u32[]{:S(2)}, u32[]{:S(2)}) collective-permute-start(bf16[2,64,640]{2,1,0:T(8,128)(2,1)S(1)} %shard_map.124.refs_0_), channel_id=1, source_target_pairs={{0,2},{1,3},{2,0},{3,1},{4,6},{5,7},{6,4},{7,5},{8,10},{9,11},{10,... | collective-permute-start | bytes 491528 | tf_op jit(solution)/shard_map/ppermute | solution.py:26
  25.9 1.6 %collective-permute-start.9 = (bf16[128,896]{1,0:T(8,128)(2,1)S(1)}, bf16[128,896]{1,0:T(8,128)(2,1)S(1)}, u32[]{:S(2)}, u32[]{:S(2)}) collective-permute-start(bf16[128,896]{1,0:T(8,128)(2,1)S(1)} %shard_map.126), channel_id=1, source_target_pairs={{0,1},{1,0},{2,3},{3,2},{4,5},{5,4},{6,7},{7,6},{8,9},{9,8},{10,11... | collective-permute-start | bytes 688136 | tf_op jit(solution)/shard_map/ppermute | solution.py:26
  27.6 7.8 %collective-permute-start.11 = (bf16[128,896]{1,0:T(8,128)(2,1)S(1)}, bf16[128,896]{1,0:T(8,128)(2,1)S(1)}, u32[]{:S(2)}, u32[]{:S(2)}) collective-permute-start(bf16[128,896]{1,0:T(8,128)(2,1)S(1)} %add_convert_fusion), channel_id=1, source_target_pairs={{0,2},{1,3},{2,0},{3,1},{4,6},{5,7},{6,4},{7,5},{8,10},{9,11},{10,... | collective-permute-start | bytes 688136 | tf_op jit(solution)/shard_map/ppermute | solution.py:26
  29.0 6.5 %collective-permute-start.10 = (bf16[128,896]{1,0:T(8,128)(2,1)S(1)}, bf16[128,896]{1,0:T(8,128)(2,1)S(1)}, u32[]{:S(2)}, u32[]{:S(2)}) collective-permute-start(bf16[128,896]{1,0:T(8,128)(2,1)S(1)} %get-tuple-element.44), channel_id=1, source_target_pairs={{0,1},{1,0},{2,3},{3,2},{4,5},{5,4},{6,7},{7,6},{8,9},{9,8},{10,11... | collective-permute-start | bytes 688136 | tf_op jit(solution)/shard_map/ppermute | solution.py:26
  29.3 1.5 %collective-permute-start.12 = (bf16[2,64,512]{2,1,0:T(8,128)(2,1)S(1)}, bf16[2,64,512]{2,1,0:T(8,128)(2,1)S(1)}, u32[]{:S(2)}, u32[]{:S(2)}) collective-permute-start(bf16[2,64,512]{2,1,0:T(8,128)(2,1)S(1)} %shard_map.129.mine), channel_id=1, source_target_pairs={{0,1},{1,0},{2,3},{3,2},{4,5},{5,4},{6,7},{7,6},{8,9},{9,8},{10,11... | collective-permute-start | bytes 393224 | tf_op jit(solution)/shard_map/ppermute | solution.py:26
  35.6 6.2 %collective-permute-start.13 = (bf16[32,896]{1,0:T(8,128)(2,1)S(1)}, bf16[32,896]{1,0:T(8,128)(2,1)S(1)}, u32[]{:S(2)}, u32[]{:S(2)}) collective-permute-start(bf16[32,896]{1,0:T(8,128)(2,1)S(1)} %get-tuple-element.54), channel_id=1, source_target_pairs={{0,12},{4,8},{8,4},{12,0},{1,13},{5,9},{9,5},{13,1},{2,14},{6,10},... | collective-permute-start | bytes 172040 | tf_op jit(solution)/shard_map/ppermute | solution.py:26
  37.6 5.8 %collective-permute-start.14 = (bf16[32,896]{1,0:T(8,128)(2,1)S(1)}, bf16[32,896]{1,0:T(8,128)(2,1)S(1)}, u32[]{:S(2)}, u32[]{:S(2)}) collective-permute-start(bf16[32,896]{1,0:T(8,128)(2,1)S(1)} %get-tuple-element.53), channel_id=1, source_target_pairs={{0,8},{4,12},{8,0},{12,4},{1,9},{5,13},{9,1},{13,5},{2,10},{6,14},... | collective-permute-start | bytes 172040 | tf_op jit(solution)/shard_map/ppermute | solution.py:26
  37.7 5.7 %collective-permute-start.15 = (bf16[32,896]{1,0:T(8,128)(2,1)S(1)}, bf16[32,896]{1,0:T(8,128)(2,1)S(1)}, u32[]{:S(2)}, u32[]{:S(2)}) collective-permute-start(bf16[32,896]{1,0:T(8,128)(2,1)S(1)} %get-tuple-element.52), channel_id=1, source_target_pairs={{0,4},{4,0},{8,12},{12,8},{1,5},{5,1},{9,13},{13,9},{2,6},{6,2},{1... | collective-permute-start | bytes 172040 | tf_op jit(solution)/shard_map/ppermute | solution.py:26
  (5 other events, 25.3 us)

commit v12 on v11

--- a/solution.py
+++ b/solution.py
@@ -293,11 +293,11 @@
         far = down_call(act, down, [(s, 1) for s in steps], ways)
         far, act, states = lax.optimization_barrier((far, act, states))
         far = [send(p, "tp", other_core) for p in far]
-        *own, there = down_call(act, down, [(s, 0) for s in steps] + [(0, 1)], ways)
-        there = send(there, "tp", other_core)
+        own = down_call(act, down, [(s, 0) for s in steps], ways)
         sums = [added(a, b).astype(bf16) for a, b in zip(own, far)]
         act, sums, states = lax.optimization_barrier((act, sums, states))
-        (here,) = down_call(act, down, [(0, 0)], ways)
+        there, here = down_call(act, down, [(0, 1), (0, 0)], ways)
+        there = send(there, "tp", other_core)
     else:
         spot, core = spot_and_core()
         size = width // n_tp

time: 44.2 us -> 44.8 us (1.014)
  waiting for transfers between devices: 13.6 us -> 14.1 us
    ppermute x16, waiting for transfers between devices: 13.6 us -> 14.1 us  [send(): return lax.ppermute(value, axis, [(i, target(i)) for i in range(size)])]
  transfers between devices with their start and end apart: 16 -> 16, of which waited for: 6 -> 8; matrix products, arithmetic and copies ran while one was open for 0% -> 0% of each run, Pallas kernels for 23% -> 22%
where the time goes in v12:
time: 44.8 us; the launch traced here: 44.6 us
  starting transfers between devices  17.6 us (39%)
  waiting for transfers between devices  14.1 us (31%)
  Pallas kernels  11 us (25%)
  between operations  0.98 us (2%)
  other arithmetic  0.87 us (2%)
    ppermute x16, starting transfers between devices, send(): return lax.ppermute(value, axis, [(i, target(i)) for i in range(size)])  17.6 us
    ppermute x16, waiting for transfers between devices, send(): return lax.ppermute(value, axis, [(i, target(i)) for i in range(size)])  14.1 us
    pallas_call x9, Pallas kernels, local_call(): pl.pallas_call(kernel, out_shape=outs, in_specs=specs, out_specs=jax.tree...  11 us
  transfers between devices with their start and end apart: 16, of which 8 were waited for; matrix products, arithmetic and copies ran while one was open for 0% of the time, Pallas kernels for 22%

profile of v12, /device:TPU:0, one launch (start us, length us, event | category | flops | bytes accessed | tf_op | source)
XLA Modules:
  0.0 44.6 jit_solution(3760013186077420652)
XLA Ops:
  0.7 1.0 %shard_map.122.refs_0_ = bf16[32,1024]{1,0:T(8,128)(2,1)S(1)} custom-call(bf16[32,3584]{1,0:T(8,128)(2,1)} %refs_4_.1, s32[8,32]{1,0:T(8,128)} %bitcast.9), custom_call_target="tpu_custom_call" | custom-call | flops 99999997952 | tf_op jit(solution)/shard_map/pallas_call | solution.py:45
  1.8 5.1 %collective-permute-start.2 = (bf16[32,1024]{1,0:T(8,128)(2,1)S(1)}, bf16[32,1024]{1,0:T(8,128)(2,1)S(1)}, u32[]{:S(2)}, u32[]{:S(2)}) collective-permute-start(bf16[32,1024]{1,0:T(8,128)(2,1)S(1)} %shard_map.122.refs_0_), channel_id=1, source_target_pairs={{0,12},{4,8},{8,4},{12,0},{1,13},{5,9},{9,5},{13,1},{2,14},{6,10},... | collective-permute-start | bytes 196616 | tf_op jit(solution)/shard_map/ppermute | solution.py:26
  6.9 1.7 %shard_map.123 = (bf16[2,64,640]{2,1,0:T(8,128)(2,1)S(1)}, bf16[2,64,640]{2,1,0:T(8,128)(2,1)S(1)}) custom-call(bf16[2,128,512]{2,1,0:T(8,128)(2,1)S(1)} %copy-done.5, bf16[2,64,128]{2,1,0:T(8,128)(2,1)S(1)} %copy-done.7, bf16[2,512,512]{2,1,0:T(8,128)(2,1)S(1)} %copy-done.4, bf16[2,64,512]{2,1,0:T(8,128)(2,1)S(1)} %copy-done.6, s32[2]{0:T(128)S(1)} %copy-done.8), custom_call_target="tpu_custom_call" | custom-call | flops 2000000000 | tf_op jit(solution)/shard_map/pallas_call | solution.py:45
  8.7 0.7 %collective-permute-start.1 = (bf16[32,1024]{1,0:T(8,128)(2,1)S(1)}, bf16[32,1024]{1,0:T(8,128)(2,1)S(1)}, u32[]{:S(2)}, u32[]{:S(2)}) collective-permute-start(bf16[32,1024]{1,0:T(8,128)(2,1)S(1)} %shard_map.122.refs_0_), channel_id=1, source_target_pairs={{0,8},{4,12},{8,0},{12,4},{1,9},{5,13},{9,1},{13,5},{2,10},{6,14},... | collective-permute-start | bytes 196616 | tf_op jit(solution)/shard_map/ppermute | solution.py:26
  9.4 1.7 %collective-permute-start.5 = (bf16[32,896]{1,0:T(8,128)(2,1)S(1)}, bf16[32,896]{1,0:T(8,128)(2,1)S(1)}, u32[]{:S(2)}, u32[]{:S(2)}) collective-permute-start(bf16[32,896]{1,0:T(8,128)(2,1)S(1)} %slice.41), channel_id=1, source_target_pairs={{0,2},{1,3},{2,0},{3,1},{4,6},{5,7},{6,4},{7,5},{8,10},{9,11},{10,... | collective-permute-start | bytes 172040 | tf_op jit(solution)/shard_map/ppermute | solution.py:26
  11.0 2.2 %collective-permute-done.refs_1_ = bf16[32,1024]{1,0:T(8,128)(2,1)S(1)} collective-permute-done((bf16[32,1024]{1,0:T(8,128)(2,1)S(1)}, bf16[32,1024]{1,0:T(8,128)(2,1)S(1)}, u32[]{:S(2)}, u32[]{:S(2)}) %collective-permute-start) | collective-permute-done | bytes 65568 | tf_op jit(solution)/shard_map/ppermute | solution.py:26
  13.2 1.1 %collective-permute-done.1.refs_2_ = bf16[32,1024]{1,0:T(8,128)(2,1)S(1)} collective-permute-done((bf16[32,1024]{1,0:T(8,128)(2,1)S(1)}, bf16[32,1024]{1,0:T(8,128)(2,1)S(1)}, u32[]{:S(2)}, u32[]{:S(2)}) %collective-permute-start.1) | collective-permute-done | bytes 65568 | tf_op jit(solution)/shard_map/ppermute | solution.py:26
  14.6 1.6 %collective-permute-start.4 = (bf16[64,896]{1,0:T(8,128)(2,1)S(1)}, bf16[64,896]{1,0:T(8,128)(2,1)S(1)}, u32[]{:S(2)}, u32[]{:S(2)}) collective-permute-start(bf16[64,896]{1,0:T(8,128)(2,1)S(1)} %pad_maximum_fusion.2), channel_id=1, source_target_pairs={{0,2},{1,3},{2,0},{3,1},{4,6},{5,7},{6,4},{7,5},{8,10},{9,11},{10,... | collective-permute-start | bytes 344072 | tf_op jit(solution)/shard_map/ppermute | solution.py:26
  16.3 3.2 %collective-permute-done.4 = bf16[64,896]{1,0:T(8,128)(2,1)S(1)} collective-permute-done((bf16[64,896]{1,0:T(8,128)(2,1)S(1)}, bf16[64,896]{1,0:T(8,128)(2,1)S(1)}, u32[]{:S(2)}, u32[]{:S(2)}) %collective-permute-start.4) | collective-permute-done | bytes 114720 | tf_op jit(solution)/shard_map/ppermute | solution.py:26
  19.6 1.6 %collective-permute-start.8 = (bf16[2,64,640]{2,1,0:T(8,128)(2,1)S(1)}, bf16[2,64,640]{2,1,0:T(8,128)(2,1)S(1)}, u32[]{:S(2)}, u32[]{:S(2)}) collective-permute-start(bf16[2,64,640]{2,1,0:T(8,128)(2,1)S(1)} %shard_map.124.refs_0_), channel_id=1, source_target_pairs={{0,2},{1,3},{2,0},{3,1},{4,6},{5,7},{6,4},{7,5},{8,10},{9,11},{10,... | collective-permute-start | bytes 491528 | tf_op jit(solution)/shard_map/ppermute | solution.py:26
  21.2 4.3 %shard_map.125.act = bf16[128,2048]{1,0:T(8,128)(2,1)S(1)} custom-call(bf16[32,1024]{1,0:T(8,128)(2,1)S(1)} %shard_map.122.refs_0_, bf16[32,1024]{1,0:T(8,128)(2,1)S(1)} %collective-permute-done.refs_1_, bf16[32,1024]{1,0:T(8,128)(2,1)S(1)} %collective-permute-done.1.refs_2_, bf16[32,1024]{1,0:T(8,128)(2,1)S(1)} %collective-permute-done.2.refs_3_, ...), custom_call_target="tpu_custom_call" | custom-call | tf_op jit(solution)/shard_map/pallas_call | solution.py:45
  25.5 0.7 %shard_map.126 = bf16[128,896]{1,0:T(8,128)(2,1)S(1)} custom-call(bf16[128,2048]{1,0:T(8,128)(2,1)S(1)} %shard_map.125.act, bf16[2048,3584]{1,0:T(8,128)(2,1)S(1)} %bitcast.5), custom_call_target="tpu_custom_call" | custom-call | tf_op jit(solution)/shard_map/pallas_call | solution.py:45
  26.6 0.7 %shard_map.127 = bf16[128,896]{1,0:T(8,128)(2,1)S(1)} custom-call(bf16[128,2048]{1,0:T(8,128)(2,1)S(1)} %shard_map.125.act, bf16[2048,3584]{1,0:T(8,128)(2,1)S(1)} %bitcast.6), custom_call_target="tpu_custom_call" | custom-call | tf_op jit(solution)/shard_map/pallas_call | solution.py:45
  27.9 1.4 %collective-permute-start.11 = (bf16[128,896]{1,0:T(8,128)(2,1)S(1)}, bf16[128,896]{1,0:T(8,128)(2,1)S(1)}, u32[]{:S(2)}, u32[]{:S(2)}) collective-permute-start(bf16[128,896]{1,0:T(8,128)(2,1)S(1)} %add_convert_fusion), channel_id=1, source_target_pairs={{0,2},{1,3},{2,0},{3,1},{4,6},{5,7},{6,4},{7,5},{8,10},{9,11},{10,... | collective-permute-start | bytes 688136 | tf_op jit(solution)/shard_map/ppermute | solution.py:26
  29.3 1.3 %shard_map.128 = (bf16[128,896]{1,0:T(8,128)(2,1)S(1)}, bf16[128,896]{1,0:T(8,128)(2,1)S(1)}) custom-call(bf16[128,2048]{1,0:T(8,128)(2,1)S(1)} %shard_map.125.act, bf16[2048,3584]{1,0:T(8,128)(2,1)S(1)} %bitcast.7), custom_call_target="tpu_custom_call" | custom-call | tf_op jit(solution)/shard_map/pallas_call | solution.py:45
  31.5 1.0 %collective-permute-done.12.theirs = bf16[2,64,512]{2,1,0:T(8,128)(2,1)S(1)} collective-permute-done((bf16[2,64,512]{2,1,0:T(8,128)(2,1)S(1)}, bf16[2,64,512]{2,1,0:T(8,128)(2,1)S(1)}, u32[]{:S(2)}, u32[]{:S(2)}) %collective-permute-start.12) | collective-permute-done | bytes 131104 | tf_op jit(solution)/shard_map/ppermute | solution.py:26
  32.5 0.7 %shard_map.130 = bf16[2,128,512]{2,1,0:T(8,128)(2,1)} custom-call(bf16[2,64,512]{2,1,0:T(8,128)(2,1)S(1)} %shard_map.129.mine, bf16[2,64,512]{2,1,0:T(8,128)(2,1)S(1)} %collective-permute-done.12.theirs), custom_call_target="tpu_custom_call" | custom-call | tf_op jit(solution)/shard_map/pallas_call | solution.py:45
  33.2 2.5 %collective-permute-done.11 = bf16[128,896]{1,0:T(8,128)(2,1)S(1)} collective-permute-done((bf16[128,896]{1,0:T(8,128)(2,1)S(1)}, bf16[128,896]{1,0:T(8,128)(2,1)S(1)}, u32[]{:S(2)}, u32[]{:S(2)}) %collective-permute-start.11) | collective-permute-done | bytes 229408 | tf_op jit(solution)/shard_map/ppermute | solution.py:26
  35.8 1.8 %collective-permute-start.13 = (bf16[32,896]{1,0:T(8,128)(2,1)S(1)}, bf16[32,896]{1,0:T(8,128)(2,1)S(1)}, u32[]{:S(2)}, u32[]{:S(2)}) collective-permute-start(bf16[32,896]{1,0:T(8,128)(2,1)S(1)} %get-tuple-element.54), channel_id=1, source_target_pairs={{0,12},{4,8},{8,4},{12,0},{1,13},{5,9},{9,5},{13,1},{2,14},{6,10},... | collective-permute-start | bytes 172040 | tf_op jit(solution)/shard_map/ppermute | solution.py:26
  37.6 1.4 %collective-permute-start.14 = (bf16[32,896]{1,0:T(8,128)(2,1)S(1)}, bf16[32,896]{1,0:T(8,128)(2,1)S(1)}, u32[]{:S(2)}, u32[]{:S(2)}) collective-permute-start(bf16[32,896]{1,0:T(8,128)(2,1)S(1)} %get-tuple-element.53), channel_id=1, source_target_pairs={{0,8},{4,12},{8,0},{12,4},{1,9},{5,13},{9,1},{13,5},{2,10},{6,14},... | collective-permute-start | bytes 172040 | tf_op jit(solution)/shard_map/ppermute | solution.py:26
  39.0 1.4 %collective-permute-start.15 = (bf16[32,896]{1,0:T(8,128)(2,1)S(1)}, bf16[32,896]{1,0:T(8,128)(2,1)S(1)}, u32[]{:S(2)}, u32[]{:S(2)}) collective-permute-start(bf16[32,896]{1,0:T(8,128)(2,1)S(1)} %get-tuple-element.52), channel_id=1, source_target_pairs={{0,4},{4,0},{8,12},{12,8},{1,5},{5,1},{9,13},{13,9},{2,6},{6,2},{1... | collective-permute-start | bytes 172040 | tf_op jit(solution)/shard_map/ppermute | solution.py:26
  40.3 2.0 %collective-permute-done.13 = bf16[32,896]{1,0:T(8,128)(2,1)S(1)} collective-permute-done((bf16[32,896]{1,0:T(8,128)(2,1)S(1)}, bf16[32,896]{1,0:T(8,128)(2,1)S(1)}, u32[]{:S(2)}, u32[]{:S(2)}) %collective-permute-start.13) | collective-permute-done | bytes 57376 | tf_op jit(solution)/shard_map/ppermute | solution.py:26
  42.3 1.6 %collective-permute-done.14 = bf16[32,896]{1,0:T(8,128)(2,1)S(1)} collective-permute-done((bf16[32,896]{1,0:T(8,128)(2,1)S(1)}, bf16[32,896]{1,0:T(8,128)(2,1)S(1)}, u32[]{:S(2)}, u32[]{:S(2)}) %collective-permute-start.14) | collective-permute-done | bytes 57376 | tf_op jit(solution)/shard_map/ppermute | solution.py:26
  44.0 0.6 %add_convert_fusion.1 = bf16[32,896]{1,0:T(8,128)(2,1)} fusion(f32[32,896]{1,0:T(8,128)S(1)} %convert_add_fusion.1, bf16[32,896]{1,0:T(8,128)(2,1)S(1)} %collective-permute-done.15), kind=kLoop, calls=%fused_computation.5 | loop fusion | flops 86016 | bytes 229376 | tf_op jit(solution)/shard_map/convert_element_type | solution.py:324
  (58 shorter events, 2.6 us)
Async XLA Ops:
  0.6 6.2 %copy-start.4 = (bf16[2,512,512]{2,1,0:T(8,128)(2,1)S(1)}, bf16[2,512,512]{2,1,0:T(8,128)(2,1)}, u32[]{:S(2)}) copy-start(bf16[2,512,512]{2,1,0:T(8,128)(2,1)} %keys.1) | copy-start | bytes 3145732
  0.6 6.2 %copy-start.5 = (bf16[2,128,512]{2,1,0:T(8,128)(2,1)S(1)}, bf16[2,128,512]{2,1,0:T(8,128)(2,1)}, u32[]{:S(2)}) copy-start(bf16[2,128,512]{2,1,0:T(8,128)(2,1)} %q_lat) | copy-start | bytes 786436
  0.7 6.2 %copy-start.6 = (bf16[2,64,512]{2,1,0:T(8,128)(2,1)S(1)}, bf16[2,64,512]{2,1,0:T(8,128)(2,1)}, u32[]{:S(2)}) copy-start(bf16[2,64,512]{2,1,0:T(8,128)(2,1)} %rope.1) | copy-start | bytes 393220
  0.7 20.5 %copy-start = (bf16[8,3584,256]{2,1,0:T(8,128)(2,1)S(1)}, bf16[8,3584,256]{2,1,0:T(8,128)(2,1)}, u32[]{:S(2)}) copy-start(bf16[8,3584,256]{2,1,0:T(8,128)(2,1)} %refs_10_.1) | copy-start | bytes 44040196
  0.7 20.5 %copy-start.1 = (bf16[8,3584,256]{2,1,0:T(8,128)(2,1)S(1)}, bf16[8,3584,256]{2,1,0:T(8,128)(2,1)}, u32[]{:S(2)}) copy-start(bf16[8,3584,256]{2,1,0:T(8,128)(2,1)} %refs_11_.1) | copy-start | bytes 44040196
  0.7 20.5 %copy-start.2 = (bf16[32,3584]{1,0:T(8,128)(2,1)S(1)}, bf16[32,3584]{1,0:T(8,128)(2,1)}, u32[]{:S(2)}) copy-start(bf16[32,3584]{1,0:T(8,128)(2,1)} %refs_4_.1) | copy-start | bytes 688132
  0.7 20.5 %copy-start.3 = (bf16[3584,32]{0,1:T(8,128)(2,1)S(1)}, bf16[3584,32]{0,1:T(8,128)(2,1)}, u32[]{:S(2)}) copy-start(bf16[3584,32]{0,1:T(8,128)(2,1)} %param.13) | copy-start | bytes 688132
  1.8 7.6 %collective-permute-start.2 = (bf16[32,1024]{1,0:T(8,128)(2,1)S(1)}, bf16[32,1024]{1,0:T(8,128)(2,1)S(1)}, u32[]{:S(2)}, u32[]{:S(2)}) collective-permute-start(bf16[32,1024]{1,0:T(8,128)(2,1)S(1)} %shard_map.122.refs_0_), channel_id=1, source_target_pairs={{0,12},{4,8},{8,4},{12,0},{1,13},{5,9},{9,5},{13,1},{2,14},{6,10},... | collective-permute-start | bytes 196616 | tf_op jit(solution)/shard_map/ppermute | solution.py:26
  6.9 18.6 %slice-start = ((s8[14680064]{0:T(1024)(128)(4,1)}), s8[4194304]{0:T(1024)(128)(4,1)S(1)}, s32[]{:S(2)}) async-start(s8[14680064]{0:T(1024)(128)(4,1)} %bitcast.3), calls=%async_computation | async-start | bytes 8388608
  8.6 4.6 %collective-permute-start = (bf16[32,1024]{1,0:T(8,128)(2,1)S(1)}, bf16[32,1024]{1,0:T(8,128)(2,1)S(1)}, u32[]{:S(2)}, u32[]{:S(2)}) collective-permute-start(bf16[32,1024]{1,0:T(8,128)(2,1)S(1)} %shard_map.122.refs_0_), channel_id=1, source_target_pairs={{0,4},{4,0},{8,12},{12,8},{1,5},{5,1},{9,13},{13,9},{2,6},{6,2},{1... | collective-permute-start | bytes 196616 | tf_op jit(solution)/shard_map/ppermute | solution.py:26
  8.7 5.6 %collective-permute-start.1 = (bf16[32,1024]{1,0:T(8,128)(2,1)S(1)}, bf16[32,1024]{1,0:T(8,128)(2,1)S(1)}, u32[]{:S(2)}, u32[]{:S(2)}) collective-permute-start(bf16[32,1024]{1,0:T(8,128)(2,1)S(1)} %shard_map.122.refs_0_), channel_id=1, source_target_pairs={{0,8},{4,12},{8,0},{12,4},{1,9},{5,13},{9,1},{13,5},{2,10},{6,14},... | collective-permute-start | bytes 196616 | tf_op jit(solution)/shard_map/ppermute | solution.py:26
  9.3 5.0 %collective-permute-start.3 = (bf16[2,64,640]{2,1,0:T(8,128)(2,1)S(1)}, bf16[2,64,640]{2,1,0:T(8,128)(2,1)S(1)}, u32[]{:S(2)}, u32[]{:S(2)}) collective-permute-start(bf16[2,64,640]{2,1,0:T(8,128)(2,1)S(1)} %get-tuple-element.32), channel_id=1, source_target_pairs={{0,1},{1,0},{2,3},{3,2},{4,5},{5,4},{6,7},{7,6},{8,9},{9,8},{10,11... | collective-permute-start | bytes 491528 | tf_op jit(solution)/shard_map/ppermute | solution.py:26
  9.4 10.1 %collective-permute-start.5 = (bf16[32,896]{1,0:T(8,128)(2,1)S(1)}, bf16[32,896]{1,0:T(8,128)(2,1)S(1)}, u32[]{:S(2)}, u32[]{:S(2)}) collective-permute-start(bf16[32,896]{1,0:T(8,128)(2,1)S(1)} %slice.41), channel_id=1, source_target_pairs={{0,2},{1,3},{2,0},{3,1},{4,6},{5,7},{6,4},{7,5},{8,10},{9,11},{10,... | collective-permute-start | bytes 172040 | tf_op jit(solution)/shard_map/ppermute | solution.py:26
  14.6 4.9 %collective-permute-start.4 = (bf16[64,896]{1,0:T(8,128)(2,1)S(1)}, bf16[64,896]{1,0:T(8,128)(2,1)S(1)}, u32[]{:S(2)}, u32[]{:S(2)}) collective-permute-start(bf16[64,896]{1,0:T(8,128)(2,1)S(1)} %pad_maximum_fusion.2), channel_id=1, source_target_pairs={{0,2},{1,3},{2,0},{3,1},{4,6},{5,7},{6,4},{7,5},{8,10},{9,11},{10,... | collective-permute-start | bytes 344072 | tf_op jit(solution)/shard_map/ppermute | solution.py:26
  16.2 5.0 %collective-permute-start.6 = (bf16[96,896]{1,0:T(8,128)(2,1)S(1)}, bf16[96,896]{1,0:T(8,128)(2,1)S(1)}, u32[]{:S(2)}, u32[]{:S(2)}) collective-permute-start(bf16[96,896]{1,0:T(8,128)(2,1)S(1)} %pad_maximum_fusion.refs_5_), channel_id=1, source_target_pairs={{0,1},{1,0},{2,3},{3,2},{4,5},{5,4},{6,7},{7,6},{8,9},{9,8},{10,11... | collective-permute-start | bytes 516104 | tf_op jit(solution)/shard_map/ppermute | solution.py:26
  19.5 1.6 %collective-permute-start.7 = (bf16[96,896]{1,0:T(8,128)(2,1)S(1)}, bf16[96,896]{1,0:T(8,128)(2,1)S(1)}, u32[]{:S(2)}, u32[]{:S(2)}) collective-permute-start(bf16[96,896]{1,0:T(8,128)(2,1)S(1)} %pad_maximum_fusion.1.refs_6_), channel_id=1, source_target_pairs={{0,1},{1,0},{2,3},{3,2},{4,5},{5,4},{6,7},{7,6},{8,9},{9,8},{10,11... | collective-permute-start | bytes 516104 | tf_op jit(solution)/shard_map/ppermute | solution.py:26
  19.6 6.7 %collective-permute-start.8 = (bf16[2,64,640]{2,1,0:T(8,128)(2,1)S(1)}, bf16[2,64,640]{2,1,0:T(8,128)(2,1)S(1)}, u32[]{:S(2)}, u32[]{:S(2)}) collective-permute-start(bf16[2,64,640]{2,1,0:T(8,128)(2,1)S(1)} %shard_map.124.refs_0_), channel_id=1, source_target_pairs={{0,2},{1,3},{2,0},{3,1},{4,6},{5,7},{6,4},{7,5},{8,10},{9,11},{10,... | collective-permute-start | bytes 491528 | tf_op jit(solution)/shard_map/ppermute | solution.py:26
  26.3 1.6 %collective-permute-start.9 = (bf16[128,896]{1,0:T(8,128)(2,1)S(1)}, bf16[128,896]{1,0:T(8,128)(2,1)S(1)}, u32[]{:S(2)}, u32[]{:S(2)}) collective-permute-start(bf16[128,896]{1,0:T(8,128)(2,1)S(1)} %shard_map.126), channel_id=1, source_target_pairs={{0,1},{1,0},{2,3},{3,2},{4,5},{5,4},{6,7},{7,6},{8,9},{9,8},{10,11... | collective-permute-start | bytes 688136 | tf_op jit(solution)/shard_map/ppermute | solution.py:26
  27.9 7.8 %collective-permute-start.11 = (bf16[128,896]{1,0:T(8,128)(2,1)S(1)}, bf16[128,896]{1,0:T(8,128)(2,1)S(1)}, u32[]{:S(2)}, u32[]{:S(2)}) collective-permute-start(bf16[128,896]{1,0:T(8,128)(2,1)S(1)} %add_convert_fusion), channel_id=1, source_target_pairs={{0,2},{1,3},{2,0},{3,1},{4,6},{5,7},{6,4},{7,5},{8,10},{9,11},{10,... | collective-permute-start | bytes 688136 | tf_op jit(solution)/shard_map/ppermute | solution.py:26
  30.6 5.1 %collective-permute-start.10 = (bf16[128,896]{1,0:T(8,128)(2,1)S(1)}, bf16[128,896]{1,0:T(8,128)(2,1)S(1)}, u32[]{:S(2)}, u32[]{:S(2)}) collective-permute-start(bf16[128,896]{1,0:T(8,128)(2,1)S(1)} %get-tuple-element.44), channel_id=1, source_target_pairs={{0,1},{1,0},{2,3},{3,2},{4,5},{5,4},{6,7},{7,6},{8,9},{9,8},{10,11... | collective-permute-start | bytes 688136 | tf_op jit(solution)/shard_map/ppermute | solution.py:26
  31.0 1.5 %collective-permute-start.12 = (bf16[2,64,512]{2,1,0:T(8,128)(2,1)S(1)}, bf16[2,64,512]{2,1,0:T(8,128)(2,1)S(1)}, u32[]{:S(2)}, u32[]{:S(2)}) collective-permute-start(bf16[2,64,512]{2,1,0:T(8,128)(2,1)S(1)} %shard_map.129.mine), channel_id=1, source_target_pairs={{0,1},{1,0},{2,3},{3,2},{4,5},{5,4},{6,7},{7,6},{8,9},{9,8},{10,11... | collective-permute-start | bytes 393224 | tf_op jit(solution)/shard_map/ppermute | solution.py:26
  35.8 6.5 %collective-permute-start.13 = (bf16[32,896]{1,0:T(8,128)(2,1)S(1)}, bf16[32,896]{1,0:T(8,128)(2,1)S(1)}, u32[]{:S(2)}, u32[]{:S(2)}) collective-permute-start(bf16[32,896]{1,0:T(8,128)(2,1)S(1)} %get-tuple-element.54), channel_id=1, source_target_pairs={{0,12},{4,8},{8,4},{12,0},{1,13},{5,9},{9,5},{13,1},{2,14},{6,10},... | collective-permute-start | bytes 172040 | tf_op jit(solution)/shard_map/ppermute | solution.py:26
  37.6 6.3 %collective-permute-start.14 = (bf16[32,896]{1,0:T(8,128)(2,1)S(1)}, bf16[32,896]{1,0:T(8,128)(2,1)S(1)}, u32[]{:S(2)}, u32[]{:S(2)}) collective-permute-start(bf16[32,896]{1,0:T(8,128)(2,1)S(1)} %get-tuple-element.53), channel_id=1, source_target_pairs={{0,8},{4,12},{8,0},{12,4},{1,9},{5,13},{9,1},{13,5},{2,10},{6,14},... | collective-permute-start | bytes 172040 | tf_op jit(solution)/shard_map/ppermute | solution.py:26
  39.0 5.0 %collective-permute-start.15 = (bf16[32,896]{1,0:T(8,128)(2,1)S(1)}, bf16[32,896]{1,0:T(8,128)(2,1)S(1)}, u32[]{:S(2)}, u32[]{:S(2)}) collective-permute-start(bf16[32,896]{1,0:T(8,128)(2,1)S(1)} %get-tuple-element.52), channel_id=1, source_target_pairs={{0,4},{4,0},{8,12},{12,8},{1,5},{5,1},{9,13},{13,9},{2,6},{6,2},{1... | collective-permute-start | bytes 172040 | tf_op jit(solution)/shard_map/ppermute | solution.py:26
  (5 other events, 25.3 us)

commit v13 on v11

--- a/solution.py
+++ b/solution.py
@@ -267,8 +267,8 @@
     state = join([keep, send(give, "tp", other_core)], False)
     others = [s for s in reversed(range(1, n_dev)) if s != first + 1]
     rest = jnp.concatenate([near[s - 1] for s in others], axis=0)
-    rest, state = lax.optimization_barrier((rest, state))
     late = [send(rest, "tp", along_x(s, ways)) for s in range(1, spots)]
+    late, state = lax.optimization_barrier((late, state))
     mine = [jnp.concatenate(near, axis=0)]
     for a, b in zip(early, late):
         come = {s: b[i * rows : (i + 1) * rows] for i, s in enumerate(others)}

time: 44.2 us -> 43.9 us (level)
  no operation moved by 1% of the time
where the time goes in v13:
time: 43.9 us; the launch traced here: 43.8 us
  starting transfers between devices  17.5 us (40%)
  waiting for transfers between devices  13.3 us (30%)
  Pallas kernels  11 us (25%)
  between operations  1.01 us (2%)
  other arithmetic  0.85 us (2%)
    ppermute x16, starting transfers between devices, send(): return lax.ppermute(value, axis, [(i, target(i)) for i in range(size)])  17.5 us
    ppermute x16, waiting for transfers between devices, send(): return lax.ppermute(value, axis, [(i, target(i)) for i in range(size)])  13.3 us
    pallas_call x9, Pallas kernels, local_call(): pl.pallas_call(kernel, out_shape=outs, in_specs=specs, out_specs=jax.tree...  11 us
  transfers between devices with their start and end apart: 16, of which 6 were waited for; matrix products, arithmetic and copies ran while one was open for 0% of the time, Pallas kernels for 23%

profile of v13, /device:TPU:0, one launch (start us, length us, event | category | flops | bytes accessed | tf_op | source)
XLA Modules:
  0.0 43.8 jit_solution(2045469641032181693)
XLA Ops:
  0.7 1.0 %shard_map.122.refs_0_ = bf16[32,1024]{1,0:T(8,128)(2,1)S(1)} custom-call(bf16[32,3584]{1,0:T(8,128)(2,1)} %refs_4_.1, s32[8,32]{1,0:T(8,128)} %bitcast.9), custom_call_target="tpu_custom_call" | custom-call | flops 99999997952 | tf_op jit(solution)/shard_map/pallas_call | solution.py:45
  1.8 5.1 %collective-permute-start.2 = (bf16[32,1024]{1,0:T(8,128)(2,1)S(1)}, bf16[32,1024]{1,0:T(8,128)(2,1)S(1)}, u32[]{:S(2)}, u32[]{:S(2)}) collective-permute-start(bf16[32,1024]{1,0:T(8,128)(2,1)S(1)} %shard_map.122.refs_0_), channel_id=1, source_target_pairs={{0,12},{4,8},{8,4},{12,0},{1,13},{5,9},{9,5},{13,1},{2,14},{6,10},... | collective-permute-start | bytes 196616 | tf_op jit(solution)/shard_map/ppermute | solution.py:26
  6.9 1.7 %shard_map.123 = (bf16[2,64,640]{2,1,0:T(8,128)(2,1)S(1)}, bf16[2,64,640]{2,1,0:T(8,128)(2,1)S(1)}) custom-call(bf16[2,128,512]{2,1,0:T(8,128)(2,1)S(1)} %copy-done.5, bf16[2,64,128]{2,1,0:T(8,128)(2,1)S(1)} %copy-done.7, bf16[2,512,512]{2,1,0:T(8,128)(2,1)S(1)} %copy-done.4, bf16[2,64,512]{2,1,0:T(8,128)(2,1)S(1)} %copy-done.6, s32[2]{0:T(128)S(1)} %copy-done.8), custom_call_target="tpu_custom_call" | custom-call | flops 2000000000 | tf_op jit(solution)/shard_map/pallas_call | solution.py:45
  8.7 0.7 %collective-permute-start = (bf16[32,1024]{1,0:T(8,128)(2,1)S(1)}, bf16[32,1024]{1,0:T(8,128)(2,1)S(1)}, u32[]{:S(2)}, u32[]{:S(2)}) collective-permute-start(bf16[32,1024]{1,0:T(8,128)(2,1)S(1)} %shard_map.122.refs_0_), channel_id=1, source_target_pairs={{0,4},{4,0},{8,12},{12,8},{1,5},{5,1},{9,13},{13,9},{2,6},{6,2},{1... | collective-permute-start | bytes 196616 | tf_op jit(solution)/shard_map/ppermute | solution.py:26
  9.4 1.7 %collective-permute-start.5 = (bf16[32,896]{1,0:T(8,128)(2,1)S(1)}, bf16[32,896]{1,0:T(8,128)(2,1)S(1)}, u32[]{:S(2)}, u32[]{:S(2)}) collective-permute-start(bf16[32,896]{1,0:T(8,128)(2,1)S(1)} %slice.41), channel_id=1, source_target_pairs={{0,2},{1,3},{2,0},{3,1},{4,6},{5,7},{6,4},{7,5},{8,10},{9,11},{10,... | collective-permute-start | bytes 172040 | tf_op jit(solution)/shard_map/ppermute | solution.py:26
  11.0 2.9 %collective-permute-done.1.refs_2_ = bf16[32,1024]{1,0:T(8,128)(2,1)S(1)} collective-permute-done((bf16[32,1024]{1,0:T(8,128)(2,1)S(1)}, bf16[32,1024]{1,0:T(8,128)(2,1)S(1)}, u32[]{:S(2)}, u32[]{:S(2)}) %collective-permute-start.1) | collective-permute-done | bytes 65568 | tf_op jit(solution)/shard_map/ppermute | solution.py:26
  14.0 1.6 %collective-permute-start.3 = (bf16[64,896]{1,0:T(8,128)(2,1)S(1)}, bf16[64,896]{1,0:T(8,128)(2,1)S(1)}, u32[]{:S(2)}, u32[]{:S(2)}) collective-permute-start(bf16[64,896]{1,0:T(8,128)(2,1)S(1)} %pad_maximum_fusion.2), channel_id=1, source_target_pairs={{0,2},{1,3},{2,0},{3,1},{4,6},{5,7},{6,4},{7,5},{8,10},{9,11},{10,... | collective-permute-start | bytes 344072 | tf_op jit(solution)/shard_map/ppermute | solution.py:26
  15.6 0.3 shard_map.124.refs_0_
  15.9 2.9 %collective-permute-done.3 = bf16[64,896]{1,0:T(8,128)(2,1)S(1)} collective-permute-done((bf16[64,896]{1,0:T(8,128)(2,1)S(1)}, bf16[64,896]{1,0:T(8,128)(2,1)S(1)}, u32[]{:S(2)}, u32[]{:S(2)}) %collective-permute-start.3) | collective-permute-done | bytes 114720 | tf_op jit(solution)/shard_map/ppermute | solution.py:26
  19.0 1.6 %collective-permute-start.8 = (bf16[2,64,640]{2,1,0:T(8,128)(2,1)S(1)}, bf16[2,64,640]{2,1,0:T(8,128)(2,1)S(1)}, u32[]{:S(2)}, u32[]{:S(2)}) collective-permute-start(bf16[2,64,640]{2,1,0:T(8,128)(2,1)S(1)} %shard_map.124.refs_0_), channel_id=1, source_target_pairs={{0,2},{1,3},{2,0},{3,1},{4,6},{5,7},{6,4},{7,5},{8,10},{9,11},{10,... | collective-permute-start | bytes 491528 | tf_op jit(solution)/shard_map/ppermute | solution.py:26
  20.6 4.3 %shard_map.125.act = bf16[128,2048]{1,0:T(8,128)(2,1)S(1)} custom-call(bf16[32,1024]{1,0:T(8,128)(2,1)S(1)} %shard_map.122.refs_0_, bf16[32,1024]{1,0:T(8,128)(2,1)S(1)} %collective-permute-done.refs_1_, bf16[32,1024]{1,0:T(8,128)(2,1)S(1)} %collective-permute-done.1.refs_2_, bf16[32,1024]{1,0:T(8,128)(2,1)S(1)} %collective-permute-done.2.refs_3_, ...), custom_call_target="tpu_custom_call" | custom-call | tf_op jit(solution)/shard_map/pallas_call | solution.py:45
  24.9 0.7 %shard_map.126 = bf16[128,896]{1,0:T(8,128)(2,1)S(1)} custom-call(bf16[128,2048]{1,0:T(8,128)(2,1)S(1)} %shard_map.125.act, bf16[2048,3584]{1,0:T(8,128)(2,1)S(1)} %bitcast.5), custom_call_target="tpu_custom_call" | custom-call | tf_op jit(solution)/shard_map/pallas_call | solution.py:45
  25.9 1.3 %shard_map.127 = (bf16[128,896]{1,0:T(8,128)(2,1)S(1)}, bf16[128,896]{1,0:T(8,128)(2,1)S(1)}) custom-call(bf16[128,2048]{1,0:T(8,128)(2,1)S(1)} %shard_map.125.act, bf16[2048,3584]{1,0:T(8,128)(2,1)S(1)} %bitcast.6), custom_call_target="tpu_custom_call" | custom-call | tf_op jit(solution)/shard_map/pallas_call | solution.py:45
  27.3 1.4 %collective-permute-start.11 = (bf16[128,896]{1,0:T(8,128)(2,1)S(1)}, bf16[128,896]{1,0:T(8,128)(2,1)S(1)}, u32[]{:S(2)}, u32[]{:S(2)}) collective-permute-start(bf16[128,896]{1,0:T(8,128)(2,1)S(1)} %add_convert_fusion), channel_id=1, source_target_pairs={{0,2},{1,3},{2,0},{3,1},{4,6},{5,7},{6,4},{7,5},{8,10},{9,11},{10,... | collective-permute-start | bytes 688136 | tf_op jit(solution)/shard_map/ppermute | solution.py:26
  29.0 0.5 %collective-permute-start.12 = (bf16[2,64,512]{2,1,0:T(8,128)(2,1)S(1)}, bf16[2,64,512]{2,1,0:T(8,128)(2,1)S(1)}, u32[]{:S(2)}, u32[]{:S(2)}) collective-permute-start(bf16[2,64,512]{2,1,0:T(8,128)(2,1)S(1)} %shard_map.129.mine), channel_id=1, source_target_pairs={{0,1},{1,0},{2,3},{3,2},{4,5},{5,4},{6,7},{7,6},{8,9},{9,8},{10,11... | collective-permute-start | bytes 393224 | tf_op jit(solution)/shard_map/ppermute | solution.py:26
  29.5 0.7 %shard_map.128 = bf16[128,896]{1,0:T(8,128)(2,1)S(1)} custom-call(bf16[128,2048]{1,0:T(8,128)(2,1)S(1)} %shard_map.125.act, bf16[2048,3584]{1,0:T(8,128)(2,1)S(1)} %bitcast.7), custom_call_target="tpu_custom_call" | custom-call | tf_op jit(solution)/shard_map/pallas_call | solution.py:45
  30.2 0.3 collective-permute-done.12.theirs
  30.5 0.7 %shard_map.130 = bf16[2,128,512]{2,1,0:T(8,128)(2,1)} custom-call(bf16[2,64,512]{2,1,0:T(8,128)(2,1)S(1)} %shard_map.129.mine, bf16[2,64,512]{2,1,0:T(8,128)(2,1)S(1)} %collective-permute-done.12.theirs), custom_call_target="tpu_custom_call" | custom-call | tf_op jit(solution)/shard_map/pallas_call | solution.py:45
  31.2 3.9 %collective-permute-done.11 = bf16[128,896]{1,0:T(8,128)(2,1)S(1)} collective-permute-done((bf16[128,896]{1,0:T(8,128)(2,1)S(1)}, bf16[128,896]{1,0:T(8,128)(2,1)S(1)}, u32[]{:S(2)}, u32[]{:S(2)}) %collective-permute-start.11) | collective-permute-done | bytes 229408 | tf_op jit(solution)/shard_map/ppermute | solution.py:26
  35.3 2.0 %collective-permute-start.13 = (bf16[32,896]{1,0:T(8,128)(2,1)S(1)}, bf16[32,896]{1,0:T(8,128)(2,1)S(1)}, u32[]{:S(2)}, u32[]{:S(2)}) collective-permute-start(bf16[32,896]{1,0:T(8,128)(2,1)S(1)} %get-tuple-element.54), channel_id=1, source_target_pairs={{0,12},{4,8},{8,4},{12,0},{1,13},{5,9},{9,5},{13,1},{2,14},{6,10},... | collective-permute-start | bytes 172040 | tf_op jit(solution)/shard_map/ppermute | solution.py:26
  37.4 2.4 %collective-permute-start.15 = (bf16[32,896]{1,0:T(8,128)(2,1)S(1)}, bf16[32,896]{1,0:T(8,128)(2,1)S(1)}, u32[]{:S(2)}, u32[]{:S(2)}) collective-permute-start(bf16[32,896]{1,0:T(8,128)(2,1)S(1)} %get-tuple-element.52), channel_id=1, source_target_pairs={{0,4},{4,0},{8,12},{12,8},{1,5},{5,1},{9,13},{13,9},{2,6},{6,2},{1... | collective-permute-start | bytes 172040 | tf_op jit(solution)/shard_map/ppermute | solution.py:26
  39.8 1.7 %collective-permute-done.13 = bf16[32,896]{1,0:T(8,128)(2,1)S(1)} collective-permute-done((bf16[32,896]{1,0:T(8,128)(2,1)S(1)}, bf16[32,896]{1,0:T(8,128)(2,1)S(1)}, u32[]{:S(2)}, u32[]{:S(2)}) %collective-permute-start.13) | collective-permute-done | bytes 57376 | tf_op jit(solution)/shard_map/ppermute | solution.py:26
  41.5 1.6 %collective-permute-done.14 = bf16[32,896]{1,0:T(8,128)(2,1)S(1)} collective-permute-done((bf16[32,896]{1,0:T(8,128)(2,1)S(1)}, bf16[32,896]{1,0:T(8,128)(2,1)S(1)}, u32[]{:S(2)}, u32[]{:S(2)}) %collective-permute-start.14) | collective-permute-done | bytes 57376 | tf_op jit(solution)/shard_map/ppermute | solution.py:26
  43.1 0.6 %add_convert_fusion.1 = bf16[32,896]{1,0:T(8,128)(2,1)} fusion(f32[32,896]{1,0:T(8,128)S(1)} %convert_add_fusion.1, bf16[32,896]{1,0:T(8,128)(2,1)S(1)} %collective-permute-done.15), kind=kLoop, calls=%fused_computation.5 | loop fusion | flops 86016 | bytes 229376 | tf_op jit(solution)/shard_map/convert_element_type | solution.py:324
  (58 shorter events, 1.2 us)
Async XLA Ops:
  0.6 6.2 %copy-start.4 = (bf16[2,512,512]{2,1,0:T(8,128)(2,1)S(1)}, bf16[2,512,512]{2,1,0:T(8,128)(2,1)}, u32[]{:S(2)}) copy-start(bf16[2,512,512]{2,1,0:T(8,128)(2,1)} %keys.1) | copy-start | bytes 3145732
  0.6 6.2 %copy-start.5 = (bf16[2,128,512]{2,1,0:T(8,128)(2,1)S(1)}, bf16[2,128,512]{2,1,0:T(8,128)(2,1)}, u32[]{:S(2)}) copy-start(bf16[2,128,512]{2,1,0:T(8,128)(2,1)} %q_lat) | copy-start | bytes 786436
  0.7 6.2 %copy-start.6 = (bf16[2,64,512]{2,1,0:T(8,128)(2,1)S(1)}, bf16[2,64,512]{2,1,0:T(8,128)(2,1)}, u32[]{:S(2)}) copy-start(bf16[2,64,512]{2,1,0:T(8,128)(2,1)} %rope.1) | copy-start | bytes 393220
  0.7 19.8 %copy-start = (bf16[8,3584,256]{2,1,0:T(8,128)(2,1)S(1)}, bf16[8,3584,256]{2,1,0:T(8,128)(2,1)}, u32[]{:S(2)}) copy-start(bf16[8,3584,256]{2,1,0:T(8,128)(2,1)} %refs_10_.1) | copy-start | bytes 44040196
  0.7 19.8 %copy-start.1 = (bf16[8,3584,256]{2,1,0:T(8,128)(2,1)S(1)}, bf16[8,3584,256]{2,1,0:T(8,128)(2,1)}, u32[]{:S(2)}) copy-start(bf16[8,3584,256]{2,1,0:T(8,128)(2,1)} %refs_11_.1) | copy-start | bytes 44040196
  0.7 19.8 %copy-start.2 = (bf16[32,3584]{1,0:T(8,128)(2,1)S(1)}, bf16[32,3584]{1,0:T(8,128)(2,1)}, u32[]{:S(2)}) copy-start(bf16[32,3584]{1,0:T(8,128)(2,1)} %refs_4_.1) | copy-start | bytes 688132
  0.7 19.8 %copy-start.3 = (bf16[3584,32]{0,1:T(8,128)(2,1)S(1)}, bf16[3584,32]{0,1:T(8,128)(2,1)}, u32[]{:S(2)}) copy-start(bf16[3584,32]{0,1:T(8,128)(2,1)} %param.13) | copy-start | bytes 688132
  1.8 7.6 %collective-permute-start.2 = (bf16[32,1024]{1,0:T(8,128)(2,1)S(1)}, bf16[32,1024]{1,0:T(8,128)(2,1)S(1)}, u32[]{:S(2)}, u32[]{:S(2)}) collective-permute-start(bf16[32,1024]{1,0:T(8,128)(2,1)S(1)} %shard_map.122.refs_0_), channel_id=1, source_target_pairs={{0,12},{4,8},{8,4},{12,0},{1,13},{5,9},{9,5},{13,1},{2,14},{6,10},... | collective-permute-start | bytes 196616 | tf_op jit(solution)/shard_map/ppermute | solution.py:26
  6.9 18.0 %slice-start = ((s8[14680064]{0:T(1024)(128)(4,1)}), s8[4194304]{0:T(1024)(128)(4,1)S(1)}, s32[]{:S(2)}) async-start(s8[14680064]{0:T(1024)(128)(4,1)} %bitcast.3), calls=%async_computation | async-start | bytes 8388608
  8.6 5.3 %collective-permute-start.1 = (bf16[32,1024]{1,0:T(8,128)(2,1)S(1)}, bf16[32,1024]{1,0:T(8,128)(2,1)S(1)}, u32[]{:S(2)}, u32[]{:S(2)}) collective-permute-start(bf16[32,1024]{1,0:T(8,128)(2,1)S(1)} %shard_map.122.refs_0_), channel_id=1, source_target_pairs={{0,8},{4,12},{8,0},{12,4},{1,9},{5,13},{9,1},{13,5},{2,10},{6,14},... | collective-permute-start | bytes 196616 | tf_op jit(solution)/shard_map/ppermute | solution.py:26
  8.7 5.2 %collective-permute-start = (bf16[32,1024]{1,0:T(8,128)(2,1)S(1)}, bf16[32,1024]{1,0:T(8,128)(2,1)S(1)}, u32[]{:S(2)}, u32[]{:S(2)}) collective-permute-start(bf16[32,1024]{1,0:T(8,128)(2,1)S(1)} %shard_map.122.refs_0_), channel_id=1, source_target_pairs={{0,4},{4,0},{8,12},{12,8},{1,5},{5,1},{9,13},{13,9},{2,6},{6,2},{1... | collective-permute-start | bytes 196616 | tf_op jit(solution)/shard_map/ppermute | solution.py:26
  9.3 6.3 %collective-permute-start.4 = (bf16[2,64,640]{2,1,0:T(8,128)(2,1)S(1)}, bf16[2,64,640]{2,1,0:T(8,128)(2,1)S(1)}, u32[]{:S(2)}, u32[]{:S(2)}) collective-permute-start(bf16[2,64,640]{2,1,0:T(8,128)(2,1)S(1)} %get-tuple-element.32), channel_id=1, source_target_pairs={{0,1},{1,0},{2,3},{3,2},{4,5},{5,4},{6,7},{7,6},{8,9},{9,8},{10,11... | collective-permute-start | bytes 491528 | tf_op jit(solution)/shard_map/ppermute | solution.py:26
  9.4 9.5 %collective-permute-start.5 = (bf16[32,896]{1,0:T(8,128)(2,1)S(1)}, bf16[32,896]{1,0:T(8,128)(2,1)S(1)}, u32[]{:S(2)}, u32[]{:S(2)}) collective-permute-start(bf16[32,896]{1,0:T(8,128)(2,1)S(1)} %slice.41), channel_id=1, source_target_pairs={{0,2},{1,3},{2,0},{3,1},{4,6},{5,7},{6,4},{7,5},{8,10},{9,11},{10,... | collective-permute-start | bytes 172040 | tf_op jit(solution)/shard_map/ppermute | solution.py:26
  14.0 4.9 %collective-permute-start.3 = (bf16[64,896]{1,0:T(8,128)(2,1)S(1)}, bf16[64,896]{1,0:T(8,128)(2,1)S(1)}, u32[]{:S(2)}, u32[]{:S(2)}) collective-permute-start(bf16[64,896]{1,0:T(8,128)(2,1)S(1)} %pad_maximum_fusion.2), channel_id=1, source_target_pairs={{0,2},{1,3},{2,0},{3,1},{4,6},{5,7},{6,4},{7,5},{8,10},{9,11},{10,... | collective-permute-start | bytes 344072 | tf_op jit(solution)/shard_map/ppermute | solution.py:26
  15.5 5.0 %collective-permute-start.6 = (bf16[96,896]{1,0:T(8,128)(2,1)S(1)}, bf16[96,896]{1,0:T(8,128)(2,1)S(1)}, u32[]{:S(2)}, u32[]{:S(2)}) collective-permute-start(bf16[96,896]{1,0:T(8,128)(2,1)S(1)} %pad_maximum_fusion.refs_5_), channel_id=1, source_target_pairs={{0,1},{1,0},{2,3},{3,2},{4,5},{5,4},{6,7},{7,6},{8,9},{9,8},{10,11... | collective-permute-start | bytes 516104 | tf_op jit(solution)/shard_map/ppermute | solution.py:26
  18.9 1.6 %collective-permute-start.7 = (bf16[96,896]{1,0:T(8,128)(2,1)S(1)}, bf16[96,896]{1,0:T(8,128)(2,1)S(1)}, u32[]{:S(2)}, u32[]{:S(2)}) collective-permute-start(bf16[96,896]{1,0:T(8,128)(2,1)S(1)} %pad_maximum_fusion.1.refs_6_), channel_id=1, source_target_pairs={{0,1},{1,0},{2,3},{3,2},{4,5},{5,4},{6,7},{7,6},{8,9},{9,8},{10,11... | collective-permute-start | bytes 516104 | tf_op jit(solution)/shard_map/ppermute | solution.py:26
  19.0 6.7 %collective-permute-start.8 = (bf16[2,64,640]{2,1,0:T(8,128)(2,1)S(1)}, bf16[2,64,640]{2,1,0:T(8,128)(2,1)S(1)}, u32[]{:S(2)}, u32[]{:S(2)}) collective-permute-start(bf16[2,64,640]{2,1,0:T(8,128)(2,1)S(1)} %shard_map.124.refs_0_), channel_id=1, source_target_pairs={{0,2},{1,3},{2,0},{3,1},{4,6},{5,7},{6,4},{7,5},{8,10},{9,11},{10,... | collective-permute-start | bytes 491528 | tf_op jit(solution)/shard_map/ppermute | solution.py:26
  25.7 1.6 %collective-permute-start.9 = (bf16[128,896]{1,0:T(8,128)(2,1)S(1)}, bf16[128,896]{1,0:T(8,128)(2,1)S(1)}, u32[]{:S(2)}, u32[]{:S(2)}) collective-permute-start(bf16[128,896]{1,0:T(8,128)(2,1)S(1)} %shard_map.126), channel_id=1, source_target_pairs={{0,1},{1,0},{2,3},{3,2},{4,5},{5,4},{6,7},{7,6},{8,9},{9,8},{10,11... | collective-permute-start | bytes 688136 | tf_op jit(solution)/shard_map/ppermute | solution.py:26
  27.3 7.9 %collective-permute-start.11 = (bf16[128,896]{1,0:T(8,128)(2,1)S(1)}, bf16[128,896]{1,0:T(8,128)(2,1)S(1)}, u32[]{:S(2)}, u32[]{:S(2)}) collective-permute-start(bf16[128,896]{1,0:T(8,128)(2,1)S(1)} %add_convert_fusion), channel_id=1, source_target_pairs={{0,2},{1,3},{2,0},{3,1},{4,6},{5,7},{6,4},{7,5},{8,10},{9,11},{10,... | collective-permute-start | bytes 688136 | tf_op jit(solution)/shard_map/ppermute | solution.py:26
  28.7 6.5 %collective-permute-start.10 = (bf16[128,896]{1,0:T(8,128)(2,1)S(1)}, bf16[128,896]{1,0:T(8,128)(2,1)S(1)}, u32[]{:S(2)}, u32[]{:S(2)}) collective-permute-start(bf16[128,896]{1,0:T(8,128)(2,1)S(1)} %get-tuple-element.44), channel_id=1, source_target_pairs={{0,1},{1,0},{2,3},{3,2},{4,5},{5,4},{6,7},{7,6},{8,9},{9,8},{10,11... | collective-permute-start | bytes 688136 | tf_op jit(solution)/shard_map/ppermute | solution.py:26
  29.0 1.5 %collective-permute-start.12 = (bf16[2,64,512]{2,1,0:T(8,128)(2,1)S(1)}, bf16[2,64,512]{2,1,0:T(8,128)(2,1)S(1)}, u32[]{:S(2)}, u32[]{:S(2)}) collective-permute-start(bf16[2,64,512]{2,1,0:T(8,128)(2,1)S(1)} %shard_map.129.mine), channel_id=1, source_target_pairs={{0,1},{1,0},{2,3},{3,2},{4,5},{5,4},{6,7},{7,6},{8,9},{9,8},{10,11... | collective-permute-start | bytes 393224 | tf_op jit(solution)/shard_map/ppermute | solution.py:26
  35.3 6.2 %collective-permute-start.13 = (bf16[32,896]{1,0:T(8,128)(2,1)S(1)}, bf16[32,896]{1,0:T(8,128)(2,1)S(1)}, u32[]{:S(2)}, u32[]{:S(2)}) collective-permute-start(bf16[32,896]{1,0:T(8,128)(2,1)S(1)} %get-tuple-element.54), channel_id=1, source_target_pairs={{0,12},{4,8},{8,4},{12,0},{1,13},{5,9},{9,5},{13,1},{2,14},{6,10},... | collective-permute-start | bytes 172040 | tf_op jit(solution)/shard_map/ppermute | solution.py:26
  37.3 5.8 %collective-permute-start.14 = (bf16[32,896]{1,0:T(8,128)(2,1)S(1)}, bf16[32,896]{1,0:T(8,128)(2,1)S(1)}, u32[]{:S(2)}, u32[]{:S(2)}) collective-permute-start(bf16[32,896]{1,0:T(8,128)(2,1)S(1)} %get-tuple-element.53), channel_id=1, source_target_pairs={{0,8},{4,12},{8,0},{12,4},{1,9},{5,13},{9,1},{13,5},{2,10},{6,14},... | collective-permute-start | bytes 172040 | tf_op jit(solution)/shard_map/ppermute | solution.py:26
  37.4 5.7 %collective-permute-start.15 = (bf16[32,896]{1,0:T(8,128)(2,1)S(1)}, bf16[32,896]{1,0:T(8,128)(2,1)S(1)}, u32[]{:S(2)}, u32[]{:S(2)}) collective-permute-start(bf16[32,896]{1,0:T(8,128)(2,1)S(1)} %get-tuple-element.52), channel_id=1, source_target_pairs={{0,4},{4,0},{8,12},{12,8},{1,5},{5,1},{9,13},{13,9},{2,6},{6,2},{1... | collective-permute-start | bytes 172040 | tf_op jit(solution)/shard_map/ppermute | solution.py:26
  (5 other events, 25.3 us)
